TPU v7x, 32 devices: a whole 2x2x4 slice. The times are simulated.
32 devices in a mesh: groups: 2 (over x), expert: 16 (over z, y, core).
Axes of the slice: x: 2, y: 2, z: 4, core: 2. Of those that a mesh axis runs over, the one named last changes fastest.
Arguments:
- residual: bfloat16 [512, 2880], P(('groups', 'expert')), parts along dimension 0, may hold values from -6 to 6
- norm_gain: float32 [2880], replicated, may hold values from 0.1 to 1.9
- expert_ids: int32 [512, 4], P(('groups', 'expert')), parts along dimension 0, may hold values from 0 to 7, all different within a row; in each aligned block of 16 rows (0 to 15, 16 to 31, ...) at most 16 rows name the same one
- expert_weights: float32 [512, 4], P(('groups', 'expert')), parts along dimension 0, may hold values from 0.2 to 1
- gate_proj: bfloat16 [16, 2880, 720], P('expert'), may hold values from -0.109375 to 0.109375
- up_proj: bfloat16 [16, 2880, 720], P('expert'), may hold values from -0.109375 to 0.109375
- down_proj: bfloat16 [16, 720, 2880], P('expert'), may hold values from -0.15625 to 0.15625
Outputs:
- mixed: bfloat16 [512, 2880], P(('groups', 'expert')), parts along dimension 0
There are 2 independent parts, one for each index of `groups`. A program takes and returns all parts, laid end to end along the dimension named above; an argument that names none is the same for every part. Nothing has to cross between parts.
Inputs may be any that keep to these rules, and one draw needn't show every extreme that they name: `expert_ids`: in each aligned block of 16 rows (the rows of one device) no expert is named by more than 16 entries.
All inputs are finite; a program needn't handle non-finite values.
Results may differ from a plain program's by a relative error of at most 0.0063.
Values may be sent and summed in bfloat16 or wider, within the bound.
No kernel may reach another device: no remote copies, remote signals or barrier semaphores. Data moves between devices by JAX's collectives and lax.ppermute only.
A program may use at most 64 MiB of HBM per device.

v0:
```python
import jax
import jax.numpy as jnp
from jax import lax
from jax.sharding import PartitionSpec as P


def partner(value, axis, bit):
    mask = 2**bit
    pairs = [(source, source ^ mask) for source in range(lax.axis_size(axis))]
    return lax.ppermute(value, axis, pairs)


def expert_half(block, gate_w, up_w, down_w):
    flat = block.reshape(-1, block.shape[-1])
    gate = jnp.dot(flat, gate_w, preferred_element_type=jnp.float32)
    upper = jnp.dot(flat, up_w, preferred_element_type=jnp.float32)
    act = (gate * jax.nn.sigmoid(1.702 * gate) * (upper + 1.0)).astype(jnp.bfloat16)
    out = jnp.dot(act, down_w, preferred_element_type=jnp.float32).astype(jnp.bfloat16)
    return out.reshape(block.shape[:-1] + (down_w.shape[1],))


def body(residual, norm_gain, expert_ids, expert_weights, gate_proj, up_proj, down_proj):
    rows, model = residual.shape
    chosen = expert_ids.shape[1]
    devices = lax.axis_size("expert")
    experts = devices // 2
    capacity = 2 * rows * chosen // experts
    half_cap = capacity // 2
    gate_w, up_w, down_w = (gate_proj[0], up_proj[0], down_proj[0])
    x = residual.astype(jnp.float32)
    scale = lax.rsqrt(jnp.mean(x * x, axis=-1, keepdims=True) + 1e-05)
    normed = (x * scale * norm_gain).astype(jnp.bfloat16)
    flat_ids = expert_ids.reshape(rows * chosen)
    onehot = (
        flat_ids[:, None] == lax.broadcasted_iota(jnp.int32, (rows * chosen, experts), 1)
    ).astype(jnp.int32)
    slot = jnp.sum(onehot * jnp.cumsum(onehot, axis=0), axis=1) - 1
    position = flat_ids * capacity + slot
    pick = (
        position[:, None] == lax.broadcasted_iota(jnp.int32, (rows * chosen, experts * capacity), 1)
    ).astype(jnp.float32)
    place_rows = jnp.sum(pick.reshape(rows, chosen, experts * capacity), axis=1)
    send = lax.dot_general(
        place_rows.astype(jnp.bfloat16),
        normed,
        (((0,), (0,)), ((), ())),
        preferred_element_type=jnp.float32,
    )
    send = send.astype(jnp.bfloat16).reshape(experts, capacity, model)
    outgoing = send.reshape(experts, 2, half_cap, model).reshape(devices, half_cap, model)
    arrived = lax.all_to_all(outgoing, "expert", split_axis=0, concat_axis=0, tiled=True)
    other = partner(arrived, "expert", 0)
    both = expert_half(jnp.stack((arrived, other)), gate_w, up_w, down_w)
    returned = partner(both[1], "expert", 0)
    finished = (both[0].astype(jnp.float32) + returned.astype(jnp.float32)).astype(jnp.bfloat16)
    back = lax.all_to_all(finished, "expert", split_axis=0, concat_axis=0, tiled=True)
    results = back.reshape(experts, capacity, model)
    weighted = jnp.sum(
        (pick * expert_weights.reshape(rows * chosen)[:, None]).reshape(
            rows, chosen, experts * capacity
        ),
        axis=1,
    )
    combined = jnp.dot(
        weighted,
        results.reshape(experts * capacity, model).astype(jnp.float32),
        precision=lax.Precision.HIGHEST,
    )
    return (x + combined).astype(jnp.bfloat16)


def solution(mesh):
    in_specs = (
        P(("groups", "expert"), None),
        P(),
        P(("groups", "expert"), None),
        P(("groups", "expert"), None),
        P("expert", None, None),
        P("expert", None, None),
        P("expert", None, None),
    )
    out_specs = P(("groups", "expert"), None)
    return jax.shard_map(body, mesh=mesh, in_specs=in_specs, out_specs=out_specs, check_vma=False)
```

profile of v0, /device:TPU:0, one launch (start us, length us, event | category | flops | bytes accessed | tf_op | source)
XLA Modules:
  0.0 77.0 jit_solution(909006792527382461)
XLA Ops:
  0.0 0.8 copy.23
  0.8 0.1 eq.20
  0.8 0.1 fusion.27
  0.9 0.1 reduce_window_sum.11
  1.0 0.2 select_reduce_fusion.1
  1.2 0.1 sub.7
  1.3 0.1 copy.24
  1.4 0.7 multiply_add_fusion
  2.1 1.0 %fusion.21 = f32[16]{0:T(128)S(1)} fusion(bf16[16,2880]{1,0:T(8,128)(2,1)} %param.7), kind=kLoop, calls=%fused_computation.21 | loop fusion | flops 138224 | bytes 92224 | tf_op jit(solution)/shard_map/reduce_sum | solution.py:31
  3.1 0.8 %convert_reduce_fusion = (bf16[16,128]{1,0:T(8,128)(2,1)S(1)}, f32[16,128]{1,0:T(8,128)S(1)}) fusion(s32[16,4]{0,1:T(4,128)S(1)} %multiply_add_fusion, f32[16,4]{0,1:T(4,128)} %param.10), kind=kLoop, calls=%fused_computation.26 | loop fusion | flops 36864 | bytes 12800 | tf_op jit(solution)/shard_map/reduce_sum | solution.py:42
  3.9 1.4 %convolution_convert_fusion = bf16[128,2880]{0,1:T(8,128)(2,1)S(1)} fusion(bf16[16,2880]{1,0:T(8,128)(2,1)} %param.7, f32[2880]{0:T(1024)} %param.8, f32[16]{0:T(128)S(1)} %add_rsqrt_fusion, bf16[16,128]{1,0:T(8,128)(2,1)S(1)} %get-tuple-element.5), kind=kOutput, calls=%fused_computation.7 | convolution fusion | flops 12349440 | bytes 845120 | tf_op jit(solution)/shard_map/dot_general | solution.py:43
  5.3 0.4 copy.25
  5.7 0.0 copy-start.1
  5.7 27.2 %all_to_all.10 = bf16[16,8,2880]{2,1,0:T(8,128)(2,1)S(1)} all-to-all(bf16[16,8,2880]{2,1,0:T(8,128)(2,1)S(1)} %bitcast.34), channel_id=1, replica_groups=mesh['groups'=2,'expert'=16] {'expert'}, dimensions={0} | all-to-all | bytes 1474560 | tf_op jit(solution)/shard_map/all_to_all | solution.py:51
  32.8 0.8 collective-permute-start
  33.6 1.9 %collective-permute-done = bf16[16,8,2880]{2,1,0:T(8,128)(2,1)S(1)} collective-permute-done((bf16[16,8,2880]{2,1,0:T(8,128)(2,1)S(1)}, bf16[16,8,2880]{2,1,0:T(8,128)(2,1)S(1)}, u32[]{:S(2)}, u32[]{:S(2)}) %collective-permute-start) | collective-permute-done | bytes 737312 | tf_op jit(solution)/shard_map/ppermute | solution.py:10
  35.4 0.2 pad_maximum_fusion
  35.6 0.0 copy-done.1
  35.6 1.3 %fusion.4 = f32[256,720]{0,1:T(8,128)S(1)} fusion(bf16[256,2880]{1,0:T(8,128)(2,1)S(1)} %bitcast.35, bf16[1,2880,720]{1,2,0:T(8,128)(2,1)S(1)} %copy-done.1), kind=kOutput, calls=%fused_computation.4 | convolution fusion | flops 1061683200 | bytes 6359040 | tf_op jit(solution)/shard_map/dot_general | solution.py:15
  37.0 9.4 %fusion.6 = bf16[256,2880]{0,1:T(8,128)(2,1)} fusion(bf16[1,720,2880]{2,1,0:T(8,128)(2,1)} %param.13, f32[256,720]{0,1:T(8,128)S(1)} %fusion.4, bf16[256,2880]{1,0:T(8,128)(2,1)S(1)} %bitcast.36, bf16[1,2880,720]{1,2,0:T(8,128)(2,1)} %param.12), kind=kOutput, calls=%fused_computation.6 | convolution fusion | flops 2125578240 | bytes 11980800 | tf_op jit(solution)/shard_map/dot_general | solution.py:18
  46.4 1.5 %fusion.31 = (bf16[128,2880]{0,1:T(8,128)(2,1)S(1)}, f32[128,2880]{0,1:T(8,128)S(1)}) fusion(bf16[256,2880]{0,1:T(8,128)(2,1)} %fusion.6), kind=kLoop, calls=%fused_computation.38 | loop fusion | flops 368640 | bytes 3686400 | tf_op jit(solution)/shard_map/slice | solution.py:54
  47.8 1.2 %copy.27 = bf16[128,2880]{1,0:T(8,128)(2,1)} copy(bf16[128,2880]{0,1:T(8,128)(2,1)S(1)} %get-tuple-element.7) | data formatting | bytes 1474560 | tf_op jit(solution)/shard_map/slice | solution.py:54
  49.0 0.4 collective-permute-start.1
  49.4 0.5 copy.26
  49.9 1.7 %collective-permute-done.1 = bf16[16,8,2880]{2,1,0:T(8,128)(2,1)} collective-permute-done((bf16[16,8,2880]{2,1,0:T(8,128)(2,1)}, bf16[16,8,2880]{2,1,0:T(8,128)(2,1)}, u32[]{:S(2)}, u32[]{:S(2)}) %collective-permute-start.1) | collective-permute-done | bytes 737312 | tf_op jit(solution)/shard_map/ppermute | solution.py:10
  51.6 1.3 %fusion.10 = bf16[16,8,2880]{2,1,0:T(8,128)(2,1)S(1)} fusion(f32[128,2880]{1,0:T(8,128)S(1)} %copy.26, bf16[16,8,2880]{2,1,0:T(8,128)(2,1)} %collective-permute-done.1), kind=kLoop, calls=%fused_computation.12 | loop fusion | flops 1105920 | bytes 2949120 | tf_op jit(solution)/shard_map/convert_element_type | solution.py:55
  52.9 0.0 copy-start
  52.9 23.0 %all_to_all.11 = bf16[16,8,2880]{2,1,0:T(8,128)(2,1)S(1)} all-to-all(bf16[16,8,2880]{2,1,0:T(8,128)(2,1)S(1)} %fusion.10), channel_id=1, replica_groups=mesh['groups'=2,'expert'=16] {'expert'}, dimensions={0} | all-to-all | bytes 1474560 | tf_op jit(solution)/shard_map/all_to_all | solution.py:56
  75.9 0.0 copy-done
  75.9 1.1 %fusion.9 = bf16[16,2880]{1,0:T(8,128)(2,1)} fusion(f32[16,128]{1,0:T(8,128)S(1)} %get-tuple-element.6, bf16[16,8,2880]{2,1,0:T(8,128)(2,1)S(1)} %all_to_all.11, bf16[16,2880]{1,0:T(8,128)(2,1)S(1)} %copy-done), kind=kOutput, calls=%fused_computation.9 | convolution fusion | flops 70917120 | bytes 929792 | tf_op jit(solution)/shard_map/dot_general | solution.py:64
  (2 shorter events, 0.0 us)
Async XLA Ops:
  5.7 30.0 %copy-start.1 = (bf16[1,2880,720]{1,2,0:T(8,128)(2,1)S(1)}, bf16[1,2880,720]{1,2,0:T(8,128)(2,1)}, u32[]{:S(2)}) copy-start(bf16[1,2880,720]{1,2,0:T(8,128)(2,1)} %param.11) | copy-start | bytes 12441604
  32.8 2.6 %collective-permute-start = (bf16[16,8,2880]{2,1,0:T(8,128)(2,1)S(1)}, bf16[16,8,2880]{2,1,0:T(8,128)(2,1)S(1)}, u32[]{:S(2)}, u32[]{:S(2)}) collective-permute-start(bf16[16,8,2880]{2,1,0:T(8,128)(2,1)S(1)} %all_to_all.10), channel_id=1, source_target_pairs={{0,1},{1,0},{2,3},{3,2},{4,5},{5,4},{6,7},{7,6},{8,9},{9,8},{10,11... | collective-permute-start | bytes 2211848 | tf_op jit(solution)/shard_map/ppermute | solution.py:10
  49.0 2.6 %collective-permute-start.1 = (bf16[16,8,2880]{2,1,0:T(8,128)(2,1)}, bf16[16,8,2880]{2,1,0:T(8,128)(2,1)}, u32[]{:S(2)}, u32[]{:S(2)}) collective-permute-start(bf16[16,8,2880]{2,1,0:T(8,128)(2,1)} %bitcast.8), channel_id=1, source_target_pairs={{0,1},{1,0},{2,3},{3,2},{4,5},{5,4},{6,7},{7,6},{8,9},{9,8},{10,11... | collective-permute-start | bytes 2211848 | tf_op jit(solution)/shard_map/ppermute | solution.py:10
  52.9 23.0 %copy-start = (bf16[16,2880]{1,0:T(8,128)(2,1)S(1)}, bf16[16,2880]{1,0:T(8,128)(2,1)}, u32[]{:S(2)}) copy-start(bf16[16,2880]{1,0:T(8,128)(2,1)} %param.7) | copy-start | bytes 276484
where the time goes:
time: 77.7 us; the launch traced here: 77 us
  blocking collectives  50.2 us (65%)
  matrix products  13.2 us (17%)
  other arithmetic  5.79 us (7%)
  waiting for transfers between devices  3.61 us (5%)
  local copies, waits for them, and re-layouts  3.03 us (4%)
  starting transfers between devices  1.13 us (1%)
    all_to_all x1, blocking collectives, body(): lax.all_to_all(outgoing, 'expert', split_axis=0, concat_axis=0, tiled=True)  27.2 us
    all_to_all x1, blocking collectives, body(): lax.all_to_all(finished, 'expert', split_axis=0, concat_axis=0, tiled=True)  23 us
    dot_general x1, matrix products, expert_half(): jnp.dot(act, down_w, preferred_element_type=jnp.float32)  9.39 us
    ppermute x2, waiting for transfers between devices, partner(): return lax.ppermute(value, axis, pairs)  3.61 us
  transfers between devices with their start and end apart: 2, of which 2 were waited for; matrix products, arithmetic and copies ran while one was open for 1% of the time, Pallas kernels for 0%

commit v1 on v0

v1 whole, which is shorter than its diff:
```python
import jax
import jax.numpy as jnp
from jax import lax
from jax.sharding import PartitionSpec as P


def partner(value, axis, bit):
    mask = 2**bit
    pairs = [(source, source ^ mask) for source in range(lax.axis_size(axis))]
    return lax.ppermute(value, axis, pairs)


def expert_half(flat, gate_w, up_w, down_w):
    gate = jnp.dot(flat, gate_w, preferred_element_type=jnp.float32)
    upper = jnp.dot(flat, up_w, preferred_element_type=jnp.float32)
    act = (gate * jax.nn.sigmoid(1.702 * gate) * (upper + 1.0)).astype(jnp.bfloat16)
    return jnp.dot(act, down_w, preferred_element_type=jnp.float32).astype(jnp.bfloat16)


def normalised(rows, norm_gain):
    x = rows.astype(jnp.float32)
    scale = lax.rsqrt(jnp.mean(x * x, axis=-1, keepdims=True) + 1e-05)
    return (x * scale * norm_gain).astype(jnp.bfloat16)


def pair_sum(mine, theirs):
    return (mine.astype(jnp.float32) + theirs.astype(jnp.float32)).astype(jnp.bfloat16)


def slots(residual, norm_gain, expert_ids, expert_weights, gate_proj, up_proj, down_proj):
    rows, model = residual.shape
    chosen = expert_ids.shape[1]
    devices = lax.axis_size("expert")
    experts = devices // 2
    capacity = 2 * rows * chosen // experts
    half_cap = capacity // 2
    gate_w, up_w, down_w = (gate_proj[0], up_proj[0], down_proj[0])
    normed = normalised(residual, norm_gain)
    flat_ids = expert_ids.reshape(rows * chosen)
    onehot = (
        flat_ids[:, None] == lax.broadcasted_iota(jnp.int32, (rows * chosen, experts), 1)
    ).astype(jnp.int32)
    slot = jnp.sum(onehot * jnp.cumsum(onehot, axis=0), axis=1) - 1
    position = flat_ids * capacity + slot
    pick = (
        position[:, None] == lax.broadcasted_iota(jnp.int32, (rows * chosen, experts * capacity), 1)
    ).astype(jnp.float32)
    place_rows = jnp.sum(pick.reshape(rows, chosen, experts * capacity), axis=1)
    send = lax.dot_general(
        place_rows.astype(jnp.bfloat16),
        normed,
        (((0,), (0,)), ((), ())),
        preferred_element_type=jnp.float32,
    )
    outgoing = send.astype(jnp.bfloat16).reshape(devices, half_cap, model)
    arrived = lax.all_to_all(outgoing, "expert", split_axis=0, concat_axis=0, tiled=True)
    other = partner(arrived, "expert", 0)
    both = jnp.stack((arrived, other)).reshape(2 * devices * half_cap, model)
    both = expert_half(both, gate_w, up_w, down_w).reshape(2, devices, half_cap, model)
    returned = partner(both[1], "expert", 0)
    finished = pair_sum(both[0], returned)
    back = lax.all_to_all(finished, "expert", split_axis=0, concat_axis=0, tiled=True)
    weighted = jnp.sum(
        (pick * expert_weights.reshape(rows * chosen)[:, None]).reshape(
            rows, chosen, experts * capacity
        ),
        axis=1,
    )
    combined = jnp.dot(
        weighted,
        back.reshape(experts * capacity, model).astype(jnp.float32),
        precision=lax.Precision.HIGHEST,
    )
    return (residual.astype(jnp.float32) + combined).astype(jnp.bfloat16)


def ring_order(chips):
    return list(range(0, chips, 2)) + list(range(1, chips, 2))[::-1]


def ring(residual, norm_gain, expert_ids, expert_weights, gate_proj, up_proj, down_proj):
    rows, model = residual.shape
    devices = lax.axis_size("expert")
    chips = devices // 2
    far = chips // 2
    order = ring_order(chips)
    gate_w, up_w, down_w = (gate_proj[0], up_proj[0], down_proj[0])
    me = lax.axis_index("expert")
    core = me % 2

    def at(position, of_core):
        return 2 * order[position % chips] + of_core

    def ringwise(value, hops):
        pairs = [(at(i, 0), at(i + hops, 0)) for i in range(chips)]
        pairs += [(at(i, 1), at(i - hops, 1)) for i in range(chips)]
        return lax.ppermute(value, "expert", pairs)

    def swap(value):
        return partner(value, "expert", 0)

    def expert_at(hops):
        table = [0] * devices
        for i in range(chips):
            table[at(i, 0)] = order[(i + hops) % chips]
            table[at(i, 1)] = order[(i - hops) % chips]
        return jnp.take(jnp.array(table, jnp.int32), me)

    def weight_of(ids, weights, hops):
        return jnp.sum(jnp.where(ids == expert_at(hops), weights, 0.0), axis=1, keepdims=True)

    def run(block):
        return expert_half(normalised(block, norm_gain), gate_w, up_w, down_w)

    x = residual
    away = ringwise(x, far)
    chip_rows = jnp.concatenate((x, swap(x)))
    ids = jnp.concatenate((expert_ids, swap(expert_ids)))
    weights = jnp.concatenate((expert_weights, swap(expert_weights)))
    total = jnp.zeros((2 * rows, model), jnp.float32)
    travelling = chip_rows
    for hops in range(1, far):
        travelling = ringwise(travelling, 1)
        both = jnp.concatenate((travelling, swap(travelling)))
        if hops == 1:
            both = jnp.concatenate((both, chip_rows, away, swap(away)))
        out = run(both)
        block = 2 * rows
        done = pair_sum(out[:block], swap(out[block : 2 * block]))
        total += weight_of(ids, weights, hops) * ringwise(done, -hops).astype(jnp.float32)
        if hops == 1:
            here, there = (out[2 * block : 3 * block], out[3 * block :])
            here = pair_sum(here[:rows], swap(here[rows:]))
            there = pair_sum(there[:rows], swap(there[rows:]))
            own = weight_of(expert_ids, expert_weights, 0) * here.astype(jnp.float32)
            own += weight_of(expert_ids, expert_weights, far) * ringwise(there, far).astype(jnp.float32)
    own += total[:rows] + swap(total[rows:])
    return (x.astype(jnp.float32) + own).astype(jnp.bfloat16)


def body(residual, norm_gain, expert_ids, expert_weights, gate_proj, up_proj, down_proj):
    rows, chosen = expert_ids.shape
    chips = lax.axis_size("expert") // 2
    whole = 2 * rows * chosen // chips >= rows and chips % 4 == 0
    plan = ring if whole else slots
    return plan(residual, norm_gain, expert_ids, expert_weights, gate_proj, up_proj, down_proj)


def solution(mesh):
    in_specs = (
        P(("groups", "expert"), None),
        P(),
        P(("groups", "expert"), None),
        P(("groups", "expert"), None),
        P("expert", None, None),
        P("expert", None, None),
        P("expert", None, None),
    )
    out_specs = P(("groups", "expert"), None)
    return jax.shard_map(body, mesh=mesh, in_specs=in_specs, out_specs=out_specs, check_vma=False)
```

time: 77.7 us -> 80.1 us (1.031)
  blocking collectives: 50.2 us -> 0 us
  starting transfers between devices: 1.13 us -> 20 us
  matrix products: 13.2 us -> 28.8 us
  waiting for transfers between devices: 3.61 us -> 16.7 us
  local copies, waits for them, and re-layouts: 3.03 us -> 7.43 us
  between operations: 0.08 us -> 3.35 us
  other arithmetic: 5.79 us -> 3.44 us
    all_to_all x2 -> x0, blocking collectives: 50.2 us -> none  [the longest x1 27.2 us: body(): lax.all_to_all(outgoing, 'expert', split_axis=0, concat_axis=0, tiled=True)]
    ppermute x0 -> x8, waiting for transfers between devices: none -> 14.4 us  [ringwise(): return lax.ppermute(value, 'expert', pairs)]
    ppermute x0 -> x8, starting transfers between devices: none -> 13.8 us  [ringwise(): return lax.ppermute(value, 'expert', pairs)]
    dot_general x1 -> x3, matrix products: 1.34 us -> 10.8 us  [expert_half(): gate = jnp.dot(flat, gate_w, preferred_element_type=jnp.float32)]
    dot_general x1 -> x3, matrix products: 9.39 us -> 18.1 us  [expert_half(): jnp.dot(act, down_w, preferred_element_type=jnp.float32)]
    another operation x0 -> x5, local copies, waits for them, and re-layouts: none -> 6.35 us  [expert_at(): return jnp.take(jnp.array(table, jnp.int32), me)]
    ppermute x2 -> x13, starting transfers between devices: 1.13 us -> 6.12 us  [partner(): return lax.ppermute(value, axis, pairs)]
    dot_general x2 -> x0, matrix products: 2.44 us -> none  [the longest x1 1.38 us: body(): lax.dot_general(place_rows.astype(jnp.bfloat16), normed, (((0,), (0,)), (...]
  transfers between devices with their start and end apart: 2 -> 21, of which waited for: 2 -> 5; matrix products, arithmetic and copies ran while one was open for 1% -> 48% of each run, Pallas kernels for 0% -> 0%
where the time goes in v1:
time: 80.1 us; the launch traced here: 79.7 us
  matrix products  28.8 us (36%)
  starting transfers between devices  20 us (25%)
  waiting for transfers between devices  16.7 us (21%)
  local copies, waits for them, and re-layouts  7.43 us (9%)
  other arithmetic  3.44 us (4%)
  between operations  3.35 us (4%)
    dot_general x3, matrix products, expert_half(): jnp.dot(act, down_w, preferred_element_type=jnp.float32)  18.1 us
    ppermute x8, waiting for transfers between devices, ringwise(): return lax.ppermute(value, 'expert', pairs)  14.4 us
    ppermute x8, starting transfers between devices, ringwise(): return lax.ppermute(value, 'expert', pairs)  13.8 us
    dot_general x3, matrix products, expert_half(): gate = jnp.dot(flat, gate_w, preferred_element_type=jnp.float32)  10.8 us
    another operation x5, local copies, waits for them, and re-layouts, expert_at(): return jnp.take(jnp.array(table, jnp.int32), me)  6.35 us
    ppermute x13, starting transfers between devices, partner(): return lax.ppermute(value, axis, pairs)  6.12 us
    ppermute x13, waiting for transfers between devices, partner(): return lax.ppermute(value, axis, pairs)  2.22 us
  transfers between devices with their start and end apart: 21, of which 5 were waited for; matrix products, arithmetic and copies ran while one was open for 48% of the time, Pallas kernels for 0%

profile of v1, /device:TPU:0, one launch (start us, length us, event | category | flops | bytes accessed | tf_op | source)
XLA Modules:
  0.0 79.7 jit_solution(11347649617988703142)
XLA Ops:
  0.0 0.5 collective-permute-start
  0.5 1.1 %collective-permute-done = bf16[16,2880]{1,0:T(8,128)(2,1)S(1)} collective-permute-done((bf16[16,2880]{1,0:T(8,128)(2,1)}, bf16[16,2880]{1,0:T(8,128)(2,1)S(1)}, u32[]{:S(2)}, u32[]{:S(2)}) %collective-permute-start) | collective-permute-done | bytes 92192 | tf_op jit(solution)/shard_map/ppermute | solution.py:10
  1.6 0.9 %pad_maximum_fusion.2 = bf16[32,2880]{1,0:T(8,128)(2,1)S(1)} fusion(bf16[16,2880]{1,0:T(8,128)(2,1)S(1)} %collective-permute-done, bf16[16,2880]{1,0:T(8,128)(2,1)} %param.12), kind=kLoop, calls=%fused_computation.66 | loop fusion | flops 368640 | bytes 368640 | tf_op jit(solution)/shard_map/concatenate | solution.py:117
  2.5 3.0 %collective-permute-start.1 = (bf16[32,2880]{1,0:T(8,128)(2,1)S(1)}, bf16[32,2880]{1,0:T(8,128)(2,1)S(1)}, u32[]{:S(2)}, u32[]{:S(2)}) collective-permute-start(bf16[32,2880]{1,0:T(8,128)(2,1)S(1)} %pad_maximum_fusion.2), channel_id=1, source_target_pairs={{0,4},{4,8},{8,12},{12,14},{14,10},{10,6},{6,2},{2,0},{1,3},{5,1},... | collective-permute-start | bytes 552968 | tf_op jit(solution)/shard_map/ppermute | solution.py:97
  5.5 3.4 %collective-permute-start.3 = (bf16[16,2880]{1,0:T(8,128)(2,1)}, bf16[16,2880]{1,0:T(8,128)(2,1)S(1)}, u32[]{:S(2)}, u32[]{:S(2)}) collective-permute-start(bf16[16,2880]{1,0:T(8,128)(2,1)} %param.12), channel_id=1, source_target_pairs={{0,14},{4,10},{8,6},{12,2},{14,0},{10,4},{6,8},{2,12},{1,15},{5,11... | collective-permute-start | bytes 276488 | tf_op jit(solution)/shard_map/ppermute | solution.py:97
  8.9 0.5 collective-permute-start.8
  9.4 1.2 %dynamic-slice.22 = s32[1]{0:T(128)} dynamic-slice(s32[16]{0:T(128)} %constant.72.clone..sunk.2, s32[]{:T(128)S(6)} %select_n.42), dynamic_slice_sizes={1} | dynamic-slice | bytes 12 | solution.py:107
  10.7 1.2 %dynamic-slice.23 = s32[1]{0:T(128)} dynamic-slice(s32[16]{0:T(128)} %constant.75.clone..sunk.2, s32[]{:T(128)S(6)} %select_n.42), dynamic_slice_sizes={1} | dynamic-slice | bytes 12 | solution.py:107
  13.1 1.3 %dynamic-slice.24 = s32[1]{0:T(128)} dynamic-slice(s32[16]{0:T(128)} %constant.76.clone..sunk.2, s32[]{:T(128)S(6)} %select_n.42), dynamic_slice_sizes={1} | dynamic-slice | bytes 12 | solution.py:107
  15.1 1.2 %dynamic-slice.20 = s32[1]{0:T(128)} dynamic-slice(s32[16]{0:T(128)} %constant.73.clone..sunk.2, s32[]{:T(128)S(6)} %select_n.42), dynamic_slice_sizes={1} | dynamic-slice | bytes 12 | solution.py:107
  16.9 1.3 %dynamic-slice.21 = s32[1]{0:T(128)} dynamic-slice(s32[16]{0:T(128)} %constant.74.clone..sunk.2, s32[]{:T(128)S(6)} %select_n.42), dynamic_slice_sizes={1} | dynamic-slice | bytes 12 | solution.py:107
  18.9 0.0 collective-permute-done.9
  18.9 0.8 select_reduce_fusion.2
  19.7 0.1 collective-permute-start.4
  19.8 0.3 collective-permute-start.12
  20.1 1.5 %collective-permute-start.2 = (bf16[32,2880]{1,0:T(8,128)(2,1)S(1)}, bf16[32,2880]{1,0:T(8,128)(2,1)S(1)}, u32[]{:S(2)}, u32[]{:S(2)}) collective-permute-start(bf16[32,2880]{1,0:T(8,128)(2,1)S(1)} %collective-permute-done.1), channel_id=1, source_target_pairs={{0,1},{1,0},{2,3},{3,2},{4,5},{5,4},{6,7},{7,6},{8,9},{9,8},{10,11... | collective-permute-start | bytes 552968 | tf_op jit(solution)/shard_map/ppermute | solution.py:10
  21.6 1.0 %collective-permute-done.2 = bf16[32,2880]{1,0:T(8,128)(2,1)S(1)} collective-permute-done((bf16[32,2880]{1,0:T(8,128)(2,1)S(1)}, bf16[32,2880]{1,0:T(8,128)(2,1)S(1)}, u32[]{:S(2)}, u32[]{:S(2)}) %collective-permute-start.2) | collective-permute-done | bytes 184352 | tf_op jit(solution)/shard_map/ppermute | solution.py:10
  22.7 0.9 %constant_dynamic-update-slice_fusion.3 = bf16[128,2880]{1,0:T(8,128)(2,1)S(1)} fusion(bf16[128,2880]{1,0:T(8,128)(2,1)S(1)} %constant_dynamic-update-slice_fusion.4, bf16[16,2880]{1,0:T(8,128)(2,1)} %param.12), kind=kLoop, calls=%fused_computation.78 | loop fusion | bytes 186368
  23.7 0.2 fusion.27
  23.9 3.6 %fusion.16 = f32[128,720]{0,1:T(8,128)S(1)} fusion(bf16[1,2880,720]{1,2,0:T(8,128)(2,1)} %param.16, bf16[128,2880]{1,0:T(8,128)(2,1)S(1)} %constant_dynamic-update-slice_fusion, f32[2880]{0:T(1024)} %param.13, f32[128]{0:T(128)S(1)} %add_rsqrt_fusion.2), kind=kOutput, calls=%fused_computation.16 | convolution fusion | flops 532316160 | bytes 5265152 | tf_op jit(solution)/shard_map/dot_general | solution.py:14
  27.5 0.4 collective-permute-start.13
  28.0 5.6 %fusion.18 = bf16[128,2880]{1,0:T(8,128)(2,1)S(1)} fusion(bf16[1,720,2880]{2,1,0:T(8,128)(2,1)} %param.18, f32[128,720]{0,1:T(8,128)S(1)} %fusion.16, bf16[1,2880,720]{1,2,0:T(8,128)(2,1)} %param.17, bf16[128,2880]{1,0:T(8,128)(2,1)S(1)} %constant_dynamic-update-slice_fusion, f32[2880]{0:T(1024)S(1)} %copy-done.1, f32[128]{0:T(128)S(1)} %add_rsqrt_fusion.2), kind=kOutput, calls=%fused_computation.18 | convolution fusion | flops 1064263680 | bytes 10149632 | tf_op jit(solution)/shard_map/dot_general | solution.py:17
  33.5 0.2 collective-permute-start.10
  33.7 0.4 collective-permute-start.16
  34.2 0.2 fusion.51
  34.4 3.6 %fusion.14 = f32[64,720]{1,0:T(8,128)S(1)} fusion(bf16[1,2880,720]{1,2,0:T(8,128)(2,1)} %param.16, f32[2880]{0:T(1024)S(1)} %copy-done.1, f32[64]{0:T(128)S(1)} %add_rsqrt_fusion.1, bf16[32,2880]{1,0:T(8,128)(2,1)S(1)} %collective-permute-done.13, bf16[32,2880]{1,0:T(8,128)(2,1)S(1)} %collective-permute-done.12), kind=kOutput, calls=%fused_computation.14 | convolution fusion | flops 266711040 | bytes 4711936 | tf_op jit(solution)/shard_map/dot_general | solution.py:14
  38.0 6.2 %fusion.21 = bf16[64,2880]{1,0:T(8,128)(2,1)S(1)} fusion(bf16[1,720,2880]{2,1,0:T(8,128)(2,1)} %param.18, bf16[1,2880,720]{1,2,0:T(8,128)(2,1)} %param.17, f32[64,720]{1,0:T(8,128)S(1)} %fusion.14, f32[2880]{0:T(1024)S(1)} %copy-done.1, f32[64]{0:T(128)S(1)} %add_rsqrt_fusion.1, bf16[32,2880]{1,0:T(8,128)(2,1)S(1)} %collective-permute-done.13, ...), kind=kOutput, calls=%fused_computation.19 | convolution fusion | flops 532684800 | bytes 9227776 | tf_op jit(solution)/shard_map/dot_general | solution.py:17
  44.3 0.1 collective-permute-start.14
  44.4 0.4 collective-permute-start.17
  44.9 1.6 %collective-permute-start.11 = (bf16[32,2880]{1,0:T(8,128)(2,1)S(1)}, bf16[32,2880]{1,0:T(8,128)(2,1)S(1)}, u32[]{:S(2)}, u32[]{:S(2)}) collective-permute-start(bf16[32,2880]{1,0:T(8,128)(2,1)S(1)} %add_convert_fusion.2), channel_id=1, source_target_pairs={{0,2},{4,0},{8,4},{12,8},{14,12},{10,14},{6,10},{2,6},{1,5},{5,9},... | collective-permute-start | bytes 552968 | tf_op jit(solution)/shard_map/ppermute | solution.py:97
  46.5 0.2 fusion.54
  46.7 3.6 %fusion.12 = f32[64,720]{1,0:T(8,128)S(1)} fusion(bf16[1,2880,720]{1,2,0:T(8,128)(2,1)} %param.16, f32[64]{0:T(128)S(1)} %add_rsqrt_fusion, f32[2880]{0:T(1024)S(1)} %copy-done.1, bf16[32,2880]{1,0:T(8,128)(2,1)S(1)} %collective-permute-done.17, bf16[32,2880]{1,0:T(8,128)(2,1)S(1)} %collective-permute-done.16), kind=kOutput, calls=%fused_computation.12 | convolution fusion | flops 266711040 | bytes 4711936 | tf_op jit(solution)/shard_map/dot_general | solution.py:14
  50.3 0.0 copy-start.2
  50.3 0.0 copy-start.3
  50.3 0.0 copy-start
  50.3 6.3 %fusion.24 = bf16[64,2880]{1,0:T(8,128)(2,1)S(1)} fusion(bf16[1,720,2880]{2,1,0:T(8,128)(2,1)} %param.18, bf16[1,2880,720]{1,2,0:T(8,128)(2,1)} %param.17, f32[64,720]{1,0:T(8,128)S(1)} %fusion.12, f32[64]{0:T(128)S(1)} %add_rsqrt_fusion, f32[2880]{0:T(1024)S(1)} %copy-done.1, bf16[32,2880]{1,0:T(8,128)(2,1)S(1)} %collective-permute-done.17, ...), kind=kOutput, calls=%fused_computation.20 | convolution fusion | flops 532684800 | bytes 9227776 | tf_op jit(solution)/shard_map/dot_general | solution.py:17
  56.6 0.1 collective-permute-start.18
  56.8 1.7 %collective-permute-start.15 = (bf16[32,2880]{1,0:T(8,128)(2,1)S(1)}, bf16[32,2880]{1,0:T(8,128)(2,1)S(1)}, u32[]{:S(2)}, u32[]{:S(2)}) collective-permute-start(bf16[32,2880]{1,0:T(8,128)(2,1)S(1)} %add_convert_fusion.1), channel_id=1, source_target_pairs={{0,6},{4,2},{8,0},{12,4},{14,8},{10,12},{6,14},{2,10},{1,9},{5,13}... | collective-permute-start | bytes 552968 | tf_op jit(solution)/shard_map/ppermute | solution.py:97
  58.6 1.9 %collective-permute-start.19 = (bf16[32,2880]{1,0:T(8,128)(2,1)S(1)}, bf16[32,2880]{1,0:T(8,128)(2,1)S(1)}, u32[]{:S(2)}, u32[]{:S(2)}) collective-permute-start(bf16[32,2880]{1,0:T(8,128)(2,1)S(1)} %add_convert_fusion), channel_id=1, source_target_pairs={{0,10},{4,6},{8,2},{12,0},{14,4},{10,8},{6,12},{2,14},{1,13},{5,15... | collective-permute-start | bytes 552968 | tf_op jit(solution)/shard_map/ppermute | solution.py:97
  60.4 0.2 collective-permute-start.6
  60.6 0.4 collective-permute-start.5
  61.0 3.8 %collective-permute-done.15 = bf16[32,2880]{1,0:T(8,128)(2,1)S(1)} collective-permute-done((bf16[32,2880]{1,0:T(8,128)(2,1)S(1)}, bf16[32,2880]{1,0:T(8,128)(2,1)S(1)}, u32[]{:S(2)}, u32[]{:S(2)}) %collective-permute-start.15) | collective-permute-done | bytes 184352 | tf_op jit(solution)/shard_map/ppermute | solution.py:97
  64.8 4.8 %collective-permute-done.19 = bf16[32,2880]{1,0:T(8,128)(2,1)S(1)} collective-permute-done((bf16[32,2880]{1,0:T(8,128)(2,1)S(1)}, bf16[32,2880]{1,0:T(8,128)(2,1)S(1)}, u32[]{:S(2)}, u32[]{:S(2)}) %collective-permute-start.19) | collective-permute-done | bytes 184352 | tf_op jit(solution)/shard_map/ppermute | solution.py:97
  69.6 0.2 multiply_add_fusion
  69.8 1.7 %collective-permute-start.20 = (f32[16,2880]{1,0:T(8,128)S(1)}, f32[16,2880]{1,0:T(8,128)S(1)}, u32[]{:S(2)}, u32[]{:S(2)}) collective-permute-start(f32[16,2880]{1,0:T(8,128)S(1)} %slice.90), channel_id=1, source_target_pairs={{0,1},{1,0},{2,3},{3,2},{4,5},{5,4},{6,7},{7,6},{8,9},{9,8},{10,11... | collective-permute-start | bytes 552968 | tf_op jit(solution)/shard_map/ppermute | solution.py:10
  71.5 1.5 %collective-permute-start.7 = (bf16[16,2880]{1,0:T(8,128)(2,1)S(1)}, bf16[16,2880]{1,0:T(8,128)(2,1)S(1)}, u32[]{:S(2)}, u32[]{:S(2)}) collective-permute-start(bf16[16,2880]{1,0:T(8,128)(2,1)S(1)} %add_convert_fusion.3), channel_id=1, source_target_pairs={{0,14},{4,10},{8,6},{12,2},{14,0},{10,4},{6,8},{2,12},{1,15},{5,11... | collective-permute-start | bytes 276488 | tf_op jit(solution)/shard_map/ppermute | solution.py:97
  73.1 5.8 %collective-permute-done.7 = bf16[16,2880]{1,0:T(8,128)(2,1)S(1)} collective-permute-done((bf16[16,2880]{1,0:T(8,128)(2,1)S(1)}, bf16[16,2880]{1,0:T(8,128)(2,1)S(1)}, u32[]{:S(2)}, u32[]{:S(2)}) %collective-permute-start.7) | collective-permute-done | bytes 92192 | tf_op jit(solution)/shard_map/ppermute | solution.py:97
  78.9 0.8 fusion.85
  (39 shorter events, 0.4 us)
Async XLA Ops:
  0.0 28.0 %copy-start.1 = (f32[2880]{0:T(1024)S(1)}, f32[2880]{0:T(1024)}, u32[]{:S(2)}) copy-start(f32[2880]{0:T(1024)} %param.13) | copy-start | bytes 34564
  0.0 1.6 %collective-permute-start = (bf16[16,2880]{1,0:T(8,128)(2,1)}, bf16[16,2880]{1,0:T(8,128)(2,1)S(1)}, u32[]{:S(2)}, u32[]{:S(2)}) collective-permute-start(bf16[16,2880]{1,0:T(8,128)(2,1)} %param.12), channel_id=1, source_target_pairs={{0,1},{1,0},{2,3},{3,2},{4,5},{5,4},{6,7},{7,6},{8,9},{9,8},{10,11... | collective-permute-start | bytes 276488 | tf_op jit(solution)/shard_map/ppermute | solution.py:10
  2.5 17.3 %collective-permute-start.1 = (bf16[32,2880]{1,0:T(8,128)(2,1)S(1)}, bf16[32,2880]{1,0:T(8,128)(2,1)S(1)}, u32[]{:S(2)}, u32[]{:S(2)}) collective-permute-start(bf16[32,2880]{1,0:T(8,128)(2,1)S(1)} %pad_maximum_fusion.2), channel_id=1, source_target_pairs={{0,4},{4,8},{8,12},{12,14},{14,10},{10,6},{6,2},{2,0},{1,3},{5,1},... | collective-permute-start | bytes 552968 | tf_op jit(solution)/shard_map/ppermute | solution.py:97
  5.5 14.2 %collective-permute-start.3 = (bf16[16,2880]{1,0:T(8,128)(2,1)}, bf16[16,2880]{1,0:T(8,128)(2,1)S(1)}, u32[]{:S(2)}, u32[]{:S(2)}) collective-permute-start(bf16[16,2880]{1,0:T(8,128)(2,1)} %param.12), channel_id=1, source_target_pairs={{0,14},{4,10},{8,6},{12,2},{14,0},{10,4},{6,8},{2,12},{1,15},{5,11... | collective-permute-start | bytes 276488 | tf_op jit(solution)/shard_map/ppermute | solution.py:97
  8.9 10.0 %collective-permute-start.9 = (f32[16,4]{0,1:T(4,128)}, f32[16,4]{0,1:T(4,128)S(1)}, u32[]{:S(2)}, u32[]{:S(2)}) collective-permute-start(f32[16,4]{0,1:T(4,128)} %param.15), channel_id=1, source_target_pairs={{0,1},{1,0},{2,3},{3,2},{4,5},{5,4},{6,7},{7,6},{8,9},{9,8},{10,11... | collective-permute-start | bytes 776 | tf_op jit(solution)/shard_map/ppermute | solution.py:10
  8.9 10.0 %collective-permute-start.8 = (s32[16,4]{0,1:T(4,128)}, s32[16,4]{0,1:T(4,128)S(1)}, u32[]{:S(2)}, u32[]{:S(2)}) collective-permute-start(s32[16,4]{0,1:T(4,128)} %param.14), channel_id=1, source_target_pairs={{0,1},{1,0},{2,3},{3,2},{4,5},{5,4},{6,7},{7,6},{8,9},{9,8},{10,11... | collective-permute-start | bytes 776 | tf_op jit(solution)/shard_map/ppermute | solution.py:10
  19.7 3.9 %collective-permute-start.4 = (bf16[16,2880]{1,0:T(8,128)(2,1)S(1)}, bf16[16,2880]{1,0:T(8,128)(2,1)S(1)}, u32[]{:S(2)}, u32[]{:S(2)}) collective-permute-start(bf16[16,2880]{1,0:T(8,128)(2,1)S(1)} %collective-permute-done.3), channel_id=1, source_target_pairs={{0,1},{1,0},{2,3},{3,2},{4,5},{5,4},{6,7},{7,6},{8,9},{9,8},{10,11... | collective-permute-start | bytes 276488 | tf_op jit(solution)/shard_map/ppermute | solution.py:10
  19.8 7.7 %collective-permute-start.12 = (bf16[32,2880]{1,0:T(8,128)(2,1)S(1)}, bf16[32,2880]{1,0:T(8,128)(2,1)S(1)}, u32[]{:S(2)}, u32[]{:S(2)}) collective-permute-start(bf16[32,2880]{1,0:T(8,128)(2,1)S(1)} %collective-permute-done.1), channel_id=1, source_target_pairs={{0,4},{4,8},{8,12},{12,14},{14,10},{10,6},{6,2},{2,0},{1,3},{5,1},... | collective-permute-start | bytes 552968 | tf_op jit(solution)/shard_map/ppermute | solution.py:97
  20.1 2.6 %collective-permute-start.2 = (bf16[32,2880]{1,0:T(8,128)(2,1)S(1)}, bf16[32,2880]{1,0:T(8,128)(2,1)S(1)}, u32[]{:S(2)}, u32[]{:S(2)}) collective-permute-start(bf16[32,2880]{1,0:T(8,128)(2,1)S(1)} %collective-permute-done.1), channel_id=1, source_target_pairs={{0,1},{1,0},{2,3},{3,2},{4,5},{5,4},{6,7},{7,6},{8,9},{9,8},{10,11... | collective-permute-start | bytes 552968 | tf_op jit(solution)/shard_map/ppermute | solution.py:10
  27.5 6.7 %collective-permute-start.13 = (bf16[32,2880]{1,0:T(8,128)(2,1)S(1)}, bf16[32,2880]{1,0:T(8,128)(2,1)S(1)}, u32[]{:S(2)}, u32[]{:S(2)}) collective-permute-start(bf16[32,2880]{1,0:T(8,128)(2,1)S(1)} %collective-permute-done.12), channel_id=1, source_target_pairs={{0,1},{1,0},{2,3},{3,2},{4,5},{5,4},{6,7},{7,6},{8,9},{9,8},{10,11... | collective-permute-start | bytes 552968 | tf_op jit(solution)/shard_map/ppermute | solution.py:10
  33.5 11.3 %collective-permute-start.10 = (bf16[32,2880]{1,0:T(8,128)(2,1)S(1)}, bf16[32,2880]{1,0:T(8,128)(2,1)S(1)}, u32[]{:S(2)}, u32[]{:S(2)}) collective-permute-start(bf16[32,2880]{1,0:T(8,128)(2,1)S(1)} %slice.84), channel_id=1, source_target_pairs={{0,1},{1,0},{2,3},{3,2},{4,5},{5,4},{6,7},{7,6},{8,9},{9,8},{10,11... | collective-permute-start | bytes 552968 | tf_op jit(solution)/shard_map/ppermute | solution.py:10
  33.7 10.6 %collective-permute-start.16 = (bf16[32,2880]{1,0:T(8,128)(2,1)S(1)}, bf16[32,2880]{1,0:T(8,128)(2,1)S(1)}, u32[]{:S(2)}, u32[]{:S(2)}) collective-permute-start(bf16[32,2880]{1,0:T(8,128)(2,1)S(1)} %collective-permute-done.12), channel_id=1, source_target_pairs={{0,4},{4,8},{8,12},{12,14},{14,10},{10,6},{6,2},{2,0},{1,3},{5,1},... | collective-permute-start | bytes 552968 | tf_op jit(solution)/shard_map/ppermute | solution.py:97
  44.3 12.5 %collective-permute-start.14 = (bf16[32,2880]{1,0:T(8,128)(2,1)S(1)}, bf16[32,2880]{1,0:T(8,128)(2,1)S(1)}, u32[]{:S(2)}, u32[]{:S(2)}) collective-permute-start(bf16[32,2880]{1,0:T(8,128)(2,1)S(1)} %slice.86), channel_id=1, source_target_pairs={{0,1},{1,0},{2,3},{3,2},{4,5},{5,4},{6,7},{7,6},{8,9},{9,8},{10,11... | collective-permute-start | bytes 552968 | tf_op jit(solution)/shard_map/ppermute | solution.py:10
  44.4 2.1 %collective-permute-start.17 = (bf16[32,2880]{1,0:T(8,128)(2,1)S(1)}, bf16[32,2880]{1,0:T(8,128)(2,1)S(1)}, u32[]{:S(2)}, u32[]{:S(2)}) collective-permute-start(bf16[32,2880]{1,0:T(8,128)(2,1)S(1)} %collective-permute-done.16), channel_id=1, source_target_pairs={{0,1},{1,0},{2,3},{3,2},{4,5},{5,4},{6,7},{7,6},{8,9},{9,8},{10,11... | collective-permute-start | bytes 552968 | tf_op jit(solution)/shard_map/ppermute | solution.py:10
  44.9 16.1 %collective-permute-start.11 = (bf16[32,2880]{1,0:T(8,128)(2,1)S(1)}, bf16[32,2880]{1,0:T(8,128)(2,1)S(1)}, u32[]{:S(2)}, u32[]{:S(2)}) collective-permute-start(bf16[32,2880]{1,0:T(8,128)(2,1)S(1)} %add_convert_fusion.2), channel_id=1, source_target_pairs={{0,2},{4,0},{8,4},{12,8},{14,12},{10,14},{6,10},{2,6},{1,5},{5,9},... | collective-permute-start | bytes 552968 | tf_op jit(solution)/shard_map/ppermute | solution.py:97
  50.3 22.7 %copy-start.2 = (f32[16,4]{0,1:T(4,128)S(1)}, f32[16,4]{0,1:T(4,128)}, u32[]{:S(2)}) copy-start(f32[16,4]{0,1:T(4,128)} %param.15) | copy-start | bytes 772
  50.3 22.7 %copy-start.3 = (s32[16,4]{0,1:T(4,128)S(1)}, s32[16,4]{0,1:T(4,128)}, u32[]{:S(2)}) copy-start(s32[16,4]{0,1:T(4,128)} %param.14) | copy-start | bytes 772
  50.3 28.6 %copy-start = (bf16[16,2880]{1,0:T(8,128)(2,1)S(1)}, bf16[16,2880]{1,0:T(8,128)(2,1)}, u32[]{:S(2)}) copy-start(bf16[16,2880]{1,0:T(8,128)(2,1)} %param.12) | copy-start | bytes 276484
  56.6 1.9 %collective-permute-start.18 = (bf16[32,2880]{1,0:T(8,128)(2,1)S(1)}, bf16[32,2880]{1,0:T(8,128)(2,1)S(1)}, u32[]{:S(2)}, u32[]{:S(2)}) collective-permute-start(bf16[32,2880]{1,0:T(8,128)(2,1)S(1)} %slice.88), channel_id=1, source_target_pairs={{0,1},{1,0},{2,3},{3,2},{4,5},{5,4},{6,7},{7,6},{8,9},{9,8},{10,11... | collective-permute-start | bytes 552968 | tf_op jit(solution)/shard_map/ppermute | solution.py:10
  56.8 8.1 %collective-permute-start.15 = (bf16[32,2880]{1,0:T(8,128)(2,1)S(1)}, bf16[32,2880]{1,0:T(8,128)(2,1)S(1)}, u32[]{:S(2)}, u32[]{:S(2)}) collective-permute-start(bf16[32,2880]{1,0:T(8,128)(2,1)S(1)} %add_convert_fusion.1), channel_id=1, source_target_pairs={{0,6},{4,2},{8,0},{12,4},{14,8},{10,12},{6,14},{2,10},{1,9},{5,13}... | collective-permute-start | bytes 552968 | tf_op jit(solution)/shard_map/ppermute | solution.py:97
  58.6 11.0 %collective-permute-start.19 = (bf16[32,2880]{1,0:T(8,128)(2,1)S(1)}, bf16[32,2880]{1,0:T(8,128)(2,1)S(1)}, u32[]{:S(2)}, u32[]{:S(2)}) collective-permute-start(bf16[32,2880]{1,0:T(8,128)(2,1)S(1)} %add_convert_fusion), channel_id=1, source_target_pairs={{0,10},{4,6},{8,2},{12,0},{14,4},{10,8},{6,12},{2,14},{1,13},{5,15... | collective-permute-start | bytes 552968 | tf_op jit(solution)/shard_map/ppermute | solution.py:97
  60.4 11.1 %collective-permute-start.6 = (bf16[16,2880]{1,0:T(8,128)(2,1)S(1)}, bf16[16,2880]{1,0:T(8,128)(2,1)S(1)}, u32[]{:S(2)}, u32[]{:S(2)}) collective-permute-start(bf16[16,2880]{1,0:T(8,128)(2,1)S(1)} %get-tuple-element.111), channel_id=1, source_target_pairs={{0,1},{1,0},{2,3},{3,2},{4,5},{5,4},{6,7},{7,6},{8,9},{9,8},{10,11... | collective-permute-start | bytes 276488 | tf_op jit(solution)/shard_map/ppermute | solution.py:10
  60.6 12.5 %collective-permute-start.5 = (bf16[16,2880]{1,0:T(8,128)(2,1)S(1)}, bf16[16,2880]{1,0:T(8,128)(2,1)S(1)}, u32[]{:S(2)}, u32[]{:S(2)}) collective-permute-start(bf16[16,2880]{1,0:T(8,128)(2,1)S(1)} %get-tuple-element.110), channel_id=1, source_target_pairs={{0,1},{1,0},{2,3},{3,2},{4,5},{5,4},{6,7},{7,6},{8,9},{9,8},{10,11... | collective-permute-start | bytes 276488 | tf_op jit(solution)/shard_map/ppermute | solution.py:10
  69.8 9.1 %collective-permute-start.20 = (f32[16,2880]{1,0:T(8,128)S(1)}, f32[16,2880]{1,0:T(8,128)S(1)}, u32[]{:S(2)}, u32[]{:S(2)}) collective-permute-start(f32[16,2880]{1,0:T(8,128)S(1)} %slice.90), channel_id=1, source_target_pairs={{0,1},{1,0},{2,3},{3,2},{4,5},{5,4},{6,7},{7,6},{8,9},{9,8},{10,11... | collective-permute-start | bytes 552968 | tf_op jit(solution)/shard_map/ppermute | solution.py:10
  71.5 7.4 %collective-permute-start.7 = (bf16[16,2880]{1,0:T(8,128)(2,1)S(1)}, bf16[16,2880]{1,0:T(8,128)(2,1)S(1)}, u32[]{:S(2)}, u32[]{:S(2)}) collective-permute-start(bf16[16,2880]{1,0:T(8,128)(2,1)S(1)} %add_convert_fusion.3), channel_id=1, source_target_pairs={{0,14},{4,10},{8,6},{12,2},{14,0},{10,4},{6,8},{2,12},{1,15},{5,11... | collective-permute-start | bytes 276488 | tf_op jit(solution)/shard_map/ppermute | solution.py:97

commit v2 on v1

--- a/solution.py
+++ b/solution.py
@@ -1,6 +1,10 @@
+import functools
+
 import jax
 import jax.numpy as jnp
 from jax import lax
+from jax.experimental import pallas as pl
+from jax.experimental.pallas import tpu as pltpu
 from jax.sharding import PartitionSpec as P
 
 
@@ -74,8 +78,44 @@
     return (residual.astype(jnp.float32) + combined).astype(jnp.bfloat16)
 
 
-def ring_order(chips):
-    return list(range(0, chips, 2)) + list(range(1, chips, 2))[::-1]
+def expert_kernel(count, *refs):
+    blocks, (gain_ref, gate_ref, up_ref, down_ref) = refs[:count], refs[count : count + 4]
+    mine_ref, theirs_ref, normed_ref = refs[count + 4 :]
+    rows = blocks[0].shape[0]
+    for i, block in enumerate(blocks):
+        x = block[...].astype(jnp.float32)
+        scale = lax.rsqrt(jnp.mean(x * x, axis=-1, keepdims=True) + 1e-05)
+        normed_ref[pl.ds(i * rows, rows), :] = (x * scale * gain_ref[...]).astype(jnp.bfloat16)
+    normed = normed_ref[...]
+    across = (((1,), (1,)), ((), ()))
+    gate = lax.dot_general(normed, gate_ref[...], across, preferred_element_type=jnp.float32)
+    upper = lax.dot_general(normed, up_ref[...], across, preferred_element_type=jnp.float32)
+    act = (gate * jax.nn.sigmoid(1.702 * gate) * (upper + 1.0)).astype(jnp.bfloat16)
+    out = jnp.dot(act, down_ref[...], preferred_element_type=jnp.float32).astype(jnp.bfloat16)
+    half = rows * (count // 2)
+    mine_ref[...] = out[:half]
+    theirs_ref[...] = out[half:]
+
+
+def expert_parts(blocks, gain, gate_w, up_w, down_w):
+    count = len(blocks)
+    rows, model = blocks[0].shape
+    out = jax.ShapeDtypeStruct((rows * count // 2, model), jnp.bfloat16)
+    vmem = pl.BlockSpec(memory_space=pltpu.VMEM)
+    hidden = gate_w.shape[0]
+    return pl.pallas_call(
+        functools.partial(expert_kernel, count),
+        out_shape=(out, out),
+        in_specs=[vmem] * (count + 4),
+        out_specs=(vmem, vmem),
+        scratch_shapes=[pltpu.VMEM((rows * count, model), jnp.bfloat16)],
+        cost_estimate=pl.CostEstimate(
+            flops=6 * rows * count * model * hidden,
+            bytes_accessed=6 * model * hidden,
+            transcendentals=rows * count * hidden,
+        ),
+        compiler_params=pltpu.CompilerParams(vmem_limit_bytes=24 * 2**20),
+    )(*blocks, gain, gate_w, up_w, down_w)
 
 
 def ring(residual, norm_gain, expert_ids, expert_weights, gate_proj, up_proj, down_proj):
@@ -83,65 +123,59 @@
     devices = lax.axis_size("expert")
     chips = devices // 2
     far = chips // 2
-    order = ring_order(chips)
-    gate_w, up_w, down_w = (gate_proj[0], up_proj[0], down_proj[0])
-    me = lax.axis_index("expert")
-    core = me % 2
-
-    def at(position, of_core):
-        return 2 * order[position % chips] + of_core
+    order = list(range(0, chips, 2)) + list(range(1, chips, 2))[::-1]
+    held = [
+        pltpu.with_memory_space_constraint(w, pltpu.VMEM)
+        for w in (gate_proj[0].T, up_proj[0].T, down_proj[0])
+    ]
+    gain = norm_gain.reshape(1, model)
 
     def ringwise(value, hops):
-        pairs = [(at(i, 0), at(i + hops, 0)) for i in range(chips)]
-        pairs += [(at(i, 1), at(i - hops, 1)) for i in range(chips)]
+        pairs = [
+            (2 * order[i] + core, 2 * order[(i + hops) % chips] + core)
+            for i in range(chips)
+            for core in range(2)
+        ]
         return lax.ppermute(value, "expert", pairs)
 
     def swap(value):
         return partner(value, "expert", 0)
 
-    def expert_at(hops):
-        table = [0] * devices
-        for i in range(chips):
-            table[at(i, 0)] = order[(i + hops) % chips]
-            table[at(i, 1)] = order[(i - hops) % chips]
-        return jnp.take(jnp.array(table, jnp.int32), me)
-
-    def weight_of(ids, weights, hops):
-        return jnp.sum(jnp.where(ids == expert_at(hops), weights, 0.0), axis=1, keepdims=True)
-
-    def run(block):
-        return expert_half(normalised(block, norm_gain), gate_w, up_w, down_w)
+    chip = lax.axis_index("expert") // 2
+    place = jnp.where(chip % 2 == 0, chip // 2, chips - 1 - chip // 2)
+    on = (place + jnp.arange(chips)) % chips
+    expert = jnp.where(on < far, 2 * on, 2 * (chips - 1 - on) + 1)
+    weights = jnp.sum(
+        jnp.where(expert_ids[:, :, None] == expert[None, None, :], expert_weights[:, :, None], 0.0), axis=1
+    )
 
     x = residual
-    away = ringwise(x, far)
-    chip_rows = jnp.concatenate((x, swap(x)))
-    ids = jnp.concatenate((expert_ids, swap(expert_ids)))
-    weights = jnp.concatenate((expert_weights, swap(expert_weights)))
-    total = jnp.zeros((2 * rows, model), jnp.float32)
-    travelling = chip_rows
-    for hops in range(1, far):
-        travelling = ringwise(travelling, 1)
-        both = jnp.concatenate((travelling, swap(travelling)))
-        if hops == 1:
-            both = jnp.concatenate((both, chip_rows, away, swap(away)))
-        out = run(both)
-        block = 2 * rows
-        done = pair_sum(out[:block], swap(out[block : 2 * block]))
-        total += weight_of(ids, weights, hops) * ringwise(done, -hops).astype(jnp.float32)
-        if hops == 1:
-            here, there = (out[2 * block : 3 * block], out[3 * block :])
-            here = pair_sum(here[:rows], swap(here[rows:]))
-            there = pair_sum(there[:rows], swap(there[rows:]))
-            own = weight_of(expert_ids, expert_weights, 0) * here.astype(jnp.float32)
-            own += weight_of(expert_ids, expert_weights, far) * ringwise(there, far).astype(jnp.float32)
-    own += total[:rows] + swap(total[rows:])
-    return (x.astype(jnp.float32) + own).astype(jnp.bfloat16)
+    arrived = {0: x, far: ringwise(x, far)}
+    for way in (1, -1):
+        arrived[way] = ringwise(x, way)
+    for hops in range(2, far):
+        near = hops - 2 if hops > 2 else 1
+        for way in (1, -1):
+            arrived[way * hops] = ringwise(arrived[way * near], way * (hops - near))
+    near = [0, 1, -1, far]
+    beyond = [way * hops for hops in range(2, far) for way in (1, -1)]
+    finished = {}
+    for group in (near, beyond):
+        blocks = [arrived[hops] for hops in group]
+        mine, theirs = expert_parts(blocks + [swap(block) for block in blocks], gain, *held)
+        done = pair_sum(mine, swap(theirs)).reshape(len(group), rows, model)
+        for i, hops in enumerate(group):
+            finished[hops] = ringwise(done[i], -hops) if hops else done[i]
+    combined = jnp.zeros((rows, model), jnp.float32)
+    for hops, block in finished.items():
+        combined += weights[:, hops % chips][:, None] * block.astype(jnp.float32)
+    return (x.astype(jnp.float32) + combined).astype(jnp.bfloat16)
 
 
 def body(residual, norm_gain, expert_ids, expert_weights, gate_proj, up_proj, down_proj):
     rows, chosen = expert_ids.shape
     chips = lax.axis_size("expert") // 2
-    whole = 2 * rows * chosen // chips >= rows and chips % 4 == 0
+    whole = 2 * rows * chosen // chips >= rows and chips % 2 == 0 and chips >= 6
     plan = ring if whole else slots
     return plan(residual, norm_gain, expert_ids, expert_weights, gate_proj, up_proj, down_proj)
 

time: 80.1 us -> 58.3 us (0.73)
  matrix products: 28.8 us -> 0 us
  starting transfers between devices: 20 us -> 32.2 us
  waiting for transfers between devices: 16.7 us -> 9.23 us
  Pallas kernels: 0 us -> 7.09 us
  between operations: 3.35 us -> 0.1 us
  other arithmetic: 3.44 us -> 1.14 us
  local copies, waits for them, and re-layouts: 7.43 us -> 8.28 us
    dot_general x6 -> x0, matrix products: 28.8 us -> none  [the longest x3 18.1 us: expert_half(): jnp.dot(act, down_w, preferred_element_type=jnp.float32)]
    ppermute x8 -> x14, starting transfers between devices: 13.8 us -> 30.2 us  [ringwise(): return lax.ppermute(value, 'expert', pairs)]
    pallas_call x0 -> x2, Pallas kernels: none -> 7.09 us  [expert_parts(): pl.pallas_call(functools.partial(expert_kernel, count), out_shape=(out, o...]
    unnamed x13 -> x14, local copies, waits for them, and re-layouts: 0.99 us -> 7.5 us
    ppermute x8 -> x14, waiting for transfers between devices: 14.4 us -> 8.08 us  [ringwise(): return lax.ppermute(value, 'expert', pairs)]
    another operation x5 -> x0, local copies, waits for them, and re-layouts: 6.35 us -> none  [expert_at(): return jnp.take(jnp.array(table, jnp.int32), me)]
    ppermute x13 -> x10, starting transfers between devices: 6.12 us -> 2.03 us  [partner(): return lax.ppermute(value, axis, pairs)]
    reduce_sum x5 -> x1, other arithmetic: 1.41 us -> 0.07 us  [ring(): jnp.sum(jnp.where(expert_ids[:, :, None] == expert[None, None, :], expert...]
  transfers between devices with their start and end apart: 21 -> 24, of which waited for: 5 -> 7; matrix products, arithmetic and copies ran while one was open for 48% -> 2% of each run, Pallas kernels for 0% -> 12%
where the time goes in v2:
time: 58.3 us; the launch traced here: 58 us
  starting transfers between devices  32.2 us (55%)
  waiting for transfers between devices  9.23 us (16%)
  local copies, waits for them, and re-layouts  8.28 us (14%)
  Pallas kernels  7.09 us (12%)
  other arithmetic  1.14 us (2%)
    ppermute x14, starting transfers between devices, ringwise(): return lax.ppermute(value, 'expert', pairs)  30.2 us
    ppermute x14, waiting for transfers between devices, ringwise(): return lax.ppermute(value, 'expert', pairs)  8.08 us
    unnamed x14, local copies, waits for them, and re-layouts  7.5 us
    pallas_call x2, Pallas kernels, expert_parts(): pl.pallas_call(functools.partial(expert_kernel, count), out_shape=(out, o...  7.09 us
    ppermute x10, starting transfers between devices, partner(): return lax.ppermute(value, axis, pairs)  2.03 us
  transfers between devices with their start and end apart: 24, of which 7 were waited for; matrix products, arithmetic and copies ran while one was open for 2% of the time, Pallas kernels for 12%

profile of v2, /device:TPU:0, one launch (start us, length us, event | category | flops | bytes accessed | tf_op | source)
XLA Modules:
  0.0 58.0 jit_solution(15848848630483683319)
XLA Ops:
  0.0 3.0 %collective-permute-start = (bf16[16,2880]{1,0:T(8,128)(2,1)}, bf16[16,2880]{1,0:T(8,128)(2,1)S(1)}, u32[]{:S(2)}, u32[]{:S(2)}) collective-permute-start(bf16[16,2880]{1,0:T(8,128)(2,1)} %refs_0_.1), channel_id=1, source_target_pairs={{0,4},{1,5},{4,8},{5,9},{8,12},{9,13},{12,14},{13,15},{14,10},{15,... | collective-permute-start | bytes 276488 | tf_op jit(solution)/shard_map/ppermute | solution.py:139
  3.0 0.0 collective-permute-start.1
  3.0 5.0 %collective-permute-start.2 = (bf16[16,2880]{1,0:T(8,128)(2,1)}, bf16[16,2880]{1,0:T(8,128)(2,1)S(1)}, u32[]{:S(2)}, u32[]{:S(2)}) collective-permute-start(bf16[16,2880]{1,0:T(8,128)(2,1)} %refs_0_.1), channel_id=1, source_target_pairs={{0,14},{1,15},{4,10},{5,11},{8,6},{9,7},{12,2},{13,3},{14,0},{15,1... | collective-permute-start | bytes 276488 | tf_op jit(solution)/shard_map/ppermute | solution.py:139
  8.0 0.0 collective-permute-start.3
  8.0 0.5 collective-permute-start.4
  8.6 0.1 collective-permute-start.5
  8.6 2.7 %collective-permute-done.2.refs_3_ = bf16[16,2880]{1,0:T(8,128)(2,1)S(1)} collective-permute-done((bf16[16,2880]{1,0:T(8,128)(2,1)}, bf16[16,2880]{1,0:T(8,128)(2,1)S(1)}, u32[]{:S(2)}, u32[]{:S(2)}) %collective-permute-start.2) | collective-permute-done | bytes 92192 | tf_op jit(solution)/shard_map/ppermute | solution.py:139
  11.3 0.0 collective-permute-start.6
  11.3 0.7 %reshape.44.refs_8_ = f32[1,2880]{1,0:T(1,128)S(1)} reshape(f32[2880]{0:T(1024)} %param.8) | data formatting | bytes 23040 | tf_op jit(solution)/shard_map/reshape | solution.py:131
  12.1 1.5 %collective-permute-start.11 = (bf16[16,2880]{1,0:T(8,128)(2,1)S(1)}, bf16[16,2880]{1,0:T(8,128)(2,1)S(1)}, u32[]{:S(2)}, u32[]{:S(2)}) collective-permute-start(bf16[16,2880]{1,0:T(8,128)(2,1)S(1)} %collective-permute-done.refs_1_), channel_id=1, source_target_pairs={{0,4},{1,5},{4,8},{5,9},{8,12},{9,13},{12,14},{13,15},{14,10},{15,... | collective-permute-start | bytes 276488 | tf_op jit(solution)/shard_map/ppermute | solution.py:139
  13.6 0.6 collective-permute-start.12
  14.1 0.0 collective-permute-done.4.refs_5_
  14.1 2.8 %collective-permute-start.13 = (bf16[16,2880]{1,0:T(8,128)(2,1)S(1)}, bf16[16,2880]{1,0:T(8,128)(2,1)S(1)}, u32[]{:S(2)}, u32[]{:S(2)}) collective-permute-start(bf16[16,2880]{1,0:T(8,128)(2,1)S(1)} %collective-permute-done.refs_1_), channel_id=1, source_target_pairs={{0,8},{1,9},{4,12},{5,13},{8,14},{9,15},{12,10},{13,11},{14,6},{15... | collective-permute-start | bytes 276488 | tf_op jit(solution)/shard_map/ppermute | solution.py:139
  16.9 0.0 collective-permute-done.5.refs_6_
  16.9 0.2 collective-permute-start.14
  17.1 0.0 collective-permute-done.6.refs_7_
  17.1 2.2 %copy-done = bf16[1,2880,720]{1,2,0:T(8,128)(2,1)S(1)} copy-done((bf16[1,2880,720]{1,2,0:T(8,128)(2,1)S(1)}, bf16[1,2880,720]{1,2,0:T(8,128)(2,1)}, u32[]{:S(2)}) %copy-start) | copy-done | bytes 4147224
  19.3 2.2 %copy-done.2 = bf16[1,2880,720]{1,2,0:T(8,128)(2,1)S(1)} copy-done((bf16[1,2880,720]{1,2,0:T(8,128)(2,1)S(1)}, bf16[1,2880,720]{1,2,0:T(8,128)(2,1)}, u32[]{:S(2)}) %copy-start.2) | copy-done | bytes 4147224
  21.5 2.2 %copy-done.3 = bf16[1,720,2880]{2,1,0:T(8,128)(2,1)S(1)} copy-done((bf16[1,720,2880]{2,1,0:T(8,128)(2,1)S(1)}, bf16[1,720,2880]{2,1,0:T(8,128)(2,1)}, u32[]{:S(2)}) %copy-start.3) | copy-done | bytes 4147224
  23.7 0.9 %copy-done.4 = bf16[16,2880]{1,0:T(8,128)(2,1)S(1)} copy-done((bf16[16,2880]{1,0:T(8,128)(2,1)S(1)}, bf16[16,2880]{1,0:T(8,128)(2,1)}, u32[]{:S(2)}) %copy-start.4) | copy-done | bytes 92184
  24.6 3.6 %shard_map.73 = (bf16[64,2880]{1,0:T(8,128)(2,1)S(1)}, bf16[64,2880]{1,0:T(8,128)(2,1)S(1)}) custom-call(bf16[16,2880]{1,0:T(8,128)(2,1)S(1)} %copy-done.4, bf16[16,2880]{1,0:T(8,128)(2,1)S(1)} %collective-permute-done.refs_1_, bf16[16,2880]{1,0:T(8,128)(2,1)S(1)} %collective-permute-done.1.refs_2_, bf16[16,2880]{1,0:T(8,128)(2,1)S(1)} %collective-permute-done.2.refs_3_, ...), custom_call_target="tpu_custom_call" | custom-call | flops 1592524800 | bytes 12441600 | tf_op jit(solution)/shard_map/pallas_call | solution.py:106
  28.1 0.1 collective-permute-start.7
  28.2 0.0 collective-permute-done.11.refs_0_
  28.2 0.6 collective-permute-start.15
  28.8 0.1 collective-permute-start.16
  28.9 0.4 collective-permute-start.17
  29.3 0.0 collective-permute-done.14.refs_3_
  29.3 0.1 collective-permute-start.18
  29.4 0.1 select_reduce_fusion
  29.5 0.5 collective-permute-done.15.refs_4_
  30.0 0.1 collective-permute-done.16.refs_5_
  30.2 0.1 collective-permute-done.17.refs_6_
  30.3 0.3 collective-permute-done.18.refs_7_
  30.6 3.5 %shard_map.74 = (bf16[64,2880]{1,0:T(8,128)(2,1)S(1)}, bf16[64,2880]{1,0:T(8,128)(2,1)S(1)}) custom-call(bf16[16,2880]{1,0:T(8,128)(2,1)S(1)} %collective-permute-done.11.refs_0_, bf16[16,2880]{1,0:T(8,128)(2,1)S(1)} %collective-permute-done.12.refs_1_, bf16[16,2880]{1,0:T(8,128)(2,1)S(1)} %collective-permute-done.13.refs_2_, ...), custom_call_target="tpu_custom_call" | custom-call | flops 1592524800 | bytes 12441600 | tf_op jit(solution)/shard_map/pallas_call | solution.py:106
  34.2 0.2 collective-permute-start.19
  34.4 0.0 collective-permute-done.7
  34.4 0.1 add_convert_fusion.1
  34.5 4.3 %collective-permute-start.10 = (bf16[16,2880]{1,0:T(8,128)(2,1)S(1)}, bf16[16,2880]{1,0:T(8,128)(2,1)S(1)}, u32[]{:S(2)}, u32[]{:S(2)}) collective-permute-start(bf16[16,2880]{1,0:T(8,128)(2,1)S(1)} %get-tuple-element.14), channel_id=1, source_target_pairs={{0,14},{1,15},{4,10},{5,11},{8,6},{9,7},{12,2},{13,3},{14,0},{15,1... | collective-permute-start | bytes 276488 | tf_op jit(solution)/shard_map/ppermute | solution.py:139
  38.9 0.0 collective-permute-start.9
  38.9 2.0 %collective-permute-start.8 = (bf16[16,2880]{1,0:T(8,128)(2,1)S(1)}, bf16[16,2880]{1,0:T(8,128)(2,1)S(1)}, u32[]{:S(2)}, u32[]{:S(2)}) collective-permute-start(bf16[16,2880]{1,0:T(8,128)(2,1)S(1)} %get-tuple-element.13), channel_id=1, source_target_pairs={{0,2},{1,3},{4,0},{5,1},{8,4},{9,5},{12,8},{13,9},{14,12},{15,13},... | collective-permute-start | bytes 276488 | tf_op jit(solution)/shard_map/ppermute | solution.py:139
  40.9 0.1 add_convert_fusion
  41.0 0.7 %collective-permute-start.23 = (bf16[16,2880]{1,0:T(8,128)(2,1)S(1)}, bf16[16,2880]{1,0:T(8,128)(2,1)S(1)}, u32[]{:S(2)}, u32[]{:S(2)}) collective-permute-start(bf16[16,2880]{1,0:T(8,128)(2,1)S(1)} %get-tuple-element.17), channel_id=1, source_target_pairs={{0,12},{1,13},{4,14},{5,15},{8,10},{9,11},{12,6},{13,7},{14,2},{15... | collective-permute-start | bytes 276488 | tf_op jit(solution)/shard_map/ppermute | solution.py:139
  41.7 3.2 %collective-permute-start.22 = (bf16[16,2880]{1,0:T(8,128)(2,1)S(1)}, bf16[16,2880]{1,0:T(8,128)(2,1)S(1)}, u32[]{:S(2)}, u32[]{:S(2)}) collective-permute-start(bf16[16,2880]{1,0:T(8,128)(2,1)S(1)} %get-tuple-element.18), channel_id=1, source_target_pairs={{0,10},{1,11},{4,6},{5,7},{8,2},{9,3},{12,0},{13,1},{14,4},{15,5},... | collective-permute-start | bytes 276488 | tf_op jit(solution)/shard_map/ppermute | solution.py:139
  44.9 0.8 %collective-permute-start.21 = (bf16[16,2880]{1,0:T(8,128)(2,1)S(1)}, bf16[16,2880]{1,0:T(8,128)(2,1)S(1)}, u32[]{:S(2)}, u32[]{:S(2)}) collective-permute-start(bf16[16,2880]{1,0:T(8,128)(2,1)S(1)} %get-tuple-element.19), channel_id=1, source_target_pairs={{0,8},{1,9},{4,12},{5,13},{8,14},{9,15},{12,10},{13,11},{14,6},{15... | collective-permute-start | bytes 276488 | tf_op jit(solution)/shard_map/ppermute | solution.py:139
  45.7 6.1 %collective-permute-start.20 = (bf16[16,2880]{1,0:T(8,128)(2,1)S(1)}, bf16[16,2880]{1,0:T(8,128)(2,1)S(1)}, u32[]{:S(2)}, u32[]{:S(2)}) collective-permute-start(bf16[16,2880]{1,0:T(8,128)(2,1)S(1)} %get-tuple-element.16), channel_id=1, source_target_pairs={{0,6},{1,7},{4,2},{5,3},{8,0},{9,1},{12,4},{13,5},{14,8},{15,9},{1... | collective-permute-start | bytes 276488 | tf_op jit(solution)/shard_map/ppermute | solution.py:139
  51.8 2.0 %collective-permute-done.23 = bf16[16,2880]{1,0:T(8,128)(2,1)S(1)} collective-permute-done((bf16[16,2880]{1,0:T(8,128)(2,1)S(1)}, bf16[16,2880]{1,0:T(8,128)(2,1)S(1)}, u32[]{:S(2)}, u32[]{:S(2)}) %collective-permute-start.23) | collective-permute-done | bytes 92192 | tf_op jit(solution)/shard_map/ppermute | solution.py:139
  53.8 3.3 %collective-permute-done.20 = bf16[16,2880]{1,0:T(8,128)(2,1)S(1)} collective-permute-done((bf16[16,2880]{1,0:T(8,128)(2,1)S(1)}, bf16[16,2880]{1,0:T(8,128)(2,1)S(1)}, u32[]{:S(2)}, u32[]{:S(2)}) %collective-permute-start.20) | collective-permute-done | bytes 92192 | tf_op jit(solution)/shard_map/ppermute | solution.py:139
  57.2 0.9 %add_convert_fusion.2 = bf16[16,2880]{1,0:T(8,128)(2,1)} fusion(bf16[16,2880]{1,0:T(8,128)(2,1)S(1)} %collective-permute-done.23, bf16[16,2880]{1,0:T(8,128)(2,1)S(1)} %collective-permute-done.22, bf16[16,2880]{1,0:T(8,128)(2,1)S(1)} %collective-permute-done.21, bf16[16,2880]{1,0:T(8,128)(2,1)S(1)} %collective-permute-done.20, ...), kind=kLoop, calls=%fused_computation.2 | loop fusion | flops 1198080 | bytes 922112 | tf_op jit(solution)/shard_map/convert_element_type | solution.py:172
  (25 shorter events, 0.1 us)
Async XLA Ops:
  0.0 8.0 %collective-permute-start = (bf16[16,2880]{1,0:T(8,128)(2,1)}, bf16[16,2880]{1,0:T(8,128)(2,1)S(1)}, u32[]{:S(2)}, u32[]{:S(2)}) collective-permute-start(bf16[16,2880]{1,0:T(8,128)(2,1)} %refs_0_.1), channel_id=1, source_target_pairs={{0,4},{1,5},{4,8},{5,9},{8,12},{9,13},{12,14},{13,15},{14,10},{15,... | collective-permute-start | bytes 276488 | tf_op jit(solution)/shard_map/ppermute | solution.py:139
  3.0 5.5 %collective-permute-start.1 = (bf16[16,2880]{1,0:T(8,128)(2,1)}, bf16[16,2880]{1,0:T(8,128)(2,1)S(1)}, u32[]{:S(2)}, u32[]{:S(2)}) collective-permute-start(bf16[16,2880]{1,0:T(8,128)(2,1)} %refs_0_.1), channel_id=1, source_target_pairs={{0,2},{1,3},{4,0},{5,1},{8,4},{9,5},{12,8},{13,9},{14,12},{15,13},... | collective-permute-start | bytes 276488 | tf_op jit(solution)/shard_map/ppermute | solution.py:139
  3.0 8.3 %collective-permute-start.2 = (bf16[16,2880]{1,0:T(8,128)(2,1)}, bf16[16,2880]{1,0:T(8,128)(2,1)S(1)}, u32[]{:S(2)}, u32[]{:S(2)}) collective-permute-start(bf16[16,2880]{1,0:T(8,128)(2,1)} %refs_0_.1), channel_id=1, source_target_pairs={{0,14},{1,15},{4,10},{5,11},{8,6},{9,7},{12,2},{13,3},{14,0},{15,1... | collective-permute-start | bytes 276488 | tf_op jit(solution)/shard_map/ppermute | solution.py:139
  8.0 5.5 %collective-permute-start.3 = (bf16[16,2880]{1,0:T(8,128)(2,1)}, bf16[16,2880]{1,0:T(8,128)(2,1)S(1)}, u32[]{:S(2)}, u32[]{:S(2)}) collective-permute-start(bf16[16,2880]{1,0:T(8,128)(2,1)} %refs_0_.1), channel_id=1, source_target_pairs={{0,1},{1,0},{2,3},{3,2},{4,5},{5,4},{6,7},{7,6},{8,9},{9,8},{10,11... | collective-permute-start | bytes 276488 | tf_op jit(solution)/shard_map/ppermute | solution.py:14
  8.0 6.1 %collective-permute-start.4 = (bf16[16,2880]{1,0:T(8,128)(2,1)S(1)}, bf16[16,2880]{1,0:T(8,128)(2,1)S(1)}, u32[]{:S(2)}, u32[]{:S(2)}) collective-permute-start(bf16[16,2880]{1,0:T(8,128)(2,1)S(1)} %collective-permute-done.refs_1_), channel_id=1, source_target_pairs={{0,1},{1,0},{2,3},{3,2},{4,5},{5,4},{6,7},{7,6},{8,9},{9,8},{10,11... | collective-permute-start | bytes 276488 | tf_op jit(solution)/shard_map/ppermute | solution.py:14
  8.6 8.3 %collective-permute-start.5 = (bf16[16,2880]{1,0:T(8,128)(2,1)S(1)}, bf16[16,2880]{1,0:T(8,128)(2,1)S(1)}, u32[]{:S(2)}, u32[]{:S(2)}) collective-permute-start(bf16[16,2880]{1,0:T(8,128)(2,1)S(1)} %collective-permute-done.1.refs_2_), channel_id=1, source_target_pairs={{0,1},{1,0},{2,3},{3,2},{4,5},{5,4},{6,7},{7,6},{8,9},{9,8},{10,11... | collective-permute-start | bytes 276488 | tf_op jit(solution)/shard_map/ppermute | solution.py:14
  11.3 5.7 %collective-permute-start.6 = (bf16[16,2880]{1,0:T(8,128)(2,1)S(1)}, bf16[16,2880]{1,0:T(8,128)(2,1)S(1)}, u32[]{:S(2)}, u32[]{:S(2)}) collective-permute-start(bf16[16,2880]{1,0:T(8,128)(2,1)S(1)} %collective-permute-done.2.refs_3_), channel_id=1, source_target_pairs={{0,1},{1,0},{2,3},{3,2},{4,5},{5,4},{6,7},{7,6},{8,9},{9,8},{10,11... | collective-permute-start | bytes 276488 | tf_op jit(solution)/shard_map/ppermute | solution.py:14
  12.1 16.2 %collective-permute-start.11 = (bf16[16,2880]{1,0:T(8,128)(2,1)S(1)}, bf16[16,2880]{1,0:T(8,128)(2,1)S(1)}, u32[]{:S(2)}, u32[]{:S(2)}) collective-permute-start(bf16[16,2880]{1,0:T(8,128)(2,1)S(1)} %collective-permute-done.refs_1_), channel_id=1, source_target_pairs={{0,4},{1,5},{4,8},{5,9},{8,12},{9,13},{12,14},{13,15},{14,10},{15,... | collective-permute-start | bytes 276488 | tf_op jit(solution)/shard_map/ppermute | solution.py:139
  13.6 15.2 %collective-permute-start.12 = (bf16[16,2880]{1,0:T(8,128)(2,1)S(1)}, bf16[16,2880]{1,0:T(8,128)(2,1)S(1)}, u32[]{:S(2)}, u32[]{:S(2)}) collective-permute-start(bf16[16,2880]{1,0:T(8,128)(2,1)S(1)} %collective-permute-done.1.refs_2_), channel_id=1, source_target_pairs={{0,2},{1,3},{4,0},{5,1},{8,4},{9,5},{12,8},{13,9},{14,12},{15,13},... | collective-permute-start | bytes 276488 | tf_op jit(solution)/shard_map/ppermute | solution.py:139
  14.1 14.8 %collective-permute-start.13 = (bf16[16,2880]{1,0:T(8,128)(2,1)S(1)}, bf16[16,2880]{1,0:T(8,128)(2,1)S(1)}, u32[]{:S(2)}, u32[]{:S(2)}) collective-permute-start(bf16[16,2880]{1,0:T(8,128)(2,1)S(1)} %collective-permute-done.refs_1_), channel_id=1, source_target_pairs={{0,8},{1,9},{4,12},{5,13},{8,14},{9,15},{12,10},{13,11},{14,6},{15... | collective-permute-start | bytes 276488 | tf_op jit(solution)/shard_map/ppermute | solution.py:139
  16.9 12.4 %collective-permute-start.14 = (bf16[16,2880]{1,0:T(8,128)(2,1)S(1)}, bf16[16,2880]{1,0:T(8,128)(2,1)S(1)}, u32[]{:S(2)}, u32[]{:S(2)}) collective-permute-start(bf16[16,2880]{1,0:T(8,128)(2,1)S(1)} %collective-permute-done.1.refs_2_), channel_id=1, source_target_pairs={{0,6},{1,7},{4,2},{5,3},{8,0},{9,1},{12,4},{13,5},{14,8},{15,9},{1... | collective-permute-start | bytes 276488 | tf_op jit(solution)/shard_map/ppermute | solution.py:139
  17.1 2.2 %copy-start = (bf16[1,2880,720]{1,2,0:T(8,128)(2,1)S(1)}, bf16[1,2880,720]{1,2,0:T(8,128)(2,1)}, u32[]{:S(2)}) copy-start(bf16[1,2880,720]{1,2,0:T(8,128)(2,1)} %param.11) | copy-start | bytes 12441604
  19.3 2.2 %copy-start.2 = (bf16[1,2880,720]{1,2,0:T(8,128)(2,1)S(1)}, bf16[1,2880,720]{1,2,0:T(8,128)(2,1)}, u32[]{:S(2)}) copy-start(bf16[1,2880,720]{1,2,0:T(8,128)(2,1)} %param.12) | copy-start | bytes 12441604
  21.5 2.2 %copy-start.3 = (bf16[1,720,2880]{2,1,0:T(8,128)(2,1)S(1)}, bf16[1,720,2880]{2,1,0:T(8,128)(2,1)}, u32[]{:S(2)}) copy-start(bf16[1,720,2880]{2,1,0:T(8,128)(2,1)} %param.13) | copy-start | bytes 12441604
  23.7 0.9 %copy-start.4 = (bf16[16,2880]{1,0:T(8,128)(2,1)S(1)}, bf16[16,2880]{1,0:T(8,128)(2,1)}, u32[]{:S(2)}) copy-start(bf16[16,2880]{1,0:T(8,128)(2,1)} %refs_0_.1) | copy-start | bytes 276484
  24.6 4.8 %copy-start.5 = (f32[16,4]{0,1:T(4,128)S(1)}, f32[16,4]{0,1:T(4,128)}, u32[]{:S(2)}) copy-start(f32[16,4]{0,1:T(4,128)} %param.10) | copy-start | bytes 772
  24.6 4.8 %copy-start.6 = (s32[16,4]{0,1:T(4,128)S(1)}, s32[16,4]{0,1:T(4,128)}, u32[]{:S(2)}) copy-start(s32[16,4]{0,1:T(4,128)} %param.9) | copy-start | bytes 772
  24.6 6.0 %copy-start.1 = (bf16[1,2880,720]{1,2,0:T(8,128)(2,1)S(1)}, bf16[1,2880,720]{1,2,0:T(8,128)(2,1)}, u32[]{:S(2)}) copy-start(bf16[1,2880,720]{1,2,0:T(8,128)(2,1)} %param.11) | copy-start | bytes 12441604
  28.1 6.3 %collective-permute-start.7 = (bf16[64,2880]{1,0:T(8,128)(2,1)S(1)}, bf16[64,2880]{1,0:T(8,128)(2,1)S(1)}, u32[]{:S(2)}, u32[]{:S(2)}) collective-permute-start(bf16[64,2880]{1,0:T(8,128)(2,1)S(1)} %get-tuple-element.10), channel_id=1, source_target_pairs={{0,1},{1,0},{2,3},{3,2},{4,5},{5,4},{6,7},{7,6},{8,9},{9,8},{10,11... | collective-permute-start | bytes 1105928 | tf_op jit(solution)/shard_map/ppermute | solution.py:14
  28.2 1.8 %collective-permute-start.15 = (bf16[16,2880]{1,0:T(8,128)(2,1)S(1)}, bf16[16,2880]{1,0:T(8,128)(2,1)S(1)}, u32[]{:S(2)}, u32[]{:S(2)}) collective-permute-start(bf16[16,2880]{1,0:T(8,128)(2,1)S(1)} %collective-permute-done.11.refs_0_), channel_id=1, source_target_pairs={{0,1},{1,0},{2,3},{3,2},{4,5},{5,4},{6,7},{7,6},{8,9},{9,8},{10,11... | collective-permute-start | bytes 276488 | tf_op jit(solution)/shard_map/ppermute | solution.py:14
  28.8 1.4 %collective-permute-start.16 = (bf16[16,2880]{1,0:T(8,128)(2,1)S(1)}, bf16[16,2880]{1,0:T(8,128)(2,1)S(1)}, u32[]{:S(2)}, u32[]{:S(2)}) collective-permute-start(bf16[16,2880]{1,0:T(8,128)(2,1)S(1)} %collective-permute-done.12.refs_1_), channel_id=1, source_target_pairs={{0,1},{1,0},{2,3},{3,2},{4,5},{5,4},{6,7},{7,6},{8,9},{9,8},{10,11... | collective-permute-start | bytes 276488 | tf_op jit(solution)/shard_map/ppermute | solution.py:14
  28.9 1.4 %collective-permute-start.17 = (bf16[16,2880]{1,0:T(8,128)(2,1)S(1)}, bf16[16,2880]{1,0:T(8,128)(2,1)S(1)}, u32[]{:S(2)}, u32[]{:S(2)}) collective-permute-start(bf16[16,2880]{1,0:T(8,128)(2,1)S(1)} %collective-permute-done.13.refs_2_), channel_id=1, source_target_pairs={{0,1},{1,0},{2,3},{3,2},{4,5},{5,4},{6,7},{7,6},{8,9},{9,8},{10,11... | collective-permute-start | bytes 276488 | tf_op jit(solution)/shard_map/ppermute | solution.py:14
  29.3 1.3 %collective-permute-start.18 = (bf16[16,2880]{1,0:T(8,128)(2,1)S(1)}, bf16[16,2880]{1,0:T(8,128)(2,1)S(1)}, u32[]{:S(2)}, u32[]{:S(2)}) collective-permute-start(bf16[16,2880]{1,0:T(8,128)(2,1)S(1)} %collective-permute-done.14.refs_3_), channel_id=1, source_target_pairs={{0,1},{1,0},{2,3},{3,2},{4,5},{5,4},{6,7},{7,6},{8,9},{9,8},{10,11... | collective-permute-start | bytes 276488 | tf_op jit(solution)/shard_map/ppermute | solution.py:14
  34.2 6.7 %collective-permute-start.19 = (bf16[64,2880]{1,0:T(8,128)(2,1)S(1)}, bf16[64,2880]{1,0:T(8,128)(2,1)S(1)}, u32[]{:S(2)}, u32[]{:S(2)}) collective-permute-start(bf16[64,2880]{1,0:T(8,128)(2,1)S(1)} %get-tuple-element.12), channel_id=1, source_target_pairs={{0,1},{1,0},{2,3},{3,2},{4,5},{5,4},{6,7},{7,6},{8,9},{9,8},{10,11... | collective-permute-start | bytes 1105928 | tf_op jit(solution)/shard_map/ppermute | solution.py:14
  34.5 10.4 %collective-permute-start.10 = (bf16[16,2880]{1,0:T(8,128)(2,1)S(1)}, bf16[16,2880]{1,0:T(8,128)(2,1)S(1)}, u32[]{:S(2)}, u32[]{:S(2)}) collective-permute-start(bf16[16,2880]{1,0:T(8,128)(2,1)S(1)} %get-tuple-element.14), channel_id=1, source_target_pairs={{0,14},{1,15},{4,10},{5,11},{8,6},{9,7},{12,2},{13,3},{14,0},{15,1... | collective-permute-start | bytes 276488 | tf_op jit(solution)/shard_map/ppermute | solution.py:139
  38.9 6.8 %collective-permute-start.9 = (bf16[16,2880]{1,0:T(8,128)(2,1)S(1)}, bf16[16,2880]{1,0:T(8,128)(2,1)S(1)}, u32[]{:S(2)}, u32[]{:S(2)}) collective-permute-start(bf16[16,2880]{1,0:T(8,128)(2,1)S(1)} %get-tuple-element.15), channel_id=1, source_target_pairs={{0,4},{1,5},{4,8},{5,9},{8,12},{9,13},{12,14},{13,15},{14,10},{15,... | collective-permute-start | bytes 276488 | tf_op jit(solution)/shard_map/ppermute | solution.py:139
  38.9 12.9 %collective-permute-start.8 = (bf16[16,2880]{1,0:T(8,128)(2,1)S(1)}, bf16[16,2880]{1,0:T(8,128)(2,1)S(1)}, u32[]{:S(2)}, u32[]{:S(2)}) collective-permute-start(bf16[16,2880]{1,0:T(8,128)(2,1)S(1)} %get-tuple-element.13), channel_id=1, source_target_pairs={{0,2},{1,3},{4,0},{5,1},{8,4},{9,5},{12,8},{13,9},{14,12},{15,13},... | collective-permute-start | bytes 276488 | tf_op jit(solution)/shard_map/ppermute | solution.py:139
  41.0 12.8 %collective-permute-start.23 = (bf16[16,2880]{1,0:T(8,128)(2,1)S(1)}, bf16[16,2880]{1,0:T(8,128)(2,1)S(1)}, u32[]{:S(2)}, u32[]{:S(2)}) collective-permute-start(bf16[16,2880]{1,0:T(8,128)(2,1)S(1)} %get-tuple-element.17), channel_id=1, source_target_pairs={{0,12},{1,13},{4,14},{5,15},{8,10},{9,11},{12,6},{13,7},{14,2},{15... | collective-permute-start | bytes 276488 | tf_op jit(solution)/shard_map/ppermute | solution.py:139
  41.7 12.1 %collective-permute-start.22 = (bf16[16,2880]{1,0:T(8,128)(2,1)S(1)}, bf16[16,2880]{1,0:T(8,128)(2,1)S(1)}, u32[]{:S(2)}, u32[]{:S(2)}) collective-permute-start(bf16[16,2880]{1,0:T(8,128)(2,1)S(1)} %get-tuple-element.18), channel_id=1, source_target_pairs={{0,10},{1,11},{4,6},{5,7},{8,2},{9,3},{12,0},{13,1},{14,4},{15,5},... | collective-permute-start | bytes 276488 | tf_op jit(solution)/shard_map/ppermute | solution.py:139
  44.9 8.9 %collective-permute-start.21 = (bf16[16,2880]{1,0:T(8,128)(2,1)S(1)}, bf16[16,2880]{1,0:T(8,128)(2,1)S(1)}, u32[]{:S(2)}, u32[]{:S(2)}) collective-permute-start(bf16[16,2880]{1,0:T(8,128)(2,1)S(1)} %get-tuple-element.19), channel_id=1, source_target_pairs={{0,8},{1,9},{4,12},{5,13},{8,14},{9,15},{12,10},{13,11},{14,6},{15... | collective-permute-start | bytes 276488 | tf_op jit(solution)/shard_map/ppermute | solution.py:139
  45.7 11.5 %collective-permute-start.20 = (bf16[16,2880]{1,0:T(8,128)(2,1)S(1)}, bf16[16,2880]{1,0:T(8,128)(2,1)S(1)}, u32[]{:S(2)}, u32[]{:S(2)}) collective-permute-start(bf16[16,2880]{1,0:T(8,128)(2,1)S(1)} %get-tuple-element.16), channel_id=1, source_target_pairs={{0,6},{1,7},{4,2},{5,3},{8,0},{9,1},{12,4},{13,5},{14,8},{15,9},{1... | collective-permute-start | bytes 276488 | tf_op jit(solution)/shard_map/ppermute | solution.py:139

commit v3 on v2

--- a/solution.py
+++ b/solution.py
@@ -118,65 +118,79 @@
     )(*blocks, gain, gate_w, up_w, down_w)
 
 
-def ring(residual, norm_gain, expert_ids, expert_weights, gate_proj, up_proj, down_proj):
+def load_kernel(count, *refs):
+    sources, targets, sems = refs[:count], refs[count : 2 * count], refs[2 * count]
+    copies = [
+        pltpu.make_async_copy(source, target, sems.at[i])
+        for i, (source, target) in enumerate(zip(sources, targets))
+    ]
+    for copy in copies:
+        copy.start()
+    for copy in copies:
+        copy.wait()
+
+
+def load(*arrays):
+    count = len(arrays)
+    return pl.pallas_call(
+        functools.partial(load_kernel, count),
+        out_shape=tuple(pltpu.VMEM(a.shape, a.dtype) for a in arrays),
+        in_specs=[pl.BlockSpec(memory_space=pltpu.HBM)] * count,
+        out_specs=(pl.BlockSpec(memory_space=pltpu.VMEM),) * count,
+        scratch_shapes=[pltpu.SemaphoreType.DMA((count,))],
+        cost_estimate=pl.CostEstimate(
+            flops=0, bytes_accessed=2 * sum(a.size * a.dtype.itemsize for a in arrays), transcendentals=0
+        ),
+        compiler_params=pltpu.CompilerParams(vmem_limit_bytes=16 * 2**20),
+    )(*(pltpu.with_memory_space_constraint(a, pltpu.HBM) for a in arrays))
+
+
+def halves(residual, norm_gain, expert_ids, expert_weights, gate_proj, up_proj, down_proj):
     rows, model = residual.shape
-    devices = lax.axis_size("expert")
-    chips = devices // 2
-    far = chips // 2
-    order = list(range(0, chips, 2)) + list(range(1, chips, 2))[::-1]
-    held = [
-        pltpu.with_memory_space_constraint(w, pltpu.VMEM)
-        for w in (gate_proj[0].T, up_proj[0].T, down_proj[0])
-    ]
+    chips = lax.axis_size("expert") // 2
+    half = chips // 2
     gain = norm_gain.reshape(1, model)
 
-    def ringwise(value, hops):
-        pairs = [
-            (2 * order[i] + core, 2 * order[(i + hops) % chips] + core)
-            for i in range(chips)
-            for core in range(2)
-        ]
-        return lax.ppermute(value, "expert", pairs)
+    def across(value, mask):
+        pairs = [(i, i ^ (2 * mask)) for i in range(2 * chips)]
+        return lax.ppermute(value, "expert", pairs) if mask else value
 
     def swap(value):
         return partner(value, "expert", 0)
 
-    chip = lax.axis_index("expert") // 2
-    place = jnp.where(chip % 2 == 0, chip // 2, chips - 1 - chip // 2)
-    on = (place + jnp.arange(chips)) % chips
-    expert = jnp.where(on < far, 2 * on, 2 * (chips - 1 - on) + 1)
+    x = residual
+    mirrored = across(x, half)
+    near = [across(x, mask) for mask in range(half)]
+    near += [swap(block) for block in near]
+    held = load(gate_proj[0].T, up_proj[0].T, down_proj[0])
+    far = [across(mirrored, mask) for mask in range(half)]
+    far += [swap(block) for block in far]
+
+    expert = (lax.axis_index("expert") // 2) ^ jnp.arange(chips, dtype=jnp.int32)
     weights = jnp.sum(
         jnp.where(expert_ids[:, :, None] == expert[None, None, :], expert_weights[:, :, None], 0.0), axis=1
     )
-
-    x = residual
-    arrived = {0: x, far: ringwise(x, far)}
-    for way in (1, -1):
-        arrived[way] = ringwise(x, way)
-    for hops in range(2, far):
-        near = hops - 2 if hops > 2 else 1
-        for way in (1, -1):
-            arrived[way * hops] = ringwise(arrived[way * near], way * (hops - near))
-    near = [0, 1, -1, far]
-    beyond = [way * hops for hops in range(2, far) for way in (1, -1)]
-    finished = {}
-    for group in (near, beyond):
-        blocks = [arrived[hops] for hops in group]
-        mine, theirs = expert_parts(blocks + [swap(block) for block in blocks], gain, *held)
-        done = pair_sum(mine, swap(theirs)).reshape(len(group), rows, model)
-        for i, hops in enumerate(group):
-            finished[hops] = ringwise(done[i], -hops) if hops else done[i]
-    combined = jnp.zeros((rows, model), jnp.float32)
-    for hops, block in finished.items():
-        combined += weights[:, hops % chips][:, None] * block.astype(jnp.float32)
-    return (x.astype(jnp.float32) + combined).astype(jnp.bfloat16)
+    mirror_weights = across(weights[:, half:], half)
+
+    def mix(blocks, block_weights):
+        mine, theirs = expert_parts(blocks, gain, *held)
+        done = pair_sum(mine, swap(theirs)).reshape(half, rows, model)
+        total = jnp.zeros((rows, model), jnp.float32)
+        for mask in range(half):
+            total += block_weights[:, mask][:, None] * across(done[mask], mask).astype(jnp.float32)
+        return total
+
+    own = mix(near, weights[:, :half])
+    other = mix(far, mirror_weights)
+    own += across(other.astype(jnp.bfloat16), half).astype(jnp.float32)
+    return (x.astype(jnp.float32) + own).astype(jnp.bfloat16)
 
 
 def body(residual, norm_gain, expert_ids, expert_weights, gate_proj, up_proj, down_proj):
     rows, chosen = expert_ids.shape
     chips = lax.axis_size("expert") // 2
-    whole = 2 * rows * chosen // chips >= rows and chips % 2 == 0 and chips >= 6
-    plan = ring if whole else slots
+    whole = 2 * rows * chosen // chips >= rows and chips >= 4 and chips & (chips - 1) == 0
+    plan = halves if whole else slots
     return plan(residual, norm_gain, expert_ids, expert_weights, gate_proj, up_proj, down_proj)
 
 

time: 58.3 us -> 52.3 us (0.90)
  starting transfers between devices: 32.2 us -> 21.2 us
  local copies, waits for them, and re-layouts: 8.28 us -> 0.78 us
  waiting for transfers between devices: 9.23 us -> 16.3 us
  Pallas kernels: 7.09 us -> 11.8 us
  other arithmetic: 1.14 us -> 1.91 us
    ppermute x14 -> x15, starting transfers between devices: 30.2 us -> 19.9 us  [across(): return lax.ppermute(value, 'expert', pairs) if mask else value]
    unnamed x14 -> x2, local copies, waits for them, and re-layouts: 7.5 us -> 0.01 us
    ppermute x14 -> x15, waiting for transfers between devices: 8.08 us -> 13.6 us  [across(): return lax.ppermute(value, 'expert', pairs) if mask else value]
    pallas_call x0 -> x1, Pallas kernels: none -> 4.75 us  [load(): pl.pallas_call(functools.partial(load_kernel, count), out_shape=tuple((pl...]
    ppermute x10, waiting for transfers between devices: 1.14 us -> 2.75 us  [partner(): return lax.ppermute(value, axis, pairs)]
    ppermute x10, starting transfers between devices: 2.03 us -> 1.32 us  [partner(): return lax.ppermute(value, axis, pairs)]
    reduce_sum x1, other arithmetic: 0.07 us -> 0.77 us  [halves(): jnp.sum(jnp.where(expert_ids[:, :, None] == expert[None, None, :], expert...]
  transfers between devices with their start and end apart: 24 -> 25, of which waited for: 7 -> 13; matrix products, arithmetic and copies ran while one was open for 2% -> 3% of each run, Pallas kernels for 12% -> 23%
where the time goes in v3:
time: 52.3 us; the launch traced here: 52.1 us
  starting transfers between devices  21.2 us (41%)
  waiting for transfers between devices  16.3 us (31%)
  Pallas kernels  11.8 us (23%)
  other arithmetic  1.91 us (4%)
  local copies, waits for them, and re-layouts  0.78 us (1%)
    ppermute x15, starting transfers between devices, across(): return lax.ppermute(value, 'expert', pairs) if mask else value  19.9 us
    ppermute x15, waiting for transfers between devices, across(): return lax.ppermute(value, 'expert', pairs) if mask else value  13.6 us
    pallas_call x2, Pallas kernels, expert_parts(): pl.pallas_call(functools.partial(expert_kernel, count), out_shape=(out, o...  7.04 us
    pallas_call x1, Pallas kernels, load(): pl.pallas_call(functools.partial(load_kernel, count), out_shape=tuple((pl...  4.75 us
    ppermute x10, waiting for transfers between devices, partner(): return lax.ppermute(value, axis, pairs)  2.75 us
    ppermute x10, starting transfers between devices, partner(): return lax.ppermute(value, axis, pairs)  1.32 us
  transfers between devices with their start and end apart: 25, of which 13 were waited for; matrix products, arithmetic and copies ran while one was open for 3% of the time, Pallas kernels for 23%

profile of v3, /device:TPU:0, one launch (start us, length us, event | category | flops | bytes accessed | tf_op | source)
XLA Modules:
  0.0 52.1 jit_solution(3649719278129601051)
XLA Ops:
  0.0 4.0 %collective-permute-start.12 = (bf16[16,2880]{1,0:T(8,128)(2,1)}, bf16[16,2880]{1,0:T(8,128)(2,1)S(1)}, u32[]{:S(2)}, u32[]{:S(2)}) collective-permute-start(bf16[16,2880]{1,0:T(8,128)(2,1)} %refs_0_.1), channel_id=1, source_target_pairs={{0,8},{1,9},{2,10},{3,11},{4,12},{5,13},{6,14},{7,15},{8,0},{9,1},... | collective-permute-start | bytes 276488 | tf_op jit(solution)/shard_map/ppermute | solution.py:156
  4.0 1.5 %collective-permute-start = (bf16[16,2880]{1,0:T(8,128)(2,1)}, bf16[16,2880]{1,0:T(8,128)(2,1)S(1)}, u32[]{:S(2)}, u32[]{:S(2)}) collective-permute-start(bf16[16,2880]{1,0:T(8,128)(2,1)} %refs_0_.1), channel_id=1, source_target_pairs={{0,2},{1,3},{2,0},{3,1},{4,6},{5,7},{6,4},{7,5},{8,10},{9,11},{10,... | collective-permute-start | bytes 276488 | tf_op jit(solution)/shard_map/ppermute | solution.py:156
  5.6 1.6 %collective-permute-start.1 = (bf16[16,2880]{1,0:T(8,128)(2,1)}, bf16[16,2880]{1,0:T(8,128)(2,1)S(1)}, u32[]{:S(2)}, u32[]{:S(2)}) collective-permute-start(bf16[16,2880]{1,0:T(8,128)(2,1)} %refs_0_.1), channel_id=1, source_target_pairs={{0,4},{1,5},{2,6},{3,7},{4,0},{5,1},{6,2},{7,3},{8,12},{9,13},{10,... | collective-permute-start | bytes 276488 | tf_op jit(solution)/shard_map/ppermute | solution.py:156
  7.1 0.4 collective-permute-start.2
  7.5 0.0 collective-permute-start.3
  7.5 0.7 %reshape.27.refs_8_ = f32[1,2880]{1,0:T(1,128)S(1)} reshape(f32[2880]{0:T(1024)} %param.8) | data formatting | bytes 23040 | tf_op jit(solution)/shard_map/reshape | solution.py:152
  8.3 0.6 %collective-permute-done.refs_1_ = bf16[16,2880]{1,0:T(8,128)(2,1)S(1)} collective-permute-done((bf16[16,2880]{1,0:T(8,128)(2,1)}, bf16[16,2880]{1,0:T(8,128)(2,1)S(1)}, u32[]{:S(2)}, u32[]{:S(2)}) %collective-permute-start) | collective-permute-done | bytes 92192 | tf_op jit(solution)/shard_map/ppermute | solution.py:156
  8.8 0.0 collective-permute-start.4
  8.8 2.5 %collective-permute-done.1.refs_2_ = bf16[16,2880]{1,0:T(8,128)(2,1)S(1)} collective-permute-done((bf16[16,2880]{1,0:T(8,128)(2,1)}, bf16[16,2880]{1,0:T(8,128)(2,1)S(1)}, u32[]{:S(2)}, u32[]{:S(2)}) %collective-permute-start.1) | collective-permute-done | bytes 92192 | tf_op jit(solution)/shard_map/ppermute | solution.py:156
  11.4 0.0 collective-permute-start.5
  11.4 1.4 %collective-permute-done.2.refs_3_ = bf16[16,2880]{1,0:T(8,128)(2,1)S(1)} collective-permute-done((bf16[16,2880]{1,0:T(8,128)(2,1)}, bf16[16,2880]{1,0:T(8,128)(2,1)S(1)}, u32[]{:S(2)}, u32[]{:S(2)}) %collective-permute-start.2) | collective-permute-done | bytes 92192 | tf_op jit(solution)/shard_map/ppermute | solution.py:156
  12.8 0.0 collective-permute-start.6
  12.8 0.8 %select_reduce_fusion = f32[16,8]{0,1:T(8,128)S(1)} fusion(f32[16,4]{0,1:T(4,128)} %param.10, s32[16,4]{0,1:T(4,128)} %param.9, s32[8]{0:T(128)S(1)} %iota_xor_fusion), kind=kLoop, calls=%fused_computation.4 | loop fusion | flops 1408 | bytes 1056 | tf_op jit(solution)/shard_map/reduce_sum | solution.py:170
  13.6 4.8 %shard_map.73 = (bf16[720,2880]{1,0:T(8,128)(2,1)S(1)}, bf16[720,2880]{1,0:T(8,128)(2,1)S(1)}, bf16[720,2880]{1,0:T(8,128)(2,1)S(1)}) custom-call(bf16[720,2880]{1,0:T(8,128)(2,1)} %bitcast.23, bf16[720,2880]{1,0:T(8,128)(2,1)} %bitcast.24, bf16[720,2880]{1,0:T(8,128)(2,1)} %bitcast.25), custom_call_target="tpu_custom_call" | custom-call | bytes 24883200 | tf_op jit(solution)/shard_map/pallas_call | solution.py:135
  18.4 0.0 collective-permute-done.12.refs_0_
  18.4 0.8 %collective-permute-start.11 = (f32[16,4]{0,1:T(4,128)S(1)}, f32[16,4]{0,1:T(4,128)S(1)}, u32[]{:S(2)}, u32[]{:S(2)}) collective-permute-start(f32[16,4]{0,1:T(4,128)S(1)} %slice.72), channel_id=1, source_target_pairs={{0,8},{1,9},{2,10},{3,11},{4,12},{5,13},{6,14},{7,15},{8,0},{9,1},... | collective-permute-start | bytes 776 | tf_op jit(solution)/shard_map/ppermute | solution.py:156
  19.2 0.0 collective-permute-done.3.refs_4_
  19.2 0.6 %collective-permute-start.13 = (bf16[16,2880]{1,0:T(8,128)(2,1)S(1)}, bf16[16,2880]{1,0:T(8,128)(2,1)S(1)}, u32[]{:S(2)}, u32[]{:S(2)}) collective-permute-start(bf16[16,2880]{1,0:T(8,128)(2,1)S(1)} %collective-permute-done.12.refs_0_), channel_id=1, source_target_pairs={{0,2},{1,3},{2,0},{3,1},{4,6},{5,7},{6,4},{7,5},{8,10},{9,11},{10,... | collective-permute-start | bytes 276488 | tf_op jit(solution)/shard_map/ppermute | solution.py:156
  19.8 0.0 collective-permute-done.4.refs_5_
  19.8 2.8 %collective-permute-start.14 = (bf16[16,2880]{1,0:T(8,128)(2,1)S(1)}, bf16[16,2880]{1,0:T(8,128)(2,1)S(1)}, u32[]{:S(2)}, u32[]{:S(2)}) collective-permute-start(bf16[16,2880]{1,0:T(8,128)(2,1)S(1)} %collective-permute-done.12.refs_0_), channel_id=1, source_target_pairs={{0,4},{1,5},{2,6},{3,7},{4,0},{5,1},{6,2},{7,3},{8,12},{9,13},{10,... | collective-permute-start | bytes 276488 | tf_op jit(solution)/shard_map/ppermute | solution.py:156
  22.7 0.1 collective-permute-start.15
  22.8 3.5 %shard_map.74 = (bf16[64,2880]{1,0:T(8,128)(2,1)S(1)}, bf16[64,2880]{1,0:T(8,128)(2,1)S(1)}) custom-call(bf16[16,2880]{1,0:T(8,128)(2,1)S(1)} %copy-done, bf16[16,2880]{1,0:T(8,128)(2,1)S(1)} %collective-permute-done.refs_1_, bf16[16,2880]{1,0:T(8,128)(2,1)S(1)} %collective-permute-done.1.refs_2_, bf16[16,2880]{1,0:T(8,128)(2,1)S(1)} %collective-permute-done.2.refs_3_, ...), custom_call_target="tpu_custom_call" | custom-call | flops 1592524800 | bytes 12441600 | tf_op jit(solution)/shard_map/pallas_call | solution.py:106
  26.3 0.6 %collective-permute-start.7 = (bf16[64,2880]{1,0:T(8,128)(2,1)S(1)}, bf16[64,2880]{1,0:T(8,128)(2,1)S(1)}, u32[]{:S(2)}, u32[]{:S(2)}) collective-permute-start(bf16[64,2880]{1,0:T(8,128)(2,1)S(1)} %get-tuple-element.16), channel_id=1, source_target_pairs={{0,1},{1,0},{2,3},{3,2},{4,5},{5,4},{6,7},{7,6},{8,9},{9,8},{10,11... | collective-permute-start | bytes 1105928 | tf_op jit(solution)/shard_map/ppermute | solution.py:14
  26.9 0.1 collective-permute-start.17
  27.0 0.4 collective-permute-start.18
  27.4 0.7 %collective-permute-done.15.refs_3_ = bf16[16,2880]{1,0:T(8,128)(2,1)S(1)} collective-permute-done((bf16[16,2880]{1,0:T(8,128)(2,1)S(1)}, bf16[16,2880]{1,0:T(8,128)(2,1)S(1)}, u32[]{:S(2)}, u32[]{:S(2)}) %collective-permute-start.15) | collective-permute-done | bytes 92192 | tf_op jit(solution)/shard_map/ppermute | solution.py:156
  28.2 0.2 collective-permute-done.17.refs_5_
  28.4 0.1 collective-permute-done.18.refs_6_
  28.5 0.9 %collective-permute-done.19.refs_7_ = bf16[16,2880]{1,0:T(8,128)(2,1)S(1)} collective-permute-done((bf16[16,2880]{1,0:T(8,128)(2,1)S(1)}, bf16[16,2880]{1,0:T(8,128)(2,1)S(1)}, u32[]{:S(2)}, u32[]{:S(2)}) %collective-permute-start.19) | collective-permute-done | bytes 92192 | tf_op jit(solution)/shard_map/ppermute | solution.py:14
  29.4 3.5 %shard_map.75 = (bf16[64,2880]{1,0:T(8,128)(2,1)S(1)}, bf16[64,2880]{1,0:T(8,128)(2,1)S(1)}) custom-call(bf16[16,2880]{1,0:T(8,128)(2,1)S(1)} %collective-permute-done.12.refs_0_, bf16[16,2880]{1,0:T(8,128)(2,1)S(1)} %collective-permute-done.13.refs_1_, bf16[16,2880]{1,0:T(8,128)(2,1)S(1)} %collective-permute-done.14.refs_2_, ...), custom_call_target="tpu_custom_call" | custom-call | flops 1592524800 | bytes 12441600 | tf_op jit(solution)/shard_map/pallas_call | solution.py:106
  33.0 0.2 collective-permute-start.20
  33.2 0.1 add_convert_fusion.1
  33.3 1.5 %collective-permute-done.20 = bf16[64,2880]{1,0:T(8,128)(2,1)S(1)} collective-permute-done((bf16[64,2880]{1,0:T(8,128)(2,1)S(1)}, bf16[64,2880]{1,0:T(8,128)(2,1)S(1)}, u32[]{:S(2)}, u32[]{:S(2)}) %collective-permute-start.20) | collective-permute-done | bytes 368672 | tf_op jit(solution)/shard_map/ppermute | solution.py:14
  34.7 0.1 add_convert_fusion
  34.9 2.2 %collective-permute-start.23 = (bf16[16,2880]{1,0:T(8,128)(2,1)S(1)}, bf16[16,2880]{1,0:T(8,128)(2,1)S(1)}, u32[]{:S(2)}, u32[]{:S(2)}) collective-permute-start(bf16[16,2880]{1,0:T(8,128)(2,1)S(1)} %get-tuple-element.23), channel_id=1, source_target_pairs={{0,6},{1,7},{2,4},{3,5},{4,2},{5,3},{6,0},{7,1},{8,14},{9,15},{10,... | collective-permute-start | bytes 276488 | tf_op jit(solution)/shard_map/ppermute | solution.py:156
  37.0 0.2 collective-permute-start.22
  37.2 1.2 %collective-permute-start.21 = (bf16[16,2880]{1,0:T(8,128)(2,1)S(1)}, bf16[16,2880]{1,0:T(8,128)(2,1)S(1)}, u32[]{:S(2)}, u32[]{:S(2)}) collective-permute-start(bf16[16,2880]{1,0:T(8,128)(2,1)S(1)} %get-tuple-element.22), channel_id=1, source_target_pairs={{0,2},{1,3},{2,0},{3,1},{4,6},{5,7},{6,4},{7,5},{8,10},{9,11},{10,... | collective-permute-start | bytes 276488 | tf_op jit(solution)/shard_map/ppermute | solution.py:156
  38.4 2.2 %collective-permute-start.10 = (bf16[16,2880]{1,0:T(8,128)(2,1)S(1)}, bf16[16,2880]{1,0:T(8,128)(2,1)S(1)}, u32[]{:S(2)}, u32[]{:S(2)}) collective-permute-start(bf16[16,2880]{1,0:T(8,128)(2,1)S(1)} %get-tuple-element.20), channel_id=1, source_target_pairs={{0,6},{1,7},{2,4},{3,5},{4,2},{5,3},{6,0},{7,1},{8,14},{9,15},{10,... | collective-permute-start | bytes 276488 | tf_op jit(solution)/shard_map/ppermute | solution.py:156
  40.6 0.2 collective-permute-start.9
  40.8 0.6 %collective-permute-done.23 = bf16[16,2880]{1,0:T(8,128)(2,1)S(1)} collective-permute-done((bf16[16,2880]{1,0:T(8,128)(2,1)S(1)}, bf16[16,2880]{1,0:T(8,128)(2,1)S(1)}, u32[]{:S(2)}, u32[]{:S(2)}) %collective-permute-start.23) | collective-permute-done | bytes 92192 | tf_op jit(solution)/shard_map/ppermute | solution.py:156
  41.4 0.6 %collective-permute-start.8 = (bf16[16,2880]{1,0:T(8,128)(2,1)S(1)}, bf16[16,2880]{1,0:T(8,128)(2,1)S(1)}, u32[]{:S(2)}, u32[]{:S(2)}) collective-permute-start(bf16[16,2880]{1,0:T(8,128)(2,1)S(1)} %get-tuple-element.19), channel_id=1, source_target_pairs={{0,2},{1,3},{2,0},{3,1},{4,6},{5,7},{6,4},{7,5},{8,10},{9,11},{10,... | collective-permute-start | bytes 276488 | tf_op jit(solution)/shard_map/ppermute | solution.py:156
  42.0 0.6 %collective-permute-done.22 = bf16[16,2880]{1,0:T(8,128)(2,1)S(1)} collective-permute-done((bf16[16,2880]{1,0:T(8,128)(2,1)S(1)}, bf16[16,2880]{1,0:T(8,128)(2,1)S(1)}, u32[]{:S(2)}, u32[]{:S(2)}) %collective-permute-start.22) | collective-permute-done | bytes 92192 | tf_op jit(solution)/shard_map/ppermute | solution.py:156
  42.6 2.0 %collective-permute-done.21 = bf16[16,2880]{1,0:T(8,128)(2,1)S(1)} collective-permute-done((bf16[16,2880]{1,0:T(8,128)(2,1)S(1)}, bf16[16,2880]{1,0:T(8,128)(2,1)S(1)}, u32[]{:S(2)}, u32[]{:S(2)}) %collective-permute-start.21) | collective-permute-done | bytes 92192 | tf_op jit(solution)/shard_map/ppermute | solution.py:156
  44.6 0.1 add_convert_fusion.3
  44.7 1.4 %collective-permute-start.24 = (bf16[16,2880]{1,0:T(8,128)(2,1)S(1)}, bf16[16,2880]{1,0:T(8,128)(2,1)S(1)}, u32[]{:S(2)}, u32[]{:S(2)}) collective-permute-start(bf16[16,2880]{1,0:T(8,128)(2,1)S(1)} %add_convert_fusion.3), channel_id=1, source_target_pairs={{0,8},{1,9},{2,10},{3,11},{4,12},{5,13},{6,14},{7,15},{8,0},{9,1},... | collective-permute-start | bytes 276488 | tf_op jit(solution)/shard_map/ppermute | solution.py:156
  46.2 0.5 collective-permute-done.8
  46.6 4.6 %collective-permute-done.24 = bf16[16,2880]{1,0:T(8,128)(2,1)S(1)} collective-permute-done((bf16[16,2880]{1,0:T(8,128)(2,1)S(1)}, bf16[16,2880]{1,0:T(8,128)(2,1)S(1)}, u32[]{:S(2)}, u32[]{:S(2)}) %collective-permute-start.24) | collective-permute-done | bytes 92192 | tf_op jit(solution)/shard_map/ppermute | solution.py:156
  51.3 0.8 %add_convert_fusion.2 = bf16[16,2880]{1,0:T(8,128)(2,1)} fusion(bf16[16,2880]{1,0:T(8,128)(2,1)S(1)} %collective-permute-done.24, bf16[16,2880]{1,0:T(8,128)(2,1)S(1)} %collective-permute-done.10, bf16[16,2880]{1,0:T(8,128)(2,1)S(1)} %collective-permute-done.9, bf16[16,2880]{1,0:T(8,128)(2,1)S(1)} %collective-permute-done.8, bf16[16,2880]{1,0:T(8,128)(2,1)S(1)} %copy-done, ...), kind=kLoop, calls=%fused_computation.2 | loop fusion | flops 737280 | bytes 645376 | tf_op jit(solution)/shard_map/convert_element_type | solution.py:186
  (19 shorter events, 0.1 us)
Async XLA Ops:
  0.0 18.4 %collective-permute-start.12 = (bf16[16,2880]{1,0:T(8,128)(2,1)}, bf16[16,2880]{1,0:T(8,128)(2,1)S(1)}, u32[]{:S(2)}, u32[]{:S(2)}) collective-permute-start(bf16[16,2880]{1,0:T(8,128)(2,1)} %refs_0_.1), channel_id=1, source_target_pairs={{0,8},{1,9},{2,10},{3,11},{4,12},{5,13},{6,14},{7,15},{8,0},{9,1},... | collective-permute-start | bytes 276488 | tf_op jit(solution)/shard_map/ppermute | solution.py:156
  4.0 4.8 %collective-permute-start = (bf16[16,2880]{1,0:T(8,128)(2,1)}, bf16[16,2880]{1,0:T(8,128)(2,1)S(1)}, u32[]{:S(2)}, u32[]{:S(2)}) collective-permute-start(bf16[16,2880]{1,0:T(8,128)(2,1)} %refs_0_.1), channel_id=1, source_target_pairs={{0,2},{1,3},{2,0},{3,1},{4,6},{5,7},{6,4},{7,5},{8,10},{9,11},{10,... | collective-permute-start | bytes 276488 | tf_op jit(solution)/shard_map/ppermute | solution.py:156
  5.6 5.8 %collective-permute-start.1 = (bf16[16,2880]{1,0:T(8,128)(2,1)}, bf16[16,2880]{1,0:T(8,128)(2,1)S(1)}, u32[]{:S(2)}, u32[]{:S(2)}) collective-permute-start(bf16[16,2880]{1,0:T(8,128)(2,1)} %refs_0_.1), channel_id=1, source_target_pairs={{0,4},{1,5},{2,6},{3,7},{4,0},{5,1},{6,2},{7,3},{8,12},{9,13},{10,... | collective-permute-start | bytes 276488 | tf_op jit(solution)/shard_map/ppermute | solution.py:156
  7.1 5.7 %collective-permute-start.2 = (bf16[16,2880]{1,0:T(8,128)(2,1)}, bf16[16,2880]{1,0:T(8,128)(2,1)S(1)}, u32[]{:S(2)}, u32[]{:S(2)}) collective-permute-start(bf16[16,2880]{1,0:T(8,128)(2,1)} %refs_0_.1), channel_id=1, source_target_pairs={{0,6},{1,7},{2,4},{3,5},{4,2},{5,3},{6,0},{7,1},{8,14},{9,15},{10,... | collective-permute-start | bytes 276488 | tf_op jit(solution)/shard_map/ppermute | solution.py:156
  7.5 11.7 %collective-permute-start.3 = (bf16[16,2880]{1,0:T(8,128)(2,1)}, bf16[16,2880]{1,0:T(8,128)(2,1)S(1)}, u32[]{:S(2)}, u32[]{:S(2)}) collective-permute-start(bf16[16,2880]{1,0:T(8,128)(2,1)} %refs_0_.1), channel_id=1, source_target_pairs={{0,1},{1,0},{2,3},{3,2},{4,5},{5,4},{6,7},{7,6},{8,9},{9,8},{10,11... | collective-permute-start | bytes 276488 | tf_op jit(solution)/shard_map/ppermute | solution.py:14
  8.8 11.0 %collective-permute-start.4 = (bf16[16,2880]{1,0:T(8,128)(2,1)S(1)}, bf16[16,2880]{1,0:T(8,128)(2,1)S(1)}, u32[]{:S(2)}, u32[]{:S(2)}) collective-permute-start(bf16[16,2880]{1,0:T(8,128)(2,1)S(1)} %collective-permute-done.refs_1_), channel_id=1, source_target_pairs={{0,1},{1,0},{2,3},{3,2},{4,5},{5,4},{6,7},{7,6},{8,9},{9,8},{10,11... | collective-permute-start | bytes 276488 | tf_op jit(solution)/shard_map/ppermute | solution.py:14
  11.4 11.3 %collective-permute-start.5 = (bf16[16,2880]{1,0:T(8,128)(2,1)S(1)}, bf16[16,2880]{1,0:T(8,128)(2,1)S(1)}, u32[]{:S(2)}, u32[]{:S(2)}) collective-permute-start(bf16[16,2880]{1,0:T(8,128)(2,1)S(1)} %collective-permute-done.1.refs_2_), channel_id=1, source_target_pairs={{0,1},{1,0},{2,3},{3,2},{4,5},{5,4},{6,7},{7,6},{8,9},{9,8},{10,11... | collective-permute-start | bytes 276488 | tf_op jit(solution)/shard_map/ppermute | solution.py:14
  12.8 10.0 %collective-permute-start.6 = (bf16[16,2880]{1,0:T(8,128)(2,1)S(1)}, bf16[16,2880]{1,0:T(8,128)(2,1)S(1)}, u32[]{:S(2)}, u32[]{:S(2)}) collective-permute-start(bf16[16,2880]{1,0:T(8,128)(2,1)S(1)} %collective-permute-done.2.refs_3_), channel_id=1, source_target_pairs={{0,1},{1,0},{2,3},{3,2},{4,5},{5,4},{6,7},{7,6},{8,9},{9,8},{10,11... | collective-permute-start | bytes 276488 | tf_op jit(solution)/shard_map/ppermute | solution.py:14
  13.6 9.2 %copy-start = (bf16[16,2880]{1,0:T(8,128)(2,1)S(1)}, bf16[16,2880]{1,0:T(8,128)(2,1)}, u32[]{:S(2)}) copy-start(bf16[16,2880]{1,0:T(8,128)(2,1)} %refs_0_.1) | copy-start | bytes 276484
  18.4 8.0 %collective-permute-start.11 = (f32[16,4]{0,1:T(4,128)S(1)}, f32[16,4]{0,1:T(4,128)S(1)}, u32[]{:S(2)}, u32[]{:S(2)}) collective-permute-start(f32[16,4]{0,1:T(4,128)S(1)} %slice.72), channel_id=1, source_target_pairs={{0,8},{1,9},{2,10},{3,11},{4,12},{5,13},{6,14},{7,15},{8,0},{9,1},... | collective-permute-start | bytes 776 | tf_op jit(solution)/shard_map/ppermute | solution.py:156
  19.2 7.7 %collective-permute-start.13 = (bf16[16,2880]{1,0:T(8,128)(2,1)S(1)}, bf16[16,2880]{1,0:T(8,128)(2,1)S(1)}, u32[]{:S(2)}, u32[]{:S(2)}) collective-permute-start(bf16[16,2880]{1,0:T(8,128)(2,1)S(1)} %collective-permute-done.12.refs_0_), channel_id=1, source_target_pairs={{0,2},{1,3},{2,0},{3,1},{4,6},{5,7},{6,4},{7,5},{8,10},{9,11},{10,... | collective-permute-start | bytes 276488 | tf_op jit(solution)/shard_map/ppermute | solution.py:156
  19.8 7.2 %collective-permute-start.14 = (bf16[16,2880]{1,0:T(8,128)(2,1)S(1)}, bf16[16,2880]{1,0:T(8,128)(2,1)S(1)}, u32[]{:S(2)}, u32[]{:S(2)}) collective-permute-start(bf16[16,2880]{1,0:T(8,128)(2,1)S(1)} %collective-permute-done.12.refs_0_), channel_id=1, source_target_pairs={{0,4},{1,5},{2,6},{3,7},{4,0},{5,1},{6,2},{7,3},{8,12},{9,13},{10,... | collective-permute-start | bytes 276488 | tf_op jit(solution)/shard_map/ppermute | solution.py:156
  22.7 5.5 %collective-permute-start.15 = (bf16[16,2880]{1,0:T(8,128)(2,1)S(1)}, bf16[16,2880]{1,0:T(8,128)(2,1)S(1)}, u32[]{:S(2)}, u32[]{:S(2)}) collective-permute-start(bf16[16,2880]{1,0:T(8,128)(2,1)S(1)} %collective-permute-done.12.refs_0_), channel_id=1, source_target_pairs={{0,6},{1,7},{2,4},{3,5},{4,2},{5,3},{6,0},{7,1},{8,14},{9,15},{10,... | collective-permute-start | bytes 276488 | tf_op jit(solution)/shard_map/ppermute | solution.py:156
  22.8 5.4 %collective-permute-start.16 = (bf16[16,2880]{1,0:T(8,128)(2,1)S(1)}, bf16[16,2880]{1,0:T(8,128)(2,1)S(1)}, u32[]{:S(2)}, u32[]{:S(2)}) collective-permute-start(bf16[16,2880]{1,0:T(8,128)(2,1)S(1)} %collective-permute-done.12.refs_0_), channel_id=1, source_target_pairs={{0,1},{1,0},{2,3},{3,2},{4,5},{5,4},{6,7},{7,6},{8,9},{9,8},{10,11... | collective-permute-start | bytes 276488 | tf_op jit(solution)/shard_map/ppermute | solution.py:14
  26.3 6.8 %collective-permute-start.7 = (bf16[64,2880]{1,0:T(8,128)(2,1)S(1)}, bf16[64,2880]{1,0:T(8,128)(2,1)S(1)}, u32[]{:S(2)}, u32[]{:S(2)}) collective-permute-start(bf16[64,2880]{1,0:T(8,128)(2,1)S(1)} %get-tuple-element.16), channel_id=1, source_target_pairs={{0,1},{1,0},{2,3},{3,2},{4,5},{5,4},{6,7},{7,6},{8,9},{9,8},{10,11... | collective-permute-start | bytes 1105928 | tf_op jit(solution)/shard_map/ppermute | solution.py:14
  26.9 1.5 %collective-permute-start.17 = (bf16[16,2880]{1,0:T(8,128)(2,1)S(1)}, bf16[16,2880]{1,0:T(8,128)(2,1)S(1)}, u32[]{:S(2)}, u32[]{:S(2)}) collective-permute-start(bf16[16,2880]{1,0:T(8,128)(2,1)S(1)} %collective-permute-done.13.refs_1_), channel_id=1, source_target_pairs={{0,1},{1,0},{2,3},{3,2},{4,5},{5,4},{6,7},{7,6},{8,9},{9,8},{10,11... | collective-permute-start | bytes 276488 | tf_op jit(solution)/shard_map/ppermute | solution.py:14
  27.0 1.5 %collective-permute-start.18 = (bf16[16,2880]{1,0:T(8,128)(2,1)S(1)}, bf16[16,2880]{1,0:T(8,128)(2,1)S(1)}, u32[]{:S(2)}, u32[]{:S(2)}) collective-permute-start(bf16[16,2880]{1,0:T(8,128)(2,1)S(1)} %collective-permute-done.14.refs_2_), channel_id=1, source_target_pairs={{0,1},{1,0},{2,3},{3,2},{4,5},{5,4},{6,7},{7,6},{8,9},{9,8},{10,11... | collective-permute-start | bytes 276488 | tf_op jit(solution)/shard_map/ppermute | solution.py:14
  28.1 1.3 %collective-permute-start.19 = (bf16[16,2880]{1,0:T(8,128)(2,1)S(1)}, bf16[16,2880]{1,0:T(8,128)(2,1)S(1)}, u32[]{:S(2)}, u32[]{:S(2)}) collective-permute-start(bf16[16,2880]{1,0:T(8,128)(2,1)S(1)} %collective-permute-done.15.refs_3_), channel_id=1, source_target_pairs={{0,1},{1,0},{2,3},{3,2},{4,5},{5,4},{6,7},{7,6},{8,9},{9,8},{10,11... | collective-permute-start | bytes 276488 | tf_op jit(solution)/shard_map/ppermute | solution.py:14
  33.0 1.8 %collective-permute-start.20 = (bf16[64,2880]{1,0:T(8,128)(2,1)S(1)}, bf16[64,2880]{1,0:T(8,128)(2,1)S(1)}, u32[]{:S(2)}, u32[]{:S(2)}) collective-permute-start(bf16[64,2880]{1,0:T(8,128)(2,1)S(1)} %get-tuple-element.18), channel_id=1, source_target_pairs={{0,1},{1,0},{2,3},{3,2},{4,5},{5,4},{6,7},{7,6},{8,9},{9,8},{10,11... | collective-permute-start | bytes 1105928 | tf_op jit(solution)/shard_map/ppermute | solution.py:14
  34.9 6.5 %collective-permute-start.23 = (bf16[16,2880]{1,0:T(8,128)(2,1)S(1)}, bf16[16,2880]{1,0:T(8,128)(2,1)S(1)}, u32[]{:S(2)}, u32[]{:S(2)}) collective-permute-start(bf16[16,2880]{1,0:T(8,128)(2,1)S(1)} %get-tuple-element.23), channel_id=1, source_target_pairs={{0,6},{1,7},{2,4},{3,5},{4,2},{5,3},{6,0},{7,1},{8,14},{9,15},{10,... | collective-permute-start | bytes 276488 | tf_op jit(solution)/shard_map/ppermute | solution.py:156
  37.0 5.6 %collective-permute-start.22 = (bf16[16,2880]{1,0:T(8,128)(2,1)S(1)}, bf16[16,2880]{1,0:T(8,128)(2,1)S(1)}, u32[]{:S(2)}, u32[]{:S(2)}) collective-permute-start(bf16[16,2880]{1,0:T(8,128)(2,1)S(1)} %get-tuple-element.24), channel_id=1, source_target_pairs={{0,4},{1,5},{2,6},{3,7},{4,0},{5,1},{6,2},{7,3},{8,12},{9,13},{10,... | collective-permute-start | bytes 276488 | tf_op jit(solution)/shard_map/ppermute | solution.py:156
  37.2 7.4 %collective-permute-start.21 = (bf16[16,2880]{1,0:T(8,128)(2,1)S(1)}, bf16[16,2880]{1,0:T(8,128)(2,1)S(1)}, u32[]{:S(2)}, u32[]{:S(2)}) collective-permute-start(bf16[16,2880]{1,0:T(8,128)(2,1)S(1)} %get-tuple-element.22), channel_id=1, source_target_pairs={{0,2},{1,3},{2,0},{3,1},{4,6},{5,7},{6,4},{7,5},{8,10},{9,11},{10,... | collective-permute-start | bytes 276488 | tf_op jit(solution)/shard_map/ppermute | solution.py:156
  38.4 7.7 %collective-permute-start.10 = (bf16[16,2880]{1,0:T(8,128)(2,1)S(1)}, bf16[16,2880]{1,0:T(8,128)(2,1)S(1)}, u32[]{:S(2)}, u32[]{:S(2)}) collective-permute-start(bf16[16,2880]{1,0:T(8,128)(2,1)S(1)} %get-tuple-element.20), channel_id=1, source_target_pairs={{0,6},{1,7},{2,4},{3,5},{4,2},{5,3},{6,0},{7,1},{8,14},{9,15},{10,... | collective-permute-start | bytes 276488 | tf_op jit(solution)/shard_map/ppermute | solution.py:156
  40.6 5.6 %collective-permute-start.9 = (bf16[16,2880]{1,0:T(8,128)(2,1)S(1)}, bf16[16,2880]{1,0:T(8,128)(2,1)S(1)}, u32[]{:S(2)}, u32[]{:S(2)}) collective-permute-start(bf16[16,2880]{1,0:T(8,128)(2,1)S(1)} %get-tuple-element.21), channel_id=1, source_target_pairs={{0,4},{1,5},{2,6},{3,7},{4,0},{5,1},{6,2},{7,3},{8,12},{9,13},{10,... | collective-permute-start | bytes 276488 | tf_op jit(solution)/shard_map/ppermute | solution.py:156
  41.4 5.3 %collective-permute-start.8 = (bf16[16,2880]{1,0:T(8,128)(2,1)S(1)}, bf16[16,2880]{1,0:T(8,128)(2,1)S(1)}, u32[]{:S(2)}, u32[]{:S(2)}) collective-permute-start(bf16[16,2880]{1,0:T(8,128)(2,1)S(1)} %get-tuple-element.19), channel_id=1, source_target_pairs={{0,2},{1,3},{2,0},{3,1},{4,6},{5,7},{6,4},{7,5},{8,10},{9,11},{10,... | collective-permute-start | bytes 276488 | tf_op jit(solution)/shard_map/ppermute | solution.py:156
  44.7 6.5 %collective-permute-start.24 = (bf16[16,2880]{1,0:T(8,128)(2,1)S(1)}, bf16[16,2880]{1,0:T(8,128)(2,1)S(1)}, u32[]{:S(2)}, u32[]{:S(2)}) collective-permute-start(bf16[16,2880]{1,0:T(8,128)(2,1)S(1)} %add_convert_fusion.3), channel_id=1, source_target_pairs={{0,8},{1,9},{2,10},{3,11},{4,12},{5,13},{6,14},{7,15},{8,0},{9,1},... | collective-permute-start | bytes 276488 | tf_op jit(solution)/shard_map/ppermute | solution.py:156

commit v4 on v3

--- a/solution.py
+++ b/solution.py
@@ -78,36 +78,41 @@
     return (residual.astype(jnp.float32) + combined).astype(jnp.bfloat16)
 
 
-def expert_kernel(count, *refs):
-    blocks, (gain_ref, gate_ref, up_ref, down_ref) = refs[:count], refs[count : count + 4]
-    mine_ref, theirs_ref, normed_ref = refs[count + 4 :]
-    rows = blocks[0].shape[0]
+def expert_kernel(groups, *refs):
+    count = sum(groups)
+    blocks, (gain_ref, gate_ref, up_ref, down_ref, table_ref) = refs[:count], refs[count : count + 5]
+    outs, table_out_ref, normed_ref = refs[count + 5 : -2], refs[-2], refs[-1]
+    table_out_ref[...] = table_ref[...]
+    rows, model = blocks[0].shape
+    gain = gain_ref[...].reshape(1, model)
     for i, block in enumerate(blocks):
         x = block[...].astype(jnp.float32)
         scale = lax.rsqrt(jnp.mean(x * x, axis=-1, keepdims=True) + 1e-05)
-        normed_ref[pl.ds(i * rows, rows), :] = (x * scale * gain_ref[...]).astype(jnp.bfloat16)
+        normed_ref[pl.ds(i * rows, rows), :] = (x * scale * gain).astype(jnp.bfloat16)
     normed = normed_ref[...]
     across = (((1,), (1,)), ((), ()))
     gate = lax.dot_general(normed, gate_ref[...], across, preferred_element_type=jnp.float32)
     upper = lax.dot_general(normed, up_ref[...], across, preferred_element_type=jnp.float32)
     act = (gate * jax.nn.sigmoid(1.702 * gate) * (upper + 1.0)).astype(jnp.bfloat16)
     out = jnp.dot(act, down_ref[...], preferred_element_type=jnp.float32).astype(jnp.bfloat16)
-    half = rows * (count // 2)
-    mine_ref[...] = out[:half]
-    theirs_ref[...] = out[half:]
-
-
-def expert_parts(blocks, gain, gate_w, up_w, down_w):
-    count = len(blocks)
+    start = 0
+    for size, out_ref in zip(groups, outs):
+        out_ref[...] = out[start * rows : (start + size) * rows]
+        start += size
+
+
+def expert_parts(groups, gain, gate_w, up_w, down_w, table):
+    blocks = sum(groups, [])
+    sizes = tuple(len(group) for group in groups)
     rows, model = blocks[0].shape
-    out = jax.ShapeDtypeStruct((rows * count // 2, model), jnp.bfloat16)
+    count, hidden = len(blocks), gate_w.shape[0]
     vmem = pl.BlockSpec(memory_space=pltpu.VMEM)
-    hidden = gate_w.shape[0]
     return pl.pallas_call(
-        functools.partial(expert_kernel, count),
-        out_shape=(out, out),
-        in_specs=[vmem] * (count + 4),
-        out_specs=(vmem, vmem),
+        functools.partial(expert_kernel, sizes),
+        out_shape=tuple(jax.ShapeDtypeStruct((rows * size, model), jnp.bfloat16) for size in sizes)
+        + (jax.ShapeDtypeStruct(table.shape, table.dtype),),
+        in_specs=[vmem] * (count + 5),
+        out_specs=(vmem,) * (len(groups) + 1),
         scratch_shapes=[pltpu.VMEM((rows * count, model), jnp.bfloat16)],
         cost_estimate=pl.CostEstimate(
             flops=6 * rows * count * model * hidden,
@@ -115,41 +120,61 @@
             transcendentals=rows * count * hidden,
         ),
         compiler_params=pltpu.CompilerParams(vmem_limit_bytes=24 * 2**20),
-    )(*blocks, gain, gate_w, up_w, down_w)
-
-
-def load_kernel(count, *refs):
-    sources, targets, sems = refs[:count], refs[count : 2 * count], refs[2 * count]
-    copies = [
-        pltpu.make_async_copy(source, target, sems.at[i])
-        for i, (source, target) in enumerate(zip(sources, targets))
-    ]
+    )(*blocks, gain, gate_w, up_w, down_w, table)
+
+
+def load_kernel(pieces, chip_ref, ids_ref, weights_ref, *refs):
+    count = (len(refs) - 3) // 2
+    sources, near_ref, far_ref = refs[:count], refs[count], refs[count + 1]
+    targets, sems = refs[count + 2 : -1], refs[-1]
+    copies = []
+    for source, target in zip(sources, targets):
+        part = source.shape[0] // pieces
+        for piece in range(pieces):
+            span = pl.ds(piece * part, part)
+            copies.append(pltpu.make_async_copy(source.at[span], target.at[span], sems.at[len(copies)]))
     for copy in copies:
         copy.start()
+    chosen, rows = ids_ref.shape
+    half = near_ref.shape[1]
+    expert = chip_ref[0] ^ lax.broadcasted_iota(jnp.int32, (2 * half, rows), 0)
+    table = jnp.zeros((2 * half, rows), jnp.float32)
+    for k in range(chosen):
+        table += jnp.where(ids_ref[k : k + 1, :] == expert, weights_ref[k : k + 1, :], 0.0)
+    near_ref[...] = table[:half].T
+    far_ref[...] = table[half:].T
     for copy in copies:
         copy.wait()
 
 
-def load(*arrays):
-    count = len(arrays)
+def load(chip, expert_ids, expert_weights, half, arrays):
+    rows = expert_ids.shape[0]
+    pieces = 3 if all(a.shape[0] % 48 == 0 for a in arrays) else 1
+    vmem = pl.BlockSpec(memory_space=pltpu.VMEM)
+    table = jax.ShapeDtypeStruct((rows, half), jnp.float32)
     return pl.pallas_call(
-        functools.partial(load_kernel, count),
-        out_shape=tuple(pltpu.VMEM(a.shape, a.dtype) for a in arrays),
-        in_specs=[pl.BlockSpec(memory_space=pltpu.HBM)] * count,
-        out_specs=(pl.BlockSpec(memory_space=pltpu.VMEM),) * count,
-        scratch_shapes=[pltpu.SemaphoreType.DMA((count,))],
+        functools.partial(load_kernel, pieces),
+        out_shape=(table, table) + tuple(pltpu.VMEM(a.shape, a.dtype) for a in arrays),
+        in_specs=[pl.BlockSpec(memory_space=pltpu.SMEM), vmem, vmem]
+        + [pl.BlockSpec(memory_space=pltpu.HBM)] * len(arrays),
+        out_specs=(vmem,) * (2 + len(arrays)),
+        scratch_shapes=[pltpu.SemaphoreType.DMA((pieces * len(arrays),))],
         cost_estimate=pl.CostEstimate(
             flops=0, bytes_accessed=2 * sum(a.size * a.dtype.itemsize for a in arrays), transcendentals=0
         ),
         compiler_params=pltpu.CompilerParams(vmem_limit_bytes=16 * 2**20),
-    )(*(pltpu.with_memory_space_constraint(a, pltpu.HBM) for a in arrays))
+    )(
+        chip.reshape(1),
+        expert_ids.T,
+        expert_weights.T,
+        *(pltpu.with_memory_space_constraint(a, pltpu.HBM) for a in arrays),
+    )
 
 
 def halves(residual, norm_gain, expert_ids, expert_weights, gate_proj, up_proj, down_proj):
     rows, model = residual.shape
     chips = lax.axis_size("expert") // 2
     half = chips // 2
-    gain = norm_gain.reshape(1, model)
 
     def across(value, mask):
         pairs = [(i, i ^ (2 * mask)) for i in range(2 * chips)]
@@ -160,28 +185,29 @@
 
     x = residual
     mirrored = across(x, half)
-    near = [across(x, mask) for mask in range(half)]
-    near += [swap(block) for block in near]
-    held = load(gate_proj[0].T, up_proj[0].T, down_proj[0])
-    far = [across(mirrored, mask) for mask in range(half)]
-    far += [swap(block) for block in far]
-
-    expert = (lax.axis_index("expert") // 2) ^ jnp.arange(chips, dtype=jnp.int32)
-    weights = jnp.sum(
-        jnp.where(expert_ids[:, :, None] == expert[None, None, :], expert_weights[:, :, None], 0.0), axis=1
-    )
-    mirror_weights = across(weights[:, half:], half)
-
-    def mix(blocks, block_weights):
-        mine, theirs = expert_parts(blocks, gain, *held)
+    near = [across(x, mask) for mask in range(1, half)]
+    near_swapped = [swap(x)]
+    chip = lax.axis_index("expert") // 2
+    near_weights, far_weights, *held = load(
+        chip, expert_ids, expert_weights, half, (gate_proj[0].T, up_proj[0].T, down_proj[0])
+    )
+    near_weights, far_weights, *near = lax.optimization_barrier((near_weights, far_weights, *near))
+    near_swapped += [swap(block) for block in near]
+    far = [across(mirrored, mask) for mask in range(1, half)]
+    far_swapped = [swap(mirrored)] + [swap(block) for block in far]
+    *parts, mirror_weights = expert_parts(
+        (far_swapped, [mirrored] + far, near_swapped, [x] + near), norm_gain, *held, across(far_weights, half)
+    )
+
+    def mix(theirs, mine, block_weights):
         done = pair_sum(mine, swap(theirs)).reshape(half, rows, model)
         total = jnp.zeros((rows, model), jnp.float32)
         for mask in range(half):
             total += block_weights[:, mask][:, None] * across(done[mask], mask).astype(jnp.float32)
         return total
 
-    own = mix(near, weights[:, :half])
-    other = mix(far, mirror_weights)
+    other = mix(parts[0], parts[1], mirror_weights)
+    own = mix(parts[2], parts[3], near_weights)
     own += across(other.astype(jnp.bfloat16), half).astype(jnp.float32)
     return (x.astype(jnp.float32) + own).astype(jnp.bfloat16)
 

time: 52.3 us -> 47.3 us (0.904)
  waiting for transfers between devices: 16.3 us -> 11.7 us
  Pallas kernels: 11.8 us -> 8.97 us
  starting transfers between devices: 21.2 us -> 23.4 us
  local copies, waits for them, and re-layouts: 0.78 us -> 1.84 us
  other arithmetic: 1.91 us -> 1.14 us
    ppermute x15, waiting for transfers between devices: 13.6 us -> 9.8 us  [across(): return lax.ppermute(value, 'expert', pairs) if mask else value]
    pallas_call x3 -> x2, Pallas kernels: 11.8 us -> 8.97 us  [the longest x1 4.76 us: load(): pl.pallas_call(functools.partial(load_kernel, pieces), out_shape=(table,...]
    ppermute x15, starting transfers between devices: 19.9 us -> 21.3 us  [across(): return lax.ppermute(value, 'expert', pairs) if mask else value]
    unnamed x2 -> x8, local copies, waits for them, and re-layouts: 0.01 us -> 1.37 us
    ppermute x10, waiting for transfers between devices: 2.75 us -> 1.92 us  [partner(): return lax.ppermute(value, axis, pairs)]
    ppermute x10, starting transfers between devices: 1.32 us -> 2.11 us  [partner(): return lax.ppermute(value, axis, pairs)]
    reduce_sum x1 -> x0, other arithmetic: 0.77 us -> none  [halves(): jnp.sum(jnp.where(expert_ids[:, :, None] == expert[None, None, :], expert...]
    reshape x1 -> x0, local copies, waits for them, and re-layouts: 0.72 us -> none  [halves(): gain = norm_gain.reshape(1, model)]
  transfers between devices with their start and end apart: 25 -> 25, of which waited for: 13 -> 11; matrix products, arithmetic and copies ran while one was open for 3% -> 2% of each run, Pallas kernels for 23% -> 10%
where the time goes in v4:
time: 47.3 us; the launch traced here: 47.2 us
  starting transfers between devices  23.4 us (49%)
  waiting for transfers between devices  11.7 us (25%)
  Pallas kernels  8.97 us (19%)
  local copies, waits for them, and re-layouts  1.84 us (4%)
  other arithmetic  1.14 us (2%)
    ppermute x15, starting transfers between devices, across(): return lax.ppermute(value, 'expert', pairs) if mask else value  21.3 us
    ppermute x15, waiting for transfers between devices, across(): return lax.ppermute(value, 'expert', pairs) if mask else value  9.8 us
    pallas_call x1, Pallas kernels, load(): pl.pallas_call(functools.partial(load_kernel, pieces), out_shape=(table,...  4.76 us
    pallas_call x1, Pallas kernels, expert_parts(): pl.pallas_call(functools.partial(expert_kernel, sizes), out_shape=tuple((...  4.21 us
    ppermute x10, starting transfers between devices, partner(): return lax.ppermute(value, axis, pairs)  2.11 us
    ppermute x10, waiting for transfers between devices, partner(): return lax.ppermute(value, axis, pairs)  1.92 us
    unnamed x8, local copies, waits for them, and re-layouts  1.37 us
  transfers between devices with their start and end apart: 25, of which 11 were waited for; matrix products, arithmetic and copies ran while one was open for 2% of the time, Pallas kernels for 10%

profile of v4, /device:TPU:0, one launch (start us, length us, event | category | flops | bytes accessed | tf_op | source)
XLA Modules:
  0.0 47.2 jit_solution(16411033648163991389)
XLA Ops:
  0.0 4.0 %collective-permute-start.2 = (bf16[16,2880]{1,0:T(8,128)(2,1)}, bf16[16,2880]{1,0:T(8,128)(2,1)S(1)}, u32[]{:S(2)}, u32[]{:S(2)}) collective-permute-start(bf16[16,2880]{1,0:T(8,128)(2,1)} %refs_12_.1), channel_id=1, source_target_pairs={{0,6},{1,7},{2,4},{3,5},{4,2},{5,3},{6,0},{7,1},{8,14},{9,15},{10,... | collective-permute-start | bytes 276488 | tf_op jit(solution)/shard_map/ppermute | solution.py:181
  4.0 0.4 collective-permute-start.1
  4.4 0.1 collective-permute-start
  4.5 3.0 %collective-permute-start.3 = (bf16[16,2880]{1,0:T(8,128)(2,1)}, bf16[16,2880]{1,0:T(8,128)(2,1)S(1)}, u32[]{:S(2)}, u32[]{:S(2)}) collective-permute-start(bf16[16,2880]{1,0:T(8,128)(2,1)} %refs_12_.1), channel_id=1, source_target_pairs={{0,8},{1,9},{2,10},{3,11},{4,12},{5,13},{6,14},{7,15},{8,0},{9,1},... | collective-permute-start | bytes 276488 | tf_op jit(solution)/shard_map/ppermute | solution.py:181
  7.5 0.0 collective-permute-start.11
  7.5 0.7 %copy-done.2 = s32[16,4]{0,1:T(4,128)S(1)} copy-done((s32[16,4]{0,1:T(4,128)S(1)}, s32[16,4]{0,1:T(4,128)}, u32[]{:S(2)}) %copy-start.2) | copy-done | bytes 280
  8.2 0.7 %copy-done.3 = f32[16,4]{0,1:T(4,128)S(1)} copy-done((f32[16,4]{0,1:T(4,128)S(1)}, f32[16,4]{0,1:T(4,128)}, u32[]{:S(2)}) %copy-start.3) | copy-done | bytes 280
  8.9 4.8 %shard_map.73 = (f32[16,4]{1,0:T(8,128)S(1)}, f32[16,4]{1,0:T(8,128)S(1)}, bf16[720,2880]{1,0:T(8,128)(2,1)S(1)}, bf16[720,2880]{1,0:T(8,128)(2,1)S(1)}, bf16[720,2880]{1,0:T(8,128)(2,1)S(1)}) custom-call(s32[1]{0:T(128)} %bitcast.chip_ref, s32[4,16]{1,0:T(4,128)S(1)} %bitcast.10, f32[4,16]{1,0:T(4,128)S(1)} %bitcast.11, bf16[720,2880]{1,0:T(8,128)(2,1)} %bitcast.12, ...), custom_call_target="tpu_custom_call" | custom-call | bytes 24883200 | tf_op jit(solution)/shard_map/pallas_call | solution.py:155
  13.7 0.0 collective-permute-done.2.refs_15_
  13.7 0.0 collective-permute-done.1.refs_14_
  13.7 2.6 %collective-permute-start.9 = (bf16[16,2880]{1,0:T(8,128)(2,1)S(1)}, bf16[16,2880]{1,0:T(8,128)(2,1)S(1)}, u32[]{:S(2)}, u32[]{:S(2)}) collective-permute-start(bf16[16,2880]{1,0:T(8,128)(2,1)S(1)} %collective-permute-done.3.refs_4_), channel_id=1, source_target_pairs={{0,6},{1,7},{2,4},{3,5},{4,2},{5,3},{6,0},{7,1},{8,14},{9,15},{10,... | collective-permute-start | bytes 276488 | tf_op jit(solution)/shard_map/ppermute | solution.py:181
  16.3 0.5 %collective-permute-start.15 = (f32[16,4]{1,0:T(8,128)S(1)}, f32[16,4]{1,0:T(8,128)S(1)}, u32[]{:S(2)}, u32[]{:S(2)}) collective-permute-start(f32[16,4]{1,0:T(8,128)S(1)} %get-tuple-element.29), channel_id=1, source_target_pairs={{0,8},{1,9},{2,10},{3,11},{4,12},{5,13},{6,14},{7,15},{8,0},{9,1},... | collective-permute-start | bytes 776 | tf_op jit(solution)/shard_map/ppermute | solution.py:181
  16.8 0.3 collective-permute-start.7
  17.1 0.2 collective-permute-start.5
  17.3 0.0 collective-permute-done.11.refs_8_
  17.3 0.0 collective-permute-start.4
  17.3 3.6 %collective-permute-done.15.refs_20_ = f32[16,4]{1,0:T(8,128)S(1)} collective-permute-done((f32[16,4]{1,0:T(8,128)S(1)}, f32[16,4]{1,0:T(8,128)S(1)}, u32[]{:S(2)}, u32[]{:S(2)}) %collective-permute-start.15) | collective-permute-done | bytes 288 | tf_op jit(solution)/shard_map/ppermute | solution.py:181
  21.0 0.0 collective-permute-start.12
  21.0 0.5 %collective-permute-start.13 = (bf16[16,2880]{1,0:T(8,128)(2,1)S(1)}, bf16[16,2880]{1,0:T(8,128)(2,1)S(1)}, u32[]{:S(2)}, u32[]{:S(2)}) collective-permute-start(bf16[16,2880]{1,0:T(8,128)(2,1)S(1)} %collective-permute-done.1.refs_14_), channel_id=1, source_target_pairs={{0,1},{1,0},{2,3},{3,2},{4,5},{5,4},{6,7},{7,6},{8,9},{9,8},{10,11... | collective-permute-start | bytes 276488 | tf_op jit(solution)/shard_map/ppermute | solution.py:14
  21.5 0.6 %collective-permute-done.7.refs_6_ = bf16[16,2880]{1,0:T(8,128)(2,1)S(1)} collective-permute-done((bf16[16,2880]{1,0:T(8,128)(2,1)S(1)}, bf16[16,2880]{1,0:T(8,128)(2,1)S(1)}, u32[]{:S(2)}, u32[]{:S(2)}) %collective-permute-start.7) | collective-permute-done | bytes 92192 | tf_op jit(solution)/shard_map/ppermute | solution.py:181
  22.1 0.5 %collective-permute-start.10 = (bf16[16,2880]{1,0:T(8,128)(2,1)S(1)}, bf16[16,2880]{1,0:T(8,128)(2,1)S(1)}, u32[]{:S(2)}, u32[]{:S(2)}) collective-permute-start(bf16[16,2880]{1,0:T(8,128)(2,1)S(1)} %collective-permute-done.9.refs_7_), channel_id=1, source_target_pairs={{0,1},{1,0},{2,3},{3,2},{4,5},{5,4},{6,7},{7,6},{8,9},{9,8},{10,11... | collective-permute-start | bytes 276488 | tf_op jit(solution)/shard_map/ppermute | solution.py:14
  22.6 0.1 collective-permute-start.8
  22.6 0.4 collective-permute-start.6
  23.1 0.3 collective-permute-done.14.refs_11_
  23.3 0.2 collective-permute-done.10.refs_3_
  23.5 0.4 collective-permute-done.8.refs_2_
  23.9 0.2 collective-permute-done.6.refs_1_
  24.0 4.2 %shard_map.74 = (bf16[64,2880]{1,0:T(8,128)(2,1)S(1)}, bf16[64,2880]{1,0:T(8,128)(2,1)S(1)}, bf16[64,2880]{1,0:T(8,128)(2,1)S(1)}, bf16[64,2880]{1,0:T(8,128)(2,1)S(1)}, f32[16,4]{1,0:T(8,128)S(1)}) custom-call(bf16[16,2880]{1,0:T(8,128)(2,1)S(1)} %collective-permute-done.4.refs_0_, bf16[16,2880]{1,0:T(8,128)(2,1)S(1)} %collective-permute-done.6.refs_1_, ...), custom_call_target="tpu_custom_call" | custom-call | flops 3185049600 | bytes 12441600 | tf_op jit(solution)/shard_map/pallas_call | solution.py:110
  28.2 0.4 collective-permute-start.20
  28.7 0.2 collective-permute-start.16
  28.8 0.2 slice_reduce_fusion.3
  29.0 1.0 %collective-permute-done.20 = bf16[64,2880]{1,0:T(8,128)(2,1)S(1)} collective-permute-done((bf16[64,2880]{1,0:T(8,128)(2,1)S(1)}, bf16[64,2880]{1,0:T(8,128)(2,1)S(1)}, u32[]{:S(2)}, u32[]{:S(2)}) %collective-permute-start.20) | collective-permute-done | bytes 368672 | tf_op jit(solution)/shard_map/ppermute | solution.py:14
  30.0 0.1 add_convert_fusion
  30.1 1.2 %collective-permute-start.21 = (bf16[16,2880]{1,0:T(8,128)(2,1)S(1)}, bf16[16,2880]{1,0:T(8,128)(2,1)S(1)}, u32[]{:S(2)}, u32[]{:S(2)}) collective-permute-start(bf16[16,2880]{1,0:T(8,128)(2,1)S(1)} %get-tuple-element.46), channel_id=1, source_target_pairs={{0,2},{1,3},{2,0},{3,1},{4,6},{5,7},{6,4},{7,5},{8,10},{9,11},{10,... | collective-permute-start | bytes 276488 | tf_op jit(solution)/shard_map/ppermute | solution.py:181
  31.3 1.9 %collective-permute-start.23 = (bf16[16,2880]{1,0:T(8,128)(2,1)S(1)}, bf16[16,2880]{1,0:T(8,128)(2,1)S(1)}, u32[]{:S(2)}, u32[]{:S(2)}) collective-permute-start(bf16[16,2880]{1,0:T(8,128)(2,1)S(1)} %get-tuple-element.47), channel_id=1, source_target_pairs={{0,6},{1,7},{2,4},{3,5},{4,2},{5,3},{6,0},{7,1},{8,14},{9,15},{10,... | collective-permute-start | bytes 276488 | tf_op jit(solution)/shard_map/ppermute | solution.py:181
  33.3 0.4 collective-permute-start.22
  33.7 0.1 add_convert_fusion.1
  33.8 1.2 %collective-permute-start.17 = (bf16[16,2880]{1,0:T(8,128)(2,1)S(1)}, bf16[16,2880]{1,0:T(8,128)(2,1)S(1)}, u32[]{:S(2)}, u32[]{:S(2)}) collective-permute-start(bf16[16,2880]{1,0:T(8,128)(2,1)S(1)} %get-tuple-element.43), channel_id=1, source_target_pairs={{0,2},{1,3},{2,0},{3,1},{4,6},{5,7},{6,4},{7,5},{8,10},{9,11},{10,... | collective-permute-start | bytes 276488 | tf_op jit(solution)/shard_map/ppermute | solution.py:181
  35.0 1.9 %collective-permute-start.19 = (bf16[16,2880]{1,0:T(8,128)(2,1)S(1)}, bf16[16,2880]{1,0:T(8,128)(2,1)S(1)}, u32[]{:S(2)}, u32[]{:S(2)}) collective-permute-start(bf16[16,2880]{1,0:T(8,128)(2,1)S(1)} %get-tuple-element.44), channel_id=1, source_target_pairs={{0,6},{1,7},{2,4},{3,5},{4,2},{5,3},{6,0},{7,1},{8,14},{9,15},{10,... | collective-permute-start | bytes 276488 | tf_op jit(solution)/shard_map/ppermute | solution.py:181
  36.9 0.4 collective-permute-done.21
  37.3 1.2 %collective-permute-start.18 = (bf16[16,2880]{1,0:T(8,128)(2,1)S(1)}, bf16[16,2880]{1,0:T(8,128)(2,1)S(1)}, u32[]{:S(2)}, u32[]{:S(2)}) collective-permute-start(bf16[16,2880]{1,0:T(8,128)(2,1)S(1)} %get-tuple-element.45), channel_id=1, source_target_pairs={{0,4},{1,5},{2,6},{3,7},{4,0},{5,1},{6,2},{7,3},{8,12},{9,13},{10,... | collective-permute-start | bytes 276488 | tf_op jit(solution)/shard_map/ppermute | solution.py:181
  38.5 0.6 %collective-permute-done.22 = bf16[16,2880]{1,0:T(8,128)(2,1)S(1)} collective-permute-done((bf16[16,2880]{1,0:T(8,128)(2,1)S(1)}, bf16[16,2880]{1,0:T(8,128)(2,1)S(1)}, u32[]{:S(2)}, u32[]{:S(2)}) %collective-permute-start.22) | collective-permute-done | bytes 92192 | tf_op jit(solution)/shard_map/ppermute | solution.py:181
  39.2 0.1 add_convert_fusion.3
  39.3 2.2 %collective-permute-start.24 = (bf16[16,2880]{1,0:T(8,128)(2,1)S(1)}, bf16[16,2880]{1,0:T(8,128)(2,1)S(1)}, u32[]{:S(2)}, u32[]{:S(2)}) collective-permute-start(bf16[16,2880]{1,0:T(8,128)(2,1)S(1)} %add_convert_fusion.3), channel_id=1, source_target_pairs={{0,8},{1,9},{2,10},{3,11},{4,12},{5,13},{6,14},{7,15},{8,0},{9,1},... | collective-permute-start | bytes 276488 | tf_op jit(solution)/shard_map/ppermute | solution.py:181
  41.5 0.2 slice_reduce_fusion.7
  41.8 1.7 %collective-permute-done.18 = bf16[16,2880]{1,0:T(8,128)(2,1)S(1)} collective-permute-done((bf16[16,2880]{1,0:T(8,128)(2,1)S(1)}, bf16[16,2880]{1,0:T(8,128)(2,1)S(1)}, u32[]{:S(2)}, u32[]{:S(2)}) %collective-permute-start.18) | collective-permute-done | bytes 92192 | tf_op jit(solution)/shard_map/ppermute | solution.py:181
  43.5 2.9 %collective-permute-done.24 = bf16[16,2880]{1,0:T(8,128)(2,1)S(1)} collective-permute-done((bf16[16,2880]{1,0:T(8,128)(2,1)S(1)}, bf16[16,2880]{1,0:T(8,128)(2,1)S(1)}, u32[]{:S(2)}, u32[]{:S(2)}) %collective-permute-start.24) | collective-permute-done | bytes 92192 | tf_op jit(solution)/shard_map/ppermute | solution.py:181
  46.4 0.8 %add_convert_fusion.2 = bf16[16,2880]{1,0:T(8,128)(2,1)} fusion(bf16[16,2880]{1,0:T(8,128)(2,1)S(1)} %collective-permute-done.24, bf16[16,2880]{1,0:T(8,128)(2,1)S(1)} %collective-permute-done.19, bf16[16,2880]{1,0:T(8,128)(2,1)S(1)} %collective-permute-done.18, bf16[16,2880]{1,0:T(8,128)(2,1)S(1)} %collective-permute-done.17, ...), kind=kLoop, calls=%fused_computation.2 | loop fusion | flops 737280 | bytes 645376 | tf_op jit(solution)/shard_map/convert_element_type | solution.py:212
  (20 shorter events, 0.1 us)
Async XLA Ops:
  0.0 13.7 %collective-permute-start.2 = (bf16[16,2880]{1,0:T(8,128)(2,1)}, bf16[16,2880]{1,0:T(8,128)(2,1)S(1)}, u32[]{:S(2)}, u32[]{:S(2)}) collective-permute-start(bf16[16,2880]{1,0:T(8,128)(2,1)} %refs_12_.1), channel_id=1, source_target_pairs={{0,6},{1,7},{2,4},{3,5},{4,2},{5,3},{6,0},{7,1},{8,14},{9,15},{10,... | collective-permute-start | bytes 276488 | tf_op jit(solution)/shard_map/ppermute | solution.py:181
  4.0 9.7 %collective-permute-start.1 = (bf16[16,2880]{1,0:T(8,128)(2,1)}, bf16[16,2880]{1,0:T(8,128)(2,1)S(1)}, u32[]{:S(2)}, u32[]{:S(2)}) collective-permute-start(bf16[16,2880]{1,0:T(8,128)(2,1)} %refs_12_.1), channel_id=1, source_target_pairs={{0,4},{1,5},{2,6},{3,7},{4,0},{5,1},{6,2},{7,3},{8,12},{9,13},{10,... | collective-permute-start | bytes 276488 | tf_op jit(solution)/shard_map/ppermute | solution.py:181
  4.4 9.3 %collective-permute-start = (bf16[16,2880]{1,0:T(8,128)(2,1)}, bf16[16,2880]{1,0:T(8,128)(2,1)S(1)}, u32[]{:S(2)}, u32[]{:S(2)}) collective-permute-start(bf16[16,2880]{1,0:T(8,128)(2,1)} %refs_12_.1), channel_id=1, source_target_pairs={{0,2},{1,3},{2,0},{3,1},{4,6},{5,7},{6,4},{7,5},{8,10},{9,11},{10,... | collective-permute-start | bytes 276488 | tf_op jit(solution)/shard_map/ppermute | solution.py:181
  4.5 9.2 %collective-permute-start.3 = (bf16[16,2880]{1,0:T(8,128)(2,1)}, bf16[16,2880]{1,0:T(8,128)(2,1)S(1)}, u32[]{:S(2)}, u32[]{:S(2)}) collective-permute-start(bf16[16,2880]{1,0:T(8,128)(2,1)} %refs_12_.1), channel_id=1, source_target_pairs={{0,8},{1,9},{2,10},{3,11},{4,12},{5,13},{6,14},{7,15},{8,0},{9,1},... | collective-permute-start | bytes 276488 | tf_op jit(solution)/shard_map/ppermute | solution.py:181
  7.5 9.8 %collective-permute-start.11 = (bf16[16,2880]{1,0:T(8,128)(2,1)}, bf16[16,2880]{1,0:T(8,128)(2,1)S(1)}, u32[]{:S(2)}, u32[]{:S(2)}) collective-permute-start(bf16[16,2880]{1,0:T(8,128)(2,1)} %refs_12_.1), channel_id=1, source_target_pairs={{0,1},{1,0},{2,3},{3,2},{4,5},{5,4},{6,7},{7,6},{8,9},{9,8},{10,11... | collective-permute-start | bytes 276488 | tf_op jit(solution)/shard_map/ppermute | solution.py:14
  7.5 0.7 %copy-start.2 = (s32[16,4]{0,1:T(4,128)S(1)}, s32[16,4]{0,1:T(4,128)}, u32[]{:S(2)}) copy-start(s32[16,4]{0,1:T(4,128)} %param.9) | copy-start | bytes 772
  8.2 0.7 %copy-start.3 = (f32[16,4]{0,1:T(4,128)S(1)}, f32[16,4]{0,1:T(4,128)}, u32[]{:S(2)}) copy-start(f32[16,4]{0,1:T(4,128)} %param.10) | copy-start | bytes 772
  8.9 15.1 %copy-start = (bf16[16,2880]{1,0:T(8,128)(2,1)S(1)}, bf16[16,2880]{1,0:T(8,128)(2,1)}, u32[]{:S(2)}) copy-start(bf16[16,2880]{1,0:T(8,128)(2,1)} %refs_12_.1) | copy-start | bytes 276484
  8.9 15.1 %copy-start.1 = (f32[2880]{0:T(1024)S(1)}, f32[2880]{0:T(1024)}, u32[]{:S(2)}) copy-start(f32[2880]{0:T(1024)} %refs_16_.1) | copy-start | bytes 34564
  13.7 7.3 %collective-permute-start.9 = (bf16[16,2880]{1,0:T(8,128)(2,1)S(1)}, bf16[16,2880]{1,0:T(8,128)(2,1)S(1)}, u32[]{:S(2)}, u32[]{:S(2)}) collective-permute-start(bf16[16,2880]{1,0:T(8,128)(2,1)S(1)} %collective-permute-done.3.refs_4_), channel_id=1, source_target_pairs={{0,6},{1,7},{2,4},{3,5},{4,2},{5,3},{6,0},{7,1},{8,14},{9,15},{10,... | collective-permute-start | bytes 276488 | tf_op jit(solution)/shard_map/ppermute | solution.py:181
  16.3 4.7 %collective-permute-start.15 = (f32[16,4]{1,0:T(8,128)S(1)}, f32[16,4]{1,0:T(8,128)S(1)}, u32[]{:S(2)}, u32[]{:S(2)}) collective-permute-start(f32[16,4]{1,0:T(8,128)S(1)} %get-tuple-element.29), channel_id=1, source_target_pairs={{0,8},{1,9},{2,10},{3,11},{4,12},{5,13},{6,14},{7,15},{8,0},{9,1},... | collective-permute-start | bytes 776 | tf_op jit(solution)/shard_map/ppermute | solution.py:181
  16.8 5.3 %collective-permute-start.7 = (bf16[16,2880]{1,0:T(8,128)(2,1)S(1)}, bf16[16,2880]{1,0:T(8,128)(2,1)S(1)}, u32[]{:S(2)}, u32[]{:S(2)}) collective-permute-start(bf16[16,2880]{1,0:T(8,128)(2,1)S(1)} %collective-permute-done.3.refs_4_), channel_id=1, source_target_pairs={{0,4},{1,5},{2,6},{3,7},{4,0},{5,1},{6,2},{7,3},{8,12},{9,13},{10,... | collective-permute-start | bytes 276488 | tf_op jit(solution)/shard_map/ppermute | solution.py:181
  17.1 5.0 %collective-permute-start.5 = (bf16[16,2880]{1,0:T(8,128)(2,1)S(1)}, bf16[16,2880]{1,0:T(8,128)(2,1)S(1)}, u32[]{:S(2)}, u32[]{:S(2)}) collective-permute-start(bf16[16,2880]{1,0:T(8,128)(2,1)S(1)} %collective-permute-done.3.refs_4_), channel_id=1, source_target_pairs={{0,2},{1,3},{2,0},{3,1},{4,6},{5,7},{6,4},{7,5},{8,10},{9,11},{10,... | collective-permute-start | bytes 276488 | tf_op jit(solution)/shard_map/ppermute | solution.py:181
  17.3 5.2 %collective-permute-start.4 = (bf16[16,2880]{1,0:T(8,128)(2,1)S(1)}, bf16[16,2880]{1,0:T(8,128)(2,1)S(1)}, u32[]{:S(2)}, u32[]{:S(2)}) collective-permute-start(bf16[16,2880]{1,0:T(8,128)(2,1)S(1)} %collective-permute-done.3.refs_4_), channel_id=1, source_target_pairs={{0,1},{1,0},{2,3},{3,2},{4,5},{5,4},{6,7},{7,6},{8,9},{9,8},{10,11... | collective-permute-start | bytes 276488 | tf_op jit(solution)/shard_map/ppermute | solution.py:14
  21.0 1.7 %collective-permute-start.12 = (bf16[16,2880]{1,0:T(8,128)(2,1)S(1)}, bf16[16,2880]{1,0:T(8,128)(2,1)S(1)}, u32[]{:S(2)}, u32[]{:S(2)}) collective-permute-start(bf16[16,2880]{1,0:T(8,128)(2,1)S(1)} %collective-permute-done.refs_13_), channel_id=1, source_target_pairs={{0,1},{1,0},{2,3},{3,2},{4,5},{5,4},{6,7},{7,6},{8,9},{9,8},{10,11... | collective-permute-start | bytes 276488 | tf_op jit(solution)/shard_map/ppermute | solution.py:14
  21.0 2.1 %collective-permute-start.13 = (bf16[16,2880]{1,0:T(8,128)(2,1)S(1)}, bf16[16,2880]{1,0:T(8,128)(2,1)S(1)}, u32[]{:S(2)}, u32[]{:S(2)}) collective-permute-start(bf16[16,2880]{1,0:T(8,128)(2,1)S(1)} %collective-permute-done.1.refs_14_), channel_id=1, source_target_pairs={{0,1},{1,0},{2,3},{3,2},{4,5},{5,4},{6,7},{7,6},{8,9},{9,8},{10,11... | collective-permute-start | bytes 276488 | tf_op jit(solution)/shard_map/ppermute | solution.py:14
  22.0 1.3 %collective-permute-start.14 = (bf16[16,2880]{1,0:T(8,128)(2,1)S(1)}, bf16[16,2880]{1,0:T(8,128)(2,1)S(1)}, u32[]{:S(2)}, u32[]{:S(2)}) collective-permute-start(bf16[16,2880]{1,0:T(8,128)(2,1)S(1)} %collective-permute-done.2.refs_15_), channel_id=1, source_target_pairs={{0,1},{1,0},{2,3},{3,2},{4,5},{5,4},{6,7},{7,6},{8,9},{9,8},{10,11... | collective-permute-start | bytes 276488 | tf_op jit(solution)/shard_map/ppermute | solution.py:14
  22.1 1.4 %collective-permute-start.10 = (bf16[16,2880]{1,0:T(8,128)(2,1)S(1)}, bf16[16,2880]{1,0:T(8,128)(2,1)S(1)}, u32[]{:S(2)}, u32[]{:S(2)}) collective-permute-start(bf16[16,2880]{1,0:T(8,128)(2,1)S(1)} %collective-permute-done.9.refs_7_), channel_id=1, source_target_pairs={{0,1},{1,0},{2,3},{3,2},{4,5},{5,4},{6,7},{7,6},{8,9},{9,8},{10,11... | collective-permute-start | bytes 276488 | tf_op jit(solution)/shard_map/ppermute | solution.py:14
  22.6 1.3 %collective-permute-start.8 = (bf16[16,2880]{1,0:T(8,128)(2,1)S(1)}, bf16[16,2880]{1,0:T(8,128)(2,1)S(1)}, u32[]{:S(2)}, u32[]{:S(2)}) collective-permute-start(bf16[16,2880]{1,0:T(8,128)(2,1)S(1)} %collective-permute-done.7.refs_6_), channel_id=1, source_target_pairs={{0,1},{1,0},{2,3},{3,2},{4,5},{5,4},{6,7},{7,6},{8,9},{9,8},{10,11... | collective-permute-start | bytes 276488 | tf_op jit(solution)/shard_map/ppermute | solution.py:14
  22.6 1.4 %collective-permute-start.6 = (bf16[16,2880]{1,0:T(8,128)(2,1)S(1)}, bf16[16,2880]{1,0:T(8,128)(2,1)S(1)}, u32[]{:S(2)}, u32[]{:S(2)}) collective-permute-start(bf16[16,2880]{1,0:T(8,128)(2,1)S(1)} %collective-permute-done.5.refs_5_), channel_id=1, source_target_pairs={{0,1},{1,0},{2,3},{3,2},{4,5},{5,4},{6,7},{7,6},{8,9},{9,8},{10,11... | collective-permute-start | bytes 276488 | tf_op jit(solution)/shard_map/ppermute | solution.py:14
  28.2 1.8 %collective-permute-start.20 = (bf16[64,2880]{1,0:T(8,128)(2,1)S(1)}, bf16[64,2880]{1,0:T(8,128)(2,1)S(1)}, u32[]{:S(2)}, u32[]{:S(2)}) collective-permute-start(bf16[64,2880]{1,0:T(8,128)(2,1)S(1)} %get-tuple-element.34), channel_id=1, source_target_pairs={{0,1},{1,0},{2,3},{3,2},{4,5},{5,4},{6,7},{7,6},{8,9},{9,8},{10,11... | collective-permute-start | bytes 1105928 | tf_op jit(solution)/shard_map/ppermute | solution.py:14
  28.7 5.0 %collective-permute-start.16 = (bf16[64,2880]{1,0:T(8,128)(2,1)S(1)}, bf16[64,2880]{1,0:T(8,128)(2,1)S(1)}, u32[]{:S(2)}, u32[]{:S(2)}) collective-permute-start(bf16[64,2880]{1,0:T(8,128)(2,1)S(1)} %get-tuple-element.31), channel_id=1, source_target_pairs={{0,1},{1,0},{2,3},{3,2},{4,5},{5,4},{6,7},{7,6},{8,9},{9,8},{10,11... | collective-permute-start | bytes 1105928 | tf_op jit(solution)/shard_map/ppermute | solution.py:14
  30.1 7.2 %collective-permute-start.21 = (bf16[16,2880]{1,0:T(8,128)(2,1)S(1)}, bf16[16,2880]{1,0:T(8,128)(2,1)S(1)}, u32[]{:S(2)}, u32[]{:S(2)}) collective-permute-start(bf16[16,2880]{1,0:T(8,128)(2,1)S(1)} %get-tuple-element.46), channel_id=1, source_target_pairs={{0,2},{1,3},{2,0},{3,1},{4,6},{5,7},{6,4},{7,5},{8,10},{9,11},{10,... | collective-permute-start | bytes 276488 | tf_op jit(solution)/shard_map/ppermute | solution.py:181
  31.3 7.2 %collective-permute-start.23 = (bf16[16,2880]{1,0:T(8,128)(2,1)S(1)}, bf16[16,2880]{1,0:T(8,128)(2,1)S(1)}, u32[]{:S(2)}, u32[]{:S(2)}) collective-permute-start(bf16[16,2880]{1,0:T(8,128)(2,1)S(1)} %get-tuple-element.47), channel_id=1, source_target_pairs={{0,6},{1,7},{2,4},{3,5},{4,2},{5,3},{6,0},{7,1},{8,14},{9,15},{10,... | collective-permute-start | bytes 276488 | tf_op jit(solution)/shard_map/ppermute | solution.py:181
  33.3 5.9 %collective-permute-start.22 = (bf16[16,2880]{1,0:T(8,128)(2,1)S(1)}, bf16[16,2880]{1,0:T(8,128)(2,1)S(1)}, u32[]{:S(2)}, u32[]{:S(2)}) collective-permute-start(bf16[16,2880]{1,0:T(8,128)(2,1)S(1)} %get-tuple-element.48), channel_id=1, source_target_pairs={{0,4},{1,5},{2,6},{3,7},{4,0},{5,1},{6,2},{7,3},{8,12},{9,13},{10,... | collective-permute-start | bytes 276488 | tf_op jit(solution)/shard_map/ppermute | solution.py:181
  33.8 7.9 %collective-permute-start.17 = (bf16[16,2880]{1,0:T(8,128)(2,1)S(1)}, bf16[16,2880]{1,0:T(8,128)(2,1)S(1)}, u32[]{:S(2)}, u32[]{:S(2)}) collective-permute-start(bf16[16,2880]{1,0:T(8,128)(2,1)S(1)} %get-tuple-element.43), channel_id=1, source_target_pairs={{0,2},{1,3},{2,0},{3,1},{4,6},{5,7},{6,4},{7,5},{8,10},{9,11},{10,... | collective-permute-start | bytes 276488 | tf_op jit(solution)/shard_map/ppermute | solution.py:181
  35.0 6.8 %collective-permute-start.19 = (bf16[16,2880]{1,0:T(8,128)(2,1)S(1)}, bf16[16,2880]{1,0:T(8,128)(2,1)S(1)}, u32[]{:S(2)}, u32[]{:S(2)}) collective-permute-start(bf16[16,2880]{1,0:T(8,128)(2,1)S(1)} %get-tuple-element.44), channel_id=1, source_target_pairs={{0,6},{1,7},{2,4},{3,5},{4,2},{5,3},{6,0},{7,1},{8,14},{9,15},{10,... | collective-permute-start | bytes 276488 | tf_op jit(solution)/shard_map/ppermute | solution.py:181
  37.3 6.1 %collective-permute-start.18 = (bf16[16,2880]{1,0:T(8,128)(2,1)S(1)}, bf16[16,2880]{1,0:T(8,128)(2,1)S(1)}, u32[]{:S(2)}, u32[]{:S(2)}) collective-permute-start(bf16[16,2880]{1,0:T(8,128)(2,1)S(1)} %get-tuple-element.45), channel_id=1, source_target_pairs={{0,4},{1,5},{2,6},{3,7},{4,0},{5,1},{6,2},{7,3},{8,12},{9,13},{10,... | collective-permute-start | bytes 276488 | tf_op jit(solution)/shard_map/ppermute | solution.py:181
  39.3 7.0 %collective-permute-start.24 = (bf16[16,2880]{1,0:T(8,128)(2,1)S(1)}, bf16[16,2880]{1,0:T(8,128)(2,1)S(1)}, u32[]{:S(2)}, u32[]{:S(2)}) collective-permute-start(bf16[16,2880]{1,0:T(8,128)(2,1)S(1)} %add_convert_fusion.3), channel_id=1, source_target_pairs={{0,8},{1,9},{2,10},{3,11},{4,12},{5,13},{6,14},{7,15},{8,0},{9,1},... | collective-permute-start | bytes 276488 | tf_op jit(solution)/shard_map/ppermute | solution.py:181

commit v5 on v4

--- a/solution.py
+++ b/solution.py
@@ -80,8 +80,12 @@
 
 def expert_kernel(groups, *refs):
     count = sum(groups)
-    blocks, (gain_ref, gate_ref, up_ref, down_ref, table_ref) = refs[:count], refs[count : count + 5]
-    outs, table_out_ref, normed_ref = refs[count + 5 : -2], refs[-2], refs[-1]
+    blocks, (gain_ref, gate_ref, up_hbm, down_hbm, table_ref) = refs[:count], refs[count : count + 5]
+    outs, (table_out_ref, normed_ref, up_ref, down_ref, sems) = refs[count + 5 : -5], refs[-5:]
+    up_copy = pltpu.make_async_copy(up_hbm, up_ref, sems.at[0])
+    down_copy = pltpu.make_async_copy(down_hbm, down_ref, sems.at[1])
+    up_copy.start()
+    down_copy.start()
     table_out_ref[...] = table_ref[...]
     rows, model = blocks[0].shape
     gain = gain_ref[...].reshape(1, model)
@@ -92,8 +96,11 @@
     normed = normed_ref[...]
     across = (((1,), (1,)), ((), ()))
     gate = lax.dot_general(normed, gate_ref[...], across, preferred_element_type=jnp.float32)
+    gate = gate * jax.nn.sigmoid(1.702 * gate)
+    up_copy.wait()
     upper = lax.dot_general(normed, up_ref[...], across, preferred_element_type=jnp.float32)
-    act = (gate * jax.nn.sigmoid(1.702 * gate) * (upper + 1.0)).astype(jnp.bfloat16)
+    act = (gate * (upper + 1.0)).astype(jnp.bfloat16)
+    down_copy.wait()
     out = jnp.dot(act, down_ref[...], preferred_element_type=jnp.float32).astype(jnp.bfloat16)
     start = 0
     for size, out_ref in zip(groups, outs):
@@ -106,68 +113,75 @@
     sizes = tuple(len(group) for group in groups)
     rows, model = blocks[0].shape
     count, hidden = len(blocks), gate_w.shape[0]
-    vmem = pl.BlockSpec(memory_space=pltpu.VMEM)
+    vmem, hbm = pl.BlockSpec(memory_space=pltpu.VMEM), pl.BlockSpec(memory_space=pltpu.HBM)
     return pl.pallas_call(
         functools.partial(expert_kernel, sizes),
         out_shape=tuple(jax.ShapeDtypeStruct((rows * size, model), jnp.bfloat16) for size in sizes)
         + (jax.ShapeDtypeStruct(table.shape, table.dtype),),
-        in_specs=[vmem] * (count + 5),
+        in_specs=[vmem] * (count + 2) + [hbm, hbm, vmem],
         out_specs=(vmem,) * (len(groups) + 1),
-        scratch_shapes=[pltpu.VMEM((rows * count, model), jnp.bfloat16)],
+        scratch_shapes=[
+            pltpu.VMEM((rows * count, model), jnp.bfloat16),
+            pltpu.VMEM(up_w.shape, up_w.dtype),
+            pltpu.VMEM(down_w.shape, down_w.dtype),
+            pltpu.SemaphoreType.DMA((2,)),
+        ],
         cost_estimate=pl.CostEstimate(
             flops=6 * rows * count * model * hidden,
             bytes_accessed=6 * model * hidden,
             transcendentals=rows * count * hidden,
         ),
-        compiler_params=pltpu.CompilerParams(vmem_limit_bytes=24 * 2**20),
-    )(*blocks, gain, gate_w, up_w, down_w, table)
-
-
-def load_kernel(pieces, chip_ref, ids_ref, weights_ref, *refs):
-    count = (len(refs) - 3) // 2
-    sources, near_ref, far_ref = refs[:count], refs[count], refs[count + 1]
-    targets, sems = refs[count + 2 : -1], refs[-1]
-    copies = []
-    for source, target in zip(sources, targets):
-        part = source.shape[0] // pieces
-        for piece in range(pieces):
-            span = pl.ds(piece * part, part)
-            copies.append(pltpu.make_async_copy(source.at[span], target.at[span], sems.at[len(copies)]))
+        compiler_params=pltpu.CompilerParams(vmem_limit_bytes=32 * 2**20),
+    )(
+        *blocks,
+        gain,
+        gate_w,
+        *(pltpu.with_memory_space_constraint(w, pltpu.HBM) for w in (up_w, down_w)),
+        table,
+    )
+
+
+def load_kernel(chip_ref, ids_hbm, weights_hbm, source, near_ref, far_ref, target, ids_ref, weights_ref, sems):
+    copies = [
+        pltpu.make_async_copy(a, b, sems.at[i])
+        for i, (a, b) in enumerate(((ids_hbm, ids_ref), (weights_hbm, weights_ref), (source, target)))
+    ]
     for copy in copies:
         copy.start()
     chosen, rows = ids_ref.shape
     half = near_ref.shape[1]
     expert = chip_ref[0] ^ lax.broadcasted_iota(jnp.int32, (2 * half, rows), 0)
+    copies[0].wait()
+    copies[1].wait()
     table = jnp.zeros((2 * half, rows), jnp.float32)
     for k in range(chosen):
         table += jnp.where(ids_ref[k : k + 1, :] == expert, weights_ref[k : k + 1, :], 0.0)
     near_ref[...] = table[:half].T
     far_ref[...] = table[half:].T
-    for copy in copies:
-        copy.wait()
-
-
-def load(chip, expert_ids, expert_weights, half, arrays):
-    rows = expert_ids.shape[0]
-    pieces = 3 if all(a.shape[0] % 48 == 0 for a in arrays) else 1
-    vmem = pl.BlockSpec(memory_space=pltpu.VMEM)
+    copies[2].wait()
+
+
+def load(chip, expert_ids, expert_weights, half, array):
+    rows, chosen = expert_ids.shape
+    vmem, hbm = pl.BlockSpec(memory_space=pltpu.VMEM), pl.BlockSpec(memory_space=pltpu.HBM)
     table = jax.ShapeDtypeStruct((rows, half), jnp.float32)
     return pl.pallas_call(
-        functools.partial(load_kernel, pieces),
-        out_shape=(table, table) + tuple(pltpu.VMEM(a.shape, a.dtype) for a in arrays),
-        in_specs=[pl.BlockSpec(memory_space=pltpu.SMEM), vmem, vmem]
-        + [pl.BlockSpec(memory_space=pltpu.HBM)] * len(arrays),
-        out_specs=(vmem,) * (2 + len(arrays)),
-        scratch_shapes=[pltpu.SemaphoreType.DMA((pieces * len(arrays),))],
+        load_kernel,
+        out_shape=(table, table, pltpu.VMEM(array.shape, array.dtype)),
+        in_specs=[pl.BlockSpec(memory_space=pltpu.SMEM), hbm, hbm, hbm],
+        out_specs=(vmem,) * 3,
+        scratch_shapes=[
+            pltpu.VMEM((chosen, rows), expert_ids.dtype),
+            pltpu.VMEM((chosen, rows), expert_weights.dtype),
+            pltpu.SemaphoreType.DMA((3,)),
+        ],
         cost_estimate=pl.CostEstimate(
-            flops=0, bytes_accessed=2 * sum(a.size * a.dtype.itemsize for a in arrays), transcendentals=0
+            flops=0, bytes_accessed=2 * array.size * array.dtype.itemsize, transcendentals=0
         ),
         compiler_params=pltpu.CompilerParams(vmem_limit_bytes=16 * 2**20),
     )(
         chip.reshape(1),
-        expert_ids.T,
-        expert_weights.T,
-        *(pltpu.with_memory_space_constraint(a, pltpu.HBM) for a in arrays),
+        *(pltpu.with_memory_space_constraint(a, pltpu.HBM) for a in (expert_ids.T, expert_weights.T, array)),
     )
 
 
@@ -188,27 +202,31 @@
     near = [across(x, mask) for mask in range(1, half)]
     near_swapped = [swap(x)]
     chip = lax.axis_index("expert") // 2
-    near_weights, far_weights, *held = load(
-        chip, expert_ids, expert_weights, half, (gate_proj[0].T, up_proj[0].T, down_proj[0])
-    )
+    near_weights, far_weights, gate_w = load(chip, expert_ids, expert_weights, half, gate_proj[0].T)
     near_weights, far_weights, *near = lax.optimization_barrier((near_weights, far_weights, *near))
     near_swapped += [swap(block) for block in near]
     far = [across(mirrored, mask) for mask in range(1, half)]
     far_swapped = [swap(mirrored)] + [swap(block) for block in far]
     *parts, mirror_weights = expert_parts(
-        (far_swapped, [mirrored] + far, near_swapped, [x] + near), norm_gain, *held, across(far_weights, half)
-    )
-
-    def mix(theirs, mine, block_weights):
-        done = pair_sum(mine, swap(theirs)).reshape(half, rows, model)
+        (far_swapped, [mirrored] + far, near_swapped, [x] + near),
+        norm_gain,
+        gate_w,
+        up_proj[0].T,
+        down_proj[0],
+        across(far_weights, half),
+    )
+
+    def mix(done, block_weights):
+        done = done.reshape(half, rows, model)
         total = jnp.zeros((rows, model), jnp.float32)
         for mask in range(half):
             total += block_weights[:, mask][:, None] * across(done[mask], mask).astype(jnp.float32)
         return total
 
-    other = mix(parts[0], parts[1], mirror_weights)
-    own = mix(parts[2], parts[3], near_weights)
-    own += across(other.astype(jnp.bfloat16), half).astype(jnp.float32)
+    other = mix(pair_sum(parts[1], swap(parts[0])), mirror_weights).astype(jnp.bfloat16)
+    near_done = pair_sum(parts[3], swap(parts[2]))
+    other, near_done = lax.optimization_barrier((other, near_done))
+    own = across(other, half).astype(jnp.float32) + mix(near_done, near_weights)
     return (x.astype(jnp.float32) + own).astype(jnp.bfloat16)
 
 

time: 47.3 us -> 50.8 us (1.074)
  waiting for transfers between devices: 11.7 us -> 16 us
  local copies, waits for them, and re-layouts: 1.84 us -> 0.47 us
  Pallas kernels: 8.97 us -> 9.63 us
    ppermute x15, waiting for transfers between devices: 9.8 us -> 14.1 us  [across(): return lax.ppermute(value, 'expert', pairs) if mask else value]
    pallas_call x1, Pallas kernels: 4.21 us -> 7.37 us  [expert_parts(): pl.pallas_call(functools.partial(expert_kernel, sizes), out_shape=tuple((...]
    pallas_call x1, Pallas kernels: 4.76 us -> 2.26 us  [load(): pl.pallas_call(load_kernel, out_shape=(table, table, pltpu.VMEM(array.sha...]
    unnamed x8 -> x4, local copies, waits for them, and re-layouts: 1.37 us -> 0.01 us
  transfers between devices with their start and end apart: 25 -> 25, of which waited for: 11 -> 14; matrix products, arithmetic and copies ran while one was open for 2% -> 1% of each run, Pallas kernels for 10% -> 4%
where the time goes in v5:
time: 50.8 us; the launch traced here: 50.7 us
  starting transfers between devices  23.3 us (46%)
  waiting for transfers between devices  16 us (31%)
  Pallas kernels  9.63 us (19%)
  other arithmetic  1.12 us (2%)
    ppermute x15, starting transfers between devices, across(): return lax.ppermute(value, 'expert', pairs) if mask else value  21.2 us
    ppermute x15, waiting for transfers between devices, across(): return lax.ppermute(value, 'expert', pairs) if mask else value  14.1 us
    pallas_call x1, Pallas kernels, expert_parts(): pl.pallas_call(functools.partial(expert_kernel, sizes), out_shape=tuple((...  7.37 us
    pallas_call x1, Pallas kernels, load(): pl.pallas_call(load_kernel, out_shape=(table, table, pltpu.VMEM(array.sha...  2.26 us
    ppermute x10, starting transfers between devices, partner(): return lax.ppermute(value, axis, pairs)  2.11 us
    ppermute x10, waiting for transfers between devices, partner(): return lax.ppermute(value, axis, pairs)  1.92 us
  transfers between devices with their start and end apart: 25, of which 14 were waited for; matrix products, arithmetic and copies ran while one was open for 1% of the time, Pallas kernels for 4%

profile of v5, /device:TPU:0, one launch (start us, length us, event | category | flops | bytes accessed | tf_op | source)
XLA Modules:
  0.0 50.7 jit_solution(2750751150734361869)
XLA Ops:
  0.0 3.0 %collective-permute-start.10 = (bf16[16,2880]{1,0:T(8,128)(2,1)}, bf16[16,2880]{1,0:T(8,128)(2,1)S(1)}, u32[]{:S(2)}, u32[]{:S(2)}) collective-permute-start(bf16[16,2880]{1,0:T(8,128)(2,1)} %refs_12_.1), channel_id=1, source_target_pairs={{0,4},{1,5},{2,6},{3,7},{4,0},{5,1},{6,2},{7,3},{8,12},{9,13},{10,... | collective-permute-start | bytes 276488 | tf_op jit(solution)/shard_map/ppermute | solution.py:195
  3.0 1.5 %collective-permute-start.9 = (bf16[16,2880]{1,0:T(8,128)(2,1)}, bf16[16,2880]{1,0:T(8,128)(2,1)S(1)}, u32[]{:S(2)}, u32[]{:S(2)}) collective-permute-start(bf16[16,2880]{1,0:T(8,128)(2,1)} %refs_12_.1), channel_id=1, source_target_pairs={{0,2},{1,3},{2,0},{3,1},{4,6},{5,7},{6,4},{7,5},{8,10},{9,11},{10,... | collective-permute-start | bytes 276488 | tf_op jit(solution)/shard_map/ppermute | solution.py:195
  4.5 0.0 collective-permute-start.11
  4.6 3.0 %collective-permute-start = (bf16[16,2880]{1,0:T(8,128)(2,1)}, bf16[16,2880]{1,0:T(8,128)(2,1)S(1)}, u32[]{:S(2)}, u32[]{:S(2)}) collective-permute-start(bf16[16,2880]{1,0:T(8,128)(2,1)} %refs_12_.1), channel_id=1, source_target_pairs={{0,8},{1,9},{2,10},{3,11},{4,12},{5,13},{6,14},{7,15},{8,0},{9,1},... | collective-permute-start | bytes 276488 | tf_op jit(solution)/shard_map/ppermute | solution.py:195
  7.5 0.0 collective-permute-start.8
  7.5 2.3 %shard_map.73 = (f32[16,4]{1,0:T(8,128)S(1)}, f32[16,4]{1,0:T(8,128)S(1)}, bf16[720,2880]{1,0:T(8,128)(2,1)S(1)}) custom-call(s32[1]{0:T(128)} %bitcast.chip_ref, s32[4,16]{1,0:T(4,128)} %bitcast.13, f32[4,16]{1,0:T(4,128)} %bitcast.14, bf16[720,2880]{1,0:T(8,128)(2,1)} %bitcast.10), custom_call_target="tpu_custom_call" | custom-call | bytes 8294400 | tf_op jit(solution)/shard_map/pallas_call | solution.py:168
  9.8 0.0 collective-permute-done.10.refs_14_
  9.8 0.0 collective-permute-done.9.refs_13_
  9.8 0.8 %collective-permute-done.11.refs_15_ = bf16[16,2880]{1,0:T(8,128)(2,1)S(1)} collective-permute-done((bf16[16,2880]{1,0:T(8,128)(2,1)}, bf16[16,2880]{1,0:T(8,128)(2,1)S(1)}, u32[]{:S(2)}, u32[]{:S(2)}) %collective-permute-start.11) | collective-permute-done | bytes 92192 | tf_op jit(solution)/shard_map/ppermute | solution.py:195
  10.6 0.7 %collective-permute-done.refs_4_ = bf16[16,2880]{1,0:T(8,128)(2,1)S(1)} collective-permute-done((bf16[16,2880]{1,0:T(8,128)(2,1)}, bf16[16,2880]{1,0:T(8,128)(2,1)S(1)}, u32[]{:S(2)}, u32[]{:S(2)}) %collective-permute-start) | collective-permute-done | bytes 92192 | tf_op jit(solution)/shard_map/ppermute | solution.py:195
  11.3 2.9 %collective-permute-start.6 = (bf16[16,2880]{1,0:T(8,128)(2,1)S(1)}, bf16[16,2880]{1,0:T(8,128)(2,1)S(1)}, u32[]{:S(2)}, u32[]{:S(2)}) collective-permute-start(bf16[16,2880]{1,0:T(8,128)(2,1)S(1)} %collective-permute-done.refs_4_), channel_id=1, source_target_pairs={{0,6},{1,7},{2,4},{3,5},{4,2},{5,3},{6,0},{7,1},{8,14},{9,15},{10,... | collective-permute-start | bytes 276488 | tf_op jit(solution)/shard_map/ppermute | solution.py:195
  14.2 2.5 %collective-permute-start.15 = (f32[16,4]{1,0:T(8,128)S(1)}, f32[16,4]{1,0:T(8,128)S(1)}, u32[]{:S(2)}, u32[]{:S(2)}) collective-permute-start(f32[16,4]{1,0:T(8,128)S(1)} %get-tuple-element.26), channel_id=1, source_target_pairs={{0,8},{1,9},{2,10},{3,11},{4,12},{5,13},{6,14},{7,15},{8,0},{9,1},... | collective-permute-start | bytes 776 | tf_op jit(solution)/shard_map/ppermute | solution.py:195
  16.7 0.6 %collective-permute-start.2 = (bf16[16,2880]{1,0:T(8,128)(2,1)S(1)}, bf16[16,2880]{1,0:T(8,128)(2,1)S(1)}, u32[]{:S(2)}, u32[]{:S(2)}) collective-permute-start(bf16[16,2880]{1,0:T(8,128)(2,1)S(1)} %collective-permute-done.refs_4_), channel_id=1, source_target_pairs={{0,2},{1,3},{2,0},{3,1},{4,6},{5,7},{6,4},{7,5},{8,10},{9,11},{10,... | collective-permute-start | bytes 276488 | tf_op jit(solution)/shard_map/ppermute | solution.py:195
  17.3 0.0 collective-permute-done.8.refs_8_
  17.3 0.0 collective-permute-start.1
  17.3 1.6 %collective-permute-done.15.refs_20_ = f32[16,4]{1,0:T(8,128)S(1)} collective-permute-done((f32[16,4]{1,0:T(8,128)S(1)}, f32[16,4]{1,0:T(8,128)S(1)}, u32[]{:S(2)}, u32[]{:S(2)}) %collective-permute-start.15) | collective-permute-done | bytes 288 | tf_op jit(solution)/shard_map/ppermute | solution.py:195
  18.9 0.5 %collective-permute-start.13 = (bf16[16,2880]{1,0:T(8,128)(2,1)S(1)}, bf16[16,2880]{1,0:T(8,128)(2,1)S(1)}, u32[]{:S(2)}, u32[]{:S(2)}) collective-permute-start(bf16[16,2880]{1,0:T(8,128)(2,1)S(1)} %collective-permute-done.10.refs_14_), channel_id=1, source_target_pairs={{0,1},{1,0},{2,3},{3,2},{4,5},{5,4},{6,7},{7,6},{8,9},{9,8},{10,11... | collective-permute-start | bytes 276488 | tf_op jit(solution)/shard_map/ppermute | solution.py:14
  19.4 1.9 %collective-permute-done.4.refs_6_ = bf16[16,2880]{1,0:T(8,128)(2,1)S(1)} collective-permute-done((bf16[16,2880]{1,0:T(8,128)(2,1)S(1)}, bf16[16,2880]{1,0:T(8,128)(2,1)S(1)}, u32[]{:S(2)}, u32[]{:S(2)}) %collective-permute-start.4) | collective-permute-done | bytes 92192 | tf_op jit(solution)/shard_map/ppermute | solution.py:195
  21.3 0.0 collective-permute-done.2.refs_5_
  21.3 0.5 %collective-permute-start.7 = (bf16[16,2880]{1,0:T(8,128)(2,1)S(1)}, bf16[16,2880]{1,0:T(8,128)(2,1)S(1)}, u32[]{:S(2)}, u32[]{:S(2)}) collective-permute-start(bf16[16,2880]{1,0:T(8,128)(2,1)S(1)} %collective-permute-done.6.refs_7_), channel_id=1, source_target_pairs={{0,1},{1,0},{2,3},{3,2},{4,5},{5,4},{6,7},{7,6},{8,9},{9,8},{10,11... | collective-permute-start | bytes 276488 | tf_op jit(solution)/shard_map/ppermute | solution.py:14
  21.8 0.1 collective-permute-start.5
  21.9 0.4 collective-permute-start.3
  22.3 0.3 collective-permute-done.14.refs_11_
  22.6 0.2 collective-permute-done.7.refs_3_
  22.7 0.4 collective-permute-done.5.refs_2_
  23.1 0.2 collective-permute-done.3.refs_1_
  23.3 7.4 %shard_map.74 = (bf16[64,2880]{1,0:T(8,128)(2,1)S(1)}, bf16[64,2880]{1,0:T(8,128)(2,1)S(1)}, bf16[64,2880]{1,0:T(8,128)(2,1)S(1)}, bf16[64,2880]{1,0:T(8,128)(2,1)S(1)}, f32[16,4]{1,0:T(8,128)S(1)}) custom-call(bf16[16,2880]{1,0:T(8,128)(2,1)S(1)} %collective-permute-done.1.refs_0_, bf16[16,2880]{1,0:T(8,128)(2,1)S(1)} %collective-permute-done.3.refs_1_, ...), custom_call_target="tpu_custom_call" | custom-call | flops 3185049600 | bytes 12441600 | tf_op jit(solution)/shard_map/pallas_call | solution.py:117
  30.6 0.4 collective-permute-start.16
  31.1 0.2 collective-permute-start.20
  31.2 0.2 slice_reduce_fusion.7
  31.4 1.0 %collective-permute-done.16 = bf16[64,2880]{1,0:T(8,128)(2,1)S(1)} collective-permute-done((bf16[64,2880]{1,0:T(8,128)(2,1)S(1)}, bf16[64,2880]{1,0:T(8,128)(2,1)S(1)}, u32[]{:S(2)}, u32[]{:S(2)}) %collective-permute-start.16) | collective-permute-done | bytes 368672 | tf_op jit(solution)/shard_map/ppermute | solution.py:14
  32.4 0.1 add_convert_fusion.1
  32.5 0.6 %collective-permute-start.17 = (bf16[16,2880]{1,0:T(8,128)(2,1)S(1)}, bf16[16,2880]{1,0:T(8,128)(2,1)S(1)}, u32[]{:S(2)}, u32[]{:S(2)}) collective-permute-start(bf16[16,2880]{1,0:T(8,128)(2,1)S(1)} %get-tuple-element.46), channel_id=1, source_target_pairs={{0,2},{1,3},{2,0},{3,1},{4,6},{5,7},{6,4},{7,5},{8,10},{9,11},{10,... | collective-permute-start | bytes 276488 | tf_op jit(solution)/shard_map/ppermute | solution.py:195
  33.2 2.8 %collective-permute-start.19 = (bf16[16,2880]{1,0:T(8,128)(2,1)S(1)}, bf16[16,2880]{1,0:T(8,128)(2,1)S(1)}, u32[]{:S(2)}, u32[]{:S(2)}) collective-permute-start(bf16[16,2880]{1,0:T(8,128)(2,1)S(1)} %get-tuple-element.47), channel_id=1, source_target_pairs={{0,6},{1,7},{2,4},{3,5},{4,2},{5,3},{6,0},{7,1},{8,14},{9,15},{10,... | collective-permute-start | bytes 276488 | tf_op jit(solution)/shard_map/ppermute | solution.py:195
  35.9 0.2 collective-permute-start.18
  36.1 0.1 add_convert_fusion
  36.2 3.4 %collective-permute-done.17 = bf16[16,2880]{1,0:T(8,128)(2,1)S(1)} collective-permute-done((bf16[16,2880]{1,0:T(8,128)(2,1)S(1)}, bf16[16,2880]{1,0:T(8,128)(2,1)S(1)}, u32[]{:S(2)}, u32[]{:S(2)}) %collective-permute-start.17) | collective-permute-done | bytes 92192 | tf_op jit(solution)/shard_map/ppermute | solution.py:195
  39.6 1.2 %collective-permute-done.18 = bf16[16,2880]{1,0:T(8,128)(2,1)S(1)} collective-permute-done((bf16[16,2880]{1,0:T(8,128)(2,1)S(1)}, bf16[16,2880]{1,0:T(8,128)(2,1)S(1)}, u32[]{:S(2)}, u32[]{:S(2)}) %collective-permute-start.18) | collective-permute-done | bytes 92192 | tf_op jit(solution)/shard_map/ppermute | solution.py:195
  40.8 0.1 add_convert_fusion.3
  40.9 0.6 %collective-permute-start.21 = (bf16[16,2880]{1,0:T(8,128)(2,1)S(1)}, bf16[16,2880]{1,0:T(8,128)(2,1)S(1)}, u32[]{:S(2)}, u32[]{:S(2)}) collective-permute-start(bf16[16,2880]{1,0:T(8,128)(2,1)S(1)} %add_convert_fusion.3), channel_id=1, source_target_pairs={{0,8},{1,9},{2,10},{3,11},{4,12},{5,13},{6,14},{7,15},{8,0},{9,1},... | collective-permute-start | bytes 276488 | tf_op jit(solution)/shard_map/ppermute | solution.py:195
  41.6 0.6 %collective-permute-start.22 = (bf16[16,2880]{1,0:T(8,128)(2,1)S(1)}, bf16[16,2880]{1,0:T(8,128)(2,1)S(1)}, u32[]{:S(2)}, u32[]{:S(2)}) collective-permute-start(bf16[16,2880]{1,0:T(8,128)(2,1)S(1)} %get-tuple-element.43), channel_id=1, source_target_pairs={{0,2},{1,3},{2,0},{3,1},{4,6},{5,7},{6,4},{7,5},{8,10},{9,11},{10,... | collective-permute-start | bytes 276488 | tf_op jit(solution)/shard_map/ppermute | solution.py:195
  42.2 2.4 %collective-permute-start.24 = (bf16[16,2880]{1,0:T(8,128)(2,1)S(1)}, bf16[16,2880]{1,0:T(8,128)(2,1)S(1)}, u32[]{:S(2)}, u32[]{:S(2)}) collective-permute-start(bf16[16,2880]{1,0:T(8,128)(2,1)S(1)} %get-tuple-element.44), channel_id=1, source_target_pairs={{0,6},{1,7},{2,4},{3,5},{4,2},{5,3},{6,0},{7,1},{8,14},{9,15},{10,... | collective-permute-start | bytes 276488 | tf_op jit(solution)/shard_map/ppermute | solution.py:195
  44.6 0.5 %collective-permute-start.23 = (bf16[16,2880]{1,0:T(8,128)(2,1)S(1)}, bf16[16,2880]{1,0:T(8,128)(2,1)S(1)}, u32[]{:S(2)}, u32[]{:S(2)}) collective-permute-start(bf16[16,2880]{1,0:T(8,128)(2,1)S(1)} %get-tuple-element.45), channel_id=1, source_target_pairs={{0,4},{1,5},{2,6},{3,7},{4,0},{5,1},{6,2},{7,3},{8,12},{9,13},{10,... | collective-permute-start | bytes 276488 | tf_op jit(solution)/shard_map/ppermute | solution.py:195
  45.1 0.2 slice_reduce_fusion.3
  45.3 1.8 %collective-permute-done.21 = bf16[16,2880]{1,0:T(8,128)(2,1)S(1)} collective-permute-done((bf16[16,2880]{1,0:T(8,128)(2,1)S(1)}, bf16[16,2880]{1,0:T(8,128)(2,1)S(1)}, u32[]{:S(2)}, u32[]{:S(2)}) %collective-permute-start.21) | collective-permute-done | bytes 92192 | tf_op jit(solution)/shard_map/ppermute | solution.py:195
  47.1 1.8 %collective-permute-done.24 = bf16[16,2880]{1,0:T(8,128)(2,1)S(1)} collective-permute-done((bf16[16,2880]{1,0:T(8,128)(2,1)S(1)}, bf16[16,2880]{1,0:T(8,128)(2,1)S(1)}, u32[]{:S(2)}, u32[]{:S(2)}) %collective-permute-start.24) | collective-permute-done | bytes 92192 | tf_op jit(solution)/shard_map/ppermute | solution.py:195
  48.9 0.9 %collective-permute-done.23 = bf16[16,2880]{1,0:T(8,128)(2,1)S(1)} collective-permute-done((bf16[16,2880]{1,0:T(8,128)(2,1)S(1)}, bf16[16,2880]{1,0:T(8,128)(2,1)S(1)}, u32[]{:S(2)}, u32[]{:S(2)}) %collective-permute-start.23) | collective-permute-done | bytes 92192 | tf_op jit(solution)/shard_map/ppermute | solution.py:195
  49.9 0.8 %add_convert_fusion.2 = bf16[16,2880]{1,0:T(8,128)(2,1)} fusion(bf16[16,2880]{1,0:T(8,128)(2,1)S(1)} %collective-permute-done.24, bf16[16,2880]{1,0:T(8,128)(2,1)S(1)} %collective-permute-done.23, bf16[16,2880]{1,0:T(8,128)(2,1)S(1)} %collective-permute-done.22, bf16[16,2880]{1,0:T(8,128)(2,1)S(1)} %collective-permute-done.21, ...), kind=kLoop, calls=%fused_computation.2 | loop fusion | flops 737280 | bytes 645376 | tf_op jit(solution)/shard_map/convert_element_type | solution.py:230
  (16 shorter events, 0.1 us)
Async XLA Ops:
  0.0 23.3 %copy-start = (bf16[16,2880]{1,0:T(8,128)(2,1)S(1)}, bf16[16,2880]{1,0:T(8,128)(2,1)}, u32[]{:S(2)}) copy-start(bf16[16,2880]{1,0:T(8,128)(2,1)} %refs_12_.1) | copy-start | bytes 276484
  0.0 23.3 %copy-start.1 = (f32[2880]{0:T(1024)S(1)}, f32[2880]{0:T(1024)}, u32[]{:S(2)}) copy-start(f32[2880]{0:T(1024)} %refs_16_.1) | copy-start | bytes 34564
  0.0 9.8 %collective-permute-start.10 = (bf16[16,2880]{1,0:T(8,128)(2,1)}, bf16[16,2880]{1,0:T(8,128)(2,1)S(1)}, u32[]{:S(2)}, u32[]{:S(2)}) collective-permute-start(bf16[16,2880]{1,0:T(8,128)(2,1)} %refs_12_.1), channel_id=1, source_target_pairs={{0,4},{1,5},{2,6},{3,7},{4,0},{5,1},{6,2},{7,3},{8,12},{9,13},{10,... | collective-permute-start | bytes 276488 | tf_op jit(solution)/shard_map/ppermute | solution.py:195
  3.0 6.8 %collective-permute-start.9 = (bf16[16,2880]{1,0:T(8,128)(2,1)}, bf16[16,2880]{1,0:T(8,128)(2,1)S(1)}, u32[]{:S(2)}, u32[]{:S(2)}) collective-permute-start(bf16[16,2880]{1,0:T(8,128)(2,1)} %refs_12_.1), channel_id=1, source_target_pairs={{0,2},{1,3},{2,0},{3,1},{4,6},{5,7},{6,4},{7,5},{8,10},{9,11},{10,... | collective-permute-start | bytes 276488 | tf_op jit(solution)/shard_map/ppermute | solution.py:195
  4.5 6.1 %collective-permute-start.11 = (bf16[16,2880]{1,0:T(8,128)(2,1)}, bf16[16,2880]{1,0:T(8,128)(2,1)S(1)}, u32[]{:S(2)}, u32[]{:S(2)}) collective-permute-start(bf16[16,2880]{1,0:T(8,128)(2,1)} %refs_12_.1), channel_id=1, source_target_pairs={{0,6},{1,7},{2,4},{3,5},{4,2},{5,3},{6,0},{7,1},{8,14},{9,15},{10,... | collective-permute-start | bytes 276488 | tf_op jit(solution)/shard_map/ppermute | solution.py:195
  4.6 6.8 %collective-permute-start = (bf16[16,2880]{1,0:T(8,128)(2,1)}, bf16[16,2880]{1,0:T(8,128)(2,1)S(1)}, u32[]{:S(2)}, u32[]{:S(2)}) collective-permute-start(bf16[16,2880]{1,0:T(8,128)(2,1)} %refs_12_.1), channel_id=1, source_target_pairs={{0,8},{1,9},{2,10},{3,11},{4,12},{5,13},{6,14},{7,15},{8,0},{9,1},... | collective-permute-start | bytes 276488 | tf_op jit(solution)/shard_map/ppermute | solution.py:195
  7.5 9.8 %collective-permute-start.8 = (bf16[16,2880]{1,0:T(8,128)(2,1)}, bf16[16,2880]{1,0:T(8,128)(2,1)S(1)}, u32[]{:S(2)}, u32[]{:S(2)}) collective-permute-start(bf16[16,2880]{1,0:T(8,128)(2,1)} %refs_12_.1), channel_id=1, source_target_pairs={{0,1},{1,0},{2,3},{3,2},{4,5},{5,4},{6,7},{7,6},{8,9},{9,8},{10,11... | collective-permute-start | bytes 276488 | tf_op jit(solution)/shard_map/ppermute | solution.py:14
  11.3 7.5 %collective-permute-start.6 = (bf16[16,2880]{1,0:T(8,128)(2,1)S(1)}, bf16[16,2880]{1,0:T(8,128)(2,1)S(1)}, u32[]{:S(2)}, u32[]{:S(2)}) collective-permute-start(bf16[16,2880]{1,0:T(8,128)(2,1)S(1)} %collective-permute-done.refs_4_), channel_id=1, source_target_pairs={{0,6},{1,7},{2,4},{3,5},{4,2},{5,3},{6,0},{7,1},{8,14},{9,15},{10,... | collective-permute-start | bytes 276488 | tf_op jit(solution)/shard_map/ppermute | solution.py:195
  14.2 4.7 %collective-permute-start.15 = (f32[16,4]{1,0:T(8,128)S(1)}, f32[16,4]{1,0:T(8,128)S(1)}, u32[]{:S(2)}, u32[]{:S(2)}) collective-permute-start(f32[16,4]{1,0:T(8,128)S(1)} %get-tuple-element.26), channel_id=1, source_target_pairs={{0,8},{1,9},{2,10},{3,11},{4,12},{5,13},{6,14},{7,15},{8,0},{9,1},... | collective-permute-start | bytes 776 | tf_op jit(solution)/shard_map/ppermute | solution.py:195
  16.7 4.6 %collective-permute-start.4 = (bf16[16,2880]{1,0:T(8,128)(2,1)S(1)}, bf16[16,2880]{1,0:T(8,128)(2,1)S(1)}, u32[]{:S(2)}, u32[]{:S(2)}) collective-permute-start(bf16[16,2880]{1,0:T(8,128)(2,1)S(1)} %collective-permute-done.refs_4_), channel_id=1, source_target_pairs={{0,4},{1,5},{2,6},{3,7},{4,0},{5,1},{6,2},{7,3},{8,12},{9,13},{10,... | collective-permute-start | bytes 276488 | tf_op jit(solution)/shard_map/ppermute | solution.py:195
  16.7 4.6 %collective-permute-start.2 = (bf16[16,2880]{1,0:T(8,128)(2,1)S(1)}, bf16[16,2880]{1,0:T(8,128)(2,1)S(1)}, u32[]{:S(2)}, u32[]{:S(2)}) collective-permute-start(bf16[16,2880]{1,0:T(8,128)(2,1)S(1)} %collective-permute-done.refs_4_), channel_id=1, source_target_pairs={{0,2},{1,3},{2,0},{3,1},{4,6},{5,7},{6,4},{7,5},{8,10},{9,11},{10,... | collective-permute-start | bytes 276488 | tf_op jit(solution)/shard_map/ppermute | solution.py:195
  17.3 4.5 %collective-permute-start.1 = (bf16[16,2880]{1,0:T(8,128)(2,1)S(1)}, bf16[16,2880]{1,0:T(8,128)(2,1)S(1)}, u32[]{:S(2)}, u32[]{:S(2)}) collective-permute-start(bf16[16,2880]{1,0:T(8,128)(2,1)S(1)} %collective-permute-done.refs_4_), channel_id=1, source_target_pairs={{0,1},{1,0},{2,3},{3,2},{4,5},{5,4},{6,7},{7,6},{8,9},{9,8},{10,11... | collective-permute-start | bytes 276488 | tf_op jit(solution)/shard_map/ppermute | solution.py:14
  18.9 3.0 %collective-permute-start.12 = (bf16[16,2880]{1,0:T(8,128)(2,1)S(1)}, bf16[16,2880]{1,0:T(8,128)(2,1)S(1)}, u32[]{:S(2)}, u32[]{:S(2)}) collective-permute-start(bf16[16,2880]{1,0:T(8,128)(2,1)S(1)} %collective-permute-done.9.refs_13_), channel_id=1, source_target_pairs={{0,1},{1,0},{2,3},{3,2},{4,5},{5,4},{6,7},{7,6},{8,9},{9,8},{10,11... | collective-permute-start | bytes 276488 | tf_op jit(solution)/shard_map/ppermute | solution.py:14
  18.9 3.5 %collective-permute-start.13 = (bf16[16,2880]{1,0:T(8,128)(2,1)S(1)}, bf16[16,2880]{1,0:T(8,128)(2,1)S(1)}, u32[]{:S(2)}, u32[]{:S(2)}) collective-permute-start(bf16[16,2880]{1,0:T(8,128)(2,1)S(1)} %collective-permute-done.10.refs_14_), channel_id=1, source_target_pairs={{0,1},{1,0},{2,3},{3,2},{4,5},{5,4},{6,7},{7,6},{8,9},{9,8},{10,11... | collective-permute-start | bytes 276488 | tf_op jit(solution)/shard_map/ppermute | solution.py:14
  21.3 1.3 %collective-permute-start.14 = (bf16[16,2880]{1,0:T(8,128)(2,1)S(1)}, bf16[16,2880]{1,0:T(8,128)(2,1)S(1)}, u32[]{:S(2)}, u32[]{:S(2)}) collective-permute-start(bf16[16,2880]{1,0:T(8,128)(2,1)S(1)} %collective-permute-done.11.refs_15_), channel_id=1, source_target_pairs={{0,1},{1,0},{2,3},{3,2},{4,5},{5,4},{6,7},{7,6},{8,9},{9,8},{10,11... | collective-permute-start | bytes 276488 | tf_op jit(solution)/shard_map/ppermute | solution.py:14
  21.3 1.4 %collective-permute-start.7 = (bf16[16,2880]{1,0:T(8,128)(2,1)S(1)}, bf16[16,2880]{1,0:T(8,128)(2,1)S(1)}, u32[]{:S(2)}, u32[]{:S(2)}) collective-permute-start(bf16[16,2880]{1,0:T(8,128)(2,1)S(1)} %collective-permute-done.6.refs_7_), channel_id=1, source_target_pairs={{0,1},{1,0},{2,3},{3,2},{4,5},{5,4},{6,7},{7,6},{8,9},{9,8},{10,11... | collective-permute-start | bytes 276488 | tf_op jit(solution)/shard_map/ppermute | solution.py:14
  21.8 1.3 %collective-permute-start.5 = (bf16[16,2880]{1,0:T(8,128)(2,1)S(1)}, bf16[16,2880]{1,0:T(8,128)(2,1)S(1)}, u32[]{:S(2)}, u32[]{:S(2)}) collective-permute-start(bf16[16,2880]{1,0:T(8,128)(2,1)S(1)} %collective-permute-done.4.refs_6_), channel_id=1, source_target_pairs={{0,1},{1,0},{2,3},{3,2},{4,5},{5,4},{6,7},{7,6},{8,9},{9,8},{10,11... | collective-permute-start | bytes 276488 | tf_op jit(solution)/shard_map/ppermute | solution.py:14
  21.9 1.4 %collective-permute-start.3 = (bf16[16,2880]{1,0:T(8,128)(2,1)S(1)}, bf16[16,2880]{1,0:T(8,128)(2,1)S(1)}, u32[]{:S(2)}, u32[]{:S(2)}) collective-permute-start(bf16[16,2880]{1,0:T(8,128)(2,1)S(1)} %collective-permute-done.2.refs_5_), channel_id=1, source_target_pairs={{0,1},{1,0},{2,3},{3,2},{4,5},{5,4},{6,7},{7,6},{8,9},{9,8},{10,11... | collective-permute-start | bytes 276488 | tf_op jit(solution)/shard_map/ppermute | solution.py:14
  30.6 1.8 %collective-permute-start.16 = (bf16[64,2880]{1,0:T(8,128)(2,1)S(1)}, bf16[64,2880]{1,0:T(8,128)(2,1)S(1)}, u32[]{:S(2)}, u32[]{:S(2)}) collective-permute-start(bf16[64,2880]{1,0:T(8,128)(2,1)S(1)} %get-tuple-element.29), channel_id=1, source_target_pairs={{0,1},{1,0},{2,3},{3,2},{4,5},{5,4},{6,7},{7,6},{8,9},{9,8},{10,11... | collective-permute-start | bytes 1105928 | tf_op jit(solution)/shard_map/ppermute | solution.py:14
  31.1 5.0 %collective-permute-start.20 = (bf16[64,2880]{1,0:T(8,128)(2,1)S(1)}, bf16[64,2880]{1,0:T(8,128)(2,1)S(1)}, u32[]{:S(2)}, u32[]{:S(2)}) collective-permute-start(bf16[64,2880]{1,0:T(8,128)(2,1)S(1)} %get-tuple-element.31), channel_id=1, source_target_pairs={{0,1},{1,0},{2,3},{3,2},{4,5},{5,4},{6,7},{7,6},{8,9},{9,8},{10,11... | collective-permute-start | bytes 1105928 | tf_op jit(solution)/shard_map/ppermute | solution.py:14
  32.5 7.1 %collective-permute-start.17 = (bf16[16,2880]{1,0:T(8,128)(2,1)S(1)}, bf16[16,2880]{1,0:T(8,128)(2,1)S(1)}, u32[]{:S(2)}, u32[]{:S(2)}) collective-permute-start(bf16[16,2880]{1,0:T(8,128)(2,1)S(1)} %get-tuple-element.46), channel_id=1, source_target_pairs={{0,2},{1,3},{2,0},{3,1},{4,6},{5,7},{6,4},{7,5},{8,10},{9,11},{10,... | collective-permute-start | bytes 276488 | tf_op jit(solution)/shard_map/ppermute | solution.py:195
  33.2 6.4 %collective-permute-start.19 = (bf16[16,2880]{1,0:T(8,128)(2,1)S(1)}, bf16[16,2880]{1,0:T(8,128)(2,1)S(1)}, u32[]{:S(2)}, u32[]{:S(2)}) collective-permute-start(bf16[16,2880]{1,0:T(8,128)(2,1)S(1)} %get-tuple-element.47), channel_id=1, source_target_pairs={{0,6},{1,7},{2,4},{3,5},{4,2},{5,3},{6,0},{7,1},{8,14},{9,15},{10,... | collective-permute-start | bytes 276488 | tf_op jit(solution)/shard_map/ppermute | solution.py:195
  35.9 4.8 %collective-permute-start.18 = (bf16[16,2880]{1,0:T(8,128)(2,1)S(1)}, bf16[16,2880]{1,0:T(8,128)(2,1)S(1)}, u32[]{:S(2)}, u32[]{:S(2)}) collective-permute-start(bf16[16,2880]{1,0:T(8,128)(2,1)S(1)} %get-tuple-element.48), channel_id=1, source_target_pairs={{0,4},{1,5},{2,6},{3,7},{4,0},{5,1},{6,2},{7,3},{8,12},{9,13},{10,... | collective-permute-start | bytes 276488 | tf_op jit(solution)/shard_map/ppermute | solution.py:195
  40.9 6.2 %collective-permute-start.21 = (bf16[16,2880]{1,0:T(8,128)(2,1)S(1)}, bf16[16,2880]{1,0:T(8,128)(2,1)S(1)}, u32[]{:S(2)}, u32[]{:S(2)}) collective-permute-start(bf16[16,2880]{1,0:T(8,128)(2,1)S(1)} %add_convert_fusion.3), channel_id=1, source_target_pairs={{0,8},{1,9},{2,10},{3,11},{4,12},{5,13},{6,14},{7,15},{8,0},{9,1},... | collective-permute-start | bytes 276488 | tf_op jit(solution)/shard_map/ppermute | solution.py:195
  41.6 5.5 %collective-permute-start.22 = (bf16[16,2880]{1,0:T(8,128)(2,1)S(1)}, bf16[16,2880]{1,0:T(8,128)(2,1)S(1)}, u32[]{:S(2)}, u32[]{:S(2)}) collective-permute-start(bf16[16,2880]{1,0:T(8,128)(2,1)S(1)} %get-tuple-element.43), channel_id=1, source_target_pairs={{0,2},{1,3},{2,0},{3,1},{4,6},{5,7},{6,4},{7,5},{8,10},{9,11},{10,... | collective-permute-start | bytes 276488 | tf_op jit(solution)/shard_map/ppermute | solution.py:195
  42.2 6.8 %collective-permute-start.24 = (bf16[16,2880]{1,0:T(8,128)(2,1)S(1)}, bf16[16,2880]{1,0:T(8,128)(2,1)S(1)}, u32[]{:S(2)}, u32[]{:S(2)}) collective-permute-start(bf16[16,2880]{1,0:T(8,128)(2,1)S(1)} %get-tuple-element.44), channel_id=1, source_target_pairs={{0,6},{1,7},{2,4},{3,5},{4,2},{5,3},{6,0},{7,1},{8,14},{9,15},{10,... | collective-permute-start | bytes 276488 | tf_op jit(solution)/shard_map/ppermute | solution.py:195
  44.6 5.3 %collective-permute-start.23 = (bf16[16,2880]{1,0:T(8,128)(2,1)S(1)}, bf16[16,2880]{1,0:T(8,128)(2,1)S(1)}, u32[]{:S(2)}, u32[]{:S(2)}) collective-permute-start(bf16[16,2880]{1,0:T(8,128)(2,1)S(1)} %get-tuple-element.45), channel_id=1, source_target_pairs={{0,4},{1,5},{2,6},{3,7},{4,0},{5,1},{6,2},{7,3},{8,12},{9,13},{10,... | collective-permute-start | bytes 276488 | tf_op jit(solution)/shard_map/ppermute | solution.py:195

commit v6 on v5

--- a/solution.py
+++ b/solution.py
@@ -78,67 +78,115 @@
     return (residual.astype(jnp.float32) + combined).astype(jnp.bfloat16)
 
 
-def expert_kernel(groups, *refs):
-    count = sum(groups)
-    blocks, (gain_ref, gate_ref, up_hbm, down_hbm, table_ref) = refs[:count], refs[count : count + 5]
-    outs, (table_out_ref, normed_ref, up_ref, down_ref, sems) = refs[count + 5 : -5], refs[-5:]
-    up_copy = pltpu.make_async_copy(up_hbm, up_ref, sems.at[0])
-    down_copy = pltpu.make_async_copy(down_hbm, down_ref, sems.at[1])
-    up_copy.start()
-    down_copy.start()
-    table_out_ref[...] = table_ref[...]
+def pack_kernel(after, *refs):
+    refs = refs[after:]
+    blocks, gain_ref, out_ref = refs[:-2], refs[-2], refs[-1]
     rows, model = blocks[0].shape
     gain = gain_ref[...].reshape(1, model)
     for i, block in enumerate(blocks):
         x = block[...].astype(jnp.float32)
         scale = lax.rsqrt(jnp.mean(x * x, axis=-1, keepdims=True) + 1e-05)
-        normed_ref[pl.ds(i * rows, rows), :] = (x * scale * gain).astype(jnp.bfloat16)
-    normed = normed_ref[...]
+        out_ref[pl.ds(i * rows, rows), :] = (x * scale * gain).astype(jnp.bfloat16)
+
+
+def pack(blocks, gain, after=()):
+    rows, model = blocks[0].shape
+    vmem = pl.BlockSpec(memory_space=pltpu.VMEM)
+    return pl.pallas_call(
+        functools.partial(pack_kernel, len(after)),
+        out_shape=jax.ShapeDtypeStruct((rows * len(blocks), model), jnp.bfloat16),
+        in_specs=[pl.BlockSpec(memory_space=pl.ANY)] * len(after) + [vmem] * (len(blocks) + 1),
+        out_specs=vmem,
+        compiler_params=pltpu.CompilerParams(vmem_limit_bytes=8 * 2**20),
+    )(*after, *blocks, gain)
+
+
+def mix_kernel(table_ref, *refs):
+    blocks, out_ref = refs[:-1], refs[-1]
+    total = jnp.zeros(out_ref.shape, jnp.float32)
+    for i, block in enumerate(blocks):
+        total += table_ref[:, i : i + 1] * block[...].astype(jnp.float32)
+    out_ref[...] = total.astype(out_ref.dtype)
+
+
+def mixed(table, blocks):
+    vmem = pl.BlockSpec(memory_space=pltpu.VMEM)
+    return pl.pallas_call(
+        mix_kernel,
+        out_shape=jax.ShapeDtypeStruct(blocks[0].shape, blocks[0].dtype),
+        in_specs=[vmem] * (len(blocks) + 1),
+        out_specs=vmem,
+        compiler_params=pltpu.CompilerParams(vmem_limit_bytes=8 * 2**20),
+    )(table, *blocks)
+
+
+def expert_kernel(count, *refs):
+    groups, (gate_ref, up_ref, down_ref, table_ref) = refs[:count], refs[count : count + 4]
+    outs, table_out_ref, rows_ref = refs[count + 4 : -2], refs[-2], refs[-1]
+    table_out_ref[...] = table_ref[...]
+    rows = groups[0].shape[0]
+    for i, group in enumerate(groups):
+        rows_ref[pl.ds(i * rows, rows), :] = group[...]
+    normed = rows_ref[...]
     across = (((1,), (1,)), ((), ()))
     gate = lax.dot_general(normed, gate_ref[...], across, preferred_element_type=jnp.float32)
-    gate = gate * jax.nn.sigmoid(1.702 * gate)
-    up_copy.wait()
     upper = lax.dot_general(normed, up_ref[...], across, preferred_element_type=jnp.float32)
-    act = (gate * (upper + 1.0)).astype(jnp.bfloat16)
-    down_copy.wait()
+    act = (gate * jax.nn.sigmoid(1.702 * gate) * (upper + 1.0)).astype(jnp.bfloat16)
     out = jnp.dot(act, down_ref[...], preferred_element_type=jnp.float32).astype(jnp.bfloat16)
-    start = 0
-    for size, out_ref in zip(groups, outs):
-        out_ref[...] = out[start * rows : (start + size) * rows]
-        start += size
-
-
-def expert_parts(groups, gain, gate_w, up_w, down_w, table):
-    blocks = sum(groups, [])
-    sizes = tuple(len(group) for group in groups)
-    rows, model = blocks[0].shape
-    count, hidden = len(blocks), gate_w.shape[0]
-    vmem, hbm = pl.BlockSpec(memory_space=pltpu.VMEM), pl.BlockSpec(memory_space=pltpu.HBM)
-    return pl.pallas_call(
-        functools.partial(expert_kernel, sizes),
-        out_shape=tuple(jax.ShapeDtypeStruct((rows * size, model), jnp.bfloat16) for size in sizes)
+    for i, out_ref in enumerate(outs):
+        out_ref[...] = out[i * rows : (i + 1) * rows]
+
+
+def expert_parts(groups, gate_w, up_w, down_w, table):
+    count = len(groups)
+    rows, model = groups[0].shape
+    hidden = gate_w.shape[0]
+    vmem = pl.BlockSpec(memory_space=pltpu.VMEM)
+    return pl.pallas_call(
+        functools.partial(expert_kernel, count),
+        out_shape=(jax.ShapeDtypeStruct((rows, model), jnp.bfloat16),) * count
         + (jax.ShapeDtypeStruct(table.shape, table.dtype),),
-        in_specs=[vmem] * (count + 2) + [hbm, hbm, vmem],
-        out_specs=(vmem,) * (len(groups) + 1),
-        scratch_shapes=[
-            pltpu.VMEM((rows * count, model), jnp.bfloat16),
-            pltpu.VMEM(up_w.shape, up_w.dtype),
-            pltpu.VMEM(down_w.shape, down_w.dtype),
-            pltpu.SemaphoreType.DMA((2,)),
-        ],
+        in_specs=[vmem] * (count + 4),
+        out_specs=(vmem,) * (count + 1),
+        scratch_shapes=[pltpu.VMEM((rows * count, model), jnp.bfloat16)],
         cost_estimate=pl.CostEstimate(
             flops=6 * rows * count * model * hidden,
             bytes_accessed=6 * model * hidden,
             transcendentals=rows * count * hidden,
         ),
-        compiler_params=pltpu.CompilerParams(vmem_limit_bytes=32 * 2**20),
-    )(
-        *blocks,
-        gain,
-        gate_w,
-        *(pltpu.with_memory_space_constraint(w, pltpu.HBM) for w in (up_w, down_w)),
-        table,
-    )
+        compiler_params=pltpu.CompilerParams(vmem_limit_bytes=24 * 2**20),
+    )(*groups, gate_w, up_w, down_w, table)
+
+
+def read_kernel(count, *refs):
+    sources, targets = refs[1 : count + 1], refs[count + 1 : 2 * count + 1]
+    token_ref, sems = refs[-2], refs[-1]
+    copies = [
+        pltpu.make_async_copy(source, target, sems.at[i])
+        for i, (source, target) in enumerate(zip(sources, targets))
+    ]
+    for copy in copies:
+        copy.start()
+    token_ref[0] = 0
+    for copy in copies:
+        copy.wait()
+
+
+def read(arrays, after):
+    count = len(arrays)
+    vmem, hbm = pl.BlockSpec(memory_space=pltpu.VMEM), pl.BlockSpec(memory_space=pltpu.HBM)
+    return pl.pallas_call(
+        functools.partial(read_kernel, count),
+        out_shape=tuple(pltpu.VMEM(a.shape, a.dtype) for a in arrays)
+        + (jax.ShapeDtypeStruct((1,), jnp.int32),),
+        in_specs=[pl.BlockSpec(memory_space=pl.ANY)] + [hbm] * count,
+        out_specs=(vmem,) * count + (pl.BlockSpec(memory_space=pltpu.SMEM),),
+        scratch_shapes=[pltpu.SemaphoreType.DMA((count,))],
+        cost_estimate=pl.CostEstimate(
+            flops=0, bytes_accessed=2 * sum(a.size * a.dtype.itemsize for a in arrays), transcendentals=0
+        ),
+        compiler_params=pltpu.CompilerParams(vmem_limit_bytes=16 * 2**20),
+    )(after, *(pltpu.with_memory_space_constraint(a, pltpu.HBM) for a in arrays))
 
 
 def load_kernel(chip_ref, ids_hbm, weights_hbm, source, near_ref, far_ref, target, ids_ref, weights_ref, sems):
@@ -180,7 +228,7 @@
         ),
         compiler_params=pltpu.CompilerParams(vmem_limit_bytes=16 * 2**20),
     )(
-        chip.reshape(1),
+        chip,
         *(pltpu.with_memory_space_constraint(a, pltpu.HBM) for a in (expert_ids.T, expert_weights.T, array)),
     )
 
@@ -200,34 +248,27 @@
     x = residual
     mirrored = across(x, half)
     near = [across(x, mask) for mask in range(1, half)]
-    near_swapped = [swap(x)]
-    chip = lax.axis_index("expert") // 2
+    chip = (lax.axis_index("expert") // 2).reshape(1)
     near_weights, far_weights, gate_w = load(chip, expert_ids, expert_weights, half, gate_proj[0].T)
-    near_weights, far_weights, *near = lax.optimization_barrier((near_weights, far_weights, *near))
-    near_swapped += [swap(block) for block in near]
     far = [across(mirrored, mask) for mask in range(1, half)]
-    far_swapped = [swap(mirrored)] + [swap(block) for block in far]
-    *parts, mirror_weights = expert_parts(
-        (far_swapped, [mirrored] + far, near_swapped, [x] + near),
-        norm_gain,
-        gate_w,
-        up_proj[0].T,
-        down_proj[0],
-        across(far_weights, half),
-    )
-
-    def mix(done, block_weights):
+    near_rows = pack([x] + near, norm_gain, (near_weights, mirrored))
+    near_swapped = swap(near_rows)
+    up_w, down_w, token = read((up_proj[0].T, down_proj[0]), near_swapped)
+    far_rows = pack([mirrored] + far, norm_gain, (token,))
+    groups = (swap(far_rows), far_rows, near_swapped, near_rows)
+    *parts, far_weights = expert_parts(groups, gate_w, up_w, down_w, far_weights)
+    mirror_weights = across(far_weights, half)
+
+    def give_back(done):
         done = done.reshape(half, rows, model)
-        total = jnp.zeros((rows, model), jnp.float32)
-        for mask in range(half):
-            total += block_weights[:, mask][:, None] * across(done[mask], mask).astype(jnp.float32)
-        return total
-
-    other = mix(pair_sum(parts[1], swap(parts[0])), mirror_weights).astype(jnp.bfloat16)
-    near_done = pair_sum(parts[3], swap(parts[2]))
-    other, near_done = lax.optimization_barrier((other, near_done))
-    own = across(other, half).astype(jnp.float32) + mix(near_done, near_weights)
-    return (x.astype(jnp.float32) + own).astype(jnp.bfloat16)
+        return [across(done[mask], mask) for mask in range(half)]
+
+    far_blocks = give_back(pair_sum(parts[1], swap(parts[0])))
+    near_blocks = give_back(pair_sum(parts[3], swap(parts[2])))
+    total = x.astype(jnp.float32) + across(mixed(mirror_weights, far_blocks), half).astype(jnp.float32)
+    for mask, block in enumerate(near_blocks):
+        total += near_weights[:, mask][:, None] * block.astype(jnp.float32)
+    return total.astype(jnp.bfloat16)
 
 
 def body(residual, norm_gain, expert_ids, expert_weights, gate_proj, up_proj, down_proj):

time: 50.8 us -> 46.7 us (0.919)
  waiting for transfers between devices: 16 us -> 12.8 us
  starting transfers between devices: 23.3 us -> 21 us
  Pallas kernels: 9.63 us -> 11.4 us
    ppermute x15, waiting for transfers between devices: 14.1 us -> 10.5 us  [across(): return lax.ppermute(value, 'expert', pairs) if mask else value]
    pallas_call x1 -> x5, Pallas kernels: 7.37 us -> 9.12 us  [the longest x1 4.03 us: read(): pl.pallas_call(functools.partial(read_kernel, count), out_shape=tuple((pl...]
    ppermute x10 -> x4, starting transfers between devices: 2.11 us -> 0.42 us  [partner(): return lax.ppermute(value, axis, pairs)]
    ppermute x15, starting transfers between devices: 21.2 us -> 20.6 us  [across(): return lax.ppermute(value, 'expert', pairs) if mask else value]
    ppermute x10 -> x4, waiting for transfers between devices: 1.92 us -> 2.29 us  [partner(): return lax.ppermute(value, axis, pairs)]
  transfers between devices with their start and end apart: 25 -> 19, of which waited for: 14 -> 11; matrix products, arithmetic and copies ran while one was open for 1% -> 1% of each run, Pallas kernels for 4% -> 14%
where the time goes in v6:
time: 46.7 us; the launch traced here: 46.5 us
  starting transfers between devices  21 us (45%)
  waiting for transfers between devices  12.8 us (27%)
  Pallas kernels  11.4 us (24%)
  other arithmetic  0.98 us (2%)
    ppermute x15, starting transfers between devices, across(): return lax.ppermute(value, 'expert', pairs) if mask else value  20.6 us
    ppermute x15, waiting for transfers between devices, across(): return lax.ppermute(value, 'expert', pairs) if mask else value  10.5 us
    pallas_call x1, Pallas kernels, read(): pl.pallas_call(functools.partial(read_kernel, count), out_shape=tuple((pl...  4.03 us
    pallas_call x1, Pallas kernels, expert_parts(): pl.pallas_call(functools.partial(expert_kernel, count), out_shape=(jax.Sh...  3.92 us
    ppermute x4, waiting for transfers between devices, partner(): return lax.ppermute(value, axis, pairs)  2.29 us
    pallas_call x1, Pallas kernels, load(): pl.pallas_call(load_kernel, out_shape=(table, table, pltpu.VMEM(array.sha...  2.26 us
    pallas_call x2, Pallas kernels, pack(): pl.pallas_call(functools.partial(pack_kernel, len(after)), out_shape=jax....  1.04 us
  transfers between devices with their start and end apart: 19, of which 11 were waited for; matrix products, arithmetic and copies ran while one was open for 1% of the time, Pallas kernels for 14%

profile of v6, /device:TPU:0, one launch (start us, length us, event | category | flops | bytes accessed | tf_op | source)
XLA Modules:
  0.0 46.5 jit_solution(18281616273444533001)
XLA Ops:
  0.0 3.0 %collective-permute-start.2 = (bf16[16,2880]{1,0:T(8,128)(2,1)}, bf16[16,2880]{1,0:T(8,128)(2,1)S(1)}, u32[]{:S(2)}, u32[]{:S(2)}) collective-permute-start(bf16[16,2880]{1,0:T(8,128)(2,1)} %refs_2_.1), channel_id=1, source_target_pairs={{0,4},{1,5},{2,6},{3,7},{4,0},{5,1},{6,2},{7,3},{8,12},{9,13},{10,... | collective-permute-start | bytes 276488 | tf_op jit(solution)/shard_map/ppermute | solution.py:243
  3.0 1.5 %collective-permute-start.1 = (bf16[16,2880]{1,0:T(8,128)(2,1)}, bf16[16,2880]{1,0:T(8,128)(2,1)S(1)}, u32[]{:S(2)}, u32[]{:S(2)}) collective-permute-start(bf16[16,2880]{1,0:T(8,128)(2,1)} %refs_2_.1), channel_id=1, source_target_pairs={{0,2},{1,3},{2,0},{3,1},{4,6},{5,7},{6,4},{7,5},{8,10},{9,11},{10,... | collective-permute-start | bytes 276488 | tf_op jit(solution)/shard_map/ppermute | solution.py:243
  4.5 2.6 %collective-permute-start = (bf16[16,2880]{1,0:T(8,128)(2,1)}, bf16[16,2880]{1,0:T(8,128)(2,1)S(1)}, u32[]{:S(2)}, u32[]{:S(2)}) collective-permute-start(bf16[16,2880]{1,0:T(8,128)(2,1)} %refs_2_.1), channel_id=1, source_target_pairs={{0,8},{1,9},{2,10},{3,11},{4,12},{5,13},{6,14},{7,15},{8,0},{9,1},... | collective-permute-start | bytes 276488 | tf_op jit(solution)/shard_map/ppermute | solution.py:243
  7.1 0.4 collective-permute-start.3
  7.5 2.3 %shard_map.73 = (f32[16,4]{1,0:T(8,128)S(1)}, f32[16,4]{1,0:T(8,128)S(1)}, bf16[720,2880]{1,0:T(8,128)(2,1)S(1)}) custom-call(s32[1]{0:T(128)} %bitcast.chip_ref, s32[4,16]{1,0:T(4,128)} %bitcast.13, f32[4,16]{1,0:T(4,128)} %bitcast.14, bf16[720,2880]{1,0:T(8,128)(2,1)} %bitcast.12), custom_call_target="tpu_custom_call" | custom-call | bytes 8294400 | tf_op jit(solution)/shard_map/pallas_call | solution.py:216
  9.8 0.0 collective-permute-done.2.refs_4_
  9.8 0.0 collective-permute-done.1.refs_3_
  9.8 1.7 %collective-permute-done.refs_1_ = bf16[16,2880]{1,0:T(8,128)(2,1)S(1)} collective-permute-done((bf16[16,2880]{1,0:T(8,128)(2,1)}, bf16[16,2880]{1,0:T(8,128)(2,1)S(1)}, u32[]{:S(2)}, u32[]{:S(2)}) %collective-permute-start) | collective-permute-done | bytes 92192 | tf_op jit(solution)/shard_map/ppermute | solution.py:243
  11.5 1.3 %collective-permute-done.3.refs_5_ = bf16[16,2880]{1,0:T(8,128)(2,1)S(1)} collective-permute-done((bf16[16,2880]{1,0:T(8,128)(2,1)}, bf16[16,2880]{1,0:T(8,128)(2,1)S(1)}, u32[]{:S(2)}, u32[]{:S(2)}) %collective-permute-start.3) | collective-permute-done | bytes 92192 | tf_op jit(solution)/shard_map/ppermute | solution.py:243
  12.8 0.2 shard_map.74.refs_3_
  13.0 0.1 collective-permute-start.4
  13.1 1.4 %collective-permute-start.7 = (bf16[16,2880]{1,0:T(8,128)(2,1)S(1)}, bf16[16,2880]{1,0:T(8,128)(2,1)S(1)}, u32[]{:S(2)}, u32[]{:S(2)}) collective-permute-start(bf16[16,2880]{1,0:T(8,128)(2,1)S(1)} %collective-permute-done.refs_1_), channel_id=1, source_target_pairs={{0,6},{1,7},{2,4},{3,5},{4,2},{5,3},{6,0},{7,1},{8,14},{9,15},{10,... | collective-permute-start | bytes 276488 | tf_op jit(solution)/shard_map/ppermute | solution.py:243
  14.5 1.1 %collective-permute-start.6 = (bf16[16,2880]{1,0:T(8,128)(2,1)S(1)}, bf16[16,2880]{1,0:T(8,128)(2,1)S(1)}, u32[]{:S(2)}, u32[]{:S(2)}) collective-permute-start(bf16[16,2880]{1,0:T(8,128)(2,1)S(1)} %collective-permute-done.refs_1_), channel_id=1, source_target_pairs={{0,4},{1,5},{2,6},{3,7},{4,0},{5,1},{6,2},{7,3},{8,12},{9,13},{10,... | collective-permute-start | bytes 276488 | tf_op jit(solution)/shard_map/ppermute | solution.py:243
  15.6 1.0 %collective-permute-start.5 = (bf16[16,2880]{1,0:T(8,128)(2,1)S(1)}, bf16[16,2880]{1,0:T(8,128)(2,1)S(1)}, u32[]{:S(2)}, u32[]{:S(2)}) collective-permute-start(bf16[16,2880]{1,0:T(8,128)(2,1)S(1)} %collective-permute-done.refs_1_), channel_id=1, source_target_pairs={{0,2},{1,3},{2,0},{3,1},{4,6},{5,7},{6,4},{7,5},{8,10},{9,11},{10,... | collective-permute-start | bytes 276488 | tf_op jit(solution)/shard_map/ppermute | solution.py:243
  16.7 0.0 collective-permute-done.4.refs_0_.refs_2_
  16.7 4.0 %shard_map.75 = (bf16[720,2880]{1,0:T(8,128)(2,1)S(1)}, bf16[720,2880]{1,0:T(8,128)(2,1)S(1)}, s32[1]{0:T(128)}) custom-call(bf16[64,2880]{1,0:T(8,128)(2,1)S(1)} %collective-permute-done.4.refs_0_.refs_2_, bf16[720,2880]{1,0:T(8,128)(2,1)} %bitcast.10, bf16[720,2880]{1,0:T(8,128)(2,1)} %bitcast.11), custom_call_target="tpu_custom_call" | custom-call | bytes 16588800 | tf_op jit(solution)/shard_map/pallas_call | solution.py:178
  20.7 0.0 collective-permute-done.7.refs_4_
  20.7 0.0 collective-permute-done.6.refs_3_
  20.7 0.4 collective-permute-done.5.refs_2_
  21.2 0.8 %shard_map.76.refs_1_ = bf16[64,2880]{1,0:T(8,128)(2,1)S(1)} custom-call(s32[1]{0:T(128)} %get-tuple-element.17.refs_0_, bf16[16,2880]{1,0:T(8,128)(2,1)S(1)} %collective-permute-done.refs_1_, bf16[16,2880]{1,0:T(8,128)(2,1)S(1)} %collective-permute-done.5.refs_2_, bf16[16,2880]{1,0:T(8,128)(2,1)S(1)} %collective-permute-done.6.refs_3_, ...), custom_call_target="tpu_custom_call" | custom-call | tf_op jit(solution)/shard_map/pallas_call | solution.py:95
  22.0 0.1 collective-permute-start.8
  22.1 1.7 %collective-permute-done.8.refs_0_ = bf16[64,2880]{1,0:T(8,128)(2,1)S(1)} collective-permute-done((bf16[64,2880]{1,0:T(8,128)(2,1)S(1)}, bf16[64,2880]{1,0:T(8,128)(2,1)S(1)}, u32[]{:S(2)}, u32[]{:S(2)}) %collective-permute-start.8) | collective-permute-done | bytes 368672 | tf_op jit(solution)/shard_map/ppermute | solution.py:14
  23.8 3.9 %shard_map.77 = (bf16[64,2880]{1,0:T(8,128)(2,1)S(1)}, bf16[64,2880]{1,0:T(8,128)(2,1)S(1)}, bf16[64,2880]{1,0:T(8,128)(2,1)S(1)}, bf16[64,2880]{1,0:T(8,128)(2,1)S(1)}, f32[16,4]{1,0:T(8,128)S(1)}) custom-call(bf16[64,2880]{1,0:T(8,128)(2,1)S(1)} %collective-permute-done.8.refs_0_, bf16[64,2880]{1,0:T(8,128)(2,1)S(1)} %shard_map.76.refs_1_, ...), custom_call_target="tpu_custom_call" | custom-call | flops 3185049600 | bytes 12441600 | tf_op jit(solution)/shard_map/pallas_call | solution.py:145
  27.7 0.2 collective-permute-start.10
  27.9 0.9 %collective-permute-start.9 = (f32[16,4]{1,0:T(8,128)S(1)}, f32[16,4]{1,0:T(8,128)S(1)}, u32[]{:S(2)}, u32[]{:S(2)}) collective-permute-start(f32[16,4]{1,0:T(8,128)S(1)} %get-tuple-element.22), channel_id=1, source_target_pairs={{0,8},{1,9},{2,10},{3,11},{4,12},{5,13},{6,14},{7,15},{8,0},{9,1},... | collective-permute-start | bytes 776 | tf_op jit(solution)/shard_map/ppermute | solution.py:243
  28.8 0.1 collective-permute-start.15
  28.9 0.6 %collective-permute-done.10 = bf16[64,2880]{1,0:T(8,128)(2,1)S(1)} collective-permute-done((bf16[64,2880]{1,0:T(8,128)(2,1)S(1)}, bf16[64,2880]{1,0:T(8,128)(2,1)S(1)}, u32[]{:S(2)}, u32[]{:S(2)}) %collective-permute-start.10) | collective-permute-done | bytes 368672 | tf_op jit(solution)/shard_map/ppermute | solution.py:14
  29.5 0.1 add_convert_fusion.1
  29.6 1.4 %collective-permute-start.13 = (bf16[16,2880]{1,0:T(8,128)(2,1)S(1)}, bf16[16,2880]{1,0:T(8,128)(2,1)S(1)}, u32[]{:S(2)}, u32[]{:S(2)}) collective-permute-start(bf16[16,2880]{1,0:T(8,128)(2,1)S(1)} %get-tuple-element.31), channel_id=1, source_target_pairs={{0,6},{1,7},{2,4},{3,5},{4,2},{5,3},{6,0},{7,1},{8,14},{9,15},{10,... | collective-permute-start | bytes 276488 | tf_op jit(solution)/shard_map/ppermute | solution.py:243
  31.0 1.1 %collective-permute-start.12 = (bf16[16,2880]{1,0:T(8,128)(2,1)S(1)}, bf16[16,2880]{1,0:T(8,128)(2,1)S(1)}, u32[]{:S(2)}, u32[]{:S(2)}) collective-permute-start(bf16[16,2880]{1,0:T(8,128)(2,1)S(1)} %get-tuple-element.32), channel_id=1, source_target_pairs={{0,4},{1,5},{2,6},{3,7},{4,0},{5,1},{6,2},{7,3},{8,12},{9,13},{10,... | collective-permute-start | bytes 276488 | tf_op jit(solution)/shard_map/ppermute | solution.py:243
  32.1 1.0 %collective-permute-start.11 = (bf16[16,2880]{1,0:T(8,128)(2,1)S(1)}, bf16[16,2880]{1,0:T(8,128)(2,1)S(1)}, u32[]{:S(2)}, u32[]{:S(2)}) collective-permute-start(bf16[16,2880]{1,0:T(8,128)(2,1)S(1)} %get-tuple-element.33), channel_id=1, source_target_pairs={{0,2},{1,3},{2,0},{3,1},{4,6},{5,7},{6,4},{7,5},{8,10},{9,11},{10,... | collective-permute-start | bytes 276488 | tf_op jit(solution)/shard_map/ppermute | solution.py:243
  33.1 0.0 collective-permute-done.15
  33.1 0.1 add_convert_fusion
  33.3 1.1 %collective-permute-start.16 = (bf16[16,2880]{1,0:T(8,128)(2,1)S(1)}, bf16[16,2880]{1,0:T(8,128)(2,1)S(1)}, u32[]{:S(2)}, u32[]{:S(2)}) collective-permute-start(bf16[16,2880]{1,0:T(8,128)(2,1)S(1)} %get-tuple-element.35), channel_id=1, source_target_pairs={{0,2},{1,3},{2,0},{3,1},{4,6},{5,7},{6,4},{7,5},{8,10},{9,11},{10,... | collective-permute-start | bytes 276488 | tf_op jit(solution)/shard_map/ppermute | solution.py:243
  34.4 0.0 collective-permute-done.9.table_ref
  34.4 1.6 %collective-permute-start.18 = (bf16[16,2880]{1,0:T(8,128)(2,1)S(1)}, bf16[16,2880]{1,0:T(8,128)(2,1)S(1)}, u32[]{:S(2)}, u32[]{:S(2)}) collective-permute-start(bf16[16,2880]{1,0:T(8,128)(2,1)S(1)} %get-tuple-element.36), channel_id=1, source_target_pairs={{0,6},{1,7},{2,4},{3,5},{4,2},{5,3},{6,0},{7,1},{8,14},{9,15},{10,... | collective-permute-start | bytes 276488 | tf_op jit(solution)/shard_map/ppermute | solution.py:243
  35.9 0.2 collective-permute-done.13.refs_3_
  36.1 1.1 %collective-permute-start.17 = (bf16[16,2880]{1,0:T(8,128)(2,1)S(1)}, bf16[16,2880]{1,0:T(8,128)(2,1)S(1)}, u32[]{:S(2)}, u32[]{:S(2)}) collective-permute-start(bf16[16,2880]{1,0:T(8,128)(2,1)S(1)} %get-tuple-element.37), channel_id=1, source_target_pairs={{0,4},{1,5},{2,6},{3,7},{4,0},{5,1},{6,2},{7,3},{8,12},{9,13},{10,... | collective-permute-start | bytes 276488 | tf_op jit(solution)/shard_map/ppermute | solution.py:243
  37.2 0.1 collective-permute-done.12.refs_2_
  37.3 1.8 %collective-permute-done.11.refs_1_ = bf16[16,2880]{1,0:T(8,128)(2,1)S(1)} collective-permute-done((bf16[16,2880]{1,0:T(8,128)(2,1)S(1)}, bf16[16,2880]{1,0:T(8,128)(2,1)S(1)}, u32[]{:S(2)}, u32[]{:S(2)}) %collective-permute-start.11) | collective-permute-done | bytes 92192 | tf_op jit(solution)/shard_map/ppermute | solution.py:243
  39.1 0.1 shard_map.78
  39.2 1.4 %collective-permute-start.14 = (bf16[16,2880]{1,0:T(8,128)(2,1)S(1)}, bf16[16,2880]{1,0:T(8,128)(2,1)S(1)}, u32[]{:S(2)}, u32[]{:S(2)}) collective-permute-start(bf16[16,2880]{1,0:T(8,128)(2,1)S(1)} %shard_map.78), channel_id=1, source_target_pairs={{0,8},{1,9},{2,10},{3,11},{4,12},{5,13},{6,14},{7,15},{8,0},{9,1},... | collective-permute-start | bytes 276488 | tf_op jit(solution)/shard_map/ppermute | solution.py:243
  40.6 0.2 slice_reduce_fusion.3
  40.8 0.6 %collective-permute-done.16 = bf16[16,2880]{1,0:T(8,128)(2,1)S(1)} collective-permute-done((bf16[16,2880]{1,0:T(8,128)(2,1)S(1)}, bf16[16,2880]{1,0:T(8,128)(2,1)S(1)}, u32[]{:S(2)}, u32[]{:S(2)}) %collective-permute-start.16) | collective-permute-done | bytes 92192 | tf_op jit(solution)/shard_map/ppermute | solution.py:243
  41.4 0.0 collective-permute-done.18
  41.4 0.6 %collective-permute-done.17 = bf16[16,2880]{1,0:T(8,128)(2,1)S(1)} collective-permute-done((bf16[16,2880]{1,0:T(8,128)(2,1)S(1)}, bf16[16,2880]{1,0:T(8,128)(2,1)S(1)}, u32[]{:S(2)}, u32[]{:S(2)}) %collective-permute-start.17) | collective-permute-done | bytes 92192 | tf_op jit(solution)/shard_map/ppermute | solution.py:243
  41.9 3.8 %collective-permute-done.14 = bf16[16,2880]{1,0:T(8,128)(2,1)S(1)} collective-permute-done((bf16[16,2880]{1,0:T(8,128)(2,1)S(1)}, bf16[16,2880]{1,0:T(8,128)(2,1)S(1)}, u32[]{:S(2)}, u32[]{:S(2)}) %collective-permute-start.14) | collective-permute-done | bytes 92192 | tf_op jit(solution)/shard_map/ppermute | solution.py:243
  45.8 0.8 %add_convert_fusion.2 = bf16[16,2880]{1,0:T(8,128)(2,1)} fusion(bf16[16,2880]{1,0:T(8,128)(2,1)S(1)} %collective-permute-done.18, bf16[16,2880]{1,0:T(8,128)(2,1)S(1)} %collective-permute-done.17, bf16[16,2880]{1,0:T(8,128)(2,1)S(1)} %collective-permute-done.16, bf16[16,2880]{1,0:T(8,128)(2,1)S(1)} %collective-permute-done.14, ...), kind=kLoop, calls=%fused_computation.2 | loop fusion | flops 737280 | bytes 645376 | tf_op jit(solution)/shard_map/convert_element_type | solution.py:271
  (6 shorter events, 0.1 us)
Async XLA Ops:
  0.0 12.8 %copy-start = (bf16[16,2880]{1,0:T(8,128)(2,1)S(1)}, bf16[16,2880]{1,0:T(8,128)(2,1)}, u32[]{:S(2)}) copy-start(bf16[16,2880]{1,0:T(8,128)(2,1)} %refs_2_.1) | copy-start | bytes 276484
  0.0 12.8 %copy-start.1 = (f32[2880]{0:T(1024)S(1)}, f32[2880]{0:T(1024)}, u32[]{:S(2)}) copy-start(f32[2880]{0:T(1024)} %refs_5_.1) | copy-start | bytes 34564
  0.0 9.8 %collective-permute-start.2 = (bf16[16,2880]{1,0:T(8,128)(2,1)}, bf16[16,2880]{1,0:T(8,128)(2,1)S(1)}, u32[]{:S(2)}, u32[]{:S(2)}) collective-permute-start(bf16[16,2880]{1,0:T(8,128)(2,1)} %refs_2_.1), channel_id=1, source_target_pairs={{0,4},{1,5},{2,6},{3,7},{4,0},{5,1},{6,2},{7,3},{8,12},{9,13},{10,... | collective-permute-start | bytes 276488 | tf_op jit(solution)/shard_map/ppermute | solution.py:243
  3.0 6.8 %collective-permute-start.1 = (bf16[16,2880]{1,0:T(8,128)(2,1)}, bf16[16,2880]{1,0:T(8,128)(2,1)S(1)}, u32[]{:S(2)}, u32[]{:S(2)}) collective-permute-start(bf16[16,2880]{1,0:T(8,128)(2,1)} %refs_2_.1), channel_id=1, source_target_pairs={{0,2},{1,3},{2,0},{3,1},{4,6},{5,7},{6,4},{7,5},{8,10},{9,11},{10,... | collective-permute-start | bytes 276488 | tf_op jit(solution)/shard_map/ppermute | solution.py:243
  4.5 7.0 %collective-permute-start = (bf16[16,2880]{1,0:T(8,128)(2,1)}, bf16[16,2880]{1,0:T(8,128)(2,1)S(1)}, u32[]{:S(2)}, u32[]{:S(2)}) collective-permute-start(bf16[16,2880]{1,0:T(8,128)(2,1)} %refs_2_.1), channel_id=1, source_target_pairs={{0,8},{1,9},{2,10},{3,11},{4,12},{5,13},{6,14},{7,15},{8,0},{9,1},... | collective-permute-start | bytes 276488 | tf_op jit(solution)/shard_map/ppermute | solution.py:243
  7.1 5.7 %collective-permute-start.3 = (bf16[16,2880]{1,0:T(8,128)(2,1)}, bf16[16,2880]{1,0:T(8,128)(2,1)S(1)}, u32[]{:S(2)}, u32[]{:S(2)}) collective-permute-start(bf16[16,2880]{1,0:T(8,128)(2,1)} %refs_2_.1), channel_id=1, source_target_pairs={{0,6},{1,7},{2,4},{3,5},{4,2},{5,3},{6,0},{7,1},{8,14},{9,15},{10,... | collective-permute-start | bytes 276488 | tf_op jit(solution)/shard_map/ppermute | solution.py:243
  13.0 3.6 %collective-permute-start.4 = (bf16[64,2880]{1,0:T(8,128)(2,1)S(1)}, bf16[64,2880]{1,0:T(8,128)(2,1)S(1)}, u32[]{:S(2)}, u32[]{:S(2)}) collective-permute-start(bf16[64,2880]{1,0:T(8,128)(2,1)S(1)} %shard_map.74.refs_3_), channel_id=1, source_target_pairs={{0,1},{1,0},{2,3},{3,2},{4,5},{5,4},{6,7},{7,6},{8,9},{9,8},{10,11... | collective-permute-start | bytes 1105928 | tf_op jit(solution)/shard_map/ppermute | solution.py:14
  13.1 7.6 %collective-permute-start.7 = (bf16[16,2880]{1,0:T(8,128)(2,1)S(1)}, bf16[16,2880]{1,0:T(8,128)(2,1)S(1)}, u32[]{:S(2)}, u32[]{:S(2)}) collective-permute-start(bf16[16,2880]{1,0:T(8,128)(2,1)S(1)} %collective-permute-done.refs_1_), channel_id=1, source_target_pairs={{0,6},{1,7},{2,4},{3,5},{4,2},{5,3},{6,0},{7,1},{8,14},{9,15},{10,... | collective-permute-start | bytes 276488 | tf_op jit(solution)/shard_map/ppermute | solution.py:243
  14.5 6.2 %collective-permute-start.6 = (bf16[16,2880]{1,0:T(8,128)(2,1)S(1)}, bf16[16,2880]{1,0:T(8,128)(2,1)S(1)}, u32[]{:S(2)}, u32[]{:S(2)}) collective-permute-start(bf16[16,2880]{1,0:T(8,128)(2,1)S(1)} %collective-permute-done.refs_1_), channel_id=1, source_target_pairs={{0,4},{1,5},{2,6},{3,7},{4,0},{5,1},{6,2},{7,3},{8,12},{9,13},{10,... | collective-permute-start | bytes 276488 | tf_op jit(solution)/shard_map/ppermute | solution.py:243
  15.6 5.5 %collective-permute-start.5 = (bf16[16,2880]{1,0:T(8,128)(2,1)S(1)}, bf16[16,2880]{1,0:T(8,128)(2,1)S(1)}, u32[]{:S(2)}, u32[]{:S(2)}) collective-permute-start(bf16[16,2880]{1,0:T(8,128)(2,1)S(1)} %collective-permute-done.refs_1_), channel_id=1, source_target_pairs={{0,2},{1,3},{2,0},{3,1},{4,6},{5,7},{6,4},{7,5},{8,10},{9,11},{10,... | collective-permute-start | bytes 276488 | tf_op jit(solution)/shard_map/ppermute | solution.py:243
  22.0 1.8 %collective-permute-start.8 = (bf16[64,2880]{1,0:T(8,128)(2,1)S(1)}, bf16[64,2880]{1,0:T(8,128)(2,1)S(1)}, u32[]{:S(2)}, u32[]{:S(2)}) collective-permute-start(bf16[64,2880]{1,0:T(8,128)(2,1)S(1)} %shard_map.76.refs_1_), channel_id=1, source_target_pairs={{0,1},{1,0},{2,3},{3,2},{4,5},{5,4},{6,7},{7,6},{8,9},{9,8},{10,11... | collective-permute-start | bytes 1105928 | tf_op jit(solution)/shard_map/ppermute | solution.py:14
  27.7 1.8 %collective-permute-start.10 = (bf16[64,2880]{1,0:T(8,128)(2,1)S(1)}, bf16[64,2880]{1,0:T(8,128)(2,1)S(1)}, u32[]{:S(2)}, u32[]{:S(2)}) collective-permute-start(bf16[64,2880]{1,0:T(8,128)(2,1)S(1)} %get-tuple-element.24), channel_id=1, source_target_pairs={{0,1},{1,0},{2,3},{3,2},{4,5},{5,4},{6,7},{7,6},{8,9},{9,8},{10,11... | collective-permute-start | bytes 1105928 | tf_op jit(solution)/shard_map/ppermute | solution.py:14
  27.9 6.5 %collective-permute-start.9 = (f32[16,4]{1,0:T(8,128)S(1)}, f32[16,4]{1,0:T(8,128)S(1)}, u32[]{:S(2)}, u32[]{:S(2)}) collective-permute-start(f32[16,4]{1,0:T(8,128)S(1)} %get-tuple-element.22), channel_id=1, source_target_pairs={{0,8},{1,9},{2,10},{3,11},{4,12},{5,13},{6,14},{7,15},{8,0},{9,1},... | collective-permute-start | bytes 776 | tf_op jit(solution)/shard_map/ppermute | solution.py:243
  28.8 4.4 %collective-permute-start.15 = (bf16[64,2880]{1,0:T(8,128)(2,1)S(1)}, bf16[64,2880]{1,0:T(8,128)(2,1)S(1)}, u32[]{:S(2)}, u32[]{:S(2)}) collective-permute-start(bf16[64,2880]{1,0:T(8,128)(2,1)S(1)} %get-tuple-element.26), channel_id=1, source_target_pairs={{0,1},{1,0},{2,3},{3,2},{4,5},{5,4},{6,7},{7,6},{8,9},{9,8},{10,11... | collective-permute-start | bytes 1105928 | tf_op jit(solution)/shard_map/ppermute | solution.py:14
  29.6 6.5 %collective-permute-start.13 = (bf16[16,2880]{1,0:T(8,128)(2,1)S(1)}, bf16[16,2880]{1,0:T(8,128)(2,1)S(1)}, u32[]{:S(2)}, u32[]{:S(2)}) collective-permute-start(bf16[16,2880]{1,0:T(8,128)(2,1)S(1)} %get-tuple-element.31), channel_id=1, source_target_pairs={{0,6},{1,7},{2,4},{3,5},{4,2},{5,3},{6,0},{7,1},{8,14},{9,15},{10,... | collective-permute-start | bytes 276488 | tf_op jit(solution)/shard_map/ppermute | solution.py:243
  31.0 6.3 %collective-permute-start.12 = (bf16[16,2880]{1,0:T(8,128)(2,1)S(1)}, bf16[16,2880]{1,0:T(8,128)(2,1)S(1)}, u32[]{:S(2)}, u32[]{:S(2)}) collective-permute-start(bf16[16,2880]{1,0:T(8,128)(2,1)S(1)} %get-tuple-element.32), channel_id=1, source_target_pairs={{0,4},{1,5},{2,6},{3,7},{4,0},{5,1},{6,2},{7,3},{8,12},{9,13},{10,... | collective-permute-start | bytes 276488 | tf_op jit(solution)/shard_map/ppermute | solution.py:243
  32.1 6.9 %collective-permute-start.11 = (bf16[16,2880]{1,0:T(8,128)(2,1)S(1)}, bf16[16,2880]{1,0:T(8,128)(2,1)S(1)}, u32[]{:S(2)}, u32[]{:S(2)}) collective-permute-start(bf16[16,2880]{1,0:T(8,128)(2,1)S(1)} %get-tuple-element.33), channel_id=1, source_target_pairs={{0,2},{1,3},{2,0},{3,1},{4,6},{5,7},{6,4},{7,5},{8,10},{9,11},{10,... | collective-permute-start | bytes 276488 | tf_op jit(solution)/shard_map/ppermute | solution.py:243
  33.3 8.1 %collective-permute-start.16 = (bf16[16,2880]{1,0:T(8,128)(2,1)S(1)}, bf16[16,2880]{1,0:T(8,128)(2,1)S(1)}, u32[]{:S(2)}, u32[]{:S(2)}) collective-permute-start(bf16[16,2880]{1,0:T(8,128)(2,1)S(1)} %get-tuple-element.35), channel_id=1, source_target_pairs={{0,2},{1,3},{2,0},{3,1},{4,6},{5,7},{6,4},{7,5},{8,10},{9,11},{10,... | collective-permute-start | bytes 276488 | tf_op jit(solution)/shard_map/ppermute | solution.py:243
  34.4 7.0 %collective-permute-start.18 = (bf16[16,2880]{1,0:T(8,128)(2,1)S(1)}, bf16[16,2880]{1,0:T(8,128)(2,1)S(1)}, u32[]{:S(2)}, u32[]{:S(2)}) collective-permute-start(bf16[16,2880]{1,0:T(8,128)(2,1)S(1)} %get-tuple-element.36), channel_id=1, source_target_pairs={{0,6},{1,7},{2,4},{3,5},{4,2},{5,3},{6,0},{7,1},{8,14},{9,15},{10,... | collective-permute-start | bytes 276488 | tf_op jit(solution)/shard_map/ppermute | solution.py:243
  36.1 5.8 %collective-permute-start.17 = (bf16[16,2880]{1,0:T(8,128)(2,1)S(1)}, bf16[16,2880]{1,0:T(8,128)(2,1)S(1)}, u32[]{:S(2)}, u32[]{:S(2)}) collective-permute-start(bf16[16,2880]{1,0:T(8,128)(2,1)S(1)} %get-tuple-element.37), channel_id=1, source_target_pairs={{0,4},{1,5},{2,6},{3,7},{4,0},{5,1},{6,2},{7,3},{8,12},{9,13},{10,... | collective-permute-start | bytes 276488 | tf_op jit(solution)/shard_map/ppermute | solution.py:243
  39.2 6.5 %collective-permute-start.14 = (bf16[16,2880]{1,0:T(8,128)(2,1)S(1)}, bf16[16,2880]{1,0:T(8,128)(2,1)S(1)}, u32[]{:S(2)}, u32[]{:S(2)}) collective-permute-start(bf16[16,2880]{1,0:T(8,128)(2,1)S(1)} %shard_map.78), channel_id=1, source_target_pairs={{0,8},{1,9},{2,10},{3,11},{4,12},{5,13},{6,14},{7,15},{8,0},{9,1},... | collective-permute-start | bytes 276488 | tf_op jit(solution)/shard_map/ppermute | solution.py:243

commit v7 on v6

--- a/solution.py
+++ b/solution.py
@@ -78,25 +78,27 @@
     return (residual.astype(jnp.float32) + combined).astype(jnp.bfloat16)
 
 
-def pack_kernel(after, *refs):
-    refs = refs[after:]
-    blocks, gain_ref, out_ref = refs[:-2], refs[-2], refs[-1]
+def pack_kernel(after, sizes, *refs):
+    blocks, gain_ref, outs = refs[after : -1 - len(sizes)], refs[-1 - len(sizes)], refs[-len(sizes) :]
     rows, model = blocks[0].shape
     gain = gain_ref[...].reshape(1, model)
-    for i, block in enumerate(blocks):
+    places = [(out, i) for out, size in zip(outs, sizes) for i in range(size)]
+    for block, (out_ref, i) in zip(blocks, places):
         x = block[...].astype(jnp.float32)
         scale = lax.rsqrt(jnp.mean(x * x, axis=-1, keepdims=True) + 1e-05)
         out_ref[pl.ds(i * rows, rows), :] = (x * scale * gain).astype(jnp.bfloat16)
 
 
-def pack(blocks, gain, after=()):
+def pack(groups, gain, after):
+    blocks = sum(groups, [])
+    sizes = tuple(len(group) for group in groups)
     rows, model = blocks[0].shape
     vmem = pl.BlockSpec(memory_space=pltpu.VMEM)
     return pl.pallas_call(
-        functools.partial(pack_kernel, len(after)),
-        out_shape=jax.ShapeDtypeStruct((rows * len(blocks), model), jnp.bfloat16),
+        functools.partial(pack_kernel, len(after), sizes),
+        out_shape=tuple(jax.ShapeDtypeStruct((rows * size, model), jnp.bfloat16) for size in sizes),
         in_specs=[pl.BlockSpec(memory_space=pl.ANY)] * len(after) + [vmem] * (len(blocks) + 1),
-        out_specs=vmem,
+        out_specs=(vmem,) * len(sizes),
         compiler_params=pltpu.CompilerParams(vmem_limit_bytes=8 * 2**20),
     )(*after, *blocks, gain)
 
@@ -122,52 +124,47 @@
 
 def expert_kernel(count, *refs):
     groups, (gate_ref, up_ref, down_ref, table_ref) = refs[:count], refs[count : count + 4]
-    outs, table_out_ref, rows_ref = refs[count + 4 : -2], refs[-2], refs[-1]
+    outs, table_out_ref = refs[count + 4 : -1], refs[-1]
     table_out_ref[...] = table_ref[...]
-    rows = groups[0].shape[0]
-    for i, group in enumerate(groups):
-        rows_ref[pl.ds(i * rows, rows), :] = group[...]
-    normed = rows_ref[...]
+    normed = jnp.concatenate([group[...] for group in groups])
     across = (((1,), (1,)), ((), ()))
     gate = lax.dot_general(normed, gate_ref[...], across, preferred_element_type=jnp.float32)
     upper = lax.dot_general(normed, up_ref[...], across, preferred_element_type=jnp.float32)
     act = (gate * jax.nn.sigmoid(1.702 * gate) * (upper + 1.0)).astype(jnp.bfloat16)
     out = jnp.dot(act, down_ref[...], preferred_element_type=jnp.float32).astype(jnp.bfloat16)
-    for i, out_ref in enumerate(outs):
-        out_ref[...] = out[i * rows : (i + 1) * rows]
-
-
-def expert_parts(groups, gate_w, up_w, down_w, table):
-    count = len(groups)
-    rows, model = groups[0].shape
-    hidden = gate_w.shape[0]
+    start = 0
+    for out_ref in outs:
+        rows = out_ref.shape[0]
+        out_ref[...] = out[start : start + rows]
+        start += rows
+
+
+def expert_parts(groups, sizes, gate_w, up_w, down_w, table):
+    count, rows = len(groups), sum(sizes)
+    hidden, model = gate_w.shape
     vmem = pl.BlockSpec(memory_space=pltpu.VMEM)
     return pl.pallas_call(
         functools.partial(expert_kernel, count),
-        out_shape=(jax.ShapeDtypeStruct((rows, model), jnp.bfloat16),) * count
+        out_shape=tuple(jax.ShapeDtypeStruct((size, model), jnp.bfloat16) for size in sizes)
         + (jax.ShapeDtypeStruct(table.shape, table.dtype),),
         in_specs=[vmem] * (count + 4),
-        out_specs=(vmem,) * (count + 1),
-        scratch_shapes=[pltpu.VMEM((rows * count, model), jnp.bfloat16)],
+        out_specs=(vmem,) * (len(sizes) + 1),
         cost_estimate=pl.CostEstimate(
-            flops=6 * rows * count * model * hidden,
-            bytes_accessed=6 * model * hidden,
-            transcendentals=rows * count * hidden,
+            flops=6 * rows * model * hidden, bytes_accessed=6 * model * hidden, transcendentals=rows * hidden
         ),
         compiler_params=pltpu.CompilerParams(vmem_limit_bytes=24 * 2**20),
     )(*groups, gate_w, up_w, down_w, table)
 
 
-def read_kernel(count, *refs):
-    sources, targets = refs[1 : count + 1], refs[count + 1 : 2 * count + 1]
-    token_ref, sems = refs[-2], refs[-1]
+def read_kernel(after, *refs):
+    refs, sems = refs[after:-1], refs[-1]
+    sources, targets = refs[: len(refs) // 2], refs[len(refs) // 2 :]
     copies = [
         pltpu.make_async_copy(source, target, sems.at[i])
         for i, (source, target) in enumerate(zip(sources, targets))
     ]
     for copy in copies:
         copy.start()
-    token_ref[0] = 0
     for copy in copies:
         copy.wait()
 
@@ -176,17 +173,16 @@
     count = len(arrays)
     vmem, hbm = pl.BlockSpec(memory_space=pltpu.VMEM), pl.BlockSpec(memory_space=pltpu.HBM)
     return pl.pallas_call(
-        functools.partial(read_kernel, count),
-        out_shape=tuple(pltpu.VMEM(a.shape, a.dtype) for a in arrays)
-        + (jax.ShapeDtypeStruct((1,), jnp.int32),),
-        in_specs=[pl.BlockSpec(memory_space=pl.ANY)] + [hbm] * count,
-        out_specs=(vmem,) * count + (pl.BlockSpec(memory_space=pltpu.SMEM),),
+        functools.partial(read_kernel, len(after)),
+        out_shape=tuple(pltpu.VMEM(a.shape, a.dtype) for a in arrays),
+        in_specs=[pl.BlockSpec(memory_space=pl.ANY)] * len(after) + [hbm] * count,
+        out_specs=(vmem,) * count,
         scratch_shapes=[pltpu.SemaphoreType.DMA((count,))],
         cost_estimate=pl.CostEstimate(
             flops=0, bytes_accessed=2 * sum(a.size * a.dtype.itemsize for a in arrays), transcendentals=0
         ),
         compiler_params=pltpu.CompilerParams(vmem_limit_bytes=16 * 2**20),
-    )(after, *(pltpu.with_memory_space_constraint(a, pltpu.HBM) for a in arrays))
+    )(*after, *(pltpu.with_memory_space_constraint(a, pltpu.HBM) for a in arrays))
 
 
 def load_kernel(chip_ref, ids_hbm, weights_hbm, source, near_ref, far_ref, target, ids_ref, weights_ref, sems):
@@ -250,13 +246,20 @@
     near = [across(x, mask) for mask in range(1, half)]
     chip = (lax.axis_index("expert") // 2).reshape(1)
     near_weights, far_weights, gate_w = load(chip, expert_ids, expert_weights, half, gate_proj[0].T)
+    (mirrored,) = pack(([mirrored],), norm_gain, (near_weights,))
     far = [across(mirrored, mask) for mask in range(1, half)]
-    near_rows = pack([x] + near, norm_gain, (near_weights, mirrored))
-    near_swapped = swap(near_rows)
-    up_w, down_w, token = read((up_proj[0].T, down_proj[0]), near_swapped)
-    far_rows = pack([mirrored] + far, norm_gain, (token,))
-    groups = (swap(far_rows), far_rows, near_swapped, near_rows)
-    *parts, far_weights = expert_parts(groups, gate_w, up_w, down_w, far_weights)
+    mirror_swapped = swap(mirrored)
+    up_w, down_w = read((up_proj[0].T, down_proj[0]), (mirror_swapped, *near))
+    far_swapped = [swap(block) for block in far]
+    (near_rows,) = pack(([x] + near,), norm_gain, (up_w, *far))
+    *parts, far_weights = expert_parts(
+        (mirror_swapped, *far_swapped, mirrored, *far, swap(near_rows), near_rows),
+        (half * rows,) * 4,
+        gate_w,
+        up_w,
+        down_w,
+        far_weights,
+    )
     mirror_weights = across(far_weights, half)
 
     def give_back(done):

time: 46.7 us -> 42.5 us (0.910)
  waiting for transfers between devices: 12.8 us -> 7.09 us
  starting transfers between devices: 21 us -> 23.7 us
  Pallas kernels: 11.4 us -> 10.2 us
    ppermute x15, waiting for transfers between devices: 10.5 us -> 6 us  [across(): return lax.ppermute(value, 'expert', pairs) if mask else value]
    ppermute x15, starting transfers between devices: 20.6 us -> 22.3 us  [across(): return lax.ppermute(value, 'expert', pairs) if mask else value]
    ppermute x4 -> x7, waiting for transfers between devices: 2.29 us -> 1.09 us  [partner(): return lax.ppermute(value, axis, pairs)]
    pallas_call x4, Pallas kernels: 8.98 us -> 7.79 us  [the longest x1 3.92 us: expert_parts(): pl.pallas_call(functools.partial(expert_kernel, count), out_shape=tuple((...]
    ppermute x4 -> x7, starting transfers between devices: 0.42 us -> 1.45 us  [partner(): return lax.ppermute(value, axis, pairs)]
  transfers between devices with their start and end apart: 19 -> 22, of which waited for: 11 -> 8; matrix products, arithmetic and copies ran while one was open for 1% -> 1% of each run, Pallas kernels for 14% -> 14%
where the time goes in v7:
time: 42.5 us; the launch traced here: 42.4 us
  starting transfers between devices  23.7 us (56%)
  Pallas kernels  10.2 us (24%)
  waiting for transfers between devices  7.09 us (17%)
  other arithmetic  0.98 us (2%)
    ppermute x15, starting transfers between devices, across(): return lax.ppermute(value, 'expert', pairs) if mask else value  22.3 us
    ppermute x15, waiting for transfers between devices, across(): return lax.ppermute(value, 'expert', pairs) if mask else value  6 us
    pallas_call x1, Pallas kernels, expert_parts(): pl.pallas_call(functools.partial(expert_kernel, count), out_shape=tuple((...  3.92 us
    pallas_call x1, Pallas kernels, read(): pl.pallas_call(functools.partial(read_kernel, len(after)), out_shape=tupl...  3.54 us
    pallas_call x1, Pallas kernels, load(): pl.pallas_call(load_kernel, out_shape=(table, table, pltpu.VMEM(array.sha...  2.26 us
    ppermute x7, starting transfers between devices, partner(): return lax.ppermute(value, axis, pairs)  1.45 us
    ppermute x7, waiting for transfers between devices, partner(): return lax.ppermute(value, axis, pairs)  1.09 us
  transfers between devices with their start and end apart: 22, of which 8 were waited for; matrix products, arithmetic and copies ran while one was open for 1% of the time, Pallas kernels for 14%

profile of v7, /device:TPU:0, one launch (start us, length us, event | category | flops | bytes accessed | tf_op | source)
XLA Modules:
  0.0 42.4 jit_solution(37986903170649330)
XLA Ops:
  0.0 4.0 %collective-permute-start = (bf16[16,2880]{1,0:T(8,128)(2,1)}, bf16[16,2880]{1,0:T(8,128)(2,1)S(1)}, u32[]{:S(2)}, u32[]{:S(2)}) collective-permute-start(bf16[16,2880]{1,0:T(8,128)(2,1)} %refs_4_.1), channel_id=1, source_target_pairs={{0,8},{1,9},{2,10},{3,11},{4,12},{5,13},{6,14},{7,15},{8,0},{9,1},... | collective-permute-start | bytes 276488 | tf_op jit(solution)/shard_map/ppermute | solution.py:239
  4.0 1.6 %collective-permute-start.9 = (bf16[16,2880]{1,0:T(8,128)(2,1)}, bf16[16,2880]{1,0:T(8,128)(2,1)S(1)}, u32[]{:S(2)}, u32[]{:S(2)}) collective-permute-start(bf16[16,2880]{1,0:T(8,128)(2,1)} %refs_4_.1), channel_id=1, source_target_pairs={{0,4},{1,5},{2,6},{3,7},{4,0},{5,1},{6,2},{7,3},{8,12},{9,13},{10,... | collective-permute-start | bytes 276488 | tf_op jit(solution)/shard_map/ppermute | solution.py:239
  5.6 1.5 %collective-permute-start.8 = (bf16[16,2880]{1,0:T(8,128)(2,1)}, bf16[16,2880]{1,0:T(8,128)(2,1)S(1)}, u32[]{:S(2)}, u32[]{:S(2)}) collective-permute-start(bf16[16,2880]{1,0:T(8,128)(2,1)} %refs_4_.1), channel_id=1, source_target_pairs={{0,2},{1,3},{2,0},{3,1},{4,6},{5,7},{6,4},{7,5},{8,10},{9,11},{10,... | collective-permute-start | bytes 276488 | tf_op jit(solution)/shard_map/ppermute | solution.py:239
  7.1 0.4 collective-permute-start.10
  7.5 2.3 %shard_map.73 = (f32[16,4]{1,0:T(8,128)S(1)}, f32[16,4]{1,0:T(8,128)S(1)}, bf16[720,2880]{1,0:T(8,128)(2,1)S(1)}) custom-call(s32[1]{0:T(128)} %bitcast.chip_ref, s32[4,16]{1,0:T(4,128)} %bitcast.13, f32[4,16]{1,0:T(4,128)} %bitcast.14, bf16[720,2880]{1,0:T(8,128)(2,1)} %bitcast.12), custom_call_target="tpu_custom_call" | custom-call | bytes 8294400 | tf_op jit(solution)/shard_map/pallas_call | solution.py:212
  9.8 0.0 collective-permute-done.refs_1_
  9.8 0.1 shard_map.74.refs_4_
  9.9 0.1 collective-permute-start.1
  10.0 2.6 %collective-permute-start.6 = (bf16[16,2880]{1,0:T(8,128)(2,1)S(1)}, bf16[16,2880]{1,0:T(8,128)(2,1)S(1)}, u32[]{:S(2)}, u32[]{:S(2)}) collective-permute-start(bf16[16,2880]{1,0:T(8,128)(2,1)S(1)} %shard_map.74.refs_4_), channel_id=1, source_target_pairs={{0,6},{1,7},{2,4},{3,5},{4,2},{5,3},{6,0},{7,1},{8,14},{9,15},{10,... | collective-permute-start | bytes 276488 | tf_op jit(solution)/shard_map/ppermute | solution.py:239
  12.6 0.0 collective-permute-done.9.refs_2_.refs_6_
  12.6 0.5 %collective-permute-start.4 = (bf16[16,2880]{1,0:T(8,128)(2,1)S(1)}, bf16[16,2880]{1,0:T(8,128)(2,1)S(1)}, u32[]{:S(2)}, u32[]{:S(2)}) collective-permute-start(bf16[16,2880]{1,0:T(8,128)(2,1)S(1)} %shard_map.74.refs_4_), channel_id=1, source_target_pairs={{0,4},{1,5},{2,6},{3,7},{4,0},{5,1},{6,2},{7,3},{8,12},{9,13},{10,... | collective-permute-start | bytes 276488 | tf_op jit(solution)/shard_map/ppermute | solution.py:239
  13.1 0.0 collective-permute-done.8.refs_1_.refs_5_
  13.1 0.6 %collective-permute-start.2 = (bf16[16,2880]{1,0:T(8,128)(2,1)S(1)}, bf16[16,2880]{1,0:T(8,128)(2,1)S(1)}, u32[]{:S(2)}, u32[]{:S(2)}) collective-permute-start(bf16[16,2880]{1,0:T(8,128)(2,1)S(1)} %shard_map.74.refs_4_), channel_id=1, source_target_pairs={{0,2},{1,3},{2,0},{3,1},{4,6},{5,7},{6,4},{7,5},{8,10},{9,11},{10,... | collective-permute-start | bytes 276488 | tf_op jit(solution)/shard_map/ppermute | solution.py:239
  13.7 0.0 collective-permute-done.1.refs_0_
  13.7 3.5 %shard_map.75 = (bf16[720,2880]{1,0:T(8,128)(2,1)S(1)}, bf16[720,2880]{1,0:T(8,128)(2,1)S(1)}) custom-call(bf16[16,2880]{1,0:T(8,128)(2,1)S(1)} %collective-permute-done.1.refs_0_, bf16[16,2880]{1,0:T(8,128)(2,1)S(1)} %collective-permute-done.8.refs_1_.refs_5_, bf16[16,2880]{1,0:T(8,128)(2,1)S(1)} %collective-permute-done.9.refs_2_.refs_6_, ...), custom_call_target="tpu_custom_call" | custom-call | bytes 16588800 | tf_op jit(solution)/shard_map/pallas_call | solution.py:175
  17.2 0.9 %collective-permute-done.4.refs_2_.refs_6_ = bf16[16,2880]{1,0:T(8,128)(2,1)S(1)} collective-permute-done((bf16[16,2880]{1,0:T(8,128)(2,1)S(1)}, bf16[16,2880]{1,0:T(8,128)(2,1)S(1)}, u32[]{:S(2)}, u32[]{:S(2)}) %collective-permute-start.4) | collective-permute-done | bytes 92192 | tf_op jit(solution)/shard_map/ppermute | solution.py:239
  18.1 0.2 shard_map.76.refs_9_
  18.3 0.1 collective-permute-start.11
  18.4 0.5 %collective-permute-start.7 = (bf16[16,2880]{1,0:T(8,128)(2,1)S(1)}, bf16[16,2880]{1,0:T(8,128)(2,1)S(1)}, u32[]{:S(2)}, u32[]{:S(2)}) collective-permute-start(bf16[16,2880]{1,0:T(8,128)(2,1)S(1)} %collective-permute-done.6.refs_3_.refs_7_), channel_id=1, source_target_pairs={{0,1},{1,0},{2,3},{3,2},{4,5},{5,4},{6,7},{7,6},{8,9},{9,8},{10,11... | collective-permute-start | bytes 276488 | tf_op jit(solution)/shard_map/ppermute | solution.py:14
  18.9 0.1 collective-permute-start.5
  19.0 0.4 %collective-permute-start.3 = (bf16[16,2880]{1,0:T(8,128)(2,1)S(1)}, bf16[16,2880]{1,0:T(8,128)(2,1)S(1)}, u32[]{:S(2)}, u32[]{:S(2)}) collective-permute-start(bf16[16,2880]{1,0:T(8,128)(2,1)S(1)} %collective-permute-done.2.refs_1_.refs_5_), channel_id=1, source_target_pairs={{0,1},{1,0},{2,3},{3,2},{4,5},{5,4},{6,7},{7,6},{8,9},{9,8},{10,11... | collective-permute-start | bytes 276488 | tf_op jit(solution)/shard_map/ppermute | solution.py:14
  19.4 0.8 %collective-permute-done.7.refs_3_ = bf16[16,2880]{1,0:T(8,128)(2,1)S(1)} collective-permute-done((bf16[16,2880]{1,0:T(8,128)(2,1)S(1)}, bf16[16,2880]{1,0:T(8,128)(2,1)S(1)}, u32[]{:S(2)}, u32[]{:S(2)}) %collective-permute-start.7) | collective-permute-done | bytes 92192 | tf_op jit(solution)/shard_map/ppermute | solution.py:14
  20.2 0.1 collective-permute-done.5.refs_2_
  20.4 0.1 collective-permute-done.3.refs_1_
  20.5 0.0 collective-permute-done.11.refs_8_
  20.5 3.9 %shard_map.77 = (bf16[64,2880]{1,0:T(8,128)(2,1)S(1)}, bf16[64,2880]{1,0:T(8,128)(2,1)S(1)}, bf16[64,2880]{1,0:T(8,128)(2,1)S(1)}, bf16[64,2880]{1,0:T(8,128)(2,1)S(1)}, f32[16,4]{1,0:T(8,128)S(1)}) custom-call(bf16[16,2880]{1,0:T(8,128)(2,1)S(1)} %collective-permute-done.1.refs_0_, bf16[16,2880]{1,0:T(8,128)(2,1)S(1)} %collective-permute-done.3.refs_1_, ...), custom_call_target="tpu_custom_call" | custom-call | flops 3185049600 | bytes 12441600 | tf_op jit(solution)/shard_map/pallas_call | solution.py:146
  24.4 0.3 collective-permute-start.13
  24.7 1.5 %collective-permute-start.12 = (f32[16,4]{1,0:T(8,128)S(1)}, f32[16,4]{1,0:T(8,128)S(1)}, u32[]{:S(2)}, u32[]{:S(2)}) collective-permute-start(f32[16,4]{1,0:T(8,128)S(1)} %get-tuple-element.20), channel_id=1, source_target_pairs={{0,8},{1,9},{2,10},{3,11},{4,12},{5,13},{6,14},{7,15},{8,0},{9,1},... | collective-permute-start | bytes 776 | tf_op jit(solution)/shard_map/ppermute | solution.py:239
  26.2 0.0 collective-permute-start.18
  26.2 0.0 collective-permute-done.13
  26.2 0.1 add_convert_fusion.1
  26.4 2.7 %collective-permute-start.16 = (bf16[16,2880]{1,0:T(8,128)(2,1)S(1)}, bf16[16,2880]{1,0:T(8,128)(2,1)S(1)}, u32[]{:S(2)}, u32[]{:S(2)}) collective-permute-start(bf16[16,2880]{1,0:T(8,128)(2,1)S(1)} %get-tuple-element.29), channel_id=1, source_target_pairs={{0,6},{1,7},{2,4},{3,5},{4,2},{5,3},{6,0},{7,1},{8,14},{9,15},{10,... | collective-permute-start | bytes 276488 | tf_op jit(solution)/shard_map/ppermute | solution.py:239
  29.1 0.2 collective-permute-start.15
  29.3 0.6 %collective-permute-start.14 = (bf16[16,2880]{1,0:T(8,128)(2,1)S(1)}, bf16[16,2880]{1,0:T(8,128)(2,1)S(1)}, u32[]{:S(2)}, u32[]{:S(2)}) collective-permute-start(bf16[16,2880]{1,0:T(8,128)(2,1)S(1)} %get-tuple-element.31), channel_id=1, source_target_pairs={{0,2},{1,3},{2,0},{3,1},{4,6},{5,7},{6,4},{7,5},{8,10},{9,11},{10,... | collective-permute-start | bytes 276488 | tf_op jit(solution)/shard_map/ppermute | solution.py:239
  29.9 0.0 collective-permute-done.18
  29.9 0.1 add_convert_fusion
  30.1 1.5 %collective-permute-start.19 = (bf16[16,2880]{1,0:T(8,128)(2,1)S(1)}, bf16[16,2880]{1,0:T(8,128)(2,1)S(1)}, u32[]{:S(2)}, u32[]{:S(2)}) collective-permute-start(bf16[16,2880]{1,0:T(8,128)(2,1)S(1)} %get-tuple-element.33), channel_id=1, source_target_pairs={{0,2},{1,3},{2,0},{3,1},{4,6},{5,7},{6,4},{7,5},{8,10},{9,11},{10,... | collective-permute-start | bytes 276488 | tf_op jit(solution)/shard_map/ppermute | solution.py:239
  31.6 1.8 %collective-permute-start.21 = (bf16[16,2880]{1,0:T(8,128)(2,1)S(1)}, bf16[16,2880]{1,0:T(8,128)(2,1)S(1)}, u32[]{:S(2)}, u32[]{:S(2)}) collective-permute-start(bf16[16,2880]{1,0:T(8,128)(2,1)S(1)} %get-tuple-element.34), channel_id=1, source_target_pairs={{0,6},{1,7},{2,4},{3,5},{4,2},{5,3},{6,0},{7,1},{8,14},{9,15},{10,... | collective-permute-start | bytes 276488 | tf_op jit(solution)/shard_map/ppermute | solution.py:239
  33.4 1.3 %collective-permute-start.20 = (bf16[16,2880]{1,0:T(8,128)(2,1)S(1)}, bf16[16,2880]{1,0:T(8,128)(2,1)S(1)}, u32[]{:S(2)}, u32[]{:S(2)}) collective-permute-start(bf16[16,2880]{1,0:T(8,128)(2,1)S(1)} %get-tuple-element.35), channel_id=1, source_target_pairs={{0,4},{1,5},{2,6},{3,7},{4,0},{5,1},{6,2},{7,3},{8,12},{9,13},{10,... | collective-permute-start | bytes 276488 | tf_op jit(solution)/shard_map/ppermute | solution.py:239
  34.6 0.0 collective-permute-done.15.refs_2_
  34.7 1.3 %collective-permute-done.14.refs_1_ = bf16[16,2880]{1,0:T(8,128)(2,1)S(1)} collective-permute-done((bf16[16,2880]{1,0:T(8,128)(2,1)S(1)}, bf16[16,2880]{1,0:T(8,128)(2,1)S(1)}, u32[]{:S(2)}, u32[]{:S(2)}) %collective-permute-start.14) | collective-permute-done | bytes 92192 | tf_op jit(solution)/shard_map/ppermute | solution.py:239
  35.9 0.1 shard_map.78
  36.1 1.5 %collective-permute-start.17 = (bf16[16,2880]{1,0:T(8,128)(2,1)S(1)}, bf16[16,2880]{1,0:T(8,128)(2,1)S(1)}, u32[]{:S(2)}, u32[]{:S(2)}) collective-permute-start(bf16[16,2880]{1,0:T(8,128)(2,1)S(1)} %shard_map.78), channel_id=1, source_target_pairs={{0,8},{1,9},{2,10},{3,11},{4,12},{5,13},{6,14},{7,15},{8,0},{9,1},... | collective-permute-start | bytes 276488 | tf_op jit(solution)/shard_map/ppermute | solution.py:239
  37.6 0.2 slice_reduce_fusion.3
  37.8 0.7 %collective-permute-done.19 = bf16[16,2880]{1,0:T(8,128)(2,1)S(1)} collective-permute-done((bf16[16,2880]{1,0:T(8,128)(2,1)S(1)}, bf16[16,2880]{1,0:T(8,128)(2,1)S(1)}, u32[]{:S(2)}, u32[]{:S(2)}) %collective-permute-start.19) | collective-permute-done | bytes 92192 | tf_op jit(solution)/shard_map/ppermute | solution.py:239
  38.5 0.7 %collective-permute-done.20 = bf16[16,2880]{1,0:T(8,128)(2,1)S(1)} collective-permute-done((bf16[16,2880]{1,0:T(8,128)(2,1)S(1)}, bf16[16,2880]{1,0:T(8,128)(2,1)S(1)}, u32[]{:S(2)}, u32[]{:S(2)}) %collective-permute-start.20) | collective-permute-done | bytes 92192 | tf_op jit(solution)/shard_map/ppermute | solution.py:239
  39.2 2.4 %collective-permute-done.17 = bf16[16,2880]{1,0:T(8,128)(2,1)S(1)} collective-permute-done((bf16[16,2880]{1,0:T(8,128)(2,1)S(1)}, bf16[16,2880]{1,0:T(8,128)(2,1)S(1)}, u32[]{:S(2)}, u32[]{:S(2)}) %collective-permute-start.17) | collective-permute-done | bytes 92192 | tf_op jit(solution)/shard_map/ppermute | solution.py:239
  41.6 0.8 %add_convert_fusion.2 = bf16[16,2880]{1,0:T(8,128)(2,1)} fusion(bf16[16,2880]{1,0:T(8,128)(2,1)S(1)} %collective-permute-done.21, bf16[16,2880]{1,0:T(8,128)(2,1)S(1)} %collective-permute-done.20, bf16[16,2880]{1,0:T(8,128)(2,1)S(1)} %collective-permute-done.19, bf16[16,2880]{1,0:T(8,128)(2,1)S(1)} %collective-permute-done.17, ...), kind=kLoop, calls=%fused_computation.2 | loop fusion | flops 737280 | bytes 645376 | tf_op jit(solution)/shard_map/convert_element_type | solution.py:274
  (12 shorter events, 0.1 us)
Async XLA Ops:
  0.0 9.8 %copy-start.1 = (f32[2880]{0:T(1024)S(1)}, f32[2880]{0:T(1024)}, u32[]{:S(2)}) copy-start(f32[2880]{0:T(1024)} %refs_8_.1) | copy-start | bytes 34564
  0.0 9.8 %collective-permute-start = (bf16[16,2880]{1,0:T(8,128)(2,1)}, bf16[16,2880]{1,0:T(8,128)(2,1)S(1)}, u32[]{:S(2)}, u32[]{:S(2)}) collective-permute-start(bf16[16,2880]{1,0:T(8,128)(2,1)} %refs_4_.1), channel_id=1, source_target_pairs={{0,8},{1,9},{2,10},{3,11},{4,12},{5,13},{6,14},{7,15},{8,0},{9,1},... | collective-permute-start | bytes 276488 | tf_op jit(solution)/shard_map/ppermute | solution.py:239
  4.0 8.6 %collective-permute-start.9 = (bf16[16,2880]{1,0:T(8,128)(2,1)}, bf16[16,2880]{1,0:T(8,128)(2,1)S(1)}, u32[]{:S(2)}, u32[]{:S(2)}) collective-permute-start(bf16[16,2880]{1,0:T(8,128)(2,1)} %refs_4_.1), channel_id=1, source_target_pairs={{0,4},{1,5},{2,6},{3,7},{4,0},{5,1},{6,2},{7,3},{8,12},{9,13},{10,... | collective-permute-start | bytes 276488 | tf_op jit(solution)/shard_map/ppermute | solution.py:239
  5.6 7.5 %collective-permute-start.8 = (bf16[16,2880]{1,0:T(8,128)(2,1)}, bf16[16,2880]{1,0:T(8,128)(2,1)S(1)}, u32[]{:S(2)}, u32[]{:S(2)}) collective-permute-start(bf16[16,2880]{1,0:T(8,128)(2,1)} %refs_4_.1), channel_id=1, source_target_pairs={{0,2},{1,3},{2,0},{3,1},{4,6},{5,7},{6,4},{7,5},{8,10},{9,11},{10,... | collective-permute-start | bytes 276488 | tf_op jit(solution)/shard_map/ppermute | solution.py:239
  7.1 6.5 %collective-permute-start.10 = (bf16[16,2880]{1,0:T(8,128)(2,1)}, bf16[16,2880]{1,0:T(8,128)(2,1)S(1)}, u32[]{:S(2)}, u32[]{:S(2)}) collective-permute-start(bf16[16,2880]{1,0:T(8,128)(2,1)} %refs_4_.1), channel_id=1, source_target_pairs={{0,6},{1,7},{2,4},{3,5},{4,2},{5,3},{6,0},{7,1},{8,14},{9,15},{10,... | collective-permute-start | bytes 276488 | tf_op jit(solution)/shard_map/ppermute | solution.py:239
  9.9 3.7 %collective-permute-start.1 = (bf16[16,2880]{1,0:T(8,128)(2,1)S(1)}, bf16[16,2880]{1,0:T(8,128)(2,1)S(1)}, u32[]{:S(2)}, u32[]{:S(2)}) collective-permute-start(bf16[16,2880]{1,0:T(8,128)(2,1)S(1)} %shard_map.74.refs_4_), channel_id=1, source_target_pairs={{0,1},{1,0},{2,3},{3,2},{4,5},{5,4},{6,7},{7,6},{8,9},{9,8},{10,11... | collective-permute-start | bytes 276488 | tf_op jit(solution)/shard_map/ppermute | solution.py:14
  10.0 7.2 %collective-permute-start.6 = (bf16[16,2880]{1,0:T(8,128)(2,1)S(1)}, bf16[16,2880]{1,0:T(8,128)(2,1)S(1)}, u32[]{:S(2)}, u32[]{:S(2)}) collective-permute-start(bf16[16,2880]{1,0:T(8,128)(2,1)S(1)} %shard_map.74.refs_4_), channel_id=1, source_target_pairs={{0,6},{1,7},{2,4},{3,5},{4,2},{5,3},{6,0},{7,1},{8,14},{9,15},{10,... | collective-permute-start | bytes 276488 | tf_op jit(solution)/shard_map/ppermute | solution.py:239
  12.6 5.5 %collective-permute-start.4 = (bf16[16,2880]{1,0:T(8,128)(2,1)S(1)}, bf16[16,2880]{1,0:T(8,128)(2,1)S(1)}, u32[]{:S(2)}, u32[]{:S(2)}) collective-permute-start(bf16[16,2880]{1,0:T(8,128)(2,1)S(1)} %shard_map.74.refs_4_), channel_id=1, source_target_pairs={{0,4},{1,5},{2,6},{3,7},{4,0},{5,1},{6,2},{7,3},{8,12},{9,13},{10,... | collective-permute-start | bytes 276488 | tf_op jit(solution)/shard_map/ppermute | solution.py:239
  13.1 5.0 %collective-permute-start.2 = (bf16[16,2880]{1,0:T(8,128)(2,1)S(1)}, bf16[16,2880]{1,0:T(8,128)(2,1)S(1)}, u32[]{:S(2)}, u32[]{:S(2)}) collective-permute-start(bf16[16,2880]{1,0:T(8,128)(2,1)S(1)} %shard_map.74.refs_4_), channel_id=1, source_target_pairs={{0,2},{1,3},{2,0},{3,1},{4,6},{5,7},{6,4},{7,5},{8,10},{9,11},{10,... | collective-permute-start | bytes 276488 | tf_op jit(solution)/shard_map/ppermute | solution.py:239
  13.7 4.5 %copy-start = (bf16[16,2880]{1,0:T(8,128)(2,1)S(1)}, bf16[16,2880]{1,0:T(8,128)(2,1)}, u32[]{:S(2)}) copy-start(bf16[16,2880]{1,0:T(8,128)(2,1)} %refs_4_.1) | copy-start | bytes 276484
  18.3 2.2 %collective-permute-start.11 = (bf16[64,2880]{1,0:T(8,128)(2,1)S(1)}, bf16[64,2880]{1,0:T(8,128)(2,1)S(1)}, u32[]{:S(2)}, u32[]{:S(2)}) collective-permute-start(bf16[64,2880]{1,0:T(8,128)(2,1)S(1)} %shard_map.76.refs_9_), channel_id=1, source_target_pairs={{0,1},{1,0},{2,3},{3,2},{4,5},{5,4},{6,7},{7,6},{8,9},{9,8},{10,11... | collective-permute-start | bytes 1105928 | tf_op jit(solution)/shard_map/ppermute | solution.py:14
  18.4 1.8 %collective-permute-start.7 = (bf16[16,2880]{1,0:T(8,128)(2,1)S(1)}, bf16[16,2880]{1,0:T(8,128)(2,1)S(1)}, u32[]{:S(2)}, u32[]{:S(2)}) collective-permute-start(bf16[16,2880]{1,0:T(8,128)(2,1)S(1)} %collective-permute-done.6.refs_3_.refs_7_), channel_id=1, source_target_pairs={{0,1},{1,0},{2,3},{3,2},{4,5},{5,4},{6,7},{7,6},{8,9},{9,8},{10,11... | collective-permute-start | bytes 276488 | tf_op jit(solution)/shard_map/ppermute | solution.py:14
  18.9 1.5 %collective-permute-start.5 = (bf16[16,2880]{1,0:T(8,128)(2,1)S(1)}, bf16[16,2880]{1,0:T(8,128)(2,1)S(1)}, u32[]{:S(2)}, u32[]{:S(2)}) collective-permute-start(bf16[16,2880]{1,0:T(8,128)(2,1)S(1)} %collective-permute-done.4.refs_2_.refs_6_), channel_id=1, source_target_pairs={{0,1},{1,0},{2,3},{3,2},{4,5},{5,4},{6,7},{7,6},{8,9},{9,8},{10,11... | collective-permute-start | bytes 276488 | tf_op jit(solution)/shard_map/ppermute | solution.py:14
  19.0 1.5 %collective-permute-start.3 = (bf16[16,2880]{1,0:T(8,128)(2,1)S(1)}, bf16[16,2880]{1,0:T(8,128)(2,1)S(1)}, u32[]{:S(2)}, u32[]{:S(2)}) collective-permute-start(bf16[16,2880]{1,0:T(8,128)(2,1)S(1)} %collective-permute-done.2.refs_1_.refs_5_), channel_id=1, source_target_pairs={{0,1},{1,0},{2,3},{3,2},{4,5},{5,4},{6,7},{7,6},{8,9},{9,8},{10,11... | collective-permute-start | bytes 276488 | tf_op jit(solution)/shard_map/ppermute | solution.py:14
  24.4 1.8 %collective-permute-start.13 = (bf16[64,2880]{1,0:T(8,128)(2,1)S(1)}, bf16[64,2880]{1,0:T(8,128)(2,1)S(1)}, u32[]{:S(2)}, u32[]{:S(2)}) collective-permute-start(bf16[64,2880]{1,0:T(8,128)(2,1)S(1)} %get-tuple-element.22), channel_id=1, source_target_pairs={{0,1},{1,0},{2,3},{3,2},{4,5},{5,4},{6,7},{7,6},{8,9},{9,8},{10,11... | collective-permute-start | bytes 1105928 | tf_op jit(solution)/shard_map/ppermute | solution.py:14
  24.7 6.8 %collective-permute-start.12 = (f32[16,4]{1,0:T(8,128)S(1)}, f32[16,4]{1,0:T(8,128)S(1)}, u32[]{:S(2)}, u32[]{:S(2)}) collective-permute-start(f32[16,4]{1,0:T(8,128)S(1)} %get-tuple-element.20), channel_id=1, source_target_pairs={{0,8},{1,9},{2,10},{3,11},{4,12},{5,13},{6,14},{7,15},{8,0},{9,1},... | collective-permute-start | bytes 776 | tf_op jit(solution)/shard_map/ppermute | solution.py:239
  26.2 3.7 %collective-permute-start.18 = (bf16[64,2880]{1,0:T(8,128)(2,1)S(1)}, bf16[64,2880]{1,0:T(8,128)(2,1)S(1)}, u32[]{:S(2)}, u32[]{:S(2)}) collective-permute-start(bf16[64,2880]{1,0:T(8,128)(2,1)S(1)} %get-tuple-element.24), channel_id=1, source_target_pairs={{0,1},{1,0},{2,3},{3,2},{4,5},{5,4},{6,7},{7,6},{8,9},{9,8},{10,11... | collective-permute-start | bytes 1105928 | tf_op jit(solution)/shard_map/ppermute | solution.py:14
  26.4 7.0 %collective-permute-start.16 = (bf16[16,2880]{1,0:T(8,128)(2,1)S(1)}, bf16[16,2880]{1,0:T(8,128)(2,1)S(1)}, u32[]{:S(2)}, u32[]{:S(2)}) collective-permute-start(bf16[16,2880]{1,0:T(8,128)(2,1)S(1)} %get-tuple-element.29), channel_id=1, source_target_pairs={{0,6},{1,7},{2,4},{3,5},{4,2},{5,3},{6,0},{7,1},{8,14},{9,15},{10,... | collective-permute-start | bytes 276488 | tf_op jit(solution)/shard_map/ppermute | solution.py:239
  29.1 5.5 %collective-permute-start.15 = (bf16[16,2880]{1,0:T(8,128)(2,1)S(1)}, bf16[16,2880]{1,0:T(8,128)(2,1)S(1)}, u32[]{:S(2)}, u32[]{:S(2)}) collective-permute-start(bf16[16,2880]{1,0:T(8,128)(2,1)S(1)} %get-tuple-element.30), channel_id=1, source_target_pairs={{0,4},{1,5},{2,6},{3,7},{4,0},{5,1},{6,2},{7,3},{8,12},{9,13},{10,... | collective-permute-start | bytes 276488 | tf_op jit(solution)/shard_map/ppermute | solution.py:239
  29.3 6.6 %collective-permute-start.14 = (bf16[16,2880]{1,0:T(8,128)(2,1)S(1)}, bf16[16,2880]{1,0:T(8,128)(2,1)S(1)}, u32[]{:S(2)}, u32[]{:S(2)}) collective-permute-start(bf16[16,2880]{1,0:T(8,128)(2,1)S(1)} %get-tuple-element.31), channel_id=1, source_target_pairs={{0,2},{1,3},{2,0},{3,1},{4,6},{5,7},{6,4},{7,5},{8,10},{9,11},{10,... | collective-permute-start | bytes 276488 | tf_op jit(solution)/shard_map/ppermute | solution.py:239
  30.1 8.5 %collective-permute-start.19 = (bf16[16,2880]{1,0:T(8,128)(2,1)S(1)}, bf16[16,2880]{1,0:T(8,128)(2,1)S(1)}, u32[]{:S(2)}, u32[]{:S(2)}) collective-permute-start(bf16[16,2880]{1,0:T(8,128)(2,1)S(1)} %get-tuple-element.33), channel_id=1, source_target_pairs={{0,2},{1,3},{2,0},{3,1},{4,6},{5,7},{6,4},{7,5},{8,10},{9,11},{10,... | collective-permute-start | bytes 276488 | tf_op jit(solution)/shard_map/ppermute | solution.py:239
  31.6 7.0 %collective-permute-start.21 = (bf16[16,2880]{1,0:T(8,128)(2,1)S(1)}, bf16[16,2880]{1,0:T(8,128)(2,1)S(1)}, u32[]{:S(2)}, u32[]{:S(2)}) collective-permute-start(bf16[16,2880]{1,0:T(8,128)(2,1)S(1)} %get-tuple-element.34), channel_id=1, source_target_pairs={{0,6},{1,7},{2,4},{3,5},{4,2},{5,3},{6,0},{7,1},{8,14},{9,15},{10,... | collective-permute-start | bytes 276488 | tf_op jit(solution)/shard_map/ppermute | solution.py:239
  33.4 5.8 %collective-permute-start.20 = (bf16[16,2880]{1,0:T(8,128)(2,1)S(1)}, bf16[16,2880]{1,0:T(8,128)(2,1)S(1)}, u32[]{:S(2)}, u32[]{:S(2)}) collective-permute-start(bf16[16,2880]{1,0:T(8,128)(2,1)S(1)} %get-tuple-element.35), channel_id=1, source_target_pairs={{0,4},{1,5},{2,6},{3,7},{4,0},{5,1},{6,2},{7,3},{8,12},{9,13},{10,... | collective-permute-start | bytes 276488 | tf_op jit(solution)/shard_map/ppermute | solution.py:239
  36.1 5.5 %collective-permute-start.17 = (bf16[16,2880]{1,0:T(8,128)(2,1)S(1)}, bf16[16,2880]{1,0:T(8,128)(2,1)S(1)}, u32[]{:S(2)}, u32[]{:S(2)}) collective-permute-start(bf16[16,2880]{1,0:T(8,128)(2,1)S(1)} %shard_map.78), channel_id=1, source_target_pairs={{0,8},{1,9},{2,10},{3,11},{4,12},{5,13},{6,14},{7,15},{8,0},{9,1},... | collective-permute-start | bytes 276488 | tf_op jit(solution)/shard_map/ppermute | solution.py:239

commit v8 on v7

--- a/solution.py
+++ b/solution.py
@@ -103,6 +103,70 @@
     )(*after, *blocks, gain)
 
 
+def read_kernel(count, after, chip_ref, ids_hbm, weights_hbm, *refs):
+    sources, (near_ref, far_ref, *refs) = refs[:count], refs[count + after :]
+    targets, (ids_ref, weights_ref, sems) = refs[:count], refs[count:]
+    pairs = [(ids_hbm, ids_ref), (weights_hbm, weights_ref), *zip(sources, targets)]
+    copies = [pltpu.make_async_copy(a, b, sems.at[i]) for i, (a, b) in enumerate(pairs)]
+    for copy in copies:
+        copy.start()
+    chosen, rows = ids_ref.shape
+    half = near_ref.shape[1]
+    expert = chip_ref[0] ^ lax.broadcasted_iota(jnp.int32, (2 * half, rows), 0)
+    copies[0].wait()
+    copies[1].wait()
+    table = jnp.zeros((2 * half, rows), jnp.float32)
+    for k in range(chosen):
+        table += jnp.where(ids_ref[k : k + 1, :] == expert, weights_ref[k : k + 1, :], 0.0)
+    near_ref[...] = table[:half].T
+    far_ref[...] = table[half:].T
+    for copy in copies[2:]:
+        copy.wait()
+
+
+def read(chip, expert_ids, expert_weights, half, arrays, after):
+    rows, chosen = expert_ids.shape
+    count = len(arrays)
+    vmem, hbm = pl.BlockSpec(memory_space=pltpu.VMEM), pl.BlockSpec(memory_space=pltpu.HBM)
+    table = jax.ShapeDtypeStruct((rows, half), jnp.float32)
+    in_hbm = [pltpu.with_memory_space_constraint(a, pltpu.HBM) for a in (expert_ids.T, expert_weights.T, *arrays)]
+    return pl.pallas_call(
+        functools.partial(read_kernel, count, len(after)),
+        out_shape=(table, table) + tuple(pltpu.VMEM(a.shape, a.dtype) for a in arrays),
+        in_specs=[pl.BlockSpec(memory_space=pltpu.SMEM)]
+        + [hbm] * len(in_hbm)
+        + [pl.BlockSpec(memory_space=pl.ANY)] * len(after),
+        out_specs=(vmem,) * (2 + count),
+        scratch_shapes=[
+            pltpu.VMEM((chosen, rows), expert_ids.dtype),
+            pltpu.VMEM((chosen, rows), expert_weights.dtype),
+            pltpu.SemaphoreType.DMA((2 + count,)),
+        ],
+        cost_estimate=pl.CostEstimate(
+            flops=0, bytes_accessed=2 * sum(a.size * a.dtype.itemsize for a in arrays), transcendentals=0
+        ),
+        compiler_params=pltpu.CompilerParams(vmem_limit_bytes=16 * 2**20),
+    )(chip, *in_hbm, *after)
+
+
+def sum_kernel(masks, after, mine_ref, theirs_ref, *refs):
+    for mask, out_ref in zip(masks, refs[after:]):
+        rows = pl.ds(mask * out_ref.shape[0], out_ref.shape[0])
+        total = mine_ref[rows, :].astype(jnp.float32) + theirs_ref[rows, :].astype(jnp.float32)
+        out_ref[...] = total.astype(out_ref.dtype)
+
+
+def sums(mine, theirs, rows, masks, after=()):
+    vmem = pl.BlockSpec(memory_space=pltpu.VMEM)
+    return pl.pallas_call(
+        functools.partial(sum_kernel, masks, len(after)),
+        out_shape=(jax.ShapeDtypeStruct((rows, mine.shape[1]), mine.dtype),) * len(masks),
+        in_specs=[vmem] * 2 + [pl.BlockSpec(memory_space=pl.ANY)] * len(after),
+        out_specs=(vmem,) * len(masks),
+        compiler_params=pltpu.CompilerParams(vmem_limit_bytes=8 * 2**20),
+    )(mine, theirs, *after)
+
+
 def mix_kernel(table_ref, *refs):
     blocks, out_ref = refs[:-1], refs[-1]
     total = jnp.zeros(out_ref.shape, jnp.float32)
@@ -156,79 +220,6 @@
     )(*groups, gate_w, up_w, down_w, table)
 
 
-def read_kernel(after, *refs):
-    refs, sems = refs[after:-1], refs[-1]
-    sources, targets = refs[: len(refs) // 2], refs[len(refs) // 2 :]
-    copies = [
-        pltpu.make_async_copy(source, target, sems.at[i])
-        for i, (source, target) in enumerate(zip(sources, targets))
-    ]
-    for copy in copies:
-        copy.start()
-    for copy in copies:
-        copy.wait()
-
-
-def read(arrays, after):
-    count = len(arrays)
-    vmem, hbm = pl.BlockSpec(memory_space=pltpu.VMEM), pl.BlockSpec(memory_space=pltpu.HBM)
-    return pl.pallas_call(
-        functools.partial(read_kernel, len(after)),
-        out_shape=tuple(pltpu.VMEM(a.shape, a.dtype) for a in arrays),
-        in_specs=[pl.BlockSpec(memory_space=pl.ANY)] * len(after) + [hbm] * count,
-        out_specs=(vmem,) * count,
-        scratch_shapes=[pltpu.SemaphoreType.DMA((count,))],
-        cost_estimate=pl.CostEstimate(
-            flops=0, bytes_accessed=2 * sum(a.size * a.dtype.itemsize for a in arrays), transcendentals=0
-        ),
-        compiler_params=pltpu.CompilerParams(vmem_limit_bytes=16 * 2**20),
-    )(*after, *(pltpu.with_memory_space_constraint(a, pltpu.HBM) for a in arrays))
-
-
-def load_kernel(chip_ref, ids_hbm, weights_hbm, source, near_ref, far_ref, target, ids_ref, weights_ref, sems):
-    copies = [
-        pltpu.make_async_copy(a, b, sems.at[i])
-        for i, (a, b) in enumerate(((ids_hbm, ids_ref), (weights_hbm, weights_ref), (source, target)))
-    ]
-    for copy in copies:
-        copy.start()
-    chosen, rows = ids_ref.shape
-    half = near_ref.shape[1]
-    expert = chip_ref[0] ^ lax.broadcasted_iota(jnp.int32, (2 * half, rows), 0)
-    copies[0].wait()
-    copies[1].wait()
-    table = jnp.zeros((2 * half, rows), jnp.float32)
-    for k in range(chosen):
-        table += jnp.where(ids_ref[k : k + 1, :] == expert, weights_ref[k : k + 1, :], 0.0)
-    near_ref[...] = table[:half].T
-    far_ref[...] = table[half:].T
-    copies[2].wait()
-
-
-def load(chip, expert_ids, expert_weights, half, array):
-    rows, chosen = expert_ids.shape
-    vmem, hbm = pl.BlockSpec(memory_space=pltpu.VMEM), pl.BlockSpec(memory_space=pltpu.HBM)
-    table = jax.ShapeDtypeStruct((rows, half), jnp.float32)
-    return pl.pallas_call(
-        load_kernel,
-        out_shape=(table, table, pltpu.VMEM(array.shape, array.dtype)),
-        in_specs=[pl.BlockSpec(memory_space=pltpu.SMEM), hbm, hbm, hbm],
-        out_specs=(vmem,) * 3,
-        scratch_shapes=[
-            pltpu.VMEM((chosen, rows), expert_ids.dtype),
-            pltpu.VMEM((chosen, rows), expert_weights.dtype),
-            pltpu.SemaphoreType.DMA((3,)),
-        ],
-        cost_estimate=pl.CostEstimate(
-            flops=0, bytes_accessed=2 * array.size * array.dtype.itemsize, transcendentals=0
-        ),
-        compiler_params=pltpu.CompilerParams(vmem_limit_bytes=16 * 2**20),
-    )(
-        chip,
-        *(pltpu.with_memory_space_constraint(a, pltpu.HBM) for a in (expert_ids.T, expert_weights.T, array)),
-    )
-
-
 def halves(residual, norm_gain, expert_ids, expert_weights, gate_proj, up_proj, down_proj):
     rows, model = residual.shape
     chips = lax.axis_size("expert") // 2
@@ -244,32 +235,38 @@
     x = residual
     mirrored = across(x, half)
     near = [across(x, mask) for mask in range(1, half)]
-    chip = (lax.axis_index("expert") // 2).reshape(1)
-    near_weights, far_weights, gate_w = load(chip, expert_ids, expert_weights, half, gate_proj[0].T)
-    (mirrored,) = pack(([mirrored],), norm_gain, (near_weights,))
     far = [across(mirrored, mask) for mask in range(1, half)]
     mirror_swapped = swap(mirrored)
-    up_w, down_w = read((up_proj[0].T, down_proj[0]), (mirror_swapped, *near))
-    far_swapped = [swap(block) for block in far]
-    (near_rows,) = pack(([x] + near,), norm_gain, (up_w, *far))
+    near_weights, far_weights, *held = read(
+        (lax.axis_index("expert") // 2).reshape(1),
+        expert_ids,
+        expert_weights,
+        half,
+        (gate_proj[0].T, up_proj[0].T, down_proj[0]),
+        (mirror_swapped, *near),
+    )
+    mine, mirror_theirs, mirror_mine = pack(
+        (far + [x] + near, [mirror_swapped], [mirrored]), norm_gain, tuple(held)
+    )
     *parts, far_weights = expert_parts(
-        (mirror_swapped, *far_swapped, mirrored, *far, swap(near_rows), near_rows),
-        (half * rows,) * 4,
-        gate_w,
-        up_w,
-        down_w,
-        far_weights,
+        (mirror_theirs, swap(mine), mirror_mine, mine), (half * rows,) * 4, *held, far_weights
     )
     mirror_weights = across(far_weights, half)
 
-    def give_back(done):
-        done = done.reshape(half, rows, model)
-        return [across(done[mask], mask) for mask in range(half)]
-
-    far_blocks = give_back(pair_sum(parts[1], swap(parts[0])))
-    near_blocks = give_back(pair_sum(parts[3], swap(parts[2])))
-    total = x.astype(jnp.float32) + across(mixed(mirror_weights, far_blocks), half).astype(jnp.float32)
-    for mask, block in enumerate(near_blocks):
+    def give_back(mine, theirs, masks, after=()):
+        done = sums(mine, theirs, rows, masks, after)
+        return {mask: across(block, mask) for mask, block in zip(masks, done)}
+
+    far_theirs, near_theirs, far_mine, near_mine = parts
+    near_swapped = swap(near_theirs)
+    far_blocks = give_back(far_mine, swap(far_theirs), tuple(range(half)))
+    other = mixed(mirror_weights, [far_blocks[mask] for mask in range(half)])
+    short = tuple(mask for mask in range(1, half) if mask & (mask - 1) == 0)
+    long = tuple(mask for mask in range(half) if mask not in short)
+    near_blocks = give_back(near_mine, near_swapped, long)
+    near_blocks |= give_back(near_mine, near_swapped, short, (other,))
+    total = x.astype(jnp.float32) + across(other, half).astype(jnp.float32)
+    for mask, block in near_blocks.items():
         total += near_weights[:, mask][:, None] * block.astype(jnp.float32)
     return total.astype(jnp.bfloat16)
 

time: 42.5 us -> 44.3 us (1.042)
  starting transfers between devices: 23.7 us -> 25.8 us
  Pallas kernels: 10.2 us -> 9.43 us
  waiting for transfers between devices: 7.09 us -> 7.84 us
    ppermute x15, starting transfers between devices: 22.3 us -> 25.1 us  [across(): return lax.ppermute(value, 'expert', pairs) if mask else value]
    ppermute x7 -> x4, waiting for transfers between devices: 1.09 us -> 3.28 us  [partner(): return lax.ppermute(value, axis, pairs)]
    ppermute x15, waiting for transfers between devices: 6 us -> 4.56 us  [across(): return lax.ppermute(value, 'expert', pairs) if mask else value]
    pallas_call x2 -> x4, Pallas kernels: 5.8 us -> 4.99 us  [the longest x1 4.79 us: read(): pl.pallas_call(functools.partial(read_kernel, count, len(after)), out_sha...]
    ppermute x7 -> x4, starting transfers between devices: 1.45 us -> 0.65 us  [partner(): return lax.ppermute(value, axis, pairs)]
  transfers between devices with their start and end apart: 22 -> 19, of which waited for: 8 -> 8; matrix products, arithmetic and copies ran while one was open for 1% -> 0% of each run, Pallas kernels for 14% -> 12%
where the time goes in v8:
time: 44.3 us; the launch traced here: 44.2 us
  starting transfers between devices  25.8 us (58%)
  Pallas kernels  9.43 us (21%)
  waiting for transfers between devices  7.84 us (18%)
  other arithmetic  0.79 us (2%)
    ppermute x15, starting transfers between devices, across(): return lax.ppermute(value, 'expert', pairs) if mask else value  25.1 us
    pallas_call x1, Pallas kernels, read(): pl.pallas_call(functools.partial(read_kernel, count, len(after)), out_sha...  4.79 us
    ppermute x15, waiting for transfers between devices, across(): return lax.ppermute(value, 'expert', pairs) if mask else value  4.56 us
    pallas_call x1, Pallas kernels, expert_parts(): pl.pallas_call(functools.partial(expert_kernel, count), out_shape=tuple((...  3.93 us
    ppermute x4, waiting for transfers between devices, partner(): return lax.ppermute(value, axis, pairs)  3.28 us
  transfers between devices with their start and end apart: 19, of which 8 were waited for; matrix products, arithmetic and copies ran while one was open for 0% of the time, Pallas kernels for 12%

profile of v8, /device:TPU:0, one launch (start us, length us, event | category | flops | bytes accessed | tf_op | source)
XLA Modules:
  0.0 44.2 jit_solution(1656910046867228688)
XLA Ops:
  0.0 4.0 %collective-permute-start = (bf16[16,2880]{1,0:T(8,128)(2,1)}, bf16[16,2880]{1,0:T(8,128)(2,1)S(1)}, u32[]{:S(2)}, u32[]{:S(2)}) collective-permute-start(bf16[16,2880]{1,0:T(8,128)(2,1)} %refs_6_.1), channel_id=1, source_target_pairs={{0,8},{1,9},{2,10},{3,11},{4,12},{5,13},{6,14},{7,15},{8,0},{9,1},... | collective-permute-start | bytes 276488 | tf_op jit(solution)/shard_map/ppermute | solution.py:230
  4.0 1.6 %collective-permute-start.3 = (bf16[16,2880]{1,0:T(8,128)(2,1)}, bf16[16,2880]{1,0:T(8,128)(2,1)S(1)}, u32[]{:S(2)}, u32[]{:S(2)}) collective-permute-start(bf16[16,2880]{1,0:T(8,128)(2,1)} %refs_6_.1), channel_id=1, source_target_pairs={{0,4},{1,5},{2,6},{3,7},{4,0},{5,1},{6,2},{7,3},{8,12},{9,13},{10,... | collective-permute-start | bytes 276488 | tf_op jit(solution)/shard_map/ppermute | solution.py:230
  5.6 1.5 %collective-permute-start.2 = (bf16[16,2880]{1,0:T(8,128)(2,1)}, bf16[16,2880]{1,0:T(8,128)(2,1)S(1)}, u32[]{:S(2)}, u32[]{:S(2)}) collective-permute-start(bf16[16,2880]{1,0:T(8,128)(2,1)} %refs_6_.1), channel_id=1, source_target_pairs={{0,2},{1,3},{2,0},{3,1},{4,6},{5,7},{6,4},{7,5},{8,10},{9,11},{10,... | collective-permute-start | bytes 276488 | tf_op jit(solution)/shard_map/ppermute | solution.py:230
  7.1 0.4 collective-permute-start.4
  7.5 1.2 %collective-permute-done.refs_11_ = bf16[16,2880]{1,0:T(8,128)(2,1)S(1)} collective-permute-done((bf16[16,2880]{1,0:T(8,128)(2,1)}, bf16[16,2880]{1,0:T(8,128)(2,1)S(1)}, u32[]{:S(2)}, u32[]{:S(2)}) %collective-permute-start) | collective-permute-done | bytes 92192 | tf_op jit(solution)/shard_map/ppermute | solution.py:230
  8.8 0.0 collective-permute-start.1
  8.8 2.0 %collective-permute-start.7 = (bf16[16,2880]{1,0:T(8,128)(2,1)S(1)}, bf16[16,2880]{1,0:T(8,128)(2,1)S(1)}, u32[]{:S(2)}, u32[]{:S(2)}) collective-permute-start(bf16[16,2880]{1,0:T(8,128)(2,1)S(1)} %collective-permute-done.refs_11_), channel_id=1, source_target_pairs={{0,6},{1,7},{2,4},{3,5},{4,2},{5,3},{6,0},{7,1},{8,14},{9,15},{10,... | collective-permute-start | bytes 276488 | tf_op jit(solution)/shard_map/ppermute | solution.py:230
  10.8 0.0 collective-permute-done.3.refs_5_.refs_8_
  10.8 1.1 %collective-permute-start.6 = (bf16[16,2880]{1,0:T(8,128)(2,1)S(1)}, bf16[16,2880]{1,0:T(8,128)(2,1)S(1)}, u32[]{:S(2)}, u32[]{:S(2)}) collective-permute-start(bf16[16,2880]{1,0:T(8,128)(2,1)S(1)} %collective-permute-done.refs_11_), channel_id=1, source_target_pairs={{0,4},{1,5},{2,6},{3,7},{4,0},{5,1},{6,2},{7,3},{8,12},{9,13},{10,... | collective-permute-start | bytes 276488 | tf_op jit(solution)/shard_map/ppermute | solution.py:230
  11.9 0.0 collective-permute-done.2.refs_4_.refs_7_
  11.9 1.8 %collective-permute-start.5 = (bf16[16,2880]{1,0:T(8,128)(2,1)S(1)}, bf16[16,2880]{1,0:T(8,128)(2,1)S(1)}, u32[]{:S(2)}, u32[]{:S(2)}) collective-permute-start(bf16[16,2880]{1,0:T(8,128)(2,1)S(1)} %collective-permute-done.refs_11_), channel_id=1, source_target_pairs={{0,2},{1,3},{2,0},{3,1},{4,6},{5,7},{6,4},{7,5},{8,10},{9,11},{10,... | collective-permute-start | bytes 276488 | tf_op jit(solution)/shard_map/ppermute | solution.py:230
  13.7 0.0 collective-permute-done.4.refs_6_.refs_9_
  13.7 0.0 collective-permute-done.1.refs_3_.refs_10_
  13.7 0.0 copy-start.1
  13.7 4.8 %shard_map.73 = (f32[16,4]{1,0:T(8,128)S(1)}, f32[16,4]{1,0:T(8,128)S(1)}, bf16[720,2880]{1,0:T(8,128)(2,1)S(1)}, bf16[720,2880]{1,0:T(8,128)(2,1)S(1)}, bf16[720,2880]{1,0:T(8,128)(2,1)S(1)}) custom-call(s32[1]{0:T(128)} %bitcast.chip_ref, s32[4,16]{1,0:T(4,128)} %bitcast.13, f32[4,16]{1,0:T(4,128)} %bitcast.14, bf16[720,2880]{1,0:T(8,128)(2,1)} %bitcast.10, ...), custom_call_target="tpu_custom_call" | custom-call | bytes 24883200 | tf_op jit(solution)/shard_map/pallas_call | solution.py:133
  18.5 0.0 collective-permute-done.7.refs_5_
  18.5 0.0 collective-permute-done.6.refs_4_
  18.5 0.0 collective-permute-done.5.refs_3_
  18.5 0.0 copy-done
  18.5 0.0 copy-done.1
  18.5 0.4 shard_map.74
  18.9 0.1 collective-permute-start.8
  19.0 2.1 %collective-permute-done.8.refs_1_ = bf16[112,2880]{1,0:T(8,128)(2,1)S(1)} collective-permute-done((bf16[112,2880]{1,0:T(8,128)(2,1)S(1)}, bf16[112,2880]{1,0:T(8,128)(2,1)S(1)}, u32[]{:S(2)}, u32[]{:S(2)}) %collective-permute-start.8) | collective-permute-done | bytes 645152 | tf_op jit(solution)/shard_map/ppermute | solution.py:14
  21.1 3.9 %shard_map.75 = (bf16[64,2880]{1,0:T(8,128)(2,1)S(1)}, bf16[64,2880]{1,0:T(8,128)(2,1)S(1)}, bf16[64,2880]{1,0:T(8,128)(2,1)S(1)}, bf16[64,2880]{1,0:T(8,128)(2,1)S(1)}, f32[16,4]{1,0:T(8,128)S(1)}) custom-call(bf16[16,2880]{1,0:T(8,128)(2,1)S(1)} %get-tuple-element.29.refs_0_, bf16[112,2880]{1,0:T(8,128)(2,1)S(1)} %collective-permute-done.8.refs_1_, ...), custom_call_target="tpu_custom_call" | custom-call | flops 3185049600 | bytes 12441600 | tf_op jit(solution)/shard_map/pallas_call | solution.py:210
  25.0 0.2 collective-permute-start.10
  25.2 0.4 collective-permute-start.15
  25.6 1.2 %collective-permute-done.10.theirs_ref = bf16[64,2880]{1,0:T(8,128)(2,1)S(1)} collective-permute-done((bf16[64,2880]{1,0:T(8,128)(2,1)S(1)}, bf16[64,2880]{1,0:T(8,128)(2,1)S(1)}, u32[]{:S(2)}, u32[]{:S(2)}) %collective-permute-start.10) | collective-permute-done | bytes 368672 | tf_op jit(solution)/shard_map/ppermute | solution.py:14
  26.8 0.1 shard_map.76
  26.9 0.3 collective-permute-start.11
  27.2 0.9 %collective-permute-start.12 = (bf16[16,2880]{1,0:T(8,128)(2,1)S(1)}, bf16[16,2880]{1,0:T(8,128)(2,1)S(1)}, u32[]{:S(2)}, u32[]{:S(2)}) collective-permute-start(bf16[16,2880]{1,0:T(8,128)(2,1)S(1)} %get-tuple-element.38), channel_id=1, source_target_pairs={{0,4},{1,5},{2,6},{3,7},{4,0},{5,1},{6,2},{7,3},{8,12},{9,13},{10,... | collective-permute-start | bytes 276488 | tf_op jit(solution)/shard_map/ppermute | solution.py:230
  28.1 2.3 %collective-permute-start.13 = (bf16[16,2880]{1,0:T(8,128)(2,1)S(1)}, bf16[16,2880]{1,0:T(8,128)(2,1)S(1)}, u32[]{:S(2)}, u32[]{:S(2)}) collective-permute-start(bf16[16,2880]{1,0:T(8,128)(2,1)S(1)} %get-tuple-element.39), channel_id=1, source_target_pairs={{0,6},{1,7},{2,4},{3,5},{4,2},{5,3},{6,0},{7,1},{8,14},{9,15},{10,... | collective-permute-start | bytes 276488 | tf_op jit(solution)/shard_map/ppermute | solution.py:230
  30.4 1.5 %collective-permute-start.9 = (f32[16,4]{1,0:T(8,128)S(1)}, f32[16,4]{1,0:T(8,128)S(1)}, u32[]{:S(2)}, u32[]{:S(2)}) collective-permute-start(f32[16,4]{1,0:T(8,128)S(1)} %get-tuple-element.33), channel_id=1, source_target_pairs={{0,8},{1,9},{2,10},{3,11},{4,12},{5,13},{6,14},{7,15},{8,0},{9,1},... | collective-permute-start | bytes 776 | tf_op jit(solution)/shard_map/ppermute | solution.py:230
  31.9 0.0 collective-permute-done.15.theirs_ref
  32.0 2.4 %collective-permute-start.16 = (bf16[16,2880]{1,0:T(8,128)(2,1)S(1)}, bf16[16,2880]{1,0:T(8,128)(2,1)S(1)}, u32[]{:S(2)}, u32[]{:S(2)}) collective-permute-start(bf16[16,2880]{1,0:T(8,128)(2,1)S(1)} %get-tuple-element.44), channel_id=1, source_target_pairs={{0,6},{1,7},{2,4},{3,5},{4,2},{5,3},{6,0},{7,1},{8,14},{9,15},{10,... | collective-permute-start | bytes 276488 | tf_op jit(solution)/shard_map/ppermute | solution.py:230
  34.4 0.7 %collective-permute-done.9.table_ref = f32[16,4]{1,0:T(8,128)S(1)} collective-permute-done((f32[16,4]{1,0:T(8,128)S(1)}, f32[16,4]{1,0:T(8,128)S(1)}, u32[]{:S(2)}, u32[]{:S(2)}) %collective-permute-start.9) | collective-permute-done | bytes 288 | tf_op jit(solution)/shard_map/ppermute | solution.py:230
  35.1 0.0 collective-permute-done.11.refs_1_
  35.1 0.0 collective-permute-done.12.refs_2_
  35.1 0.3 collective-permute-done.13.refs_3_
  35.4 0.1 shard_map.77.refs_0_
  35.5 2.4 %collective-permute-start.14 = (bf16[16,2880]{1,0:T(8,128)(2,1)S(1)}, bf16[16,2880]{1,0:T(8,128)(2,1)S(1)}, u32[]{:S(2)}, u32[]{:S(2)}) collective-permute-start(bf16[16,2880]{1,0:T(8,128)(2,1)S(1)} %shard_map.77.refs_0_), channel_id=1, source_target_pairs={{0,8},{1,9},{2,10},{3,11},{4,12},{5,13},{6,14},{7,15},{8,0},{9,1},... | collective-permute-start | bytes 276488 | tf_op jit(solution)/shard_map/ppermute | solution.py:230
  38.0 0.8 %collective-permute-start.17 = (bf16[16,2880]{1,0:T(8,128)(2,1)S(1)}, bf16[16,2880]{1,0:T(8,128)(2,1)S(1)}, u32[]{:S(2)}, u32[]{:S(2)}) collective-permute-start(bf16[16,2880]{1,0:T(8,128)(2,1)S(1)} %get-tuple-element.45), channel_id=1, source_target_pairs={{0,2},{1,3},{2,0},{3,1},{4,6},{5,7},{6,4},{7,5},{8,10},{9,11},{10,... | collective-permute-start | bytes 276488 | tf_op jit(solution)/shard_map/ppermute | solution.py:230
  38.8 2.1 %collective-permute-start.18 = (bf16[16,2880]{1,0:T(8,128)(2,1)S(1)}, bf16[16,2880]{1,0:T(8,128)(2,1)S(1)}, u32[]{:S(2)}, u32[]{:S(2)}) collective-permute-start(bf16[16,2880]{1,0:T(8,128)(2,1)S(1)} %get-tuple-element.46), channel_id=1, source_target_pairs={{0,4},{1,5},{2,6},{3,7},{4,0},{5,1},{6,2},{7,3},{8,12},{9,13},{10,... | collective-permute-start | bytes 276488 | tf_op jit(solution)/shard_map/ppermute | solution.py:230
  40.8 0.2 slice_reduce_fusion.3
  41.1 0.0 collective-permute-done.16
  41.1 0.1 collective-permute-done.14
  41.2 1.4 %collective-permute-done.17 = bf16[16,2880]{1,0:T(8,128)(2,1)S(1)} collective-permute-done((bf16[16,2880]{1,0:T(8,128)(2,1)S(1)}, bf16[16,2880]{1,0:T(8,128)(2,1)S(1)}, u32[]{:S(2)}, u32[]{:S(2)}) %collective-permute-start.17) | collective-permute-done | bytes 92192 | tf_op jit(solution)/shard_map/ppermute | solution.py:230
  42.6 0.8 %collective-permute-done.18 = bf16[16,2880]{1,0:T(8,128)(2,1)S(1)} collective-permute-done((bf16[16,2880]{1,0:T(8,128)(2,1)S(1)}, bf16[16,2880]{1,0:T(8,128)(2,1)S(1)}, u32[]{:S(2)}, u32[]{:S(2)}) %collective-permute-start.18) | collective-permute-done | bytes 92192 | tf_op jit(solution)/shard_map/ppermute | solution.py:230
  43.4 0.8 %add_convert_fusion = bf16[16,2880]{1,0:T(8,128)(2,1)} fusion(bf16[16,2880]{1,0:T(8,128)(2,1)S(1)} %collective-permute-done.18, bf16[16,2880]{1,0:T(8,128)(2,1)S(1)} %collective-permute-done.17, bf16[16,2880]{1,0:T(8,128)(2,1)S(1)} %collective-permute-done.16, bf16[16,2880]{1,0:T(8,128)(2,1)S(1)} %get-tuple-element.43, ...), kind=kLoop, calls=%fused_computation | loop fusion | flops 737280 | bytes 645376 | tf_op jit(solution)/shard_map/convert_element_type | solution.py:271
  (3 shorter events, 0.1 us)
Async XLA Ops:
  0.0 8.8 %collective-permute-start = (bf16[16,2880]{1,0:T(8,128)(2,1)}, bf16[16,2880]{1,0:T(8,128)(2,1)S(1)}, u32[]{:S(2)}, u32[]{:S(2)}) collective-permute-start(bf16[16,2880]{1,0:T(8,128)(2,1)} %refs_6_.1), channel_id=1, source_target_pairs={{0,8},{1,9},{2,10},{3,11},{4,12},{5,13},{6,14},{7,15},{8,0},{9,1},... | collective-permute-start | bytes 276488 | tf_op jit(solution)/shard_map/ppermute | solution.py:230
  4.0 6.7 %collective-permute-start.3 = (bf16[16,2880]{1,0:T(8,128)(2,1)}, bf16[16,2880]{1,0:T(8,128)(2,1)S(1)}, u32[]{:S(2)}, u32[]{:S(2)}) collective-permute-start(bf16[16,2880]{1,0:T(8,128)(2,1)} %refs_6_.1), channel_id=1, source_target_pairs={{0,4},{1,5},{2,6},{3,7},{4,0},{5,1},{6,2},{7,3},{8,12},{9,13},{10,... | collective-permute-start | bytes 276488 | tf_op jit(solution)/shard_map/ppermute | solution.py:230
  5.6 6.3 %collective-permute-start.2 = (bf16[16,2880]{1,0:T(8,128)(2,1)}, bf16[16,2880]{1,0:T(8,128)(2,1)S(1)}, u32[]{:S(2)}, u32[]{:S(2)}) collective-permute-start(bf16[16,2880]{1,0:T(8,128)(2,1)} %refs_6_.1), channel_id=1, source_target_pairs={{0,2},{1,3},{2,0},{3,1},{4,6},{5,7},{6,4},{7,5},{8,10},{9,11},{10,... | collective-permute-start | bytes 276488 | tf_op jit(solution)/shard_map/ppermute | solution.py:230
  7.1 6.5 %collective-permute-start.4 = (bf16[16,2880]{1,0:T(8,128)(2,1)}, bf16[16,2880]{1,0:T(8,128)(2,1)S(1)}, u32[]{:S(2)}, u32[]{:S(2)}) collective-permute-start(bf16[16,2880]{1,0:T(8,128)(2,1)} %refs_6_.1), channel_id=1, source_target_pairs={{0,6},{1,7},{2,4},{3,5},{4,2},{5,3},{6,0},{7,1},{8,14},{9,15},{10,... | collective-permute-start | bytes 276488 | tf_op jit(solution)/shard_map/ppermute | solution.py:230
  8.8 4.9 %collective-permute-start.1 = (bf16[16,2880]{1,0:T(8,128)(2,1)S(1)}, bf16[16,2880]{1,0:T(8,128)(2,1)S(1)}, u32[]{:S(2)}, u32[]{:S(2)}) collective-permute-start(bf16[16,2880]{1,0:T(8,128)(2,1)S(1)} %collective-permute-done.refs_11_), channel_id=1, source_target_pairs={{0,1},{1,0},{2,3},{3,2},{4,5},{5,4},{6,7},{7,6},{8,9},{9,8},{10,11... | collective-permute-start | bytes 276488 | tf_op jit(solution)/shard_map/ppermute | solution.py:14
  8.8 9.7 %collective-permute-start.7 = (bf16[16,2880]{1,0:T(8,128)(2,1)S(1)}, bf16[16,2880]{1,0:T(8,128)(2,1)S(1)}, u32[]{:S(2)}, u32[]{:S(2)}) collective-permute-start(bf16[16,2880]{1,0:T(8,128)(2,1)S(1)} %collective-permute-done.refs_11_), channel_id=1, source_target_pairs={{0,6},{1,7},{2,4},{3,5},{4,2},{5,3},{6,0},{7,1},{8,14},{9,15},{10,... | collective-permute-start | bytes 276488 | tf_op jit(solution)/shard_map/ppermute | solution.py:230
  10.8 7.7 %collective-permute-start.6 = (bf16[16,2880]{1,0:T(8,128)(2,1)S(1)}, bf16[16,2880]{1,0:T(8,128)(2,1)S(1)}, u32[]{:S(2)}, u32[]{:S(2)}) collective-permute-start(bf16[16,2880]{1,0:T(8,128)(2,1)S(1)} %collective-permute-done.refs_11_), channel_id=1, source_target_pairs={{0,4},{1,5},{2,6},{3,7},{4,0},{5,1},{6,2},{7,3},{8,12},{9,13},{10,... | collective-permute-start | bytes 276488 | tf_op jit(solution)/shard_map/ppermute | solution.py:230
  11.9 6.6 %collective-permute-start.5 = (bf16[16,2880]{1,0:T(8,128)(2,1)S(1)}, bf16[16,2880]{1,0:T(8,128)(2,1)S(1)}, u32[]{:S(2)}, u32[]{:S(2)}) collective-permute-start(bf16[16,2880]{1,0:T(8,128)(2,1)S(1)} %collective-permute-done.refs_11_), channel_id=1, source_target_pairs={{0,2},{1,3},{2,0},{3,1},{4,6},{5,7},{6,4},{7,5},{8,10},{9,11},{10,... | collective-permute-start | bytes 276488 | tf_op jit(solution)/shard_map/ppermute | solution.py:230
  13.7 4.9 %copy-start = (bf16[16,2880]{1,0:T(8,128)(2,1)S(1)}, bf16[16,2880]{1,0:T(8,128)(2,1)}, u32[]{:S(2)}) copy-start(bf16[16,2880]{1,0:T(8,128)(2,1)} %refs_6_.1) | copy-start | bytes 276484
  13.7 4.9 %copy-start.1 = (f32[2880]{0:T(1024)S(1)}, f32[2880]{0:T(1024)}, u32[]{:S(2)}) copy-start(f32[2880]{0:T(1024)} %refs_12_.1) | copy-start | bytes 34564
  18.9 2.2 %collective-permute-start.8 = (bf16[112,2880]{1,0:T(8,128)(2,1)S(1)}, bf16[112,2880]{1,0:T(8,128)(2,1)S(1)}, u32[]{:S(2)}, u32[]{:S(2)}) collective-permute-start(bf16[112,2880]{1,0:T(8,128)(2,1)S(1)} %get-tuple-element.30.refs_3_), channel_id=1, source_target_pairs={{0,1},{1,0},{2,3},{3,2},{4,5},{5,4},{6,7},{7,6},{8,9},{9,8},{10,11... | collective-permute-start | bytes 1935368 | tf_op jit(solution)/shard_map/ppermute | solution.py:14
  25.0 1.8 %collective-permute-start.10 = (bf16[64,2880]{1,0:T(8,128)(2,1)S(1)}, bf16[64,2880]{1,0:T(8,128)(2,1)S(1)}, u32[]{:S(2)}, u32[]{:S(2)}) collective-permute-start(bf16[64,2880]{1,0:T(8,128)(2,1)S(1)} %get-tuple-element.35), channel_id=1, source_target_pairs={{0,1},{1,0},{2,3},{3,2},{4,5},{5,4},{6,7},{7,6},{8,9},{9,8},{10,11... | collective-permute-start | bytes 1105928 | tf_op jit(solution)/shard_map/ppermute | solution.py:14
  25.2 6.7 %collective-permute-start.15 = (bf16[64,2880]{1,0:T(8,128)(2,1)S(1)}, bf16[64,2880]{1,0:T(8,128)(2,1)S(1)}, u32[]{:S(2)}, u32[]{:S(2)}) collective-permute-start(bf16[64,2880]{1,0:T(8,128)(2,1)S(1)} %get-tuple-element.42), channel_id=1, source_target_pairs={{0,1},{1,0},{2,3},{3,2},{4,5},{5,4},{6,7},{7,6},{8,9},{9,8},{10,11... | collective-permute-start | bytes 1105928 | tf_op jit(solution)/shard_map/ppermute | solution.py:14
  26.9 8.2 %collective-permute-start.11 = (bf16[16,2880]{1,0:T(8,128)(2,1)S(1)}, bf16[16,2880]{1,0:T(8,128)(2,1)S(1)}, u32[]{:S(2)}, u32[]{:S(2)}) collective-permute-start(bf16[16,2880]{1,0:T(8,128)(2,1)S(1)} %get-tuple-element.37), channel_id=1, source_target_pairs={{0,2},{1,3},{2,0},{3,1},{4,6},{5,7},{6,4},{7,5},{8,10},{9,11},{10,... | collective-permute-start | bytes 276488 | tf_op jit(solution)/shard_map/ppermute | solution.py:230
  27.2 7.9 %collective-permute-start.12 = (bf16[16,2880]{1,0:T(8,128)(2,1)S(1)}, bf16[16,2880]{1,0:T(8,128)(2,1)S(1)}, u32[]{:S(2)}, u32[]{:S(2)}) collective-permute-start(bf16[16,2880]{1,0:T(8,128)(2,1)S(1)} %get-tuple-element.38), channel_id=1, source_target_pairs={{0,4},{1,5},{2,6},{3,7},{4,0},{5,1},{6,2},{7,3},{8,12},{9,13},{10,... | collective-permute-start | bytes 276488 | tf_op jit(solution)/shard_map/ppermute | solution.py:230
  28.1 7.3 %collective-permute-start.13 = (bf16[16,2880]{1,0:T(8,128)(2,1)S(1)}, bf16[16,2880]{1,0:T(8,128)(2,1)S(1)}, u32[]{:S(2)}, u32[]{:S(2)}) collective-permute-start(bf16[16,2880]{1,0:T(8,128)(2,1)S(1)} %get-tuple-element.39), channel_id=1, source_target_pairs={{0,6},{1,7},{2,4},{3,5},{4,2},{5,3},{6,0},{7,1},{8,14},{9,15},{10,... | collective-permute-start | bytes 276488 | tf_op jit(solution)/shard_map/ppermute | solution.py:230
  30.4 4.7 %collective-permute-start.9 = (f32[16,4]{1,0:T(8,128)S(1)}, f32[16,4]{1,0:T(8,128)S(1)}, u32[]{:S(2)}, u32[]{:S(2)}) collective-permute-start(f32[16,4]{1,0:T(8,128)S(1)} %get-tuple-element.33), channel_id=1, source_target_pairs={{0,8},{1,9},{2,10},{3,11},{4,12},{5,13},{6,14},{7,15},{8,0},{9,1},... | collective-permute-start | bytes 776 | tf_op jit(solution)/shard_map/ppermute | solution.py:230
  32.0 9.1 %collective-permute-start.16 = (bf16[16,2880]{1,0:T(8,128)(2,1)S(1)}, bf16[16,2880]{1,0:T(8,128)(2,1)S(1)}, u32[]{:S(2)}, u32[]{:S(2)}) collective-permute-start(bf16[16,2880]{1,0:T(8,128)(2,1)S(1)} %get-tuple-element.44), channel_id=1, source_target_pairs={{0,6},{1,7},{2,4},{3,5},{4,2},{5,3},{6,0},{7,1},{8,14},{9,15},{10,... | collective-permute-start | bytes 276488 | tf_op jit(solution)/shard_map/ppermute | solution.py:230
  35.5 5.6 %collective-permute-start.14 = (bf16[16,2880]{1,0:T(8,128)(2,1)S(1)}, bf16[16,2880]{1,0:T(8,128)(2,1)S(1)}, u32[]{:S(2)}, u32[]{:S(2)}) collective-permute-start(bf16[16,2880]{1,0:T(8,128)(2,1)S(1)} %shard_map.77.refs_0_), channel_id=1, source_target_pairs={{0,8},{1,9},{2,10},{3,11},{4,12},{5,13},{6,14},{7,15},{8,0},{9,1},... | collective-permute-start | bytes 276488 | tf_op jit(solution)/shard_map/ppermute | solution.py:230
  38.0 4.6 %collective-permute-start.17 = (bf16[16,2880]{1,0:T(8,128)(2,1)S(1)}, bf16[16,2880]{1,0:T(8,128)(2,1)S(1)}, u32[]{:S(2)}, u32[]{:S(2)}) collective-permute-start(bf16[16,2880]{1,0:T(8,128)(2,1)S(1)} %get-tuple-element.45), channel_id=1, source_target_pairs={{0,2},{1,3},{2,0},{3,1},{4,6},{5,7},{6,4},{7,5},{8,10},{9,11},{10,... | collective-permute-start | bytes 276488 | tf_op jit(solution)/shard_map/ppermute | solution.py:230
  38.8 4.6 %collective-permute-start.18 = (bf16[16,2880]{1,0:T(8,128)(2,1)S(1)}, bf16[16,2880]{1,0:T(8,128)(2,1)S(1)}, u32[]{:S(2)}, u32[]{:S(2)}) collective-permute-start(bf16[16,2880]{1,0:T(8,128)(2,1)S(1)} %get-tuple-element.46), channel_id=1, source_target_pairs={{0,4},{1,5},{2,6},{3,7},{4,0},{5,1},{6,2},{7,3},{8,12},{9,13},{10,... | collective-permute-start | bytes 276488 | tf_op jit(solution)/shard_map/ppermute | solution.py:230

commit v9 on v7

--- a/solution.py
+++ b/solution.py
@@ -103,6 +103,31 @@
     )(*after, *blocks, gain)
 
 
+def relay_kernel(after, *refs):
+    block_ref, own_ref, gain_ref, out_ref, both_ref = refs[after:]
+    rows, model = block_ref.shape
+    gain = gain_ref[...].reshape(1, model)
+    for i, ref in enumerate((block_ref, own_ref)):
+        x = ref[...].astype(jnp.float32)
+        scale = lax.rsqrt(jnp.mean(x * x, axis=-1, keepdims=True) + 1e-05)
+        normed = (x * scale * gain).astype(jnp.bfloat16)
+        both_ref[pl.ds(i * rows, rows), :] = normed
+        if i == 0:
+            out_ref[...] = normed
+
+
+def relay(block, own, gain, after):
+    rows, model = block.shape
+    vmem = pl.BlockSpec(memory_space=pltpu.VMEM)
+    return pl.pallas_call(
+        functools.partial(relay_kernel, len(after)),
+        out_shape=tuple(jax.ShapeDtypeStruct((n * rows, model), jnp.bfloat16) for n in (1, 2)),
+        in_specs=[pl.BlockSpec(memory_space=pl.ANY)] * len(after) + [vmem] * 3,
+        out_specs=(vmem,) * 2,
+        compiler_params=pltpu.CompilerParams(vmem_limit_bytes=8 * 2**20),
+    )(*after, block, own, gain)
+
+
 def mix_kernel(table_ref, *refs):
     blocks, out_ref = refs[:-1], refs[-1]
     total = jnp.zeros(out_ref.shape, jnp.float32)
@@ -122,11 +147,11 @@
     )(table, *blocks)
 
 
-def expert_kernel(count, *refs):
-    groups, (gate_ref, up_ref, down_ref, table_ref) = refs[:count], refs[count : count + 4]
+def expert_kernel(count, pieces, rows, *refs):
+    arrays, (gate_ref, up_ref, down_ref, table_ref) = refs[:count], refs[count : count + 4]
     outs, table_out_ref = refs[count + 4 : -1], refs[-1]
     table_out_ref[...] = table_ref[...]
-    normed = jnp.concatenate([group[...] for group in groups])
+    normed = jnp.concatenate([arrays[i][block * rows : (block + 1) * rows, :] for i, block in pieces])
     across = (((1,), (1,)), ((), ()))
     gate = lax.dot_general(normed, gate_ref[...], across, preferred_element_type=jnp.float32)
     upper = lax.dot_general(normed, up_ref[...], across, preferred_element_type=jnp.float32)
@@ -139,21 +164,30 @@
         start += rows
 
 
-def expert_parts(groups, sizes, gate_w, up_w, down_w, table):
-    count, rows = len(groups), sum(sizes)
+def expert_parts(groups, rows, gate_w, up_w, down_w, table):
+    arrays = []
+    pieces = []
+    for array, block in sum(groups, []):
+        known = [i for i, other in enumerate(arrays) if other is array]
+        pieces.append((known[0] if known else len(arrays), block))
+        arrays += [] if known else [array]
+    sizes = tuple(rows * len(group) for group in groups)
+    count = len(arrays)
     hidden, model = gate_w.shape
     vmem = pl.BlockSpec(memory_space=pltpu.VMEM)
     return pl.pallas_call(
-        functools.partial(expert_kernel, count),
+        functools.partial(expert_kernel, count, tuple(pieces), rows),
         out_shape=tuple(jax.ShapeDtypeStruct((size, model), jnp.bfloat16) for size in sizes)
         + (jax.ShapeDtypeStruct(table.shape, table.dtype),),
         in_specs=[vmem] * (count + 4),
         out_specs=(vmem,) * (len(sizes) + 1),
         cost_estimate=pl.CostEstimate(
-            flops=6 * rows * model * hidden, bytes_accessed=6 * model * hidden, transcendentals=rows * hidden
+            flops=6 * sum(sizes) * model * hidden,
+            bytes_accessed=6 * model * hidden,
+            transcendentals=sum(sizes) * hidden,
         ),
         compiler_params=pltpu.CompilerParams(vmem_limit_bytes=24 * 2**20),
-    )(*groups, gate_w, up_w, down_w, table)
+    )(*arrays, gate_w, up_w, down_w, table)
 
 
 def read_kernel(after, *refs):
@@ -243,22 +277,26 @@
 
     x = residual
     mirrored = across(x, half)
-    near = [across(x, mask) for mask in range(1, half)]
+    short = [mask for mask in range(1, half) if mask & (mask - 1) == 0]
+    long = [mask for mask in range(1, half) if mask not in short]
+    near = [across(x, mask) for mask in short]
     chip = (lax.axis_index("expert") // 2).reshape(1)
     near_weights, far_weights, gate_w = load(chip, expert_ids, expert_weights, half, gate_proj[0].T)
-    (mirrored,) = pack(([mirrored],), norm_gain, (near_weights,))
-    far = [across(mirrored, mask) for mask in range(1, half)]
-    mirror_swapped = swap(mirrored)
-    up_w, down_w = read((up_proj[0].T, down_proj[0]), (mirror_swapped, *near))
-    far_swapped = [swap(block) for block in far]
-    (near_rows,) = pack(([x] + near,), norm_gain, (up_w, *far))
+    mirrored, both = relay(mirrored, x, norm_gain, (near_weights, *near))
+    far = {0: mirrored} | {mask: across(mirrored, mask) for mask in short} | {mask: across(both, mask) for mask in long}
+    far_swapped = {0: swap(mirrored)}
+    up_w, down_w = read((up_proj[0].T, down_proj[0]), (far_swapped[0], *near))
+    far_swapped |= {mask: swap(far[mask]) for mask in short + long}
+    (near_rows,) = pack(([x] + near,), norm_gain, (up_w, *(far[mask] for mask in short + long)))
+
+    def groups(far, near):
+        at = {mask: (near, i) for i, mask in enumerate([0] + short)} | {mask: (far[mask], 1) for mask in long}
+        return [(far[mask], 0) for mask in range(half)], [at[mask] for mask in range(half)]
+
+    far_theirs, near_theirs = groups(far_swapped, swap(near_rows))
+    far_mine, near_mine = groups(far, near_rows)
     *parts, far_weights = expert_parts(
-        (mirror_swapped, *far_swapped, mirrored, *far, swap(near_rows), near_rows),
-        (half * rows,) * 4,
-        gate_w,
-        up_w,
-        down_w,
-        far_weights,
+        (far_theirs, far_mine, near_theirs, near_mine), rows, gate_w, up_w, down_w, far_weights
     )
     mirror_weights = across(far_weights, half)
 

time: 42.5 us -> 44.2 us (1.040)
  waiting for transfers between devices: 7.09 us -> 9.67 us
  starting transfers between devices: 23.7 us -> 22.8 us
    ppermute x15 -> x14, waiting for transfers between devices: 6 us -> 8.49 us  [across(): return lax.ppermute(value, 'expert', pairs) if mask else value]
    ppermute x15 -> x14, starting transfers between devices: 22.3 us -> 21.4 us  [across(): return lax.ppermute(value, 'expert', pairs) if mask else value]
    pallas_call x1 -> x2, Pallas kernels: 3.92 us -> 4.08 us  [the longest x1 3.92 us: expert_parts(): pl.pallas_call(functools.partial(expert_kernel, count, tuple(pieces), row...]
  transfers between devices with their start and end apart: 22 -> 21, of which waited for: 8 -> 9; matrix products, arithmetic and copies ran while one was open for 1% -> 1% of each run, Pallas kernels for 14% -> 13%
where the time goes in v9:
time: 44.2 us; the launch traced here: 44 us
  starting transfers between devices  22.8 us (52%)
  Pallas kernels  10.2 us (23%)
  waiting for transfers between devices  9.67 us (22%)
  other arithmetic  0.98 us (2%)
    ppermute x14, starting transfers between devices, across(): return lax.ppermute(value, 'expert', pairs) if mask else value  21.4 us
    ppermute x14, waiting for transfers between devices, across(): return lax.ppermute(value, 'expert', pairs) if mask else value  8.49 us
    pallas_call x1, Pallas kernels, expert_parts(): pl.pallas_call(functools.partial(expert_kernel, count, tuple(pieces), row...  3.92 us
    pallas_call x1, Pallas kernels, read(): pl.pallas_call(functools.partial(read_kernel, len(after)), out_shape=tupl...  3.51 us
    pallas_call x1, Pallas kernels, load(): pl.pallas_call(load_kernel, out_shape=(table, table, pltpu.VMEM(array.sha...  2.26 us
    ppermute x7, starting transfers between devices, partner(): return lax.ppermute(value, axis, pairs)  1.38 us
    ppermute x7, waiting for transfers between devices, partner(): return lax.ppermute(value, axis, pairs)  1.18 us
  transfers between devices with their start and end apart: 21, of which 9 were waited for; matrix products, arithmetic and copies ran while one was open for 1% of the time, Pallas kernels for 13%

profile of v9, /device:TPU:0, one launch (start us, length us, event | category | flops | bytes accessed | tf_op | source)
XLA Modules:
  0.0 44.0 jit_solution(3366397016748095495)
XLA Ops:
  0.0 4.0 %collective-permute-start.2 = (bf16[16,2880]{1,0:T(8,128)(2,1)}, bf16[16,2880]{1,0:T(8,128)(2,1)S(1)}, u32[]{:S(2)}, u32[]{:S(2)}) collective-permute-start(bf16[16,2880]{1,0:T(8,128)(2,1)} %refs_4_.3), channel_id=1, source_target_pairs={{0,8},{1,9},{2,10},{3,11},{4,12},{5,13},{6,14},{7,15},{8,0},{9,1},... | collective-permute-start | bytes 276488 | tf_op jit(solution)/shard_map/ppermute | solution.py:273
  4.0 1.6 %collective-permute-start.1 = (bf16[16,2880]{1,0:T(8,128)(2,1)}, bf16[16,2880]{1,0:T(8,128)(2,1)S(1)}, u32[]{:S(2)}, u32[]{:S(2)}) collective-permute-start(bf16[16,2880]{1,0:T(8,128)(2,1)} %refs_4_.3), channel_id=1, source_target_pairs={{0,4},{1,5},{2,6},{3,7},{4,0},{5,1},{6,2},{7,3},{8,12},{9,13},{10,... | collective-permute-start | bytes 276488 | tf_op jit(solution)/shard_map/ppermute | solution.py:273
  5.6 1.5 %collective-permute-start = (bf16[16,2880]{1,0:T(8,128)(2,1)}, bf16[16,2880]{1,0:T(8,128)(2,1)S(1)}, u32[]{:S(2)}, u32[]{:S(2)}) collective-permute-start(bf16[16,2880]{1,0:T(8,128)(2,1)} %refs_4_.3), channel_id=1, source_target_pairs={{0,2},{1,3},{2,0},{3,1},{4,6},{5,7},{6,4},{7,5},{8,10},{9,11},{10,... | collective-permute-start | bytes 276488 | tf_op jit(solution)/shard_map/ppermute | solution.py:273
  7.1 2.3 %shard_map.73 = (f32[16,4]{1,0:T(8,128)S(1)}, f32[16,4]{1,0:T(8,128)S(1)}, bf16[720,2880]{1,0:T(8,128)(2,1)S(1)}) custom-call(s32[1]{0:T(128)} %bitcast.chip_ref, s32[4,16]{1,0:T(4,128)} %bitcast.13, f32[4,16]{1,0:T(4,128)} %bitcast.14, bf16[720,2880]{1,0:T(8,128)(2,1)} %bitcast.10), custom_call_target="tpu_custom_call" | custom-call | bytes 8294400 | tf_op jit(solution)/shard_map/pallas_call | solution.py:246
  9.4 0.0 collective-permute-done.2.refs_3_
  9.4 0.0 collective-permute-done.1.refs_2_.refs_6_
  9.4 1.0 %collective-permute-done.refs_1_.refs_5_ = bf16[16,2880]{1,0:T(8,128)(2,1)S(1)} collective-permute-done((bf16[16,2880]{1,0:T(8,128)(2,1)}, bf16[16,2880]{1,0:T(8,128)(2,1)S(1)}, u32[]{:S(2)}, u32[]{:S(2)}) %collective-permute-start) | collective-permute-done | bytes 92192 | tf_op jit(solution)/shard_map/ppermute | solution.py:273
  10.4 0.2 shard_map.74
  10.6 1.5 %collective-permute-start.8 = (bf16[32,2880]{1,0:T(8,128)(2,1)S(1)}, bf16[32,2880]{1,0:T(8,128)(2,1)S(1)}, u32[]{:S(2)}, u32[]{:S(2)}) collective-permute-start(bf16[32,2880]{1,0:T(8,128)(2,1)S(1)} %get-tuple-element.19), channel_id=1, source_target_pairs={{0,6},{1,7},{2,4},{3,5},{4,2},{5,3},{6,0},{7,1},{8,14},{9,15},{10,... | collective-permute-start | bytes 552968 | tf_op jit(solution)/shard_map/ppermute | solution.py:273
  12.0 0.0 collective-permute-start.3
  12.0 1.6 %collective-permute-start.6 = (bf16[16,2880]{1,0:T(8,128)(2,1)S(1)}, bf16[16,2880]{1,0:T(8,128)(2,1)S(1)}, u32[]{:S(2)}, u32[]{:S(2)}) collective-permute-start(bf16[16,2880]{1,0:T(8,128)(2,1)S(1)} %get-tuple-element.18.refs_4_), channel_id=1, source_target_pairs={{0,4},{1,5},{2,6},{3,7},{4,0},{5,1},{6,2},{7,3},{8,12},{9,13},{10,... | collective-permute-start | bytes 276488 | tf_op jit(solution)/shard_map/ppermute | solution.py:273
  13.6 0.5 %collective-permute-start.4 = (bf16[16,2880]{1,0:T(8,128)(2,1)S(1)}, bf16[16,2880]{1,0:T(8,128)(2,1)S(1)}, u32[]{:S(2)}, u32[]{:S(2)}) collective-permute-start(bf16[16,2880]{1,0:T(8,128)(2,1)S(1)} %get-tuple-element.18.refs_4_), channel_id=1, source_target_pairs={{0,2},{1,3},{2,0},{3,1},{4,6},{5,7},{6,4},{7,5},{8,10},{9,11},{10,... | collective-permute-start | bytes 276488 | tf_op jit(solution)/shard_map/ppermute | solution.py:273
  14.1 0.0 collective-permute-done.3.refs_0_
  14.1 3.5 %shard_map.75 = (bf16[720,2880]{1,0:T(8,128)(2,1)S(1)}, bf16[720,2880]{1,0:T(8,128)(2,1)S(1)}) custom-call(bf16[16,2880]{1,0:T(8,128)(2,1)S(1)} %collective-permute-done.3.refs_0_, bf16[16,2880]{1,0:T(8,128)(2,1)S(1)} %collective-permute-done.refs_1_.refs_5_, bf16[16,2880]{1,0:T(8,128)(2,1)S(1)} %collective-permute-done.1.refs_2_.refs_6_, ...), custom_call_target="tpu_custom_call" | custom-call | bytes 16588800 | tf_op jit(solution)/shard_map/pallas_call | solution.py:209
  17.7 1.6 %collective-permute-done.6.refs_2_.refs_6_ = bf16[16,2880]{1,0:T(8,128)(2,1)S(1)} collective-permute-done((bf16[16,2880]{1,0:T(8,128)(2,1)S(1)}, bf16[16,2880]{1,0:T(8,128)(2,1)S(1)}, u32[]{:S(2)}, u32[]{:S(2)}) %collective-permute-start.6) | collective-permute-done | bytes 92192 | tf_op jit(solution)/shard_map/ppermute | solution.py:273
  19.2 0.6 %collective-permute-done.4.refs_1_.refs_5_ = bf16[16,2880]{1,0:T(8,128)(2,1)S(1)} collective-permute-done((bf16[16,2880]{1,0:T(8,128)(2,1)S(1)}, bf16[16,2880]{1,0:T(8,128)(2,1)S(1)}, u32[]{:S(2)}, u32[]{:S(2)}) %collective-permute-start.4) | collective-permute-done | bytes 92192 | tf_op jit(solution)/shard_map/ppermute | solution.py:273
  19.8 0.2 shard_map.76.refs_9_
  20.0 0.1 collective-permute-start.10
  20.1 0.5 %collective-permute-start.9 = (bf16[32,2880]{1,0:T(8,128)(2,1)S(1)}, bf16[32,2880]{1,0:T(8,128)(2,1)S(1)}, u32[]{:S(2)}, u32[]{:S(2)}) collective-permute-start(bf16[32,2880]{1,0:T(8,128)(2,1)S(1)} %collective-permute-done.8.refs_3_.refs_7_), channel_id=1, source_target_pairs={{0,1},{1,0},{2,3},{3,2},{4,5},{5,4},{6,7},{7,6},{8,9},{9,8},{10,11... | collective-permute-start | bytes 552968 | tf_op jit(solution)/shard_map/ppermute | solution.py:14
  20.6 0.1 collective-permute-start.7
  20.7 0.4 collective-permute-start.5
  21.1 0.9 %collective-permute-done.7.refs_2_ = bf16[16,2880]{1,0:T(8,128)(2,1)S(1)} collective-permute-done((bf16[16,2880]{1,0:T(8,128)(2,1)S(1)}, bf16[16,2880]{1,0:T(8,128)(2,1)S(1)}, u32[]{:S(2)}, u32[]{:S(2)}) %collective-permute-start.7) | collective-permute-done | bytes 92192 | tf_op jit(solution)/shard_map/ppermute | solution.py:14
  22.0 0.1 collective-permute-done.5.refs_1_
  22.2 3.9 %shard_map.77 = (bf16[64,2880]{1,0:T(8,128)(2,1)S(1)}, bf16[64,2880]{1,0:T(8,128)(2,1)S(1)}, bf16[64,2880]{1,0:T(8,128)(2,1)S(1)}, bf16[64,2880]{1,0:T(8,128)(2,1)S(1)}, f32[16,4]{1,0:T(8,128)S(1)}) custom-call(bf16[16,2880]{1,0:T(8,128)(2,1)S(1)} %collective-permute-done.3.refs_0_, bf16[16,2880]{1,0:T(8,128)(2,1)S(1)} %collective-permute-done.5.refs_1_, ...), custom_call_target="tpu_custom_call" | custom-call | flops 3185049600 | bytes 12441600 | tf_op jit(solution)/shard_map/pallas_call | solution.py:178
  26.1 0.3 collective-permute-start.12
  26.4 1.4 %collective-permute-start.11 = (f32[16,4]{1,0:T(8,128)S(1)}, f32[16,4]{1,0:T(8,128)S(1)}, u32[]{:S(2)}, u32[]{:S(2)}) collective-permute-start(f32[16,4]{1,0:T(8,128)S(1)} %get-tuple-element.24), channel_id=1, source_target_pairs={{0,8},{1,9},{2,10},{3,11},{4,12},{5,13},{6,14},{7,15},{8,0},{9,1},... | collective-permute-start | bytes 776 | tf_op jit(solution)/shard_map/ppermute | solution.py:273
  27.8 0.0 collective-permute-start.17
  27.8 0.1 collective-permute-done.12
  27.9 0.1 add_convert_fusion.1
  28.0 2.6 %collective-permute-start.15 = (bf16[16,2880]{1,0:T(8,128)(2,1)S(1)}, bf16[16,2880]{1,0:T(8,128)(2,1)S(1)}, u32[]{:S(2)}, u32[]{:S(2)}) collective-permute-start(bf16[16,2880]{1,0:T(8,128)(2,1)S(1)} %get-tuple-element.33), channel_id=1, source_target_pairs={{0,6},{1,7},{2,4},{3,5},{4,2},{5,3},{6,0},{7,1},{8,14},{9,15},{10,... | collective-permute-start | bytes 276488 | tf_op jit(solution)/shard_map/ppermute | solution.py:273
  30.6 0.0 collective-permute-start.14
  30.6 0.9 %collective-permute-start.13 = (bf16[16,2880]{1,0:T(8,128)(2,1)S(1)}, bf16[16,2880]{1,0:T(8,128)(2,1)S(1)}, u32[]{:S(2)}, u32[]{:S(2)}) collective-permute-start(bf16[16,2880]{1,0:T(8,128)(2,1)S(1)} %get-tuple-element.35), channel_id=1, source_target_pairs={{0,2},{1,3},{2,0},{3,1},{4,6},{5,7},{6,4},{7,5},{8,10},{9,11},{10,... | collective-permute-start | bytes 276488 | tf_op jit(solution)/shard_map/ppermute | solution.py:273
  31.6 0.0 collective-permute-done.17
  31.6 0.1 add_convert_fusion
  31.7 1.2 %collective-permute-start.18 = (bf16[16,2880]{1,0:T(8,128)(2,1)S(1)}, bf16[16,2880]{1,0:T(8,128)(2,1)S(1)}, u32[]{:S(2)}, u32[]{:S(2)}) collective-permute-start(bf16[16,2880]{1,0:T(8,128)(2,1)S(1)} %get-tuple-element.37), channel_id=1, source_target_pairs={{0,2},{1,3},{2,0},{3,1},{4,6},{5,7},{6,4},{7,5},{8,10},{9,11},{10,... | collective-permute-start | bytes 276488 | tf_op jit(solution)/shard_map/ppermute | solution.py:273
  32.8 0.0 collective-permute-done.11.table_ref
  32.8 2.1 %collective-permute-start.20 = (bf16[16,2880]{1,0:T(8,128)(2,1)S(1)}, bf16[16,2880]{1,0:T(8,128)(2,1)S(1)}, u32[]{:S(2)}, u32[]{:S(2)}) collective-permute-start(bf16[16,2880]{1,0:T(8,128)(2,1)S(1)} %get-tuple-element.38), channel_id=1, source_target_pairs={{0,6},{1,7},{2,4},{3,5},{4,2},{5,3},{6,0},{7,1},{8,14},{9,15},{10,... | collective-permute-start | bytes 276488 | tf_op jit(solution)/shard_map/ppermute | solution.py:273
  34.9 0.0 collective-permute-done.15.refs_3_
  34.9 1.2 %collective-permute-start.19 = (bf16[16,2880]{1,0:T(8,128)(2,1)S(1)}, bf16[16,2880]{1,0:T(8,128)(2,1)S(1)}, u32[]{:S(2)}, u32[]{:S(2)}) collective-permute-start(bf16[16,2880]{1,0:T(8,128)(2,1)S(1)} %get-tuple-element.39), channel_id=1, source_target_pairs={{0,4},{1,5},{2,6},{3,7},{4,0},{5,1},{6,2},{7,3},{8,12},{9,13},{10,... | collective-permute-start | bytes 276488 | tf_op jit(solution)/shard_map/ppermute | solution.py:273
  36.2 0.0 collective-permute-done.14.refs_2_
  36.2 1.4 %collective-permute-done.13.refs_1_ = bf16[16,2880]{1,0:T(8,128)(2,1)S(1)} collective-permute-done((bf16[16,2880]{1,0:T(8,128)(2,1)S(1)}, bf16[16,2880]{1,0:T(8,128)(2,1)S(1)}, u32[]{:S(2)}, u32[]{:S(2)}) %collective-permute-start.13) | collective-permute-done | bytes 92192 | tf_op jit(solution)/shard_map/ppermute | solution.py:273
  37.5 0.1 shard_map.78
  37.7 1.4 %collective-permute-start.16 = (bf16[16,2880]{1,0:T(8,128)(2,1)S(1)}, bf16[16,2880]{1,0:T(8,128)(2,1)S(1)}, u32[]{:S(2)}, u32[]{:S(2)}) collective-permute-start(bf16[16,2880]{1,0:T(8,128)(2,1)S(1)} %shard_map.78), channel_id=1, source_target_pairs={{0,8},{1,9},{2,10},{3,11},{4,12},{5,13},{6,14},{7,15},{8,0},{9,1},... | collective-permute-start | bytes 276488 | tf_op jit(solution)/shard_map/ppermute | solution.py:273
  39.1 0.2 slice_reduce_fusion.3
  39.3 0.8 %collective-permute-done.18 = bf16[16,2880]{1,0:T(8,128)(2,1)S(1)} collective-permute-done((bf16[16,2880]{1,0:T(8,128)(2,1)S(1)}, bf16[16,2880]{1,0:T(8,128)(2,1)S(1)}, u32[]{:S(2)}, u32[]{:S(2)}) %collective-permute-start.18) | collective-permute-done | bytes 92192 | tf_op jit(solution)/shard_map/ppermute | solution.py:273
  40.1 0.0 collective-permute-done.19
  40.1 3.1 %collective-permute-done.16 = bf16[16,2880]{1,0:T(8,128)(2,1)S(1)} collective-permute-done((bf16[16,2880]{1,0:T(8,128)(2,1)S(1)}, bf16[16,2880]{1,0:T(8,128)(2,1)S(1)}, u32[]{:S(2)}, u32[]{:S(2)}) %collective-permute-start.16) | collective-permute-done | bytes 92192 | tf_op jit(solution)/shard_map/ppermute | solution.py:273
  43.2 0.8 %add_convert_fusion.2 = bf16[16,2880]{1,0:T(8,128)(2,1)} fusion(bf16[16,2880]{1,0:T(8,128)(2,1)S(1)} %collective-permute-done.20, bf16[16,2880]{1,0:T(8,128)(2,1)S(1)} %collective-permute-done.19, bf16[16,2880]{1,0:T(8,128)(2,1)S(1)} %collective-permute-done.18, bf16[16,2880]{1,0:T(8,128)(2,1)S(1)} %collective-permute-done.16, ...), kind=kLoop, calls=%fused_computation.2 | loop fusion | flops 737280 | bytes 645376 | tf_op jit(solution)/shard_map/convert_element_type | solution.py:312
  (10 shorter events, 0.1 us)
Async XLA Ops:
  0.0 10.4 %copy-start = (bf16[16,2880]{1,0:T(8,128)(2,1)S(1)}, bf16[16,2880]{1,0:T(8,128)(2,1)}, u32[]{:S(2)}) copy-start(bf16[16,2880]{1,0:T(8,128)(2,1)} %refs_4_.3) | copy-start | bytes 276484
  0.0 10.4 %copy-start.1 = (f32[2880]{0:T(1024)S(1)}, f32[2880]{0:T(1024)}, u32[]{:S(2)}) copy-start(f32[2880]{0:T(1024)} %refs_7_.1) | copy-start | bytes 34564
  0.0 9.4 %collective-permute-start.2 = (bf16[16,2880]{1,0:T(8,128)(2,1)}, bf16[16,2880]{1,0:T(8,128)(2,1)S(1)}, u32[]{:S(2)}, u32[]{:S(2)}) collective-permute-start(bf16[16,2880]{1,0:T(8,128)(2,1)} %refs_4_.3), channel_id=1, source_target_pairs={{0,8},{1,9},{2,10},{3,11},{4,12},{5,13},{6,14},{7,15},{8,0},{9,1},... | collective-permute-start | bytes 276488 | tf_op jit(solution)/shard_map/ppermute | solution.py:273
  4.0 5.4 %collective-permute-start.1 = (bf16[16,2880]{1,0:T(8,128)(2,1)}, bf16[16,2880]{1,0:T(8,128)(2,1)S(1)}, u32[]{:S(2)}, u32[]{:S(2)}) collective-permute-start(bf16[16,2880]{1,0:T(8,128)(2,1)} %refs_4_.3), channel_id=1, source_target_pairs={{0,4},{1,5},{2,6},{3,7},{4,0},{5,1},{6,2},{7,3},{8,12},{9,13},{10,... | collective-permute-start | bytes 276488 | tf_op jit(solution)/shard_map/ppermute | solution.py:273
  5.6 4.8 %collective-permute-start = (bf16[16,2880]{1,0:T(8,128)(2,1)}, bf16[16,2880]{1,0:T(8,128)(2,1)S(1)}, u32[]{:S(2)}, u32[]{:S(2)}) collective-permute-start(bf16[16,2880]{1,0:T(8,128)(2,1)} %refs_4_.3), channel_id=1, source_target_pairs={{0,2},{1,3},{2,0},{3,1},{4,6},{5,7},{6,4},{7,5},{8,10},{9,11},{10,... | collective-permute-start | bytes 276488 | tf_op jit(solution)/shard_map/ppermute | solution.py:273
  10.6 9.2 %collective-permute-start.8 = (bf16[32,2880]{1,0:T(8,128)(2,1)S(1)}, bf16[32,2880]{1,0:T(8,128)(2,1)S(1)}, u32[]{:S(2)}, u32[]{:S(2)}) collective-permute-start(bf16[32,2880]{1,0:T(8,128)(2,1)S(1)} %get-tuple-element.19), channel_id=1, source_target_pairs={{0,6},{1,7},{2,4},{3,5},{4,2},{5,3},{6,0},{7,1},{8,14},{9,15},{10,... | collective-permute-start | bytes 552968 | tf_op jit(solution)/shard_map/ppermute | solution.py:273
  12.0 2.1 %collective-permute-start.3 = (bf16[16,2880]{1,0:T(8,128)(2,1)S(1)}, bf16[16,2880]{1,0:T(8,128)(2,1)S(1)}, u32[]{:S(2)}, u32[]{:S(2)}) collective-permute-start(bf16[16,2880]{1,0:T(8,128)(2,1)S(1)} %get-tuple-element.18.refs_4_), channel_id=1, source_target_pairs={{0,1},{1,0},{2,3},{3,2},{4,5},{5,4},{6,7},{7,6},{8,9},{9,8},{10,11... | collective-permute-start | bytes 276488 | tf_op jit(solution)/shard_map/ppermute | solution.py:14
  12.0 7.2 %collective-permute-start.6 = (bf16[16,2880]{1,0:T(8,128)(2,1)S(1)}, bf16[16,2880]{1,0:T(8,128)(2,1)S(1)}, u32[]{:S(2)}, u32[]{:S(2)}) collective-permute-start(bf16[16,2880]{1,0:T(8,128)(2,1)S(1)} %get-tuple-element.18.refs_4_), channel_id=1, source_target_pairs={{0,4},{1,5},{2,6},{3,7},{4,0},{5,1},{6,2},{7,3},{8,12},{9,13},{10,... | collective-permute-start | bytes 276488 | tf_op jit(solution)/shard_map/ppermute | solution.py:273
  13.6 6.2 %collective-permute-start.4 = (bf16[16,2880]{1,0:T(8,128)(2,1)S(1)}, bf16[16,2880]{1,0:T(8,128)(2,1)S(1)}, u32[]{:S(2)}, u32[]{:S(2)}) collective-permute-start(bf16[16,2880]{1,0:T(8,128)(2,1)S(1)} %get-tuple-element.18.refs_4_), channel_id=1, source_target_pairs={{0,2},{1,3},{2,0},{3,1},{4,6},{5,7},{6,4},{7,5},{8,10},{9,11},{10,... | collective-permute-start | bytes 276488 | tf_op jit(solution)/shard_map/ppermute | solution.py:273
  20.0 2.2 %collective-permute-start.10 = (bf16[48,2880]{1,0:T(8,128)(2,1)S(1)}, bf16[48,2880]{1,0:T(8,128)(2,1)S(1)}, u32[]{:S(2)}, u32[]{:S(2)}) collective-permute-start(bf16[48,2880]{1,0:T(8,128)(2,1)S(1)} %shard_map.76.refs_9_), channel_id=1, source_target_pairs={{0,1},{1,0},{2,3},{3,2},{4,5},{5,4},{6,7},{7,6},{8,9},{9,8},{10,11... | collective-permute-start | bytes 829448 | tf_op jit(solution)/shard_map/ppermute | solution.py:14
  20.1 2.1 %collective-permute-start.9 = (bf16[32,2880]{1,0:T(8,128)(2,1)S(1)}, bf16[32,2880]{1,0:T(8,128)(2,1)S(1)}, u32[]{:S(2)}, u32[]{:S(2)}) collective-permute-start(bf16[32,2880]{1,0:T(8,128)(2,1)S(1)} %collective-permute-done.8.refs_3_.refs_7_), channel_id=1, source_target_pairs={{0,1},{1,0},{2,3},{3,2},{4,5},{5,4},{6,7},{7,6},{8,9},{9,8},{10,11... | collective-permute-start | bytes 552968 | tf_op jit(solution)/shard_map/ppermute | solution.py:14
  20.6 1.5 %collective-permute-start.7 = (bf16[16,2880]{1,0:T(8,128)(2,1)S(1)}, bf16[16,2880]{1,0:T(8,128)(2,1)S(1)}, u32[]{:S(2)}, u32[]{:S(2)}) collective-permute-start(bf16[16,2880]{1,0:T(8,128)(2,1)S(1)} %collective-permute-done.6.refs_2_.refs_6_), channel_id=1, source_target_pairs={{0,1},{1,0},{2,3},{3,2},{4,5},{5,4},{6,7},{7,6},{8,9},{9,8},{10,11... | collective-permute-start | bytes 276488 | tf_op jit(solution)/shard_map/ppermute | solution.py:14
  20.7 1.5 %collective-permute-start.5 = (bf16[16,2880]{1,0:T(8,128)(2,1)S(1)}, bf16[16,2880]{1,0:T(8,128)(2,1)S(1)}, u32[]{:S(2)}, u32[]{:S(2)}) collective-permute-start(bf16[16,2880]{1,0:T(8,128)(2,1)S(1)} %collective-permute-done.4.refs_1_.refs_5_), channel_id=1, source_target_pairs={{0,1},{1,0},{2,3},{3,2},{4,5},{5,4},{6,7},{7,6},{8,9},{9,8},{10,11... | collective-permute-start | bytes 276488 | tf_op jit(solution)/shard_map/ppermute | solution.py:14
  26.1 1.8 %collective-permute-start.12 = (bf16[64,2880]{1,0:T(8,128)(2,1)S(1)}, bf16[64,2880]{1,0:T(8,128)(2,1)S(1)}, u32[]{:S(2)}, u32[]{:S(2)}) collective-permute-start(bf16[64,2880]{1,0:T(8,128)(2,1)S(1)} %get-tuple-element.26), channel_id=1, source_target_pairs={{0,1},{1,0},{2,3},{3,2},{4,5},{5,4},{6,7},{7,6},{8,9},{9,8},{10,11... | collective-permute-start | bytes 1105928 | tf_op jit(solution)/shard_map/ppermute | solution.py:14
  26.4 6.5 %collective-permute-start.11 = (f32[16,4]{1,0:T(8,128)S(1)}, f32[16,4]{1,0:T(8,128)S(1)}, u32[]{:S(2)}, u32[]{:S(2)}) collective-permute-start(f32[16,4]{1,0:T(8,128)S(1)} %get-tuple-element.24), channel_id=1, source_target_pairs={{0,8},{1,9},{2,10},{3,11},{4,12},{5,13},{6,14},{7,15},{8,0},{9,1},... | collective-permute-start | bytes 776 | tf_op jit(solution)/shard_map/ppermute | solution.py:273
  27.8 3.8 %collective-permute-start.17 = (bf16[64,2880]{1,0:T(8,128)(2,1)S(1)}, bf16[64,2880]{1,0:T(8,128)(2,1)S(1)}, u32[]{:S(2)}, u32[]{:S(2)}) collective-permute-start(bf16[64,2880]{1,0:T(8,128)(2,1)S(1)} %get-tuple-element.28), channel_id=1, source_target_pairs={{0,1},{1,0},{2,3},{3,2},{4,5},{5,4},{6,7},{7,6},{8,9},{9,8},{10,11... | collective-permute-start | bytes 1105928 | tf_op jit(solution)/shard_map/ppermute | solution.py:14
  28.0 6.9 %collective-permute-start.15 = (bf16[16,2880]{1,0:T(8,128)(2,1)S(1)}, bf16[16,2880]{1,0:T(8,128)(2,1)S(1)}, u32[]{:S(2)}, u32[]{:S(2)}) collective-permute-start(bf16[16,2880]{1,0:T(8,128)(2,1)S(1)} %get-tuple-element.33), channel_id=1, source_target_pairs={{0,6},{1,7},{2,4},{3,5},{4,2},{5,3},{6,0},{7,1},{8,14},{9,15},{10,... | collective-permute-start | bytes 276488 | tf_op jit(solution)/shard_map/ppermute | solution.py:273
  30.6 5.5 %collective-permute-start.14 = (bf16[16,2880]{1,0:T(8,128)(2,1)S(1)}, bf16[16,2880]{1,0:T(8,128)(2,1)S(1)}, u32[]{:S(2)}, u32[]{:S(2)}) collective-permute-start(bf16[16,2880]{1,0:T(8,128)(2,1)S(1)} %get-tuple-element.34), channel_id=1, source_target_pairs={{0,4},{1,5},{2,6},{3,7},{4,0},{5,1},{6,2},{7,3},{8,12},{9,13},{10,... | collective-permute-start | bytes 276488 | tf_op jit(solution)/shard_map/ppermute | solution.py:273
  30.6 6.9 %collective-permute-start.13 = (bf16[16,2880]{1,0:T(8,128)(2,1)S(1)}, bf16[16,2880]{1,0:T(8,128)(2,1)S(1)}, u32[]{:S(2)}, u32[]{:S(2)}) collective-permute-start(bf16[16,2880]{1,0:T(8,128)(2,1)S(1)} %get-tuple-element.35), channel_id=1, source_target_pairs={{0,2},{1,3},{2,0},{3,1},{4,6},{5,7},{6,4},{7,5},{8,10},{9,11},{10,... | collective-permute-start | bytes 276488 | tf_op jit(solution)/shard_map/ppermute | solution.py:273
  31.7 8.4 %collective-permute-start.18 = (bf16[16,2880]{1,0:T(8,128)(2,1)S(1)}, bf16[16,2880]{1,0:T(8,128)(2,1)S(1)}, u32[]{:S(2)}, u32[]{:S(2)}) collective-permute-start(bf16[16,2880]{1,0:T(8,128)(2,1)S(1)} %get-tuple-element.37), channel_id=1, source_target_pairs={{0,2},{1,3},{2,0},{3,1},{4,6},{5,7},{6,4},{7,5},{8,10},{9,11},{10,... | collective-permute-start | bytes 276488 | tf_op jit(solution)/shard_map/ppermute | solution.py:273
  32.8 7.2 %collective-permute-start.20 = (bf16[16,2880]{1,0:T(8,128)(2,1)S(1)}, bf16[16,2880]{1,0:T(8,128)(2,1)S(1)}, u32[]{:S(2)}, u32[]{:S(2)}) collective-permute-start(bf16[16,2880]{1,0:T(8,128)(2,1)S(1)} %get-tuple-element.38), channel_id=1, source_target_pairs={{0,6},{1,7},{2,4},{3,5},{4,2},{5,3},{6,0},{7,1},{8,14},{9,15},{10,... | collective-permute-start | bytes 276488 | tf_op jit(solution)/shard_map/ppermute | solution.py:273
  34.9 5.2 %collective-permute-start.19 = (bf16[16,2880]{1,0:T(8,128)(2,1)S(1)}, bf16[16,2880]{1,0:T(8,128)(2,1)S(1)}, u32[]{:S(2)}, u32[]{:S(2)}) collective-permute-start(bf16[16,2880]{1,0:T(8,128)(2,1)S(1)} %get-tuple-element.39), channel_id=1, source_target_pairs={{0,4},{1,5},{2,6},{3,7},{4,0},{5,1},{6,2},{7,3},{8,12},{9,13},{10,... | collective-permute-start | bytes 276488 | tf_op jit(solution)/shard_map/ppermute | solution.py:273
  37.7 5.5 %collective-permute-start.16 = (bf16[16,2880]{1,0:T(8,128)(2,1)S(1)}, bf16[16,2880]{1,0:T(8,128)(2,1)S(1)}, u32[]{:S(2)}, u32[]{:S(2)}) collective-permute-start(bf16[16,2880]{1,0:T(8,128)(2,1)S(1)} %shard_map.78), channel_id=1, source_target_pairs={{0,8},{1,9},{2,10},{3,11},{4,12},{5,13},{6,14},{7,15},{8,0},{9,1},... | collective-permute-start | bytes 276488 | tf_op jit(solution)/shard_map/ppermute | solution.py:273

commit v10 on v7

--- a/solution.py
+++ b/solution.py
@@ -103,18 +103,18 @@
     )(*after, *blocks, gain)
 
 
-def mix_kernel(table_ref, *refs):
+def mix_kernel(columns, table_ref, *refs):
     blocks, out_ref = refs[:-1], refs[-1]
     total = jnp.zeros(out_ref.shape, jnp.float32)
-    for i, block in enumerate(blocks):
-        total += table_ref[:, i : i + 1] * block[...].astype(jnp.float32)
+    for column, block in zip(columns, blocks):
+        total += table_ref[:, column : column + 1] * block[...].astype(jnp.float32)
     out_ref[...] = total.astype(out_ref.dtype)
 
 
-def mixed(table, blocks):
+def mixed(table, columns, blocks):
     vmem = pl.BlockSpec(memory_space=pltpu.VMEM)
     return pl.pallas_call(
-        mix_kernel,
+        functools.partial(mix_kernel, columns),
         out_shape=jax.ShapeDtypeStruct(blocks[0].shape, blocks[0].dtype),
         in_specs=[vmem] * (len(blocks) + 1),
         out_specs=vmem,
@@ -262,15 +262,20 @@
     )
     mirror_weights = across(far_weights, half)
 
-    def give_back(done):
-        done = done.reshape(half, rows, model)
-        return [across(done[mask], mask) for mask in range(half)]
-
-    far_blocks = give_back(pair_sum(parts[1], swap(parts[0])))
-    near_blocks = give_back(pair_sum(parts[3], swap(parts[2])))
-    total = x.astype(jnp.float32) + across(mixed(mirror_weights, far_blocks), half).astype(jnp.float32)
-    for mask, block in enumerate(near_blocks):
-        total += near_weights[:, mask][:, None] * block.astype(jnp.float32)
+    def blocks_of(done):
+        return list(done.reshape(half, rows, model))
+
+    done = blocks_of(pair_sum(parts[1], swap(parts[0])))
+    via = (0,) + tuple(mask for mask in range(1, half) if mask & (mask - 1) == 0)
+    other = mixed(mirror_weights, via, [across(done[mask], mask) for mask in via])
+    home = [
+        (far_weights[:, mask], across(done[mask], half ^ mask)) for mask in range(half) if mask not in via
+    ]
+    done = blocks_of(pair_sum(parts[3], swap(parts[2])))
+    home += [(near_weights[:, mask], across(done[mask], mask)) for mask in range(half)]
+    total = x.astype(jnp.float32) + across(other, half).astype(jnp.float32)
+    for column, block in home:
+        total += column[:, None] * block.astype(jnp.float32)
     return total.astype(jnp.bfloat16)
 
 

time: 42.5 us -> 47.1 us (1.11)
  waiting for transfers between devices: 7.09 us -> 13 us
  starting transfers between devices: 23.7 us -> 22.2 us
    ppermute x15, waiting for transfers between devices: 6 us -> 11.9 us  [across(): return lax.ppermute(value, 'expert', pairs) if mask else value]
    ppermute x15, starting transfers between devices: 22.3 us -> 20.7 us  [across(): return lax.ppermute(value, 'expert', pairs) if mask else value]
  transfers between devices with their start and end apart: 22 -> 22, of which waited for: 8 -> 7; matrix products, arithmetic and copies ran while one was open for 1% -> 1% of each run, Pallas kernels for 14% -> 13%
where the time goes in v10:
time: 47.1 us; the launch traced here: 47 us
  starting transfers between devices  22.2 us (47%)
  waiting for transfers between devices  13 us (28%)
  Pallas kernels  10.2 us (22%)
  other arithmetic  1 us (2%)
    ppermute x15, starting transfers between devices, across(): return lax.ppermute(value, 'expert', pairs) if mask else value  20.7 us
    ppermute x15, waiting for transfers between devices, across(): return lax.ppermute(value, 'expert', pairs) if mask else value  11.9 us
    pallas_call x1, Pallas kernels, expert_parts(): pl.pallas_call(functools.partial(expert_kernel, count), out_shape=tuple((...  3.92 us
    pallas_call x1, Pallas kernels, read(): pl.pallas_call(functools.partial(read_kernel, len(after)), out_shape=tupl...  3.54 us
    pallas_call x1, Pallas kernels, load(): pl.pallas_call(load_kernel, out_shape=(table, table, pltpu.VMEM(array.sha...  2.26 us
    ppermute x7, starting transfers between devices, partner(): return lax.ppermute(value, axis, pairs)  1.45 us
    ppermute x7, waiting for transfers between devices, partner(): return lax.ppermute(value, axis, pairs)  1.09 us
  transfers between devices with their start and end apart: 22, of which 7 were waited for; matrix products, arithmetic and copies ran while one was open for 1% of the time, Pallas kernels for 13%

profile of v10, /device:TPU:0, one launch (start us, length us, event | category | flops | bytes accessed | tf_op | source)
XLA Modules:
  0.0 47.0 jit_solution(1689979640758608849)
XLA Ops:
  0.0 4.0 %collective-permute-start = (bf16[16,2880]{1,0:T(8,128)(2,1)}, bf16[16,2880]{1,0:T(8,128)(2,1)S(1)}, u32[]{:S(2)}, u32[]{:S(2)}) collective-permute-start(bf16[16,2880]{1,0:T(8,128)(2,1)} %refs_4_.1), channel_id=1, source_target_pairs={{0,8},{1,9},{2,10},{3,11},{4,12},{5,13},{6,14},{7,15},{8,0},{9,1},... | collective-permute-start | bytes 276488 | tf_op jit(solution)/shard_map/ppermute | solution.py:239
  4.0 1.6 %collective-permute-start.9 = (bf16[16,2880]{1,0:T(8,128)(2,1)}, bf16[16,2880]{1,0:T(8,128)(2,1)S(1)}, u32[]{:S(2)}, u32[]{:S(2)}) collective-permute-start(bf16[16,2880]{1,0:T(8,128)(2,1)} %refs_4_.1), channel_id=1, source_target_pairs={{0,4},{1,5},{2,6},{3,7},{4,0},{5,1},{6,2},{7,3},{8,12},{9,13},{10,... | collective-permute-start | bytes 276488 | tf_op jit(solution)/shard_map/ppermute | solution.py:239
  5.6 1.5 %collective-permute-start.8 = (bf16[16,2880]{1,0:T(8,128)(2,1)}, bf16[16,2880]{1,0:T(8,128)(2,1)S(1)}, u32[]{:S(2)}, u32[]{:S(2)}) collective-permute-start(bf16[16,2880]{1,0:T(8,128)(2,1)} %refs_4_.1), channel_id=1, source_target_pairs={{0,2},{1,3},{2,0},{3,1},{4,6},{5,7},{6,4},{7,5},{8,10},{9,11},{10,... | collective-permute-start | bytes 276488 | tf_op jit(solution)/shard_map/ppermute | solution.py:239
  7.1 0.4 collective-permute-start.10
  7.5 2.3 %shard_map.73 = (f32[16,4]{1,0:T(8,128)S(1)}, f32[16,4]{1,0:T(8,128)S(1)}, bf16[720,2880]{1,0:T(8,128)(2,1)S(1)}) custom-call(s32[1]{0:T(128)} %bitcast.chip_ref, s32[4,16]{1,0:T(4,128)} %bitcast.13, f32[4,16]{1,0:T(4,128)} %bitcast.14, bf16[720,2880]{1,0:T(8,128)(2,1)} %bitcast.12), custom_call_target="tpu_custom_call" | custom-call | bytes 8294400 | tf_op jit(solution)/shard_map/pallas_call | solution.py:212
  9.8 0.0 collective-permute-done.refs_1_
  9.8 0.1 shard_map.74.refs_4_
  9.9 0.1 collective-permute-start.1
  10.0 2.6 %collective-permute-start.6 = (bf16[16,2880]{1,0:T(8,128)(2,1)S(1)}, bf16[16,2880]{1,0:T(8,128)(2,1)S(1)}, u32[]{:S(2)}, u32[]{:S(2)}) collective-permute-start(bf16[16,2880]{1,0:T(8,128)(2,1)S(1)} %shard_map.74.refs_4_), channel_id=1, source_target_pairs={{0,6},{1,7},{2,4},{3,5},{4,2},{5,3},{6,0},{7,1},{8,14},{9,15},{10,... | collective-permute-start | bytes 276488 | tf_op jit(solution)/shard_map/ppermute | solution.py:239
  12.6 0.0 collective-permute-done.9.refs_2_.refs_6_
  12.6 0.5 collective-permute-start.4
  13.1 0.0 collective-permute-done.8.refs_1_.refs_5_
  13.1 0.6 %collective-permute-start.2 = (bf16[16,2880]{1,0:T(8,128)(2,1)S(1)}, bf16[16,2880]{1,0:T(8,128)(2,1)S(1)}, u32[]{:S(2)}, u32[]{:S(2)}) collective-permute-start(bf16[16,2880]{1,0:T(8,128)(2,1)S(1)} %shard_map.74.refs_4_), channel_id=1, source_target_pairs={{0,2},{1,3},{2,0},{3,1},{4,6},{5,7},{6,4},{7,5},{8,10},{9,11},{10,... | collective-permute-start | bytes 276488 | tf_op jit(solution)/shard_map/ppermute | solution.py:239
  13.7 0.0 collective-permute-done.10.refs_3_.refs_7_
  13.7 0.0 collective-permute-done.1.refs_0_
  13.7 3.5 %shard_map.75 = (bf16[720,2880]{1,0:T(8,128)(2,1)S(1)}, bf16[720,2880]{1,0:T(8,128)(2,1)S(1)}) custom-call(bf16[16,2880]{1,0:T(8,128)(2,1)S(1)} %collective-permute-done.1.refs_0_, bf16[16,2880]{1,0:T(8,128)(2,1)S(1)} %collective-permute-done.8.refs_1_.refs_5_, bf16[16,2880]{1,0:T(8,128)(2,1)S(1)} %collective-permute-done.9.refs_2_.refs_6_, ...), custom_call_target="tpu_custom_call" | custom-call | bytes 16588800 | tf_op jit(solution)/shard_map/pallas_call | solution.py:175
  17.2 0.0 collective-permute-done.6.refs_3_.refs_7_
  17.2 0.9 %collective-permute-done.4.refs_2_.refs_6_ = bf16[16,2880]{1,0:T(8,128)(2,1)S(1)} collective-permute-done((bf16[16,2880]{1,0:T(8,128)(2,1)S(1)}, bf16[16,2880]{1,0:T(8,128)(2,1)S(1)}, u32[]{:S(2)}, u32[]{:S(2)}) %collective-permute-start.4) | collective-permute-done | bytes 92192 | tf_op jit(solution)/shard_map/ppermute | solution.py:239
  18.1 0.2 shard_map.76.refs_9_
  18.3 0.1 collective-permute-start.11
  18.4 0.5 %collective-permute-start.7 = (bf16[16,2880]{1,0:T(8,128)(2,1)S(1)}, bf16[16,2880]{1,0:T(8,128)(2,1)S(1)}, u32[]{:S(2)}, u32[]{:S(2)}) collective-permute-start(bf16[16,2880]{1,0:T(8,128)(2,1)S(1)} %collective-permute-done.6.refs_3_.refs_7_), channel_id=1, source_target_pairs={{0,1},{1,0},{2,3},{3,2},{4,5},{5,4},{6,7},{7,6},{8,9},{9,8},{10,11... | collective-permute-start | bytes 276488 | tf_op jit(solution)/shard_map/ppermute | solution.py:14
  18.9 0.1 collective-permute-start.5
  19.0 0.4 collective-permute-start.3
  19.4 0.8 %collective-permute-done.7.refs_3_ = bf16[16,2880]{1,0:T(8,128)(2,1)S(1)} collective-permute-done((bf16[16,2880]{1,0:T(8,128)(2,1)S(1)}, bf16[16,2880]{1,0:T(8,128)(2,1)S(1)}, u32[]{:S(2)}, u32[]{:S(2)}) %collective-permute-start.7) | collective-permute-done | bytes 92192 | tf_op jit(solution)/shard_map/ppermute | solution.py:14
  20.2 0.1 collective-permute-done.5.refs_2_
  20.4 0.1 collective-permute-done.3.refs_1_
  20.5 3.9 %shard_map.77 = (bf16[64,2880]{1,0:T(8,128)(2,1)S(1)}, bf16[64,2880]{1,0:T(8,128)(2,1)S(1)}, bf16[64,2880]{1,0:T(8,128)(2,1)S(1)}, bf16[64,2880]{1,0:T(8,128)(2,1)S(1)}, f32[16,4]{1,0:T(8,128)S(1)}) custom-call(bf16[16,2880]{1,0:T(8,128)(2,1)S(1)} %collective-permute-done.1.refs_0_, bf16[16,2880]{1,0:T(8,128)(2,1)S(1)} %collective-permute-done.3.refs_1_, ...), custom_call_target="tpu_custom_call" | custom-call | flops 3185049600 | bytes 12441600 | tf_op jit(solution)/shard_map/pallas_call | solution.py:146
  24.4 0.3 collective-permute-start.13
  24.7 0.2 slice_reduce_fusion.3
  24.9 1.6 %collective-permute-start.12 = (f32[16,4]{1,0:T(8,128)S(1)}, f32[16,4]{1,0:T(8,128)S(1)}, u32[]{:S(2)}, u32[]{:S(2)}) collective-permute-start(f32[16,4]{1,0:T(8,128)S(1)} %get-tuple-element.20), channel_id=1, source_target_pairs={{0,8},{1,9},{2,10},{3,11},{4,12},{5,13},{6,14},{7,15},{8,0},{9,1},... | collective-permute-start | bytes 776 | tf_op jit(solution)/shard_map/ppermute | solution.py:239
  26.5 0.0 collective-permute-start.18
  26.5 0.1 add_convert_fusion.1
  26.7 1.8 %collective-permute-start.15 = (bf16[16,2880]{1,0:T(8,128)(2,1)S(1)}, bf16[16,2880]{1,0:T(8,128)(2,1)S(1)}, u32[]{:S(2)}, u32[]{:S(2)}) collective-permute-start(bf16[16,2880]{1,0:T(8,128)(2,1)S(1)} %get-tuple-element.29), channel_id=1, source_target_pairs={{0,4},{1,5},{2,6},{3,7},{4,0},{5,1},{6,2},{7,3},{8,12},{9,13},{10,... | collective-permute-start | bytes 276488 | tf_op jit(solution)/shard_map/ppermute | solution.py:239
  28.5 2.0 %collective-permute-start.17 = (bf16[16,2880]{1,0:T(8,128)(2,1)S(1)}, bf16[16,2880]{1,0:T(8,128)(2,1)S(1)}, u32[]{:S(2)}, u32[]{:S(2)}) collective-permute-start(bf16[16,2880]{1,0:T(8,128)(2,1)S(1)} %get-tuple-element.30), channel_id=1, source_target_pairs={{0,14},{1,15},{2,12},{3,13},{4,10},{5,11},{6,8},{7,9},{8,6},{9,7},... | collective-permute-start | bytes 276488 | tf_op jit(solution)/shard_map/ppermute | solution.py:239
  30.5 0.6 %collective-permute-start.14 = (bf16[16,2880]{1,0:T(8,128)(2,1)S(1)}, bf16[16,2880]{1,0:T(8,128)(2,1)S(1)}, u32[]{:S(2)}, u32[]{:S(2)}) collective-permute-start(bf16[16,2880]{1,0:T(8,128)(2,1)S(1)} %get-tuple-element.31), channel_id=1, source_target_pairs={{0,2},{1,3},{2,0},{3,1},{4,6},{5,7},{6,4},{7,5},{8,10},{9,11},{10,... | collective-permute-start | bytes 276488 | tf_op jit(solution)/shard_map/ppermute | solution.py:239
  31.1 0.0 collective-permute-done.18
  31.1 0.1 add_convert_fusion
  31.2 1.5 %collective-permute-start.19 = (bf16[16,2880]{1,0:T(8,128)(2,1)S(1)}, bf16[16,2880]{1,0:T(8,128)(2,1)S(1)}, u32[]{:S(2)}, u32[]{:S(2)}) collective-permute-start(bf16[16,2880]{1,0:T(8,128)(2,1)S(1)} %get-tuple-element.33), channel_id=1, source_target_pairs={{0,2},{1,3},{2,0},{3,1},{4,6},{5,7},{6,4},{7,5},{8,10},{9,11},{10,... | collective-permute-start | bytes 276488 | tf_op jit(solution)/shard_map/ppermute | solution.py:239
  32.7 0.7 %collective-permute-start.21 = (bf16[16,2880]{1,0:T(8,128)(2,1)S(1)}, bf16[16,2880]{1,0:T(8,128)(2,1)S(1)}, u32[]{:S(2)}, u32[]{:S(2)}) collective-permute-start(bf16[16,2880]{1,0:T(8,128)(2,1)S(1)} %get-tuple-element.34), channel_id=1, source_target_pairs={{0,6},{1,7},{2,4},{3,5},{4,2},{5,3},{6,0},{7,1},{8,14},{9,15},{10,... | collective-permute-start | bytes 276488 | tf_op jit(solution)/shard_map/ppermute | solution.py:239
  33.4 0.0 collective-permute-done.15.refs_2_
  33.4 1.3 %collective-permute-start.20 = (bf16[16,2880]{1,0:T(8,128)(2,1)S(1)}, bf16[16,2880]{1,0:T(8,128)(2,1)S(1)}, u32[]{:S(2)}, u32[]{:S(2)}) collective-permute-start(bf16[16,2880]{1,0:T(8,128)(2,1)S(1)} %get-tuple-element.35), channel_id=1, source_target_pairs={{0,4},{1,5},{2,6},{3,7},{4,0},{5,1},{6,2},{7,3},{8,12},{9,13},{10,... | collective-permute-start | bytes 276488 | tf_op jit(solution)/shard_map/ppermute | solution.py:239
  34.8 5.3 %collective-permute-done.14.refs_1_ = bf16[16,2880]{1,0:T(8,128)(2,1)S(1)} collective-permute-done((bf16[16,2880]{1,0:T(8,128)(2,1)S(1)}, bf16[16,2880]{1,0:T(8,128)(2,1)S(1)}, u32[]{:S(2)}, u32[]{:S(2)}) %collective-permute-start.14) | collective-permute-done | bytes 92192 | tf_op jit(solution)/shard_map/ppermute | solution.py:239
  40.1 0.1 shard_map.78
  40.2 0.1 collective-permute-start.16
  40.3 0.2 slice_reduce_fusion.4
  40.5 0.6 %collective-permute-done.19 = bf16[16,2880]{1,0:T(8,128)(2,1)S(1)} collective-permute-done((bf16[16,2880]{1,0:T(8,128)(2,1)S(1)}, bf16[16,2880]{1,0:T(8,128)(2,1)S(1)}, u32[]{:S(2)}, u32[]{:S(2)}) %collective-permute-start.19) | collective-permute-done | bytes 92192 | tf_op jit(solution)/shard_map/ppermute | solution.py:239
  41.1 5.1 %collective-permute-done.16 = bf16[16,2880]{1,0:T(8,128)(2,1)S(1)} collective-permute-done((bf16[16,2880]{1,0:T(8,128)(2,1)S(1)}, bf16[16,2880]{1,0:T(8,128)(2,1)S(1)}, u32[]{:S(2)}, u32[]{:S(2)}) %collective-permute-start.16) | collective-permute-done | bytes 92192 | tf_op jit(solution)/shard_map/ppermute | solution.py:239
  46.2 0.8 %add_convert_fusion.2 = bf16[16,2880]{1,0:T(8,128)(2,1)} fusion(bf16[16,2880]{1,0:T(8,128)(2,1)S(1)} %collective-permute-done.21, bf16[16,2880]{1,0:T(8,128)(2,1)S(1)} %collective-permute-done.20, bf16[16,2880]{1,0:T(8,128)(2,1)S(1)} %collective-permute-done.19, bf16[16,2880]{1,0:T(8,128)(2,1)S(1)} %collective-permute-done.17, ...), kind=kLoop, calls=%fused_computation.2 | loop fusion | flops 875520 | bytes 737600 | tf_op jit(solution)/shard_map/convert_element_type | solution.py:279
  (13 shorter events, 0.1 us)
Async XLA Ops:
  0.0 9.8 %copy-start.1 = (f32[2880]{0:T(1024)S(1)}, f32[2880]{0:T(1024)}, u32[]{:S(2)}) copy-start(f32[2880]{0:T(1024)} %refs_8_.1) | copy-start | bytes 34564
  0.0 9.8 %collective-permute-start = (bf16[16,2880]{1,0:T(8,128)(2,1)}, bf16[16,2880]{1,0:T(8,128)(2,1)S(1)}, u32[]{:S(2)}, u32[]{:S(2)}) collective-permute-start(bf16[16,2880]{1,0:T(8,128)(2,1)} %refs_4_.1), channel_id=1, source_target_pairs={{0,8},{1,9},{2,10},{3,11},{4,12},{5,13},{6,14},{7,15},{8,0},{9,1},... | collective-permute-start | bytes 276488 | tf_op jit(solution)/shard_map/ppermute | solution.py:239
  4.0 8.6 %collective-permute-start.9 = (bf16[16,2880]{1,0:T(8,128)(2,1)}, bf16[16,2880]{1,0:T(8,128)(2,1)S(1)}, u32[]{:S(2)}, u32[]{:S(2)}) collective-permute-start(bf16[16,2880]{1,0:T(8,128)(2,1)} %refs_4_.1), channel_id=1, source_target_pairs={{0,4},{1,5},{2,6},{3,7},{4,0},{5,1},{6,2},{7,3},{8,12},{9,13},{10,... | collective-permute-start | bytes 276488 | tf_op jit(solution)/shard_map/ppermute | solution.py:239
  5.6 7.5 %collective-permute-start.8 = (bf16[16,2880]{1,0:T(8,128)(2,1)}, bf16[16,2880]{1,0:T(8,128)(2,1)S(1)}, u32[]{:S(2)}, u32[]{:S(2)}) collective-permute-start(bf16[16,2880]{1,0:T(8,128)(2,1)} %refs_4_.1), channel_id=1, source_target_pairs={{0,2},{1,3},{2,0},{3,1},{4,6},{5,7},{6,4},{7,5},{8,10},{9,11},{10,... | collective-permute-start | bytes 276488 | tf_op jit(solution)/shard_map/ppermute | solution.py:239
  7.1 6.5 %collective-permute-start.10 = (bf16[16,2880]{1,0:T(8,128)(2,1)}, bf16[16,2880]{1,0:T(8,128)(2,1)S(1)}, u32[]{:S(2)}, u32[]{:S(2)}) collective-permute-start(bf16[16,2880]{1,0:T(8,128)(2,1)} %refs_4_.1), channel_id=1, source_target_pairs={{0,6},{1,7},{2,4},{3,5},{4,2},{5,3},{6,0},{7,1},{8,14},{9,15},{10,... | collective-permute-start | bytes 276488 | tf_op jit(solution)/shard_map/ppermute | solution.py:239
  9.9 3.7 %collective-permute-start.1 = (bf16[16,2880]{1,0:T(8,128)(2,1)S(1)}, bf16[16,2880]{1,0:T(8,128)(2,1)S(1)}, u32[]{:S(2)}, u32[]{:S(2)}) collective-permute-start(bf16[16,2880]{1,0:T(8,128)(2,1)S(1)} %shard_map.74.refs_4_), channel_id=1, source_target_pairs={{0,1},{1,0},{2,3},{3,2},{4,5},{5,4},{6,7},{7,6},{8,9},{9,8},{10,11... | collective-permute-start | bytes 276488 | tf_op jit(solution)/shard_map/ppermute | solution.py:14
  10.0 7.2 %collective-permute-start.6 = (bf16[16,2880]{1,0:T(8,128)(2,1)S(1)}, bf16[16,2880]{1,0:T(8,128)(2,1)S(1)}, u32[]{:S(2)}, u32[]{:S(2)}) collective-permute-start(bf16[16,2880]{1,0:T(8,128)(2,1)S(1)} %shard_map.74.refs_4_), channel_id=1, source_target_pairs={{0,6},{1,7},{2,4},{3,5},{4,2},{5,3},{6,0},{7,1},{8,14},{9,15},{10,... | collective-permute-start | bytes 276488 | tf_op jit(solution)/shard_map/ppermute | solution.py:239
  12.6 5.5 %collective-permute-start.4 = (bf16[16,2880]{1,0:T(8,128)(2,1)S(1)}, bf16[16,2880]{1,0:T(8,128)(2,1)S(1)}, u32[]{:S(2)}, u32[]{:S(2)}) collective-permute-start(bf16[16,2880]{1,0:T(8,128)(2,1)S(1)} %shard_map.74.refs_4_), channel_id=1, source_target_pairs={{0,4},{1,5},{2,6},{3,7},{4,0},{5,1},{6,2},{7,3},{8,12},{9,13},{10,... | collective-permute-start | bytes 276488 | tf_op jit(solution)/shard_map/ppermute | solution.py:239
  13.1 5.0 %collective-permute-start.2 = (bf16[16,2880]{1,0:T(8,128)(2,1)S(1)}, bf16[16,2880]{1,0:T(8,128)(2,1)S(1)}, u32[]{:S(2)}, u32[]{:S(2)}) collective-permute-start(bf16[16,2880]{1,0:T(8,128)(2,1)S(1)} %shard_map.74.refs_4_), channel_id=1, source_target_pairs={{0,2},{1,3},{2,0},{3,1},{4,6},{5,7},{6,4},{7,5},{8,10},{9,11},{10,... | collective-permute-start | bytes 276488 | tf_op jit(solution)/shard_map/ppermute | solution.py:239
  13.7 4.5 %copy-start = (bf16[16,2880]{1,0:T(8,128)(2,1)S(1)}, bf16[16,2880]{1,0:T(8,128)(2,1)}, u32[]{:S(2)}) copy-start(bf16[16,2880]{1,0:T(8,128)(2,1)} %refs_4_.1) | copy-start | bytes 276484
  18.3 2.2 %collective-permute-start.11 = (bf16[64,2880]{1,0:T(8,128)(2,1)S(1)}, bf16[64,2880]{1,0:T(8,128)(2,1)S(1)}, u32[]{:S(2)}, u32[]{:S(2)}) collective-permute-start(bf16[64,2880]{1,0:T(8,128)(2,1)S(1)} %shard_map.76.refs_9_), channel_id=1, source_target_pairs={{0,1},{1,0},{2,3},{3,2},{4,5},{5,4},{6,7},{7,6},{8,9},{9,8},{10,11... | collective-permute-start | bytes 1105928 | tf_op jit(solution)/shard_map/ppermute | solution.py:14
  18.4 1.8 %collective-permute-start.7 = (bf16[16,2880]{1,0:T(8,128)(2,1)S(1)}, bf16[16,2880]{1,0:T(8,128)(2,1)S(1)}, u32[]{:S(2)}, u32[]{:S(2)}) collective-permute-start(bf16[16,2880]{1,0:T(8,128)(2,1)S(1)} %collective-permute-done.6.refs_3_.refs_7_), channel_id=1, source_target_pairs={{0,1},{1,0},{2,3},{3,2},{4,5},{5,4},{6,7},{7,6},{8,9},{9,8},{10,11... | collective-permute-start | bytes 276488 | tf_op jit(solution)/shard_map/ppermute | solution.py:14
  18.9 1.5 %collective-permute-start.5 = (bf16[16,2880]{1,0:T(8,128)(2,1)S(1)}, bf16[16,2880]{1,0:T(8,128)(2,1)S(1)}, u32[]{:S(2)}, u32[]{:S(2)}) collective-permute-start(bf16[16,2880]{1,0:T(8,128)(2,1)S(1)} %collective-permute-done.4.refs_2_.refs_6_), channel_id=1, source_target_pairs={{0,1},{1,0},{2,3},{3,2},{4,5},{5,4},{6,7},{7,6},{8,9},{9,8},{10,11... | collective-permute-start | bytes 276488 | tf_op jit(solution)/shard_map/ppermute | solution.py:14
  19.0 1.5 %collective-permute-start.3 = (bf16[16,2880]{1,0:T(8,128)(2,1)S(1)}, bf16[16,2880]{1,0:T(8,128)(2,1)S(1)}, u32[]{:S(2)}, u32[]{:S(2)}) collective-permute-start(bf16[16,2880]{1,0:T(8,128)(2,1)S(1)} %collective-permute-done.2.refs_1_.refs_5_), channel_id=1, source_target_pairs={{0,1},{1,0},{2,3},{3,2},{4,5},{5,4},{6,7},{7,6},{8,9},{9,8},{10,11... | collective-permute-start | bytes 276488 | tf_op jit(solution)/shard_map/ppermute | solution.py:14
  24.4 2.1 %collective-permute-start.13 = (bf16[64,2880]{1,0:T(8,128)(2,1)S(1)}, bf16[64,2880]{1,0:T(8,128)(2,1)S(1)}, u32[]{:S(2)}, u32[]{:S(2)}) collective-permute-start(bf16[64,2880]{1,0:T(8,128)(2,1)S(1)} %get-tuple-element.22), channel_id=1, source_target_pairs={{0,1},{1,0},{2,3},{3,2},{4,5},{5,4},{6,7},{7,6},{8,9},{9,8},{10,11... | collective-permute-start | bytes 1105928 | tf_op jit(solution)/shard_map/ppermute | solution.py:14
  24.9 7.8 %collective-permute-start.12 = (f32[16,4]{1,0:T(8,128)S(1)}, f32[16,4]{1,0:T(8,128)S(1)}, u32[]{:S(2)}, u32[]{:S(2)}) collective-permute-start(f32[16,4]{1,0:T(8,128)S(1)} %get-tuple-element.20), channel_id=1, source_target_pairs={{0,8},{1,9},{2,10},{3,11},{4,12},{5,13},{6,14},{7,15},{8,0},{9,1},... | collective-permute-start | bytes 776 | tf_op jit(solution)/shard_map/ppermute | solution.py:239
  26.5 4.6 %collective-permute-start.18 = (bf16[64,2880]{1,0:T(8,128)(2,1)S(1)}, bf16[64,2880]{1,0:T(8,128)(2,1)S(1)}, u32[]{:S(2)}, u32[]{:S(2)}) collective-permute-start(bf16[64,2880]{1,0:T(8,128)(2,1)S(1)} %get-tuple-element.24), channel_id=1, source_target_pairs={{0,1},{1,0},{2,3},{3,2},{4,5},{5,4},{6,7},{7,6},{8,9},{9,8},{10,11... | collective-permute-start | bytes 1105928 | tf_op jit(solution)/shard_map/ppermute | solution.py:14
  26.7 6.8 %collective-permute-start.15 = (bf16[16,2880]{1,0:T(8,128)(2,1)S(1)}, bf16[16,2880]{1,0:T(8,128)(2,1)S(1)}, u32[]{:S(2)}, u32[]{:S(2)}) collective-permute-start(bf16[16,2880]{1,0:T(8,128)(2,1)S(1)} %get-tuple-element.29), channel_id=1, source_target_pairs={{0,4},{1,5},{2,6},{3,7},{4,0},{5,1},{6,2},{7,3},{8,12},{9,13},{10,... | collective-permute-start | bytes 276488 | tf_op jit(solution)/shard_map/ppermute | solution.py:239
  28.5 12.0 %collective-permute-start.17 = (bf16[16,2880]{1,0:T(8,128)(2,1)S(1)}, bf16[16,2880]{1,0:T(8,128)(2,1)S(1)}, u32[]{:S(2)}, u32[]{:S(2)}) collective-permute-start(bf16[16,2880]{1,0:T(8,128)(2,1)S(1)} %get-tuple-element.30), channel_id=1, source_target_pairs={{0,14},{1,15},{2,12},{3,13},{4,10},{5,11},{6,8},{7,9},{8,6},{9,7},... | collective-permute-start | bytes 276488 | tf_op jit(solution)/shard_map/ppermute | solution.py:239
  30.5 9.6 %collective-permute-start.14 = (bf16[16,2880]{1,0:T(8,128)(2,1)S(1)}, bf16[16,2880]{1,0:T(8,128)(2,1)S(1)}, u32[]{:S(2)}, u32[]{:S(2)}) collective-permute-start(bf16[16,2880]{1,0:T(8,128)(2,1)S(1)} %get-tuple-element.31), channel_id=1, source_target_pairs={{0,2},{1,3},{2,0},{3,1},{4,6},{5,7},{6,4},{7,5},{8,10},{9,11},{10,... | collective-permute-start | bytes 276488 | tf_op jit(solution)/shard_map/ppermute | solution.py:239
  31.2 9.9 %collective-permute-start.19 = (bf16[16,2880]{1,0:T(8,128)(2,1)S(1)}, bf16[16,2880]{1,0:T(8,128)(2,1)S(1)}, u32[]{:S(2)}, u32[]{:S(2)}) collective-permute-start(bf16[16,2880]{1,0:T(8,128)(2,1)S(1)} %get-tuple-element.33), channel_id=1, source_target_pairs={{0,2},{1,3},{2,0},{3,1},{4,6},{5,7},{6,4},{7,5},{8,10},{9,11},{10,... | collective-permute-start | bytes 276488 | tf_op jit(solution)/shard_map/ppermute | solution.py:239
  32.7 8.4 %collective-permute-start.21 = (bf16[16,2880]{1,0:T(8,128)(2,1)S(1)}, bf16[16,2880]{1,0:T(8,128)(2,1)S(1)}, u32[]{:S(2)}, u32[]{:S(2)}) collective-permute-start(bf16[16,2880]{1,0:T(8,128)(2,1)S(1)} %get-tuple-element.34), channel_id=1, source_target_pairs={{0,6},{1,7},{2,4},{3,5},{4,2},{5,3},{6,0},{7,1},{8,14},{9,15},{10,... | collective-permute-start | bytes 276488 | tf_op jit(solution)/shard_map/ppermute | solution.py:239
  33.4 7.7 %collective-permute-start.20 = (bf16[16,2880]{1,0:T(8,128)(2,1)S(1)}, bf16[16,2880]{1,0:T(8,128)(2,1)S(1)}, u32[]{:S(2)}, u32[]{:S(2)}) collective-permute-start(bf16[16,2880]{1,0:T(8,128)(2,1)S(1)} %get-tuple-element.35), channel_id=1, source_target_pairs={{0,4},{1,5},{2,6},{3,7},{4,0},{5,1},{6,2},{7,3},{8,12},{9,13},{10,... | collective-permute-start | bytes 276488 | tf_op jit(solution)/shard_map/ppermute | solution.py:239
  40.2 5.9 %collective-permute-start.16 = (bf16[16,2880]{1,0:T(8,128)(2,1)S(1)}, bf16[16,2880]{1,0:T(8,128)(2,1)S(1)}, u32[]{:S(2)}, u32[]{:S(2)}) collective-permute-start(bf16[16,2880]{1,0:T(8,128)(2,1)S(1)} %shard_map.78), channel_id=1, source_target_pairs={{0,8},{1,9},{2,10},{3,11},{4,12},{5,13},{6,14},{7,15},{8,0},{9,1},... | collective-permute-start | bytes 276488 | tf_op jit(solution)/shard_map/ppermute | solution.py:239

commit v11 on v7

--- a/solution.py
+++ b/solution.py
@@ -128,9 +128,9 @@
     table_out_ref[...] = table_ref[...]
     normed = jnp.concatenate([group[...] for group in groups])
     across = (((1,), (1,)), ((), ()))
-    gate = lax.dot_general(normed, gate_ref[...], across, preferred_element_type=jnp.float32)
-    upper = lax.dot_general(normed, up_ref[...], across, preferred_element_type=jnp.float32)
-    act = (gate * jax.nn.sigmoid(1.702 * gate) * (upper + 1.0)).astype(jnp.bfloat16)
+    gate = lax.dot_general(gate_ref[...], normed, across, preferred_element_type=jnp.float32)
+    upper = lax.dot_general(up_ref[...], normed, across, preferred_element_type=jnp.float32)
+    act = (gate * jax.nn.sigmoid(1.702 * gate) * (upper + 1.0)).astype(jnp.bfloat16).T
     out = jnp.dot(act, down_ref[...], preferred_element_type=jnp.float32).astype(jnp.bfloat16)
     start = 0
     for out_ref in outs:
@@ -156,63 +156,35 @@
     )(*groups, gate_w, up_w, down_w, table)
 
 
-def read_kernel(after, *refs):
-    refs, sems = refs[after:-1], refs[-1]
-    sources, targets = refs[: len(refs) // 2], refs[len(refs) // 2 :]
-    copies = [
-        pltpu.make_async_copy(source, target, sems.at[i])
-        for i, (source, target) in enumerate(zip(sources, targets))
-    ]
+def table_kernel(chip_ref, ids_hbm, weights_hbm, gain_hbm, *refs):
+    near_ref, far_ref, gain_ref, ids_ref, weights_ref, sems = refs[-6:]
+    pairs = ((ids_hbm, ids_ref), (weights_hbm, weights_ref), (gain_hbm, gain_ref))
+    copies = [pltpu.make_async_copy(a, b, sems.at[i]) for i, (a, b) in enumerate(pairs)]
     for copy in copies:
         copy.start()
     for copy in copies:
         copy.wait()
-
-
-def read(arrays, after):
-    count = len(arrays)
-    vmem, hbm = pl.BlockSpec(memory_space=pltpu.VMEM), pl.BlockSpec(memory_space=pltpu.HBM)
-    return pl.pallas_call(
-        functools.partial(read_kernel, len(after)),
-        out_shape=tuple(pltpu.VMEM(a.shape, a.dtype) for a in arrays),
-        in_specs=[pl.BlockSpec(memory_space=pl.ANY)] * len(after) + [hbm] * count,
-        out_specs=(vmem,) * count,
-        scratch_shapes=[pltpu.SemaphoreType.DMA((count,))],
-        cost_estimate=pl.CostEstimate(
-            flops=0, bytes_accessed=2 * sum(a.size * a.dtype.itemsize for a in arrays), transcendentals=0
-        ),
-        compiler_params=pltpu.CompilerParams(vmem_limit_bytes=16 * 2**20),
-    )(*after, *(pltpu.with_memory_space_constraint(a, pltpu.HBM) for a in arrays))
-
-
-def load_kernel(chip_ref, ids_hbm, weights_hbm, source, near_ref, far_ref, target, ids_ref, weights_ref, sems):
-    copies = [
-        pltpu.make_async_copy(a, b, sems.at[i])
-        for i, (a, b) in enumerate(((ids_hbm, ids_ref), (weights_hbm, weights_ref), (source, target)))
-    ]
-    for copy in copies:
-        copy.start()
     chosen, rows = ids_ref.shape
     half = near_ref.shape[1]
     expert = chip_ref[0] ^ lax.broadcasted_iota(jnp.int32, (2 * half, rows), 0)
-    copies[0].wait()
-    copies[1].wait()
     table = jnp.zeros((2 * half, rows), jnp.float32)
     for k in range(chosen):
         table += jnp.where(ids_ref[k : k + 1, :] == expert, weights_ref[k : k + 1, :], 0.0)
     near_ref[...] = table[:half].T
     far_ref[...] = table[half:].T
-    copies[2].wait()
-
-
-def load(chip, expert_ids, expert_weights, half, array):
+
+
+def tables(chip, expert_ids, expert_weights, gain, half, beside):
     rows, chosen = expert_ids.shape
     vmem, hbm = pl.BlockSpec(memory_space=pltpu.VMEM), pl.BlockSpec(memory_space=pltpu.HBM)
     table = jax.ShapeDtypeStruct((rows, half), jnp.float32)
-    return pl.pallas_call(
-        load_kernel,
-        out_shape=(table, table, pltpu.VMEM(array.shape, array.dtype)),
-        in_specs=[pl.BlockSpec(memory_space=pltpu.SMEM), hbm, hbm, hbm],
+    in_hbm = [
+        pltpu.with_memory_space_constraint(a, pltpu.HBM) for a in (expert_ids.T, expert_weights.T, gain, *beside)
+    ]
+    return pl.pallas_call(
+        table_kernel,
+        out_shape=(table, table, jax.ShapeDtypeStruct(gain.shape, gain.dtype)),
+        in_specs=[pl.BlockSpec(memory_space=pltpu.SMEM)] + [hbm] * len(in_hbm),
         out_specs=(vmem,) * 3,
         scratch_shapes=[
             pltpu.VMEM((chosen, rows), expert_ids.dtype),
@@ -220,13 +192,10 @@
             pltpu.SemaphoreType.DMA((3,)),
         ],
         cost_estimate=pl.CostEstimate(
-            flops=0, bytes_accessed=2 * array.size * array.dtype.itemsize, transcendentals=0
+            flops=0, bytes_accessed=sum(a.size * a.dtype.itemsize for a in beside), transcendentals=0
         ),
-        compiler_params=pltpu.CompilerParams(vmem_limit_bytes=16 * 2**20),
-    )(
-        chip,
-        *(pltpu.with_memory_space_constraint(a, pltpu.HBM) for a in (expert_ids.T, expert_weights.T, array)),
-    )
+        compiler_params=pltpu.CompilerParams(vmem_limit_bytes=8 * 2**20),
+    )(chip, *in_hbm)
 
 
 def halves(residual, norm_gain, expert_ids, expert_weights, gate_proj, up_proj, down_proj):
@@ -245,19 +214,17 @@
     mirrored = across(x, half)
     near = [across(x, mask) for mask in range(1, half)]
     chip = (lax.axis_index("expert") // 2).reshape(1)
-    near_weights, far_weights, gate_w = load(chip, expert_ids, expert_weights, half, gate_proj[0].T)
-    (mirrored,) = pack(([mirrored],), norm_gain, (near_weights,))
+    held = (gate_proj[0].T, up_proj[0].T, down_proj[0])
+    near_weights, far_weights, gain = tables(chip, expert_ids, expert_weights, norm_gain, half, held)
+    (mirrored,) = pack(([mirrored],), gain, (near_weights,))
     far = [across(mirrored, mask) for mask in range(1, half)]
     mirror_swapped = swap(mirrored)
-    up_w, down_w = read((up_proj[0].T, down_proj[0]), (mirror_swapped, *near))
     far_swapped = [swap(block) for block in far]
-    (near_rows,) = pack(([x] + near,), norm_gain, (up_w, *far))
+    (near_rows,) = pack(([x] + near,), gain, (mirror_swapped, *far))
     *parts, far_weights = expert_parts(
         (mirror_swapped, *far_swapped, mirrored, *far, swap(near_rows), near_rows),
         (half * rows,) * 4,
-        gate_w,
-        up_w,
-        down_w,
+        *held,
         far_weights,
     )
     mirror_weights = across(far_weights, half)

time: 42.5 us -> 41.9 us (0.986)
  Pallas kernels: 10.2 us -> 5.25 us
  waiting for transfers between devices: 7.09 us -> 10.9 us
  starting transfers between devices: 23.7 us -> 24.3 us
    pallas_call x2 -> x1, Pallas kernels: 5.8 us -> 1 us  [tables(): pl.pallas_call(table_kernel, out_shape=(table, table, jax.ShapeDtypeStruc...]
    ppermute x15, waiting for transfers between devices: 6 us -> 9.83 us  [across(): return lax.ppermute(value, 'expert', pairs) if mask else value]
    ppermute x15, starting transfers between devices: 22.3 us -> 22.9 us  [across(): return lax.ppermute(value, 'expert', pairs) if mask else value]
  transfers between devices with their start and end apart: 22 -> 22, of which waited for: 8 -> 12; matrix products, arithmetic and copies ran while one was open for 1% -> 1% of each run, Pallas kernels for 14% -> 3%
where the time goes in v11:
time: 41.9 us; the launch traced here: 41.8 us
  starting transfers between devices  24.3 us (58%)
  waiting for transfers between devices  10.9 us (26%)
  Pallas kernels  5.25 us (13%)
  other arithmetic  0.98 us (2%)
    ppermute x15, starting transfers between devices, across(): return lax.ppermute(value, 'expert', pairs) if mask else value  22.9 us
    ppermute x15, waiting for transfers between devices, across(): return lax.ppermute(value, 'expert', pairs) if mask else value  9.83 us
    pallas_call x1, Pallas kernels, expert_parts(): pl.pallas_call(functools.partial(expert_kernel, count), out_shape=tuple((...  3.79 us
    ppermute x7, starting transfers between devices, partner(): return lax.ppermute(value, axis, pairs)  1.38 us
    ppermute x7, waiting for transfers between devices, partner(): return lax.ppermute(value, axis, pairs)  1.09 us
    pallas_call x1, Pallas kernels, tables(): pl.pallas_call(table_kernel, out_shape=(table, table, jax.ShapeDtypeStruc...  1 us
  transfers between devices with their start and end apart: 22, of which 12 were waited for; matrix products, arithmetic and copies ran while one was open for 1% of the time, Pallas kernels for 3%

profile of v11, /device:TPU:0, one launch (start us, length us, event | category | flops | bytes accessed | tf_op | source)
XLA Modules:
  0.0 41.8 jit_solution(8586476976224100461)
XLA Ops:
  0.0 4.0 %collective-permute-start = (bf16[16,2880]{1,0:T(8,128)(2,1)}, bf16[16,2880]{1,0:T(8,128)(2,1)S(1)}, u32[]{:S(2)}, u32[]{:S(2)}) collective-permute-start(bf16[16,2880]{1,0:T(8,128)(2,1)} %refs_4_.1), channel_id=1, source_target_pairs={{0,8},{1,9},{2,10},{3,11},{4,12},{5,13},{6,14},{7,15},{8,0},{9,1},... | collective-permute-start | bytes 276488 | tf_op jit(solution)/shard_map/ppermute | solution.py:208
  4.0 1.6 %collective-permute-start.9 = (bf16[16,2880]{1,0:T(8,128)(2,1)}, bf16[16,2880]{1,0:T(8,128)(2,1)S(1)}, u32[]{:S(2)}, u32[]{:S(2)}) collective-permute-start(bf16[16,2880]{1,0:T(8,128)(2,1)} %refs_4_.1), channel_id=1, source_target_pairs={{0,4},{1,5},{2,6},{3,7},{4,0},{5,1},{6,2},{7,3},{8,12},{9,13},{10,... | collective-permute-start | bytes 276488 | tf_op jit(solution)/shard_map/ppermute | solution.py:208
  5.6 1.5 %collective-permute-start.8 = (bf16[16,2880]{1,0:T(8,128)(2,1)}, bf16[16,2880]{1,0:T(8,128)(2,1)S(1)}, u32[]{:S(2)}, u32[]{:S(2)}) collective-permute-start(bf16[16,2880]{1,0:T(8,128)(2,1)} %refs_4_.1), channel_id=1, source_target_pairs={{0,2},{1,3},{2,0},{3,1},{4,6},{5,7},{6,4},{7,5},{8,10},{9,11},{10,... | collective-permute-start | bytes 276488 | tf_op jit(solution)/shard_map/ppermute | solution.py:208
  7.1 0.4 collective-permute-start.10
  7.5 1.0 %shard_map.73 = (f32[16,4]{1,0:T(8,128)S(1)}, f32[16,4]{1,0:T(8,128)S(1)}, f32[2880]{0:T(1024)S(1)}) custom-call(s32[1]{0:T(128)} %bitcast.chip_ref, s32[4,16]{1,0:T(4,128)} %bitcast.16, f32[4,16]{1,0:T(4,128)} %bitcast.17, f32[2880]{0:T(1024)} %gain_hbm.1, bf16[720,2880]{1,0:T(8,128)(2,1)} %bitcast.10, bf16[720,2880]{1,0:T(8,128)(2,1)} %bitcast.12, ...), custom_call_target="tpu_custom_call" | custom-call | bytes 12441600 | tf_op jit(solution)/shard_map/pallas_call | solution.py:184
  8.5 0.2 collective-permute-done.refs_1_
  8.8 0.1 shard_map.74.refs_4_
  8.9 2.4 %collective-permute-start.6 = (bf16[16,2880]{1,0:T(8,128)(2,1)S(1)}, bf16[16,2880]{1,0:T(8,128)(2,1)S(1)}, u32[]{:S(2)}, u32[]{:S(2)}) collective-permute-start(bf16[16,2880]{1,0:T(8,128)(2,1)S(1)} %shard_map.74.refs_4_), channel_id=1, source_target_pairs={{0,6},{1,7},{2,4},{3,5},{4,2},{5,3},{6,0},{7,1},{8,14},{9,15},{10,... | collective-permute-start | bytes 276488 | tf_op jit(solution)/shard_map/ppermute | solution.py:208
  11.3 0.8 %collective-permute-start.4 = (bf16[16,2880]{1,0:T(8,128)(2,1)S(1)}, bf16[16,2880]{1,0:T(8,128)(2,1)S(1)}, u32[]{:S(2)}, u32[]{:S(2)}) collective-permute-start(bf16[16,2880]{1,0:T(8,128)(2,1)S(1)} %shard_map.74.refs_4_), channel_id=1, source_target_pairs={{0,4},{1,5},{2,6},{3,7},{4,0},{5,1},{6,2},{7,3},{8,12},{9,13},{10,... | collective-permute-start | bytes 276488 | tf_op jit(solution)/shard_map/ppermute | solution.py:208
  12.1 0.0 collective-permute-done.9.refs_6_
  12.1 0.4 collective-permute-start.2
  12.5 0.0 collective-permute-start.1
  12.5 1.4 %collective-permute-done.10.refs_7_ = bf16[16,2880]{1,0:T(8,128)(2,1)S(1)} collective-permute-done((bf16[16,2880]{1,0:T(8,128)(2,1)}, bf16[16,2880]{1,0:T(8,128)(2,1)S(1)}, u32[]{:S(2)}, u32[]{:S(2)}) %collective-permute-start.10) | collective-permute-done | bytes 92192 | tf_op jit(solution)/shard_map/ppermute | solution.py:208
  13.9 2.0 %collective-permute-done.6.refs_3_.refs_7_ = bf16[16,2880]{1,0:T(8,128)(2,1)S(1)} collective-permute-done((bf16[16,2880]{1,0:T(8,128)(2,1)S(1)}, bf16[16,2880]{1,0:T(8,128)(2,1)S(1)}, u32[]{:S(2)}, u32[]{:S(2)}) %collective-permute-start.6) | collective-permute-done | bytes 92192 | tf_op jit(solution)/shard_map/ppermute | solution.py:208
  15.8 0.5 %collective-permute-done.4.refs_2_.refs_6_ = bf16[16,2880]{1,0:T(8,128)(2,1)S(1)} collective-permute-done((bf16[16,2880]{1,0:T(8,128)(2,1)S(1)}, bf16[16,2880]{1,0:T(8,128)(2,1)S(1)}, u32[]{:S(2)}, u32[]{:S(2)}) %collective-permute-start.4) | collective-permute-done | bytes 92192 | tf_op jit(solution)/shard_map/ppermute | solution.py:208
  16.3 0.6 %collective-permute-done.2.refs_1_.refs_5_ = bf16[16,2880]{1,0:T(8,128)(2,1)S(1)} collective-permute-done((bf16[16,2880]{1,0:T(8,128)(2,1)S(1)}, bf16[16,2880]{1,0:T(8,128)(2,1)S(1)}, u32[]{:S(2)}, u32[]{:S(2)}) %collective-permute-start.2) | collective-permute-done | bytes 92192 | tf_op jit(solution)/shard_map/ppermute | solution.py:208
  16.8 0.0 collective-permute-done.1.refs_0_
  16.9 0.2 shard_map.75.refs_9_
  17.1 0.1 collective-permute-start.11
  17.1 0.5 %collective-permute-start.7 = (bf16[16,2880]{1,0:T(8,128)(2,1)S(1)}, bf16[16,2880]{1,0:T(8,128)(2,1)S(1)}, u32[]{:S(2)}, u32[]{:S(2)}) collective-permute-start(bf16[16,2880]{1,0:T(8,128)(2,1)S(1)} %collective-permute-done.6.refs_3_.refs_7_), channel_id=1, source_target_pairs={{0,1},{1,0},{2,3},{3,2},{4,5},{5,4},{6,7},{7,6},{8,9},{9,8},{10,11... | collective-permute-start | bytes 276488 | tf_op jit(solution)/shard_map/ppermute | solution.py:14
  17.6 0.1 collective-permute-start.5
  17.7 0.4 %collective-permute-start.3 = (bf16[16,2880]{1,0:T(8,128)(2,1)S(1)}, bf16[16,2880]{1,0:T(8,128)(2,1)S(1)}, u32[]{:S(2)}, u32[]{:S(2)}) collective-permute-start(bf16[16,2880]{1,0:T(8,128)(2,1)S(1)} %collective-permute-done.2.refs_1_.refs_5_), channel_id=1, source_target_pairs={{0,1},{1,0},{2,3},{3,2},{4,5},{5,4},{6,7},{7,6},{8,9},{9,8},{10,11... | collective-permute-start | bytes 276488 | tf_op jit(solution)/shard_map/ppermute | solution.py:14
  18.1 0.8 %collective-permute-done.7.refs_3_ = bf16[16,2880]{1,0:T(8,128)(2,1)S(1)} collective-permute-done((bf16[16,2880]{1,0:T(8,128)(2,1)S(1)}, bf16[16,2880]{1,0:T(8,128)(2,1)S(1)}, u32[]{:S(2)}, u32[]{:S(2)}) %collective-permute-start.7) | collective-permute-done | bytes 92192 | tf_op jit(solution)/shard_map/ppermute | solution.py:14
  19.0 0.1 collective-permute-done.5.refs_2_
  19.1 0.1 collective-permute-done.3.refs_1_
  19.2 3.8 %shard_map.76 = (bf16[64,2880]{1,0:T(8,128)(2,1)S(1)}, bf16[64,2880]{1,0:T(8,128)(2,1)S(1)}, bf16[64,2880]{1,0:T(8,128)(2,1)S(1)}, bf16[64,2880]{1,0:T(8,128)(2,1)S(1)}, f32[16,4]{1,0:T(8,128)S(1)}) custom-call(bf16[16,2880]{1,0:T(8,128)(2,1)S(1)} %collective-permute-done.1.refs_0_, bf16[16,2880]{1,0:T(8,128)(2,1)S(1)} %collective-permute-done.3.refs_1_, ...), custom_call_target="tpu_custom_call" | custom-call | flops 3185049600 | bytes 12441600 | tf_op jit(solution)/shard_map/pallas_call | solution.py:146
  23.0 0.3 collective-permute-start.13
  23.3 2.3 %collective-permute-start.12 = (f32[16,4]{1,0:T(8,128)S(1)}, f32[16,4]{1,0:T(8,128)S(1)}, u32[]{:S(2)}, u32[]{:S(2)}) collective-permute-start(f32[16,4]{1,0:T(8,128)S(1)} %get-tuple-element.16), channel_id=1, source_target_pairs={{0,8},{1,9},{2,10},{3,11},{4,12},{5,13},{6,14},{7,15},{8,0},{9,1},... | collective-permute-start | bytes 776 | tf_op jit(solution)/shard_map/ppermute | solution.py:208
  25.6 0.0 collective-permute-start.18
  25.7 0.1 add_convert_fusion.1
  25.8 2.7 %collective-permute-start.16 = (bf16[16,2880]{1,0:T(8,128)(2,1)S(1)}, bf16[16,2880]{1,0:T(8,128)(2,1)S(1)}, u32[]{:S(2)}, u32[]{:S(2)}) collective-permute-start(bf16[16,2880]{1,0:T(8,128)(2,1)S(1)} %get-tuple-element.25), channel_id=1, source_target_pairs={{0,6},{1,7},{2,4},{3,5},{4,2},{5,3},{6,0},{7,1},{8,14},{9,15},{10,... | collective-permute-start | bytes 276488 | tf_op jit(solution)/shard_map/ppermute | solution.py:208
  28.5 0.0 collective-permute-start.15
  28.5 0.9 %collective-permute-start.14 = (bf16[16,2880]{1,0:T(8,128)(2,1)S(1)}, bf16[16,2880]{1,0:T(8,128)(2,1)S(1)}, u32[]{:S(2)}, u32[]{:S(2)}) collective-permute-start(bf16[16,2880]{1,0:T(8,128)(2,1)S(1)} %get-tuple-element.27), channel_id=1, source_target_pairs={{0,2},{1,3},{2,0},{3,1},{4,6},{5,7},{6,4},{7,5},{8,10},{9,11},{10,... | collective-permute-start | bytes 276488 | tf_op jit(solution)/shard_map/ppermute | solution.py:208
  29.4 0.0 collective-permute-done.18
  29.4 0.1 add_convert_fusion
  29.5 1.2 %collective-permute-start.19 = (bf16[16,2880]{1,0:T(8,128)(2,1)S(1)}, bf16[16,2880]{1,0:T(8,128)(2,1)S(1)}, u32[]{:S(2)}, u32[]{:S(2)}) collective-permute-start(bf16[16,2880]{1,0:T(8,128)(2,1)S(1)} %get-tuple-element.29), channel_id=1, source_target_pairs={{0,2},{1,3},{2,0},{3,1},{4,6},{5,7},{6,4},{7,5},{8,10},{9,11},{10,... | collective-permute-start | bytes 276488 | tf_op jit(solution)/shard_map/ppermute | solution.py:208
  30.7 0.0 collective-permute-done.12.table_ref
  30.7 2.2 %collective-permute-start.21 = (bf16[16,2880]{1,0:T(8,128)(2,1)S(1)}, bf16[16,2880]{1,0:T(8,128)(2,1)S(1)}, u32[]{:S(2)}, u32[]{:S(2)}) collective-permute-start(bf16[16,2880]{1,0:T(8,128)(2,1)S(1)} %get-tuple-element.30), channel_id=1, source_target_pairs={{0,6},{1,7},{2,4},{3,5},{4,2},{5,3},{6,0},{7,1},{8,14},{9,15},{10,... | collective-permute-start | bytes 276488 | tf_op jit(solution)/shard_map/ppermute | solution.py:208
  32.9 0.0 collective-permute-done.16.refs_3_
  32.9 1.2 %collective-permute-start.20 = (bf16[16,2880]{1,0:T(8,128)(2,1)S(1)}, bf16[16,2880]{1,0:T(8,128)(2,1)S(1)}, u32[]{:S(2)}, u32[]{:S(2)}) collective-permute-start(bf16[16,2880]{1,0:T(8,128)(2,1)S(1)} %get-tuple-element.31), channel_id=1, source_target_pairs={{0,4},{1,5},{2,6},{3,7},{4,0},{5,1},{6,2},{7,3},{8,12},{9,13},{10,... | collective-permute-start | bytes 276488 | tf_op jit(solution)/shard_map/ppermute | solution.py:208
  34.1 1.2 %collective-permute-done.14.refs_1_ = bf16[16,2880]{1,0:T(8,128)(2,1)S(1)} collective-permute-done((bf16[16,2880]{1,0:T(8,128)(2,1)S(1)}, bf16[16,2880]{1,0:T(8,128)(2,1)S(1)}, u32[]{:S(2)}, u32[]{:S(2)}) %collective-permute-start.14) | collective-permute-done | bytes 92192 | tf_op jit(solution)/shard_map/ppermute | solution.py:208
  35.3 0.1 shard_map.77
  35.5 1.3 %collective-permute-start.17 = (bf16[16,2880]{1,0:T(8,128)(2,1)S(1)}, bf16[16,2880]{1,0:T(8,128)(2,1)S(1)}, u32[]{:S(2)}, u32[]{:S(2)}) collective-permute-start(bf16[16,2880]{1,0:T(8,128)(2,1)S(1)} %shard_map.77), channel_id=1, source_target_pairs={{0,8},{1,9},{2,10},{3,11},{4,12},{5,13},{6,14},{7,15},{8,0},{9,1},... | collective-permute-start | bytes 276488 | tf_op jit(solution)/shard_map/ppermute | solution.py:208
  36.7 0.2 slice_reduce_fusion.3
  37.0 1.0 %collective-permute-done.19 = bf16[16,2880]{1,0:T(8,128)(2,1)S(1)} collective-permute-done((bf16[16,2880]{1,0:T(8,128)(2,1)S(1)}, bf16[16,2880]{1,0:T(8,128)(2,1)S(1)}, u32[]{:S(2)}, u32[]{:S(2)}) %collective-permute-start.19) | collective-permute-done | bytes 92192 | tf_op jit(solution)/shard_map/ppermute | solution.py:208
  37.9 0.7 %collective-permute-done.20 = bf16[16,2880]{1,0:T(8,128)(2,1)S(1)} collective-permute-done((bf16[16,2880]{1,0:T(8,128)(2,1)S(1)}, bf16[16,2880]{1,0:T(8,128)(2,1)S(1)}, u32[]{:S(2)}, u32[]{:S(2)}) %collective-permute-start.20) | collective-permute-done | bytes 92192 | tf_op jit(solution)/shard_map/ppermute | solution.py:208
  38.6 2.4 %collective-permute-done.17 = bf16[16,2880]{1,0:T(8,128)(2,1)S(1)} collective-permute-done((bf16[16,2880]{1,0:T(8,128)(2,1)S(1)}, bf16[16,2880]{1,0:T(8,128)(2,1)S(1)}, u32[]{:S(2)}, u32[]{:S(2)}) %collective-permute-start.17) | collective-permute-done | bytes 92192 | tf_op jit(solution)/shard_map/ppermute | solution.py:208
  41.0 0.8 %add_convert_fusion.2 = bf16[16,2880]{1,0:T(8,128)(2,1)} fusion(bf16[16,2880]{1,0:T(8,128)(2,1)S(1)} %collective-permute-done.21, bf16[16,2880]{1,0:T(8,128)(2,1)S(1)} %collective-permute-done.20, bf16[16,2880]{1,0:T(8,128)(2,1)S(1)} %collective-permute-done.19, bf16[16,2880]{1,0:T(8,128)(2,1)S(1)} %collective-permute-done.17, ...), kind=kLoop, calls=%fused_computation.2 | loop fusion | flops 737280 | bytes 645376 | tf_op jit(solution)/shard_map/convert_element_type | solution.py:241
  (15 shorter events, 0.1 us)
Async XLA Ops:
  0.0 8.8 %collective-permute-start = (bf16[16,2880]{1,0:T(8,128)(2,1)}, bf16[16,2880]{1,0:T(8,128)(2,1)S(1)}, u32[]{:S(2)}, u32[]{:S(2)}) collective-permute-start(bf16[16,2880]{1,0:T(8,128)(2,1)} %refs_4_.1), channel_id=1, source_target_pairs={{0,8},{1,9},{2,10},{3,11},{4,12},{5,13},{6,14},{7,15},{8,0},{9,1},... | collective-permute-start | bytes 276488 | tf_op jit(solution)/shard_map/ppermute | solution.py:208
  4.0 8.0 %collective-permute-start.9 = (bf16[16,2880]{1,0:T(8,128)(2,1)}, bf16[16,2880]{1,0:T(8,128)(2,1)S(1)}, u32[]{:S(2)}, u32[]{:S(2)}) collective-permute-start(bf16[16,2880]{1,0:T(8,128)(2,1)} %refs_4_.1), channel_id=1, source_target_pairs={{0,4},{1,5},{2,6},{3,7},{4,0},{5,1},{6,2},{7,3},{8,12},{9,13},{10,... | collective-permute-start | bytes 276488 | tf_op jit(solution)/shard_map/ppermute | solution.py:208
  5.6 6.8 %collective-permute-start.8 = (bf16[16,2880]{1,0:T(8,128)(2,1)}, bf16[16,2880]{1,0:T(8,128)(2,1)S(1)}, u32[]{:S(2)}, u32[]{:S(2)}) collective-permute-start(bf16[16,2880]{1,0:T(8,128)(2,1)} %refs_4_.1), channel_id=1, source_target_pairs={{0,2},{1,3},{2,0},{3,1},{4,6},{5,7},{6,4},{7,5},{8,10},{9,11},{10,... | collective-permute-start | bytes 276488 | tf_op jit(solution)/shard_map/ppermute | solution.py:208
  7.1 6.7 %collective-permute-start.10 = (bf16[16,2880]{1,0:T(8,128)(2,1)}, bf16[16,2880]{1,0:T(8,128)(2,1)S(1)}, u32[]{:S(2)}, u32[]{:S(2)}) collective-permute-start(bf16[16,2880]{1,0:T(8,128)(2,1)} %refs_4_.1), channel_id=1, source_target_pairs={{0,6},{1,7},{2,4},{3,5},{4,2},{5,3},{6,0},{7,1},{8,14},{9,15},{10,... | collective-permute-start | bytes 276488 | tf_op jit(solution)/shard_map/ppermute | solution.py:208
  7.5 9.3 %copy-start.3 = (bf16[16,2880]{1,0:T(8,128)(2,1)S(1)}, bf16[16,2880]{1,0:T(8,128)(2,1)}, u32[]{:S(2)}) copy-start(bf16[16,2880]{1,0:T(8,128)(2,1)} %refs_4_.1) | copy-start | bytes 276484
  7.5 11.7 %copy-start = (bf16[1,2880,720]{1,2,0:T(8,128)(2,1)S(1)}, bf16[1,2880,720]{1,2,0:T(8,128)(2,1)}, u32[]{:S(2)}) copy-start(bf16[1,2880,720]{1,2,0:T(8,128)(2,1)} %param.11) | copy-start | bytes 12441604
  7.5 11.7 %copy-start.1 = (bf16[1,2880,720]{1,2,0:T(8,128)(2,1)S(1)}, bf16[1,2880,720]{1,2,0:T(8,128)(2,1)}, u32[]{:S(2)}) copy-start(bf16[1,2880,720]{1,2,0:T(8,128)(2,1)} %param.12) | copy-start | bytes 12441604
  7.5 11.7 %copy-start.2 = (bf16[1,720,2880]{2,1,0:T(8,128)(2,1)S(1)}, bf16[1,720,2880]{2,1,0:T(8,128)(2,1)}, u32[]{:S(2)}) copy-start(bf16[1,720,2880]{2,1,0:T(8,128)(2,1)} %param.13) | copy-start | bytes 12441604
  8.9 6.9 %collective-permute-start.6 = (bf16[16,2880]{1,0:T(8,128)(2,1)S(1)}, bf16[16,2880]{1,0:T(8,128)(2,1)S(1)}, u32[]{:S(2)}, u32[]{:S(2)}) collective-permute-start(bf16[16,2880]{1,0:T(8,128)(2,1)S(1)} %shard_map.74.refs_4_), channel_id=1, source_target_pairs={{0,6},{1,7},{2,4},{3,5},{4,2},{5,3},{6,0},{7,1},{8,14},{9,15},{10,... | collective-permute-start | bytes 276488 | tf_op jit(solution)/shard_map/ppermute | solution.py:208
  11.3 5.0 %collective-permute-start.4 = (bf16[16,2880]{1,0:T(8,128)(2,1)S(1)}, bf16[16,2880]{1,0:T(8,128)(2,1)S(1)}, u32[]{:S(2)}, u32[]{:S(2)}) collective-permute-start(bf16[16,2880]{1,0:T(8,128)(2,1)S(1)} %shard_map.74.refs_4_), channel_id=1, source_target_pairs={{0,4},{1,5},{2,6},{3,7},{4,0},{5,1},{6,2},{7,3},{8,12},{9,13},{10,... | collective-permute-start | bytes 276488 | tf_op jit(solution)/shard_map/ppermute | solution.py:208
  12.1 4.8 %collective-permute-start.2 = (bf16[16,2880]{1,0:T(8,128)(2,1)S(1)}, bf16[16,2880]{1,0:T(8,128)(2,1)S(1)}, u32[]{:S(2)}, u32[]{:S(2)}) collective-permute-start(bf16[16,2880]{1,0:T(8,128)(2,1)S(1)} %shard_map.74.refs_4_), channel_id=1, source_target_pairs={{0,2},{1,3},{2,0},{3,1},{4,6},{5,7},{6,4},{7,5},{8,10},{9,11},{10,... | collective-permute-start | bytes 276488 | tf_op jit(solution)/shard_map/ppermute | solution.py:208
  12.5 4.4 %collective-permute-start.1 = (bf16[16,2880]{1,0:T(8,128)(2,1)S(1)}, bf16[16,2880]{1,0:T(8,128)(2,1)S(1)}, u32[]{:S(2)}, u32[]{:S(2)}) collective-permute-start(bf16[16,2880]{1,0:T(8,128)(2,1)S(1)} %shard_map.74.refs_4_), channel_id=1, source_target_pairs={{0,1},{1,0},{2,3},{3,2},{4,5},{5,4},{6,7},{7,6},{8,9},{9,8},{10,11... | collective-permute-start | bytes 276488 | tf_op jit(solution)/shard_map/ppermute | solution.py:14
  17.1 2.2 %collective-permute-start.11 = (bf16[64,2880]{1,0:T(8,128)(2,1)S(1)}, bf16[64,2880]{1,0:T(8,128)(2,1)S(1)}, u32[]{:S(2)}, u32[]{:S(2)}) collective-permute-start(bf16[64,2880]{1,0:T(8,128)(2,1)S(1)} %shard_map.75.refs_9_), channel_id=1, source_target_pairs={{0,1},{1,0},{2,3},{3,2},{4,5},{5,4},{6,7},{7,6},{8,9},{9,8},{10,11... | collective-permute-start | bytes 1105928 | tf_op jit(solution)/shard_map/ppermute | solution.py:14
  17.1 1.8 %collective-permute-start.7 = (bf16[16,2880]{1,0:T(8,128)(2,1)S(1)}, bf16[16,2880]{1,0:T(8,128)(2,1)S(1)}, u32[]{:S(2)}, u32[]{:S(2)}) collective-permute-start(bf16[16,2880]{1,0:T(8,128)(2,1)S(1)} %collective-permute-done.6.refs_3_.refs_7_), channel_id=1, source_target_pairs={{0,1},{1,0},{2,3},{3,2},{4,5},{5,4},{6,7},{7,6},{8,9},{9,8},{10,11... | collective-permute-start | bytes 276488 | tf_op jit(solution)/shard_map/ppermute | solution.py:14
  17.6 1.5 %collective-permute-start.5 = (bf16[16,2880]{1,0:T(8,128)(2,1)S(1)}, bf16[16,2880]{1,0:T(8,128)(2,1)S(1)}, u32[]{:S(2)}, u32[]{:S(2)}) collective-permute-start(bf16[16,2880]{1,0:T(8,128)(2,1)S(1)} %collective-permute-done.4.refs_2_.refs_6_), channel_id=1, source_target_pairs={{0,1},{1,0},{2,3},{3,2},{4,5},{5,4},{6,7},{7,6},{8,9},{9,8},{10,11... | collective-permute-start | bytes 276488 | tf_op jit(solution)/shard_map/ppermute | solution.py:14
  17.7 1.5 %collective-permute-start.3 = (bf16[16,2880]{1,0:T(8,128)(2,1)S(1)}, bf16[16,2880]{1,0:T(8,128)(2,1)S(1)}, u32[]{:S(2)}, u32[]{:S(2)}) collective-permute-start(bf16[16,2880]{1,0:T(8,128)(2,1)S(1)} %collective-permute-done.2.refs_1_.refs_5_), channel_id=1, source_target_pairs={{0,1},{1,0},{2,3},{3,2},{4,5},{5,4},{6,7},{7,6},{8,9},{9,8},{10,11... | collective-permute-start | bytes 276488 | tf_op jit(solution)/shard_map/ppermute | solution.py:14
  23.0 2.6 %collective-permute-start.13 = (bf16[64,2880]{1,0:T(8,128)(2,1)S(1)}, bf16[64,2880]{1,0:T(8,128)(2,1)S(1)}, u32[]{:S(2)}, u32[]{:S(2)}) collective-permute-start(bf16[64,2880]{1,0:T(8,128)(2,1)S(1)} %get-tuple-element.18), channel_id=1, source_target_pairs={{0,1},{1,0},{2,3},{3,2},{4,5},{5,4},{6,7},{7,6},{8,9},{9,8},{10,11... | collective-permute-start | bytes 1105928 | tf_op jit(solution)/shard_map/ppermute | solution.py:14
  23.3 7.4 %collective-permute-start.12 = (f32[16,4]{1,0:T(8,128)S(1)}, f32[16,4]{1,0:T(8,128)S(1)}, u32[]{:S(2)}, u32[]{:S(2)}) collective-permute-start(f32[16,4]{1,0:T(8,128)S(1)} %get-tuple-element.16), channel_id=1, source_target_pairs={{0,8},{1,9},{2,10},{3,11},{4,12},{5,13},{6,14},{7,15},{8,0},{9,1},... | collective-permute-start | bytes 776 | tf_op jit(solution)/shard_map/ppermute | solution.py:208
  25.6 3.7 %collective-permute-start.18 = (bf16[64,2880]{1,0:T(8,128)(2,1)S(1)}, bf16[64,2880]{1,0:T(8,128)(2,1)S(1)}, u32[]{:S(2)}, u32[]{:S(2)}) collective-permute-start(bf16[64,2880]{1,0:T(8,128)(2,1)S(1)} %get-tuple-element.20), channel_id=1, source_target_pairs={{0,1},{1,0},{2,3},{3,2},{4,5},{5,4},{6,7},{7,6},{8,9},{9,8},{10,11... | collective-permute-start | bytes 1105928 | tf_op jit(solution)/shard_map/ppermute | solution.py:14
  25.8 7.1 %collective-permute-start.16 = (bf16[16,2880]{1,0:T(8,128)(2,1)S(1)}, bf16[16,2880]{1,0:T(8,128)(2,1)S(1)}, u32[]{:S(2)}, u32[]{:S(2)}) collective-permute-start(bf16[16,2880]{1,0:T(8,128)(2,1)S(1)} %get-tuple-element.25), channel_id=1, source_target_pairs={{0,6},{1,7},{2,4},{3,5},{4,2},{5,3},{6,0},{7,1},{8,14},{9,15},{10,... | collective-permute-start | bytes 276488 | tf_op jit(solution)/shard_map/ppermute | solution.py:208
  28.5 5.7 %collective-permute-start.15 = (bf16[16,2880]{1,0:T(8,128)(2,1)S(1)}, bf16[16,2880]{1,0:T(8,128)(2,1)S(1)}, u32[]{:S(2)}, u32[]{:S(2)}) collective-permute-start(bf16[16,2880]{1,0:T(8,128)(2,1)S(1)} %get-tuple-element.26), channel_id=1, source_target_pairs={{0,4},{1,5},{2,6},{3,7},{4,0},{5,1},{6,2},{7,3},{8,12},{9,13},{10,... | collective-permute-start | bytes 276488 | tf_op jit(solution)/shard_map/ppermute | solution.py:208
  28.5 6.9 %collective-permute-start.14 = (bf16[16,2880]{1,0:T(8,128)(2,1)S(1)}, bf16[16,2880]{1,0:T(8,128)(2,1)S(1)}, u32[]{:S(2)}, u32[]{:S(2)}) collective-permute-start(bf16[16,2880]{1,0:T(8,128)(2,1)S(1)} %get-tuple-element.27), channel_id=1, source_target_pairs={{0,2},{1,3},{2,0},{3,1},{4,6},{5,7},{6,4},{7,5},{8,10},{9,11},{10,... | collective-permute-start | bytes 276488 | tf_op jit(solution)/shard_map/ppermute | solution.py:208
  29.5 8.4 %collective-permute-start.19 = (bf16[16,2880]{1,0:T(8,128)(2,1)S(1)}, bf16[16,2880]{1,0:T(8,128)(2,1)S(1)}, u32[]{:S(2)}, u32[]{:S(2)}) collective-permute-start(bf16[16,2880]{1,0:T(8,128)(2,1)S(1)} %get-tuple-element.29), channel_id=1, source_target_pairs={{0,2},{1,3},{2,0},{3,1},{4,6},{5,7},{6,4},{7,5},{8,10},{9,11},{10,... | collective-permute-start | bytes 276488 | tf_op jit(solution)/shard_map/ppermute | solution.py:208
  30.7 7.2 %collective-permute-start.21 = (bf16[16,2880]{1,0:T(8,128)(2,1)S(1)}, bf16[16,2880]{1,0:T(8,128)(2,1)S(1)}, u32[]{:S(2)}, u32[]{:S(2)}) collective-permute-start(bf16[16,2880]{1,0:T(8,128)(2,1)S(1)} %get-tuple-element.30), channel_id=1, source_target_pairs={{0,6},{1,7},{2,4},{3,5},{4,2},{5,3},{6,0},{7,1},{8,14},{9,15},{10,... | collective-permute-start | bytes 276488 | tf_op jit(solution)/shard_map/ppermute | solution.py:208
  32.9 5.7 %collective-permute-start.20 = (bf16[16,2880]{1,0:T(8,128)(2,1)S(1)}, bf16[16,2880]{1,0:T(8,128)(2,1)S(1)}, u32[]{:S(2)}, u32[]{:S(2)}) collective-permute-start(bf16[16,2880]{1,0:T(8,128)(2,1)S(1)} %get-tuple-element.31), channel_id=1, source_target_pairs={{0,4},{1,5},{2,6},{3,7},{4,0},{5,1},{6,2},{7,3},{8,12},{9,13},{10,... | collective-permute-start | bytes 276488 | tf_op jit(solution)/shard_map/ppermute | solution.py:208
  35.5 5.5 %collective-permute-start.17 = (bf16[16,2880]{1,0:T(8,128)(2,1)S(1)}, bf16[16,2880]{1,0:T(8,128)(2,1)S(1)}, u32[]{:S(2)}, u32[]{:S(2)}) collective-permute-start(bf16[16,2880]{1,0:T(8,128)(2,1)S(1)} %shard_map.77), channel_id=1, source_target_pairs={{0,8},{1,9},{2,10},{3,11},{4,12},{5,13},{6,14},{7,15},{8,0},{9,1},... | collective-permute-start | bytes 276488 | tf_op jit(solution)/shard_map/ppermute | solution.py:208

commit v12 on v11

--- a/solution.py
+++ b/solution.py
@@ -212,7 +212,8 @@
 
     x = residual
     mirrored = across(x, half)
-    near = [across(x, mask) for mask in range(1, half)]
+    order = [0] + sorted(range(1, half), key=lambda mask: (mask == half // 2, mask % 2 == 0, mask))
+    near = [across(x, mask) for mask in order[1:]]
     chip = (lax.axis_index("expert") // 2).reshape(1)
     held = (gate_proj[0].T, up_proj[0].T, down_proj[0])
     near_weights, far_weights, gain = tables(chip, expert_ids, expert_weights, norm_gain, half, held)
@@ -229,12 +230,13 @@
     )
     mirror_weights = across(far_weights, half)
 
-    def give_back(done):
+    def give_back(done, masks):
         done = done.reshape(half, rows, model)
-        return [across(done[mask], mask) for mask in range(half)]
-
-    far_blocks = give_back(pair_sum(parts[1], swap(parts[0])))
-    near_blocks = give_back(pair_sum(parts[3], swap(parts[2])))
+        blocks = [across(done[i], mask) for i, mask in enumerate(masks)]
+        return [blocks[masks.index(mask)] for mask in range(half)]
+
+    far_blocks = give_back(pair_sum(parts[1], swap(parts[0])), list(range(half)))
+    near_blocks = give_back(pair_sum(parts[3], swap(parts[2])), order)
     total = x.astype(jnp.float32) + across(mixed(mirror_weights, far_blocks), half).astype(jnp.float32)
     for mask, block in enumerate(near_blocks):
         total += near_weights[:, mask][:, None] * block.astype(jnp.float32)

time: 41.9 us -> 41.7 us (level)
  waiting for transfers between devices: 10.9 us -> 10.4 us
    ppermute x15, waiting for transfers between devices: 9.83 us -> 9.27 us  [across(): return lax.ppermute(value, 'expert', pairs) if mask else value]
where the time goes in v12:
time: 41.7 us; the launch traced here: 41.6 us
  starting transfers between devices  24.6 us (59%)
  waiting for transfers between devices  10.4 us (25%)
  Pallas kernels  5.26 us (13%)
  other arithmetic  0.98 us (2%)
    ppermute x15, starting transfers between devices, across(): return lax.ppermute(value, 'expert', pairs) if mask else value  23.2 us
    ppermute x15, waiting for transfers between devices, across(): return lax.ppermute(value, 'expert', pairs) if mask else value  9.27 us
    pallas_call x1, Pallas kernels, expert_parts(): pl.pallas_call(functools.partial(expert_kernel, count), out_shape=tuple((...  3.8 us
    ppermute x7, starting transfers between devices, partner(): return lax.ppermute(value, axis, pairs)  1.38 us
    ppermute x7, waiting for transfers between devices, partner(): return lax.ppermute(value, axis, pairs)  1.09 us
    pallas_call x1, Pallas kernels, tables(): pl.pallas_call(table_kernel, out_shape=(table, table, jax.ShapeDtypeStruc...  1 us
  transfers between devices with their start and end apart: 22, of which 12 were waited for; matrix products, arithmetic and copies ran while one was open for 1% of the time, Pallas kernels for 3%

profile of v12, /device:TPU:0, one launch (start us, length us, event | category | flops | bytes accessed | tf_op | source)
XLA Modules:
  0.0 41.6 jit_solution(8490841826991874545)
XLA Ops:
  0.0 4.0 %collective-permute-start = (bf16[16,2880]{1,0:T(8,128)(2,1)}, bf16[16,2880]{1,0:T(8,128)(2,1)S(1)}, u32[]{:S(2)}, u32[]{:S(2)}) collective-permute-start(bf16[16,2880]{1,0:T(8,128)(2,1)} %refs_4_.1), channel_id=1, source_target_pairs={{0,8},{1,9},{2,10},{3,11},{4,12},{5,13},{6,14},{7,15},{8,0},{9,1},... | collective-permute-start | bytes 276488 | tf_op jit(solution)/shard_map/ppermute | solution.py:208
  4.0 2.5 %collective-permute-start.9 = (bf16[16,2880]{1,0:T(8,128)(2,1)}, bf16[16,2880]{1,0:T(8,128)(2,1)S(1)}, u32[]{:S(2)}, u32[]{:S(2)}) collective-permute-start(bf16[16,2880]{1,0:T(8,128)(2,1)} %refs_4_.1), channel_id=1, source_target_pairs={{0,6},{1,7},{2,4},{3,5},{4,2},{5,3},{6,0},{7,1},{8,14},{9,15},{10,... | collective-permute-start | bytes 276488 | tf_op jit(solution)/shard_map/ppermute | solution.py:208
  6.6 0.5 %collective-permute-start.8 = (bf16[16,2880]{1,0:T(8,128)(2,1)}, bf16[16,2880]{1,0:T(8,128)(2,1)S(1)}, u32[]{:S(2)}, u32[]{:S(2)}) collective-permute-start(bf16[16,2880]{1,0:T(8,128)(2,1)} %refs_4_.1), channel_id=1, source_target_pairs={{0,2},{1,3},{2,0},{3,1},{4,6},{5,7},{6,4},{7,5},{8,10},{9,11},{10,... | collective-permute-start | bytes 276488 | tf_op jit(solution)/shard_map/ppermute | solution.py:208
  7.1 0.4 %collective-permute-start.10 = (bf16[16,2880]{1,0:T(8,128)(2,1)}, bf16[16,2880]{1,0:T(8,128)(2,1)S(1)}, u32[]{:S(2)}, u32[]{:S(2)}) collective-permute-start(bf16[16,2880]{1,0:T(8,128)(2,1)} %refs_4_.1), channel_id=1, source_target_pairs={{0,4},{1,5},{2,6},{3,7},{4,0},{5,1},{6,2},{7,3},{8,12},{9,13},{10,... | collective-permute-start | bytes 276488 | tf_op jit(solution)/shard_map/ppermute | solution.py:208
  7.5 1.0 %shard_map.73 = (f32[16,4]{1,0:T(8,128)S(1)}, f32[16,4]{1,0:T(8,128)S(1)}, f32[2880]{0:T(1024)S(1)}) custom-call(s32[1]{0:T(128)} %bitcast.chip_ref, s32[4,16]{1,0:T(4,128)} %bitcast.16, f32[4,16]{1,0:T(4,128)} %bitcast.17, f32[2880]{0:T(1024)} %gain_hbm.1, bf16[720,2880]{1,0:T(8,128)(2,1)} %bitcast.10, bf16[720,2880]{1,0:T(8,128)(2,1)} %bitcast.12, ...), custom_call_target="tpu_custom_call" | custom-call | bytes 12441600 | tf_op jit(solution)/shard_map/pallas_call | solution.py:184
  8.5 0.2 collective-permute-done.refs_1_
  8.8 0.1 shard_map.74.refs_4_
  8.9 2.4 %collective-permute-start.6 = (bf16[16,2880]{1,0:T(8,128)(2,1)S(1)}, bf16[16,2880]{1,0:T(8,128)(2,1)S(1)}, u32[]{:S(2)}, u32[]{:S(2)}) collective-permute-start(bf16[16,2880]{1,0:T(8,128)(2,1)S(1)} %shard_map.74.refs_4_), channel_id=1, source_target_pairs={{0,6},{1,7},{2,4},{3,5},{4,2},{5,3},{6,0},{7,1},{8,14},{9,15},{10,... | collective-permute-start | bytes 276488 | tf_op jit(solution)/shard_map/ppermute | solution.py:208
  11.3 0.8 %collective-permute-start.4 = (bf16[16,2880]{1,0:T(8,128)(2,1)S(1)}, bf16[16,2880]{1,0:T(8,128)(2,1)S(1)}, u32[]{:S(2)}, u32[]{:S(2)}) collective-permute-start(bf16[16,2880]{1,0:T(8,128)(2,1)S(1)} %shard_map.74.refs_4_), channel_id=1, source_target_pairs={{0,4},{1,5},{2,6},{3,7},{4,0},{5,1},{6,2},{7,3},{8,12},{9,13},{10,... | collective-permute-start | bytes 276488 | tf_op jit(solution)/shard_map/ppermute | solution.py:208
  12.1 0.0 collective-permute-done.9.refs_6_
  12.1 0.4 collective-permute-start.2
  12.5 0.0 collective-permute-done.8.refs_5_
  12.5 0.0 collective-permute-start.1
  12.5 0.4 %collective-permute-done.10.refs_7_ = bf16[16,2880]{1,0:T(8,128)(2,1)S(1)} collective-permute-done((bf16[16,2880]{1,0:T(8,128)(2,1)}, bf16[16,2880]{1,0:T(8,128)(2,1)S(1)}, u32[]{:S(2)}, u32[]{:S(2)}) %collective-permute-start.10) | collective-permute-done | bytes 92192 | tf_op jit(solution)/shard_map/ppermute | solution.py:208
  12.9 3.0 %collective-permute-done.6.refs_3_.refs_7_ = bf16[16,2880]{1,0:T(8,128)(2,1)S(1)} collective-permute-done((bf16[16,2880]{1,0:T(8,128)(2,1)S(1)}, bf16[16,2880]{1,0:T(8,128)(2,1)S(1)}, u32[]{:S(2)}, u32[]{:S(2)}) %collective-permute-start.6) | collective-permute-done | bytes 92192 | tf_op jit(solution)/shard_map/ppermute | solution.py:208
  15.9 0.4 collective-permute-done.4.refs_2_.refs_6_
  16.3 0.5 %collective-permute-done.2.refs_1_.refs_5_ = bf16[16,2880]{1,0:T(8,128)(2,1)S(1)} collective-permute-done((bf16[16,2880]{1,0:T(8,128)(2,1)S(1)}, bf16[16,2880]{1,0:T(8,128)(2,1)S(1)}, u32[]{:S(2)}, u32[]{:S(2)}) %collective-permute-start.2) | collective-permute-done | bytes 92192 | tf_op jit(solution)/shard_map/ppermute | solution.py:208
  16.8 0.2 shard_map.75.refs_9_
  17.0 0.1 collective-permute-start.11
  17.0 0.5 %collective-permute-start.7 = (bf16[16,2880]{1,0:T(8,128)(2,1)S(1)}, bf16[16,2880]{1,0:T(8,128)(2,1)S(1)}, u32[]{:S(2)}, u32[]{:S(2)}) collective-permute-start(bf16[16,2880]{1,0:T(8,128)(2,1)S(1)} %collective-permute-done.6.refs_3_.refs_7_), channel_id=1, source_target_pairs={{0,1},{1,0},{2,3},{3,2},{4,5},{5,4},{6,7},{7,6},{8,9},{9,8},{10,11... | collective-permute-start | bytes 276488 | tf_op jit(solution)/shard_map/ppermute | solution.py:14
  17.5 0.1 collective-permute-start.5
  17.6 0.4 %collective-permute-start.3 = (bf16[16,2880]{1,0:T(8,128)(2,1)S(1)}, bf16[16,2880]{1,0:T(8,128)(2,1)S(1)}, u32[]{:S(2)}, u32[]{:S(2)}) collective-permute-start(bf16[16,2880]{1,0:T(8,128)(2,1)S(1)} %collective-permute-done.2.refs_1_.refs_5_), channel_id=1, source_target_pairs={{0,1},{1,0},{2,3},{3,2},{4,5},{5,4},{6,7},{7,6},{8,9},{9,8},{10,11... | collective-permute-start | bytes 276488 | tf_op jit(solution)/shard_map/ppermute | solution.py:14
  18.0 0.8 %collective-permute-done.7.refs_3_ = bf16[16,2880]{1,0:T(8,128)(2,1)S(1)} collective-permute-done((bf16[16,2880]{1,0:T(8,128)(2,1)S(1)}, bf16[16,2880]{1,0:T(8,128)(2,1)S(1)}, u32[]{:S(2)}, u32[]{:S(2)}) %collective-permute-start.7) | collective-permute-done | bytes 92192 | tf_op jit(solution)/shard_map/ppermute | solution.py:14
  18.9 0.1 collective-permute-done.5.refs_2_
  19.0 0.1 collective-permute-done.3.refs_1_
  19.1 3.8 %shard_map.76 = (bf16[64,2880]{1,0:T(8,128)(2,1)S(1)}, bf16[64,2880]{1,0:T(8,128)(2,1)S(1)}, bf16[64,2880]{1,0:T(8,128)(2,1)S(1)}, bf16[64,2880]{1,0:T(8,128)(2,1)S(1)}, f32[16,4]{1,0:T(8,128)S(1)}) custom-call(bf16[16,2880]{1,0:T(8,128)(2,1)S(1)} %collective-permute-done.1.refs_0_, bf16[16,2880]{1,0:T(8,128)(2,1)S(1)} %collective-permute-done.3.refs_1_, ...), custom_call_target="tpu_custom_call" | custom-call | flops 3185049600 | bytes 12441600 | tf_op jit(solution)/shard_map/pallas_call | solution.py:146
  23.0 0.3 collective-permute-start.13
  23.2 2.4 %collective-permute-start.12 = (f32[16,4]{1,0:T(8,128)S(1)}, f32[16,4]{1,0:T(8,128)S(1)}, u32[]{:S(2)}, u32[]{:S(2)}) collective-permute-start(f32[16,4]{1,0:T(8,128)S(1)} %get-tuple-element.16), channel_id=1, source_target_pairs={{0,8},{1,9},{2,10},{3,11},{4,12},{5,13},{6,14},{7,15},{8,0},{9,1},... | collective-permute-start | bytes 776 | tf_op jit(solution)/shard_map/ppermute | solution.py:208
  25.6 0.0 collective-permute-start.18
  25.6 0.1 add_convert_fusion.1
  25.8 2.7 %collective-permute-start.16 = (bf16[16,2880]{1,0:T(8,128)(2,1)S(1)}, bf16[16,2880]{1,0:T(8,128)(2,1)S(1)}, u32[]{:S(2)}, u32[]{:S(2)}) collective-permute-start(bf16[16,2880]{1,0:T(8,128)(2,1)S(1)} %get-tuple-element.25), channel_id=1, source_target_pairs={{0,6},{1,7},{2,4},{3,5},{4,2},{5,3},{6,0},{7,1},{8,14},{9,15},{10,... | collective-permute-start | bytes 276488 | tf_op jit(solution)/shard_map/ppermute | solution.py:208
  28.5 0.0 collective-permute-start.15
  28.5 0.9 %collective-permute-start.14 = (bf16[16,2880]{1,0:T(8,128)(2,1)S(1)}, bf16[16,2880]{1,0:T(8,128)(2,1)S(1)}, u32[]{:S(2)}, u32[]{:S(2)}) collective-permute-start(bf16[16,2880]{1,0:T(8,128)(2,1)S(1)} %get-tuple-element.27), channel_id=1, source_target_pairs={{0,2},{1,3},{2,0},{3,1},{4,6},{5,7},{6,4},{7,5},{8,10},{9,11},{10,... | collective-permute-start | bytes 276488 | tf_op jit(solution)/shard_map/ppermute | solution.py:208
  29.3 0.0 collective-permute-done.18
  29.3 0.1 add_convert_fusion
  29.4 1.2 %collective-permute-start.19 = (bf16[16,2880]{1,0:T(8,128)(2,1)S(1)}, bf16[16,2880]{1,0:T(8,128)(2,1)S(1)}, u32[]{:S(2)}, u32[]{:S(2)}) collective-permute-start(bf16[16,2880]{1,0:T(8,128)(2,1)S(1)} %get-tuple-element.29), channel_id=1, source_target_pairs={{0,2},{1,3},{2,0},{3,1},{4,6},{5,7},{6,4},{7,5},{8,10},{9,11},{10,... | collective-permute-start | bytes 276488 | tf_op jit(solution)/shard_map/ppermute | solution.py:208
  30.7 2.3 %collective-permute-start.21 = (bf16[16,2880]{1,0:T(8,128)(2,1)S(1)}, bf16[16,2880]{1,0:T(8,128)(2,1)S(1)}, u32[]{:S(2)}, u32[]{:S(2)}) collective-permute-start(bf16[16,2880]{1,0:T(8,128)(2,1)S(1)} %get-tuple-element.30), channel_id=1, source_target_pairs={{0,6},{1,7},{2,4},{3,5},{4,2},{5,3},{6,0},{7,1},{8,14},{9,15},{10,... | collective-permute-start | bytes 276488 | tf_op jit(solution)/shard_map/ppermute | solution.py:208
  32.9 1.2 %collective-permute-start.20 = (bf16[16,2880]{1,0:T(8,128)(2,1)S(1)}, bf16[16,2880]{1,0:T(8,128)(2,1)S(1)}, u32[]{:S(2)}, u32[]{:S(2)}) collective-permute-start(bf16[16,2880]{1,0:T(8,128)(2,1)S(1)} %get-tuple-element.31), channel_id=1, source_target_pairs={{0,4},{1,5},{2,6},{3,7},{4,0},{5,1},{6,2},{7,3},{8,12},{9,13},{10,... | collective-permute-start | bytes 276488 | tf_op jit(solution)/shard_map/ppermute | solution.py:208
  34.2 0.0 collective-permute-done.15.refs_2_
  34.2 0.9 %collective-permute-done.14.refs_1_ = bf16[16,2880]{1,0:T(8,128)(2,1)S(1)} collective-permute-done((bf16[16,2880]{1,0:T(8,128)(2,1)S(1)}, bf16[16,2880]{1,0:T(8,128)(2,1)S(1)}, u32[]{:S(2)}, u32[]{:S(2)}) %collective-permute-start.14) | collective-permute-done | bytes 92192 | tf_op jit(solution)/shard_map/ppermute | solution.py:208
  35.1 0.1 shard_map.77
  35.2 1.5 %collective-permute-start.17 = (bf16[16,2880]{1,0:T(8,128)(2,1)S(1)}, bf16[16,2880]{1,0:T(8,128)(2,1)S(1)}, u32[]{:S(2)}, u32[]{:S(2)}) collective-permute-start(bf16[16,2880]{1,0:T(8,128)(2,1)S(1)} %shard_map.77), channel_id=1, source_target_pairs={{0,8},{1,9},{2,10},{3,11},{4,12},{5,13},{6,14},{7,15},{8,0},{9,1},... | collective-permute-start | bytes 276488 | tf_op jit(solution)/shard_map/ppermute | solution.py:208
  36.7 0.2 slice_reduce_fusion.3
  36.9 0.9 %collective-permute-done.19 = bf16[16,2880]{1,0:T(8,128)(2,1)S(1)} collective-permute-done((bf16[16,2880]{1,0:T(8,128)(2,1)S(1)}, bf16[16,2880]{1,0:T(8,128)(2,1)S(1)}, u32[]{:S(2)}, u32[]{:S(2)}) %collective-permute-start.19) | collective-permute-done | bytes 92192 | tf_op jit(solution)/shard_map/ppermute | solution.py:208
  37.9 0.0 collective-permute-done.21
  37.9 0.7 %collective-permute-done.20 = bf16[16,2880]{1,0:T(8,128)(2,1)S(1)} collective-permute-done((bf16[16,2880]{1,0:T(8,128)(2,1)S(1)}, bf16[16,2880]{1,0:T(8,128)(2,1)S(1)}, u32[]{:S(2)}, u32[]{:S(2)}) %collective-permute-start.20) | collective-permute-done | bytes 92192 | tf_op jit(solution)/shard_map/ppermute | solution.py:208
  38.6 2.2 %collective-permute-done.17 = bf16[16,2880]{1,0:T(8,128)(2,1)S(1)} collective-permute-done((bf16[16,2880]{1,0:T(8,128)(2,1)S(1)}, bf16[16,2880]{1,0:T(8,128)(2,1)S(1)}, u32[]{:S(2)}, u32[]{:S(2)}) %collective-permute-start.17) | collective-permute-done | bytes 92192 | tf_op jit(solution)/shard_map/ppermute | solution.py:208
  40.8 0.8 %add_convert_fusion.2 = bf16[16,2880]{1,0:T(8,128)(2,1)} fusion(bf16[16,2880]{1,0:T(8,128)(2,1)S(1)} %collective-permute-done.21, bf16[16,2880]{1,0:T(8,128)(2,1)S(1)} %collective-permute-done.20, bf16[16,2880]{1,0:T(8,128)(2,1)S(1)} %collective-permute-done.19, bf16[16,2880]{1,0:T(8,128)(2,1)S(1)} %collective-permute-done.17, ...), kind=kLoop, calls=%fused_computation.2 | loop fusion | flops 737280 | bytes 645376 | tf_op jit(solution)/shard_map/convert_element_type | solution.py:243
  (15 shorter events, 0.1 us)
Async XLA Ops:
  0.0 8.8 %collective-permute-start = (bf16[16,2880]{1,0:T(8,128)(2,1)}, bf16[16,2880]{1,0:T(8,128)(2,1)S(1)}, u32[]{:S(2)}, u32[]{:S(2)}) collective-permute-start(bf16[16,2880]{1,0:T(8,128)(2,1)} %refs_4_.1), channel_id=1, source_target_pairs={{0,8},{1,9},{2,10},{3,11},{4,12},{5,13},{6,14},{7,15},{8,0},{9,1},... | collective-permute-start | bytes 276488 | tf_op jit(solution)/shard_map/ppermute | solution.py:208
  4.0 8.0 %collective-permute-start.9 = (bf16[16,2880]{1,0:T(8,128)(2,1)}, bf16[16,2880]{1,0:T(8,128)(2,1)S(1)}, u32[]{:S(2)}, u32[]{:S(2)}) collective-permute-start(bf16[16,2880]{1,0:T(8,128)(2,1)} %refs_4_.1), channel_id=1, source_target_pairs={{0,6},{1,7},{2,4},{3,5},{4,2},{5,3},{6,0},{7,1},{8,14},{9,15},{10,... | collective-permute-start | bytes 276488 | tf_op jit(solution)/shard_map/ppermute | solution.py:208
  6.6 5.9 %collective-permute-start.8 = (bf16[16,2880]{1,0:T(8,128)(2,1)}, bf16[16,2880]{1,0:T(8,128)(2,1)S(1)}, u32[]{:S(2)}, u32[]{:S(2)}) collective-permute-start(bf16[16,2880]{1,0:T(8,128)(2,1)} %refs_4_.1), channel_id=1, source_target_pairs={{0,2},{1,3},{2,0},{3,1},{4,6},{5,7},{6,4},{7,5},{8,10},{9,11},{10,... | collective-permute-start | bytes 276488 | tf_op jit(solution)/shard_map/ppermute | solution.py:208
  7.1 5.9 %collective-permute-start.10 = (bf16[16,2880]{1,0:T(8,128)(2,1)}, bf16[16,2880]{1,0:T(8,128)(2,1)S(1)}, u32[]{:S(2)}, u32[]{:S(2)}) collective-permute-start(bf16[16,2880]{1,0:T(8,128)(2,1)} %refs_4_.1), channel_id=1, source_target_pairs={{0,4},{1,5},{2,6},{3,7},{4,0},{5,1},{6,2},{7,3},{8,12},{9,13},{10,... | collective-permute-start | bytes 276488 | tf_op jit(solution)/shard_map/ppermute | solution.py:208
  7.5 9.2 %copy-start.3 = (bf16[16,2880]{1,0:T(8,128)(2,1)S(1)}, bf16[16,2880]{1,0:T(8,128)(2,1)}, u32[]{:S(2)}) copy-start(bf16[16,2880]{1,0:T(8,128)(2,1)} %refs_4_.1) | copy-start | bytes 276484
  7.5 11.6 %copy-start = (bf16[1,2880,720]{1,2,0:T(8,128)(2,1)S(1)}, bf16[1,2880,720]{1,2,0:T(8,128)(2,1)}, u32[]{:S(2)}) copy-start(bf16[1,2880,720]{1,2,0:T(8,128)(2,1)} %param.11) | copy-start | bytes 12441604
  7.5 11.6 %copy-start.1 = (bf16[1,2880,720]{1,2,0:T(8,128)(2,1)S(1)}, bf16[1,2880,720]{1,2,0:T(8,128)(2,1)}, u32[]{:S(2)}) copy-start(bf16[1,2880,720]{1,2,0:T(8,128)(2,1)} %param.12) | copy-start | bytes 12441604
  7.5 11.6 %copy-start.2 = (bf16[1,720,2880]{2,1,0:T(8,128)(2,1)S(1)}, bf16[1,720,2880]{2,1,0:T(8,128)(2,1)}, u32[]{:S(2)}) copy-start(bf16[1,720,2880]{2,1,0:T(8,128)(2,1)} %param.13) | copy-start | bytes 12441604
  8.9 7.0 %collective-permute-start.6 = (bf16[16,2880]{1,0:T(8,128)(2,1)S(1)}, bf16[16,2880]{1,0:T(8,128)(2,1)S(1)}, u32[]{:S(2)}, u32[]{:S(2)}) collective-permute-start(bf16[16,2880]{1,0:T(8,128)(2,1)S(1)} %shard_map.74.refs_4_), channel_id=1, source_target_pairs={{0,6},{1,7},{2,4},{3,5},{4,2},{5,3},{6,0},{7,1},{8,14},{9,15},{10,... | collective-permute-start | bytes 276488 | tf_op jit(solution)/shard_map/ppermute | solution.py:208
  11.3 5.0 %collective-permute-start.4 = (bf16[16,2880]{1,0:T(8,128)(2,1)S(1)}, bf16[16,2880]{1,0:T(8,128)(2,1)S(1)}, u32[]{:S(2)}, u32[]{:S(2)}) collective-permute-start(bf16[16,2880]{1,0:T(8,128)(2,1)S(1)} %shard_map.74.refs_4_), channel_id=1, source_target_pairs={{0,4},{1,5},{2,6},{3,7},{4,0},{5,1},{6,2},{7,3},{8,12},{9,13},{10,... | collective-permute-start | bytes 276488 | tf_op jit(solution)/shard_map/ppermute | solution.py:208
  12.1 4.7 %collective-permute-start.2 = (bf16[16,2880]{1,0:T(8,128)(2,1)S(1)}, bf16[16,2880]{1,0:T(8,128)(2,1)S(1)}, u32[]{:S(2)}, u32[]{:S(2)}) collective-permute-start(bf16[16,2880]{1,0:T(8,128)(2,1)S(1)} %shard_map.74.refs_4_), channel_id=1, source_target_pairs={{0,2},{1,3},{2,0},{3,1},{4,6},{5,7},{6,4},{7,5},{8,10},{9,11},{10,... | collective-permute-start | bytes 276488 | tf_op jit(solution)/shard_map/ppermute | solution.py:208
  12.5 4.3 %collective-permute-start.1 = (bf16[16,2880]{1,0:T(8,128)(2,1)S(1)}, bf16[16,2880]{1,0:T(8,128)(2,1)S(1)}, u32[]{:S(2)}, u32[]{:S(2)}) collective-permute-start(bf16[16,2880]{1,0:T(8,128)(2,1)S(1)} %shard_map.74.refs_4_), channel_id=1, source_target_pairs={{0,1},{1,0},{2,3},{3,2},{4,5},{5,4},{6,7},{7,6},{8,9},{9,8},{10,11... | collective-permute-start | bytes 276488 | tf_op jit(solution)/shard_map/ppermute | solution.py:14
  17.0 2.2 %collective-permute-start.11 = (bf16[64,2880]{1,0:T(8,128)(2,1)S(1)}, bf16[64,2880]{1,0:T(8,128)(2,1)S(1)}, u32[]{:S(2)}, u32[]{:S(2)}) collective-permute-start(bf16[64,2880]{1,0:T(8,128)(2,1)S(1)} %shard_map.75.refs_9_), channel_id=1, source_target_pairs={{0,1},{1,0},{2,3},{3,2},{4,5},{5,4},{6,7},{7,6},{8,9},{9,8},{10,11... | collective-permute-start | bytes 1105928 | tf_op jit(solution)/shard_map/ppermute | solution.py:14
  17.0 1.8 %collective-permute-start.7 = (bf16[16,2880]{1,0:T(8,128)(2,1)S(1)}, bf16[16,2880]{1,0:T(8,128)(2,1)S(1)}, u32[]{:S(2)}, u32[]{:S(2)}) collective-permute-start(bf16[16,2880]{1,0:T(8,128)(2,1)S(1)} %collective-permute-done.6.refs_3_.refs_7_), channel_id=1, source_target_pairs={{0,1},{1,0},{2,3},{3,2},{4,5},{5,4},{6,7},{7,6},{8,9},{9,8},{10,11... | collective-permute-start | bytes 276488 | tf_op jit(solution)/shard_map/ppermute | solution.py:14
  17.5 1.5 %collective-permute-start.5 = (bf16[16,2880]{1,0:T(8,128)(2,1)S(1)}, bf16[16,2880]{1,0:T(8,128)(2,1)S(1)}, u32[]{:S(2)}, u32[]{:S(2)}) collective-permute-start(bf16[16,2880]{1,0:T(8,128)(2,1)S(1)} %collective-permute-done.4.refs_2_.refs_6_), channel_id=1, source_target_pairs={{0,1},{1,0},{2,3},{3,2},{4,5},{5,4},{6,7},{7,6},{8,9},{9,8},{10,11... | collective-permute-start | bytes 276488 | tf_op jit(solution)/shard_map/ppermute | solution.py:14
  17.6 1.5 %collective-permute-start.3 = (bf16[16,2880]{1,0:T(8,128)(2,1)S(1)}, bf16[16,2880]{1,0:T(8,128)(2,1)S(1)}, u32[]{:S(2)}, u32[]{:S(2)}) collective-permute-start(bf16[16,2880]{1,0:T(8,128)(2,1)S(1)} %collective-permute-done.2.refs_1_.refs_5_), channel_id=1, source_target_pairs={{0,1},{1,0},{2,3},{3,2},{4,5},{5,4},{6,7},{7,6},{8,9},{9,8},{10,11... | collective-permute-start | bytes 276488 | tf_op jit(solution)/shard_map/ppermute | solution.py:14
  23.0 2.7 %collective-permute-start.13 = (bf16[64,2880]{1,0:T(8,128)(2,1)S(1)}, bf16[64,2880]{1,0:T(8,128)(2,1)S(1)}, u32[]{:S(2)}, u32[]{:S(2)}) collective-permute-start(bf16[64,2880]{1,0:T(8,128)(2,1)S(1)} %get-tuple-element.18), channel_id=1, source_target_pairs={{0,1},{1,0},{2,3},{3,2},{4,5},{5,4},{6,7},{7,6},{8,9},{9,8},{10,11... | collective-permute-start | bytes 1105928 | tf_op jit(solution)/shard_map/ppermute | solution.py:14
  23.2 7.4 %collective-permute-start.12 = (f32[16,4]{1,0:T(8,128)S(1)}, f32[16,4]{1,0:T(8,128)S(1)}, u32[]{:S(2)}, u32[]{:S(2)}) collective-permute-start(f32[16,4]{1,0:T(8,128)S(1)} %get-tuple-element.16), channel_id=1, source_target_pairs={{0,8},{1,9},{2,10},{3,11},{4,12},{5,13},{6,14},{7,15},{8,0},{9,1},... | collective-permute-start | bytes 776 | tf_op jit(solution)/shard_map/ppermute | solution.py:208
  25.6 3.7 %collective-permute-start.18 = (bf16[64,2880]{1,0:T(8,128)(2,1)S(1)}, bf16[64,2880]{1,0:T(8,128)(2,1)S(1)}, u32[]{:S(2)}, u32[]{:S(2)}) collective-permute-start(bf16[64,2880]{1,0:T(8,128)(2,1)S(1)} %get-tuple-element.20), channel_id=1, source_target_pairs={{0,1},{1,0},{2,3},{3,2},{4,5},{5,4},{6,7},{7,6},{8,9},{9,8},{10,11... | collective-permute-start | bytes 1105928 | tf_op jit(solution)/shard_map/ppermute | solution.py:14
  25.8 7.2 %collective-permute-start.16 = (bf16[16,2880]{1,0:T(8,128)(2,1)S(1)}, bf16[16,2880]{1,0:T(8,128)(2,1)S(1)}, u32[]{:S(2)}, u32[]{:S(2)}) collective-permute-start(bf16[16,2880]{1,0:T(8,128)(2,1)S(1)} %get-tuple-element.25), channel_id=1, source_target_pairs={{0,6},{1,7},{2,4},{3,5},{4,2},{5,3},{6,0},{7,1},{8,14},{9,15},{10,... | collective-permute-start | bytes 276488 | tf_op jit(solution)/shard_map/ppermute | solution.py:208
  28.5 5.7 %collective-permute-start.15 = (bf16[16,2880]{1,0:T(8,128)(2,1)S(1)}, bf16[16,2880]{1,0:T(8,128)(2,1)S(1)}, u32[]{:S(2)}, u32[]{:S(2)}) collective-permute-start(bf16[16,2880]{1,0:T(8,128)(2,1)S(1)} %get-tuple-element.26), channel_id=1, source_target_pairs={{0,4},{1,5},{2,6},{3,7},{4,0},{5,1},{6,2},{7,3},{8,12},{9,13},{10,... | collective-permute-start | bytes 276488 | tf_op jit(solution)/shard_map/ppermute | solution.py:208
  28.5 6.6 %collective-permute-start.14 = (bf16[16,2880]{1,0:T(8,128)(2,1)S(1)}, bf16[16,2880]{1,0:T(8,128)(2,1)S(1)}, u32[]{:S(2)}, u32[]{:S(2)}) collective-permute-start(bf16[16,2880]{1,0:T(8,128)(2,1)S(1)} %get-tuple-element.27), channel_id=1, source_target_pairs={{0,2},{1,3},{2,0},{3,1},{4,6},{5,7},{6,4},{7,5},{8,10},{9,11},{10,... | collective-permute-start | bytes 276488 | tf_op jit(solution)/shard_map/ppermute | solution.py:208
  29.4 8.4 %collective-permute-start.19 = (bf16[16,2880]{1,0:T(8,128)(2,1)S(1)}, bf16[16,2880]{1,0:T(8,128)(2,1)S(1)}, u32[]{:S(2)}, u32[]{:S(2)}) collective-permute-start(bf16[16,2880]{1,0:T(8,128)(2,1)S(1)} %get-tuple-element.29), channel_id=1, source_target_pairs={{0,2},{1,3},{2,0},{3,1},{4,6},{5,7},{6,4},{7,5},{8,10},{9,11},{10,... | collective-permute-start | bytes 276488 | tf_op jit(solution)/shard_map/ppermute | solution.py:208
  30.7 7.2 %collective-permute-start.21 = (bf16[16,2880]{1,0:T(8,128)(2,1)S(1)}, bf16[16,2880]{1,0:T(8,128)(2,1)S(1)}, u32[]{:S(2)}, u32[]{:S(2)}) collective-permute-start(bf16[16,2880]{1,0:T(8,128)(2,1)S(1)} %get-tuple-element.30), channel_id=1, source_target_pairs={{0,6},{1,7},{2,4},{3,5},{4,2},{5,3},{6,0},{7,1},{8,14},{9,15},{10,... | collective-permute-start | bytes 276488 | tf_op jit(solution)/shard_map/ppermute | solution.py:208
  32.9 5.6 %collective-permute-start.20 = (bf16[16,2880]{1,0:T(8,128)(2,1)S(1)}, bf16[16,2880]{1,0:T(8,128)(2,1)S(1)}, u32[]{:S(2)}, u32[]{:S(2)}) collective-permute-start(bf16[16,2880]{1,0:T(8,128)(2,1)S(1)} %get-tuple-element.31), channel_id=1, source_target_pairs={{0,4},{1,5},{2,6},{3,7},{4,0},{5,1},{6,2},{7,3},{8,12},{9,13},{10,... | collective-permute-start | bytes 276488 | tf_op jit(solution)/shard_map/ppermute | solution.py:208
  35.2 5.5 %collective-permute-start.17 = (bf16[16,2880]{1,0:T(8,128)(2,1)S(1)}, bf16[16,2880]{1,0:T(8,128)(2,1)S(1)}, u32[]{:S(2)}, u32[]{:S(2)}) collective-permute-start(bf16[16,2880]{1,0:T(8,128)(2,1)S(1)} %shard_map.77), channel_id=1, source_target_pairs={{0,8},{1,9},{2,10},{3,11},{4,12},{5,13},{6,14},{7,15},{8,0},{9,1},... | collective-permute-start | bytes 276488 | tf_op jit(solution)/shard_map/ppermute | solution.py:208

commit v13 on v11

--- a/solution.py
+++ b/solution.py
@@ -130,7 +130,7 @@
     across = (((1,), (1,)), ((), ()))
     gate = lax.dot_general(gate_ref[...], normed, across, preferred_element_type=jnp.float32)
     upper = lax.dot_general(up_ref[...], normed, across, preferred_element_type=jnp.float32)
-    act = (gate * jax.nn.sigmoid(1.702 * gate) * (upper + 1.0)).astype(jnp.bfloat16).T
+    act = (gate * (0.5 * jnp.tanh(0.851 * gate) + 0.5) * (upper + 1.0)).astype(jnp.bfloat16).T
     out = jnp.dot(act, down_ref[...], preferred_element_type=jnp.float32).astype(jnp.bfloat16)
     start = 0
     for out_ref in outs:

time: 41.9 us -> 41.9 us (level)
  no operation moved by 1% of the time
where the time goes in v13:
time: 41.9 us; the launch traced here: 41.8 us
  starting transfers between devices  24.2 us (58%)
  waiting for transfers between devices  11 us (26%)
  Pallas kernels  5.25 us (13%)
  other arithmetic  0.98 us (2%)
    ppermute x15, starting transfers between devices, across(): return lax.ppermute(value, 'expert', pairs) if mask else value  22.8 us
    ppermute x15, waiting for transfers between devices, across(): return lax.ppermute(value, 'expert', pairs) if mask else value  9.88 us
    pallas_call x1, Pallas kernels, expert_parts(): pl.pallas_call(functools.partial(expert_kernel, count), out_shape=tuple((...  3.79 us
    ppermute x7, starting transfers between devices, partner(): return lax.ppermute(value, axis, pairs)  1.37 us
    ppermute x7, waiting for transfers between devices, partner(): return lax.ppermute(value, axis, pairs)  1.09 us
    pallas_call x1, Pallas kernels, tables(): pl.pallas_call(table_kernel, out_shape=(table, table, jax.ShapeDtypeStruc...  1 us
  transfers between devices with their start and end apart: 22, of which 12 were waited for; matrix products, arithmetic and copies ran while one was open for 1% of the time, Pallas kernels for 3%

profile of v13, /device:TPU:0, one launch (start us, length us, event | category | flops | bytes accessed | tf_op | source)
XLA Modules:
  0.0 41.8 jit_solution(6955578703693584271)
XLA Ops:
  0.0 4.0 %collective-permute-start = (bf16[16,2880]{1,0:T(8,128)(2,1)}, bf16[16,2880]{1,0:T(8,128)(2,1)S(1)}, u32[]{:S(2)}, u32[]{:S(2)}) collective-permute-start(bf16[16,2880]{1,0:T(8,128)(2,1)} %refs_4_.1), channel_id=1, source_target_pairs={{0,8},{1,9},{2,10},{3,11},{4,12},{5,13},{6,14},{7,15},{8,0},{9,1},... | collective-permute-start | bytes 276488 | tf_op jit(solution)/shard_map/ppermute | solution.py:208
  4.0 1.6 %collective-permute-start.9 = (bf16[16,2880]{1,0:T(8,128)(2,1)}, bf16[16,2880]{1,0:T(8,128)(2,1)S(1)}, u32[]{:S(2)}, u32[]{:S(2)}) collective-permute-start(bf16[16,2880]{1,0:T(8,128)(2,1)} %refs_4_.1), channel_id=1, source_target_pairs={{0,4},{1,5},{2,6},{3,7},{4,0},{5,1},{6,2},{7,3},{8,12},{9,13},{10,... | collective-permute-start | bytes 276488 | tf_op jit(solution)/shard_map/ppermute | solution.py:208
  5.6 1.5 %collective-permute-start.8 = (bf16[16,2880]{1,0:T(8,128)(2,1)}, bf16[16,2880]{1,0:T(8,128)(2,1)S(1)}, u32[]{:S(2)}, u32[]{:S(2)}) collective-permute-start(bf16[16,2880]{1,0:T(8,128)(2,1)} %refs_4_.1), channel_id=1, source_target_pairs={{0,2},{1,3},{2,0},{3,1},{4,6},{5,7},{6,4},{7,5},{8,10},{9,11},{10,... | collective-permute-start | bytes 276488 | tf_op jit(solution)/shard_map/ppermute | solution.py:208
  7.1 0.4 collective-permute-start.10
  7.5 1.0 %shard_map.73 = (f32[16,4]{1,0:T(8,128)S(1)}, f32[16,4]{1,0:T(8,128)S(1)}, f32[2880]{0:T(1024)S(1)}) custom-call(s32[1]{0:T(128)} %bitcast.chip_ref, s32[4,16]{1,0:T(4,128)} %bitcast.16, f32[4,16]{1,0:T(4,128)} %bitcast.17, f32[2880]{0:T(1024)} %gain_hbm.1, bf16[720,2880]{1,0:T(8,128)(2,1)} %bitcast.10, bf16[720,2880]{1,0:T(8,128)(2,1)} %bitcast.12, ...), custom_call_target="tpu_custom_call" | custom-call | bytes 12441600 | tf_op jit(solution)/shard_map/pallas_call | solution.py:184
  8.5 0.2 collective-permute-done.refs_1_
  8.8 0.1 shard_map.74.refs_4_
  8.9 2.4 %collective-permute-start.6 = (bf16[16,2880]{1,0:T(8,128)(2,1)S(1)}, bf16[16,2880]{1,0:T(8,128)(2,1)S(1)}, u32[]{:S(2)}, u32[]{:S(2)}) collective-permute-start(bf16[16,2880]{1,0:T(8,128)(2,1)S(1)} %shard_map.74.refs_4_), channel_id=1, source_target_pairs={{0,6},{1,7},{2,4},{3,5},{4,2},{5,3},{6,0},{7,1},{8,14},{9,15},{10,... | collective-permute-start | bytes 276488 | tf_op jit(solution)/shard_map/ppermute | solution.py:208
  11.3 0.8 %collective-permute-start.4 = (bf16[16,2880]{1,0:T(8,128)(2,1)S(1)}, bf16[16,2880]{1,0:T(8,128)(2,1)S(1)}, u32[]{:S(2)}, u32[]{:S(2)}) collective-permute-start(bf16[16,2880]{1,0:T(8,128)(2,1)S(1)} %shard_map.74.refs_4_), channel_id=1, source_target_pairs={{0,4},{1,5},{2,6},{3,7},{4,0},{5,1},{6,2},{7,3},{8,12},{9,13},{10,... | collective-permute-start | bytes 276488 | tf_op jit(solution)/shard_map/ppermute | solution.py:208
  12.1 0.0 collective-permute-done.9.refs_6_
  12.1 0.4 collective-permute-start.2
  12.5 0.0 collective-permute-done.8.refs_5_
  12.5 0.0 collective-permute-start.1
  12.5 1.4 %collective-permute-done.10.refs_7_ = bf16[16,2880]{1,0:T(8,128)(2,1)S(1)} collective-permute-done((bf16[16,2880]{1,0:T(8,128)(2,1)}, bf16[16,2880]{1,0:T(8,128)(2,1)S(1)}, u32[]{:S(2)}, u32[]{:S(2)}) %collective-permute-start.10) | collective-permute-done | bytes 92192 | tf_op jit(solution)/shard_map/ppermute | solution.py:208
  13.9 2.0 %collective-permute-done.6.refs_3_.refs_7_ = bf16[16,2880]{1,0:T(8,128)(2,1)S(1)} collective-permute-done((bf16[16,2880]{1,0:T(8,128)(2,1)S(1)}, bf16[16,2880]{1,0:T(8,128)(2,1)S(1)}, u32[]{:S(2)}, u32[]{:S(2)}) %collective-permute-start.6) | collective-permute-done | bytes 92192 | tf_op jit(solution)/shard_map/ppermute | solution.py:208
  15.8 0.5 %collective-permute-done.4.refs_2_.refs_6_ = bf16[16,2880]{1,0:T(8,128)(2,1)S(1)} collective-permute-done((bf16[16,2880]{1,0:T(8,128)(2,1)S(1)}, bf16[16,2880]{1,0:T(8,128)(2,1)S(1)}, u32[]{:S(2)}, u32[]{:S(2)}) %collective-permute-start.4) | collective-permute-done | bytes 92192 | tf_op jit(solution)/shard_map/ppermute | solution.py:208
  16.3 0.6 %collective-permute-done.2.refs_1_.refs_5_ = bf16[16,2880]{1,0:T(8,128)(2,1)S(1)} collective-permute-done((bf16[16,2880]{1,0:T(8,128)(2,1)S(1)}, bf16[16,2880]{1,0:T(8,128)(2,1)S(1)}, u32[]{:S(2)}, u32[]{:S(2)}) %collective-permute-start.2) | collective-permute-done | bytes 92192 | tf_op jit(solution)/shard_map/ppermute | solution.py:208
  16.9 0.2 shard_map.75.refs_9_
  17.1 0.1 collective-permute-start.11
  17.1 0.5 %collective-permute-start.7 = (bf16[16,2880]{1,0:T(8,128)(2,1)S(1)}, bf16[16,2880]{1,0:T(8,128)(2,1)S(1)}, u32[]{:S(2)}, u32[]{:S(2)}) collective-permute-start(bf16[16,2880]{1,0:T(8,128)(2,1)S(1)} %collective-permute-done.6.refs_3_.refs_7_), channel_id=1, source_target_pairs={{0,1},{1,0},{2,3},{3,2},{4,5},{5,4},{6,7},{7,6},{8,9},{9,8},{10,11... | collective-permute-start | bytes 276488 | tf_op jit(solution)/shard_map/ppermute | solution.py:14
  17.6 0.1 collective-permute-start.5
  17.7 0.4 %collective-permute-start.3 = (bf16[16,2880]{1,0:T(8,128)(2,1)S(1)}, bf16[16,2880]{1,0:T(8,128)(2,1)S(1)}, u32[]{:S(2)}, u32[]{:S(2)}) collective-permute-start(bf16[16,2880]{1,0:T(8,128)(2,1)S(1)} %collective-permute-done.2.refs_1_.refs_5_), channel_id=1, source_target_pairs={{0,1},{1,0},{2,3},{3,2},{4,5},{5,4},{6,7},{7,6},{8,9},{9,8},{10,11... | collective-permute-start | bytes 276488 | tf_op jit(solution)/shard_map/ppermute | solution.py:14
  18.1 0.8 %collective-permute-done.7.refs_3_ = bf16[16,2880]{1,0:T(8,128)(2,1)S(1)} collective-permute-done((bf16[16,2880]{1,0:T(8,128)(2,1)S(1)}, bf16[16,2880]{1,0:T(8,128)(2,1)S(1)}, u32[]{:S(2)}, u32[]{:S(2)}) %collective-permute-start.7) | collective-permute-done | bytes 92192 | tf_op jit(solution)/shard_map/ppermute | solution.py:14
  19.0 0.1 collective-permute-done.5.refs_2_
  19.1 0.1 collective-permute-done.3.refs_1_
  19.2 0.0 collective-permute-done.11.refs_8_
  19.2 3.8 %shard_map.76 = (bf16[64,2880]{1,0:T(8,128)(2,1)S(1)}, bf16[64,2880]{1,0:T(8,128)(2,1)S(1)}, bf16[64,2880]{1,0:T(8,128)(2,1)S(1)}, bf16[64,2880]{1,0:T(8,128)(2,1)S(1)}, f32[16,4]{1,0:T(8,128)S(1)}) custom-call(bf16[16,2880]{1,0:T(8,128)(2,1)S(1)} %collective-permute-done.1.refs_0_, bf16[16,2880]{1,0:T(8,128)(2,1)S(1)} %collective-permute-done.3.refs_1_, ...), custom_call_target="tpu_custom_call" | custom-call | flops 3185049600 | bytes 12441600 | tf_op jit(solution)/shard_map/pallas_call | solution.py:146
  23.0 0.3 collective-permute-start.13
  23.3 2.3 %collective-permute-start.12 = (f32[16,4]{1,0:T(8,128)S(1)}, f32[16,4]{1,0:T(8,128)S(1)}, u32[]{:S(2)}, u32[]{:S(2)}) collective-permute-start(f32[16,4]{1,0:T(8,128)S(1)} %get-tuple-element.16), channel_id=1, source_target_pairs={{0,8},{1,9},{2,10},{3,11},{4,12},{5,13},{6,14},{7,15},{8,0},{9,1},... | collective-permute-start | bytes 776 | tf_op jit(solution)/shard_map/ppermute | solution.py:208
  25.6 0.0 collective-permute-start.18
  25.7 0.1 add_convert_fusion.1
  25.8 2.7 %collective-permute-start.16 = (bf16[16,2880]{1,0:T(8,128)(2,1)S(1)}, bf16[16,2880]{1,0:T(8,128)(2,1)S(1)}, u32[]{:S(2)}, u32[]{:S(2)}) collective-permute-start(bf16[16,2880]{1,0:T(8,128)(2,1)S(1)} %get-tuple-element.25), channel_id=1, source_target_pairs={{0,6},{1,7},{2,4},{3,5},{4,2},{5,3},{6,0},{7,1},{8,14},{9,15},{10,... | collective-permute-start | bytes 276488 | tf_op jit(solution)/shard_map/ppermute | solution.py:208
  28.5 0.9 %collective-permute-start.14 = (bf16[16,2880]{1,0:T(8,128)(2,1)S(1)}, bf16[16,2880]{1,0:T(8,128)(2,1)S(1)}, u32[]{:S(2)}, u32[]{:S(2)}) collective-permute-start(bf16[16,2880]{1,0:T(8,128)(2,1)S(1)} %get-tuple-element.27), channel_id=1, source_target_pairs={{0,2},{1,3},{2,0},{3,1},{4,6},{5,7},{6,4},{7,5},{8,10},{9,11},{10,... | collective-permute-start | bytes 276488 | tf_op jit(solution)/shard_map/ppermute | solution.py:208
  29.4 0.0 collective-permute-done.18
  29.4 0.1 add_convert_fusion
  29.5 1.2 %collective-permute-start.19 = (bf16[16,2880]{1,0:T(8,128)(2,1)S(1)}, bf16[16,2880]{1,0:T(8,128)(2,1)S(1)}, u32[]{:S(2)}, u32[]{:S(2)}) collective-permute-start(bf16[16,2880]{1,0:T(8,128)(2,1)S(1)} %get-tuple-element.29), channel_id=1, source_target_pairs={{0,2},{1,3},{2,0},{3,1},{4,6},{5,7},{6,4},{7,5},{8,10},{9,11},{10,... | collective-permute-start | bytes 276488 | tf_op jit(solution)/shard_map/ppermute | solution.py:208
  30.7 0.0 collective-permute-done.12.table_ref
  30.7 2.2 %collective-permute-start.21 = (bf16[16,2880]{1,0:T(8,128)(2,1)S(1)}, bf16[16,2880]{1,0:T(8,128)(2,1)S(1)}, u32[]{:S(2)}, u32[]{:S(2)}) collective-permute-start(bf16[16,2880]{1,0:T(8,128)(2,1)S(1)} %get-tuple-element.30), channel_id=1, source_target_pairs={{0,6},{1,7},{2,4},{3,5},{4,2},{5,3},{6,0},{7,1},{8,14},{9,15},{10,... | collective-permute-start | bytes 276488 | tf_op jit(solution)/shard_map/ppermute | solution.py:208
  32.9 0.0 collective-permute-done.16.refs_3_
  32.9 1.2 %collective-permute-start.20 = (bf16[16,2880]{1,0:T(8,128)(2,1)S(1)}, bf16[16,2880]{1,0:T(8,128)(2,1)S(1)}, u32[]{:S(2)}, u32[]{:S(2)}) collective-permute-start(bf16[16,2880]{1,0:T(8,128)(2,1)S(1)} %get-tuple-element.31), channel_id=1, source_target_pairs={{0,4},{1,5},{2,6},{3,7},{4,0},{5,1},{6,2},{7,3},{8,12},{9,13},{10,... | collective-permute-start | bytes 276488 | tf_op jit(solution)/shard_map/ppermute | solution.py:208
  34.1 1.2 %collective-permute-done.14.refs_1_ = bf16[16,2880]{1,0:T(8,128)(2,1)S(1)} collective-permute-done((bf16[16,2880]{1,0:T(8,128)(2,1)S(1)}, bf16[16,2880]{1,0:T(8,128)(2,1)S(1)}, u32[]{:S(2)}, u32[]{:S(2)}) %collective-permute-start.14) | collective-permute-done | bytes 92192 | tf_op jit(solution)/shard_map/ppermute | solution.py:208
  35.3 0.1 shard_map.77
  35.5 1.2 %collective-permute-start.17 = (bf16[16,2880]{1,0:T(8,128)(2,1)S(1)}, bf16[16,2880]{1,0:T(8,128)(2,1)S(1)}, u32[]{:S(2)}, u32[]{:S(2)}) collective-permute-start(bf16[16,2880]{1,0:T(8,128)(2,1)S(1)} %shard_map.77), channel_id=1, source_target_pairs={{0,8},{1,9},{2,10},{3,11},{4,12},{5,13},{6,14},{7,15},{8,0},{9,1},... | collective-permute-start | bytes 276488 | tf_op jit(solution)/shard_map/ppermute | solution.py:208
  36.7 0.2 slice_reduce_fusion.3
  36.9 1.0 %collective-permute-done.19 = bf16[16,2880]{1,0:T(8,128)(2,1)S(1)} collective-permute-done((bf16[16,2880]{1,0:T(8,128)(2,1)S(1)}, bf16[16,2880]{1,0:T(8,128)(2,1)S(1)}, u32[]{:S(2)}, u32[]{:S(2)}) %collective-permute-start.19) | collective-permute-done | bytes 92192 | tf_op jit(solution)/shard_map/ppermute | solution.py:208
  37.9 0.7 %collective-permute-done.20 = bf16[16,2880]{1,0:T(8,128)(2,1)S(1)} collective-permute-done((bf16[16,2880]{1,0:T(8,128)(2,1)S(1)}, bf16[16,2880]{1,0:T(8,128)(2,1)S(1)}, u32[]{:S(2)}, u32[]{:S(2)}) %collective-permute-start.20) | collective-permute-done | bytes 92192 | tf_op jit(solution)/shard_map/ppermute | solution.py:208
  38.6 2.4 %collective-permute-done.17 = bf16[16,2880]{1,0:T(8,128)(2,1)S(1)} collective-permute-done((bf16[16,2880]{1,0:T(8,128)(2,1)S(1)}, bf16[16,2880]{1,0:T(8,128)(2,1)S(1)}, u32[]{:S(2)}, u32[]{:S(2)}) %collective-permute-start.17) | collective-permute-done | bytes 92192 | tf_op jit(solution)/shard_map/ppermute | solution.py:208
  41.0 0.8 %add_convert_fusion.2 = bf16[16,2880]{1,0:T(8,128)(2,1)} fusion(bf16[16,2880]{1,0:T(8,128)(2,1)S(1)} %collective-permute-done.21, bf16[16,2880]{1,0:T(8,128)(2,1)S(1)} %collective-permute-done.20, bf16[16,2880]{1,0:T(8,128)(2,1)S(1)} %collective-permute-done.19, bf16[16,2880]{1,0:T(8,128)(2,1)S(1)} %collective-permute-done.17, ...), kind=kLoop, calls=%fused_computation.2 | loop fusion | flops 737280 | bytes 645376 | tf_op jit(solution)/shard_map/convert_element_type | solution.py:241
  (15 shorter events, 0.1 us)
Async XLA Ops:
  0.0 8.8 %collective-permute-start = (bf16[16,2880]{1,0:T(8,128)(2,1)}, bf16[16,2880]{1,0:T(8,128)(2,1)S(1)}, u32[]{:S(2)}, u32[]{:S(2)}) collective-permute-start(bf16[16,2880]{1,0:T(8,128)(2,1)} %refs_4_.1), channel_id=1, source_target_pairs={{0,8},{1,9},{2,10},{3,11},{4,12},{5,13},{6,14},{7,15},{8,0},{9,1},... | collective-permute-start | bytes 276488 | tf_op jit(solution)/shard_map/ppermute | solution.py:208
  4.0 8.0 %collective-permute-start.9 = (bf16[16,2880]{1,0:T(8,128)(2,1)}, bf16[16,2880]{1,0:T(8,128)(2,1)S(1)}, u32[]{:S(2)}, u32[]{:S(2)}) collective-permute-start(bf16[16,2880]{1,0:T(8,128)(2,1)} %refs_4_.1), channel_id=1, source_target_pairs={{0,4},{1,5},{2,6},{3,7},{4,0},{5,1},{6,2},{7,3},{8,12},{9,13},{10,... | collective-permute-start | bytes 276488 | tf_op jit(solution)/shard_map/ppermute | solution.py:208
  5.6 6.8 %collective-permute-start.8 = (bf16[16,2880]{1,0:T(8,128)(2,1)}, bf16[16,2880]{1,0:T(8,128)(2,1)S(1)}, u32[]{:S(2)}, u32[]{:S(2)}) collective-permute-start(bf16[16,2880]{1,0:T(8,128)(2,1)} %refs_4_.1), channel_id=1, source_target_pairs={{0,2},{1,3},{2,0},{3,1},{4,6},{5,7},{6,4},{7,5},{8,10},{9,11},{10,... | collective-permute-start | bytes 276488 | tf_op jit(solution)/shard_map/ppermute | solution.py:208
  7.1 6.7 %collective-permute-start.10 = (bf16[16,2880]{1,0:T(8,128)(2,1)}, bf16[16,2880]{1,0:T(8,128)(2,1)S(1)}, u32[]{:S(2)}, u32[]{:S(2)}) collective-permute-start(bf16[16,2880]{1,0:T(8,128)(2,1)} %refs_4_.1), channel_id=1, source_target_pairs={{0,6},{1,7},{2,4},{3,5},{4,2},{5,3},{6,0},{7,1},{8,14},{9,15},{10,... | collective-permute-start | bytes 276488 | tf_op jit(solution)/shard_map/ppermute | solution.py:208
  7.5 9.3 %copy-start.3 = (bf16[16,2880]{1,0:T(8,128)(2,1)S(1)}, bf16[16,2880]{1,0:T(8,128)(2,1)}, u32[]{:S(2)}) copy-start(bf16[16,2880]{1,0:T(8,128)(2,1)} %refs_4_.1) | copy-start | bytes 276484
  7.5 11.7 %copy-start = (bf16[1,2880,720]{1,2,0:T(8,128)(2,1)S(1)}, bf16[1,2880,720]{1,2,0:T(8,128)(2,1)}, u32[]{:S(2)}) copy-start(bf16[1,2880,720]{1,2,0:T(8,128)(2,1)} %param.11) | copy-start | bytes 12441604
  7.5 11.7 %copy-start.1 = (bf16[1,2880,720]{1,2,0:T(8,128)(2,1)S(1)}, bf16[1,2880,720]{1,2,0:T(8,128)(2,1)}, u32[]{:S(2)}) copy-start(bf16[1,2880,720]{1,2,0:T(8,128)(2,1)} %param.12) | copy-start | bytes 12441604
  7.5 11.7 %copy-start.2 = (bf16[1,720,2880]{2,1,0:T(8,128)(2,1)S(1)}, bf16[1,720,2880]{2,1,0:T(8,128)(2,1)}, u32[]{:S(2)}) copy-start(bf16[1,720,2880]{2,1,0:T(8,128)(2,1)} %param.13) | copy-start | bytes 12441604
  8.9 6.9 %collective-permute-start.6 = (bf16[16,2880]{1,0:T(8,128)(2,1)S(1)}, bf16[16,2880]{1,0:T(8,128)(2,1)S(1)}, u32[]{:S(2)}, u32[]{:S(2)}) collective-permute-start(bf16[16,2880]{1,0:T(8,128)(2,1)S(1)} %shard_map.74.refs_4_), channel_id=1, source_target_pairs={{0,6},{1,7},{2,4},{3,5},{4,2},{5,3},{6,0},{7,1},{8,14},{9,15},{10,... | collective-permute-start | bytes 276488 | tf_op jit(solution)/shard_map/ppermute | solution.py:208
  11.3 5.0 %collective-permute-start.4 = (bf16[16,2880]{1,0:T(8,128)(2,1)S(1)}, bf16[16,2880]{1,0:T(8,128)(2,1)S(1)}, u32[]{:S(2)}, u32[]{:S(2)}) collective-permute-start(bf16[16,2880]{1,0:T(8,128)(2,1)S(1)} %shard_map.74.refs_4_), channel_id=1, source_target_pairs={{0,4},{1,5},{2,6},{3,7},{4,0},{5,1},{6,2},{7,3},{8,12},{9,13},{10,... | collective-permute-start | bytes 276488 | tf_op jit(solution)/shard_map/ppermute | solution.py:208
  12.1 4.8 %collective-permute-start.2 = (bf16[16,2880]{1,0:T(8,128)(2,1)S(1)}, bf16[16,2880]{1,0:T(8,128)(2,1)S(1)}, u32[]{:S(2)}, u32[]{:S(2)}) collective-permute-start(bf16[16,2880]{1,0:T(8,128)(2,1)S(1)} %shard_map.74.refs_4_), channel_id=1, source_target_pairs={{0,2},{1,3},{2,0},{3,1},{4,6},{5,7},{6,4},{7,5},{8,10},{9,11},{10,... | collective-permute-start | bytes 276488 | tf_op jit(solution)/shard_map/ppermute | solution.py:208
  12.5 4.4 %collective-permute-start.1 = (bf16[16,2880]{1,0:T(8,128)(2,1)S(1)}, bf16[16,2880]{1,0:T(8,128)(2,1)S(1)}, u32[]{:S(2)}, u32[]{:S(2)}) collective-permute-start(bf16[16,2880]{1,0:T(8,128)(2,1)S(1)} %shard_map.74.refs_4_), channel_id=1, source_target_pairs={{0,1},{1,0},{2,3},{3,2},{4,5},{5,4},{6,7},{7,6},{8,9},{9,8},{10,11... | collective-permute-start | bytes 276488 | tf_op jit(solution)/shard_map/ppermute | solution.py:14
  17.1 2.2 %collective-permute-start.11 = (bf16[64,2880]{1,0:T(8,128)(2,1)S(1)}, bf16[64,2880]{1,0:T(8,128)(2,1)S(1)}, u32[]{:S(2)}, u32[]{:S(2)}) collective-permute-start(bf16[64,2880]{1,0:T(8,128)(2,1)S(1)} %shard_map.75.refs_9_), channel_id=1, source_target_pairs={{0,1},{1,0},{2,3},{3,2},{4,5},{5,4},{6,7},{7,6},{8,9},{9,8},{10,11... | collective-permute-start | bytes 1105928 | tf_op jit(solution)/shard_map/ppermute | solution.py:14
  17.1 1.8 %collective-permute-start.7 = (bf16[16,2880]{1,0:T(8,128)(2,1)S(1)}, bf16[16,2880]{1,0:T(8,128)(2,1)S(1)}, u32[]{:S(2)}, u32[]{:S(2)}) collective-permute-start(bf16[16,2880]{1,0:T(8,128)(2,1)S(1)} %collective-permute-done.6.refs_3_.refs_7_), channel_id=1, source_target_pairs={{0,1},{1,0},{2,3},{3,2},{4,5},{5,4},{6,7},{7,6},{8,9},{9,8},{10,11... | collective-permute-start | bytes 276488 | tf_op jit(solution)/shard_map/ppermute | solution.py:14
  17.6 1.5 %collective-permute-start.5 = (bf16[16,2880]{1,0:T(8,128)(2,1)S(1)}, bf16[16,2880]{1,0:T(8,128)(2,1)S(1)}, u32[]{:S(2)}, u32[]{:S(2)}) collective-permute-start(bf16[16,2880]{1,0:T(8,128)(2,1)S(1)} %collective-permute-done.4.refs_2_.refs_6_), channel_id=1, source_target_pairs={{0,1},{1,0},{2,3},{3,2},{4,5},{5,4},{6,7},{7,6},{8,9},{9,8},{10,11... | collective-permute-start | bytes 276488 | tf_op jit(solution)/shard_map/ppermute | solution.py:14
  17.7 1.5 %collective-permute-start.3 = (bf16[16,2880]{1,0:T(8,128)(2,1)S(1)}, bf16[16,2880]{1,0:T(8,128)(2,1)S(1)}, u32[]{:S(2)}, u32[]{:S(2)}) collective-permute-start(bf16[16,2880]{1,0:T(8,128)(2,1)S(1)} %collective-permute-done.2.refs_1_.refs_5_), channel_id=1, source_target_pairs={{0,1},{1,0},{2,3},{3,2},{4,5},{5,4},{6,7},{7,6},{8,9},{9,8},{10,11... | collective-permute-start | bytes 276488 | tf_op jit(solution)/shard_map/ppermute | solution.py:14
  23.0 2.6 %collective-permute-start.13 = (bf16[64,2880]{1,0:T(8,128)(2,1)S(1)}, bf16[64,2880]{1,0:T(8,128)(2,1)S(1)}, u32[]{:S(2)}, u32[]{:S(2)}) collective-permute-start(bf16[64,2880]{1,0:T(8,128)(2,1)S(1)} %get-tuple-element.18), channel_id=1, source_target_pairs={{0,1},{1,0},{2,3},{3,2},{4,5},{5,4},{6,7},{7,6},{8,9},{9,8},{10,11... | collective-permute-start | bytes 1105928 | tf_op jit(solution)/shard_map/ppermute | solution.py:14
  23.3 7.4 %collective-permute-start.12 = (f32[16,4]{1,0:T(8,128)S(1)}, f32[16,4]{1,0:T(8,128)S(1)}, u32[]{:S(2)}, u32[]{:S(2)}) collective-permute-start(f32[16,4]{1,0:T(8,128)S(1)} %get-tuple-element.16), channel_id=1, source_target_pairs={{0,8},{1,9},{2,10},{3,11},{4,12},{5,13},{6,14},{7,15},{8,0},{9,1},... | collective-permute-start | bytes 776 | tf_op jit(solution)/shard_map/ppermute | solution.py:208
  25.6 3.7 %collective-permute-start.18 = (bf16[64,2880]{1,0:T(8,128)(2,1)S(1)}, bf16[64,2880]{1,0:T(8,128)(2,1)S(1)}, u32[]{:S(2)}, u32[]{:S(2)}) collective-permute-start(bf16[64,2880]{1,0:T(8,128)(2,1)S(1)} %get-tuple-element.20), channel_id=1, source_target_pairs={{0,1},{1,0},{2,3},{3,2},{4,5},{5,4},{6,7},{7,6},{8,9},{9,8},{10,11... | collective-permute-start | bytes 1105928 | tf_op jit(solution)/shard_map/ppermute | solution.py:14
  25.8 7.1 %collective-permute-start.16 = (bf16[16,2880]{1,0:T(8,128)(2,1)S(1)}, bf16[16,2880]{1,0:T(8,128)(2,1)S(1)}, u32[]{:S(2)}, u32[]{:S(2)}) collective-permute-start(bf16[16,2880]{1,0:T(8,128)(2,1)S(1)} %get-tuple-element.25), channel_id=1, source_target_pairs={{0,6},{1,7},{2,4},{3,5},{4,2},{5,3},{6,0},{7,1},{8,14},{9,15},{10,... | collective-permute-start | bytes 276488 | tf_op jit(solution)/shard_map/ppermute | solution.py:208
  28.4 5.7 %collective-permute-start.15 = (bf16[16,2880]{1,0:T(8,128)(2,1)S(1)}, bf16[16,2880]{1,0:T(8,128)(2,1)S(1)}, u32[]{:S(2)}, u32[]{:S(2)}) collective-permute-start(bf16[16,2880]{1,0:T(8,128)(2,1)S(1)} %get-tuple-element.26), channel_id=1, source_target_pairs={{0,4},{1,5},{2,6},{3,7},{4,0},{5,1},{6,2},{7,3},{8,12},{9,13},{10,... | collective-permute-start | bytes 276488 | tf_op jit(solution)/shard_map/ppermute | solution.py:208
  28.5 6.9 %collective-permute-start.14 = (bf16[16,2880]{1,0:T(8,128)(2,1)S(1)}, bf16[16,2880]{1,0:T(8,128)(2,1)S(1)}, u32[]{:S(2)}, u32[]{:S(2)}) collective-permute-start(bf16[16,2880]{1,0:T(8,128)(2,1)S(1)} %get-tuple-element.27), channel_id=1, source_target_pairs={{0,2},{1,3},{2,0},{3,1},{4,6},{5,7},{6,4},{7,5},{8,10},{9,11},{10,... | collective-permute-start | bytes 276488 | tf_op jit(solution)/shard_map/ppermute | solution.py:208
  29.5 8.4 %collective-permute-start.19 = (bf16[16,2880]{1,0:T(8,128)(2,1)S(1)}, bf16[16,2880]{1,0:T(8,128)(2,1)S(1)}, u32[]{:S(2)}, u32[]{:S(2)}) collective-permute-start(bf16[16,2880]{1,0:T(8,128)(2,1)S(1)} %get-tuple-element.29), channel_id=1, source_target_pairs={{0,2},{1,3},{2,0},{3,1},{4,6},{5,7},{6,4},{7,5},{8,10},{9,11},{10,... | collective-permute-start | bytes 276488 | tf_op jit(solution)/shard_map/ppermute | solution.py:208
  30.7 7.2 %collective-permute-start.21 = (bf16[16,2880]{1,0:T(8,128)(2,1)S(1)}, bf16[16,2880]{1,0:T(8,128)(2,1)S(1)}, u32[]{:S(2)}, u32[]{:S(2)}) collective-permute-start(bf16[16,2880]{1,0:T(8,128)(2,1)S(1)} %get-tuple-element.30), channel_id=1, source_target_pairs={{0,6},{1,7},{2,4},{3,5},{4,2},{5,3},{6,0},{7,1},{8,14},{9,15},{10,... | collective-permute-start | bytes 276488 | tf_op jit(solution)/shard_map/ppermute | solution.py:208
  32.9 5.7 %collective-permute-start.20 = (bf16[16,2880]{1,0:T(8,128)(2,1)S(1)}, bf16[16,2880]{1,0:T(8,128)(2,1)S(1)}, u32[]{:S(2)}, u32[]{:S(2)}) collective-permute-start(bf16[16,2880]{1,0:T(8,128)(2,1)S(1)} %get-tuple-element.31), channel_id=1, source_target_pairs={{0,4},{1,5},{2,6},{3,7},{4,0},{5,1},{6,2},{7,3},{8,12},{9,13},{10,... | collective-permute-start | bytes 276488 | tf_op jit(solution)/shard_map/ppermute | solution.py:208
  35.5 5.5 %collective-permute-start.17 = (bf16[16,2880]{1,0:T(8,128)(2,1)S(1)}, bf16[16,2880]{1,0:T(8,128)(2,1)S(1)}, u32[]{:S(2)}, u32[]{:S(2)}) collective-permute-start(bf16[16,2880]{1,0:T(8,128)(2,1)S(1)} %shard_map.77), channel_id=1, source_target_pairs={{0,8},{1,9},{2,10},{3,11},{4,12},{5,13},{6,14},{7,15},{8,0},{9,1},... | collective-permute-start | bytes 276488 | tf_op jit(solution)/shard_map/ppermute | solution.py:208
